TPU v7x, 32 devices: a whole 2x2x4 slice. The times are simulated.
32 devices in a mesh: dp: 2 (over y), seq: 16 (over z, x, core).
Axes of the slice: x: 2, y: 2, z: 4, core: 2. Of those that a mesh axis runs over, the one named last changes fastest.
Arguments:
- queries: bfloat16 [2, 2048, 1536], P('dp', 'seq'), may hold values from -6 to 6
- keys: bfloat16 [2, 2048, 1536], P('dp', 'seq'), may hold values from -6 to 6
- values: bfloat16 [2, 2048, 1536], P('dp', 'seq'), may hold values from -6 to 6
- segment_ids: int32 [2, 2048], P('dp'), may hold values from 0 to 31, never falling along the last dimension, each value on 1 to 128 neighbouring positions
- norm_gain: float32 [1536], replicated, may hold values from 0.25 to 1.75
- conv_kernel: float32 [31, 1536], replicated, may hold values from -1 to 1
- conv_bias: float32 [1536], replicated, may hold values from -3 to 3
- cotangent: bfloat16 [2, 2048, 1536], P('dp', 'seq'), may hold values from -6 to 6
Outputs:
- conv_out: bfloat16 [2, 2048, 1536], P('dp', 'seq')
- query_grad: bfloat16 [2, 2048, 1536], P('dp', 'seq')
- key_grad: bfloat16 [2, 2048, 1536], P('dp', 'seq')
- value_grad: bfloat16 [2, 2048, 1536], P('dp', 'seq')
- gain_grad: float32 [1536], replicated
- kernel_grad: float32 [31, 1536], replicated
- bias_grad: float32 [1536], replicated
Inputs may be any that keep to these rules, and one draw needn't show every extreme that they name: `segment_ids`: within each row, utterance numbers never fall; each utterance holds 1 to 128 frames, and some utterance exactly 128.
All inputs are finite; a program needn't handle non-finite values.
Results may differ from a plain program's by a relative error of at most 0.023.
Values may be sent and summed in bfloat16 or wider, within the bound.
No kernel may reach another device: no remote copies, remote signals or barrier semaphores. Data moves between devices by JAX's collectives and lax.ppermute only.
A program may use at most 64 MiB of HBM per device.

v0:
```python
import jax
import jax.numpy as jnp
from jax import lax
from jax.sharding import PartitionSpec as P

HEADS = 24
HEAD_DIM = 64
HEAD_BLOCK = 4
REACH = 1


EPS = 1e-05
NEG = -1e30


def shifted(block, axis, distance):
    devices = range(lax.axis_size(axis))
    route = [(i - distance, i) for i in devices if i - distance in devices]
    return lax.ppermute(block, axis, route)


def with_halo(cells, sides, width):
    for axis, dim in sides:
        count = lax.axis_size(axis)
        ends = count - 1
        head = lax.slice_in_dim(cells, 0, width, axis=dim)
        tail = lax.slice_in_dim(cells, cells.shape[dim] - width, cells.shape[dim], axis=dim)
        cells = jnp.concatenate(
            [
                lax.ppermute(tail, axis, [(i, (i + 1) % count) for i in range(ends)]),
                cells,
                lax.ppermute(head, axis, [((i + 1) % count, i) for i in range(ends)]),
            ],
            axis=dim,
        )
    return cells


def to_groups(tensor, block):
    rows_in, heads_in, dim_in = tensor.shape
    return tensor.reshape(rows_in, heads_in // block, block, dim_in).transpose(1, 0, 2, 3)


def from_groups(tensor):
    groups_in, rows_in, block, dim_in = tensor.shape
    return tensor.transpose(1, 0, 2, 3).reshape(rows_in, groups_in * block * dim_in)


def masked_logits(query_rows, key_rows, same_seg):
    factor = query_rows.shape[-1] ** (-0.5)
    logits = (
        jnp.einsum("qhe,khe->hqk", query_rows, key_rows, preferred_element_type=jnp.float32)
        * factor
    )
    return jnp.where(same_seg[None], logits, NEG)


def forward_block(query_rows, key_rows, value_rows, same_seg):
    logits = masked_logits(query_rows, key_rows, same_seg)
    row_top = jnp.max(logits, -1, keepdims=True)
    exponent = jnp.exp(logits - row_top)
    row_total = jnp.sum(exponent, -1, keepdims=True)
    attn_weights = (exponent / row_total).astype(jnp.bfloat16)
    context = jnp.einsum(
        "hqk,khe->qhe", attn_weights, value_rows, preferred_element_type=jnp.float32
    )
    return (context, (row_top + jnp.log(row_total))[..., 0])


def back_terms(query_rows, key_rows, value_rows, grad_rows, log_total, row_delta, same_seg):
    factor = query_rows.shape[-1] ** (-0.5)
    logits = masked_logits(query_rows, key_rows, same_seg)
    prob_back = jnp.exp(logits - log_total[:, :, None])
    grad_prob = jnp.einsum(
        "qhe,khe->hqk", grad_rows, value_rows, preferred_element_type=jnp.float32
    )
    grad_logit = (prob_back * (grad_prob - row_delta[:, :, None]) * factor).astype(jnp.bfloat16)
    return (prob_back.astype(jnp.bfloat16), grad_logit)


def per_device(queries, keys, values, segment_ids, norm_gain, conv_kernel, conv_bias, cotangent):
    frame_count = queries.shape[1]
    width = queries.shape[2]
    reach_rows = REACH * frame_count
    tap_count = conv_kernel.shape[0]
    half_taps = tap_count // 2
    block = HEAD_BLOCK
    group_count = HEADS // block
    start_row = lax.axis_index("seq") * frame_count
    seg_row = segment_ids[0]
    seg_padded = jnp.pad(seg_row, (reach_rows, reach_rows), constant_values=-1)
    own_seg = lax.dynamic_slice_in_dim(seg_row, start_row, frame_count)
    window_seg = lax.dynamic_slice_in_dim(seg_padded, start_row, frame_count + 2 * reach_rows)
    conv_seg = lax.dynamic_slice_in_dim(
        seg_padded, start_row + reach_rows - half_taps, frame_count + 2 * half_taps
    )
    same_fwd = own_seg[:, None] == window_seg[None, :]
    query_heads = queries[0].reshape(frame_count, HEADS, HEAD_DIM)
    key_value = jnp.stack((keys[0], values[0]), 1)
    lower_parts = []
    upper_parts = []
    hop = 1
    for offset_by in (hop, -hop):
        arrived = shifted(key_value, "seq", offset_by)
        if offset_by > 0:
            lower_parts.insert(0, arrived)
        else:
            upper_parts.append(arrived)
    key_value_wide = jnp.concatenate(lower_parts + [key_value] + upper_parts, 0)
    query_groups = to_groups(query_heads, block)
    key_groups = to_groups(key_value_wide[:, 0].reshape(-1, HEADS, HEAD_DIM), block)
    value_groups = to_groups(key_value_wide[:, 1].reshape(-1, HEADS, HEAD_DIM), block)

    def forward_group(operands):
        return forward_block(operands[0], operands[1], operands[2], same_fwd)

    context_groups, total_groups = lax.map(forward_group, (query_groups, key_groups, value_groups))
    context = from_groups(context_groups).astype(jnp.bfloat16)
    context_f = context.astype(jnp.float32)
    row_mean = jnp.mean(context_f, -1, keepdims=True)
    centred = context_f - row_mean
    inv_std = lax.rsqrt(jnp.mean(centred * centred, -1, keepdims=True) + EPS)
    normed = centred * inv_std
    conv_in = (normed * norm_gain).astype(jnp.bfloat16)
    conv_wide = with_halo(conv_in, (("seq", 0),), half_taps).astype(jnp.float32)
    same_taps = [
        (conv_seg[tap_index : tap_index + frame_count] == own_seg)[:, None]
        for tap_index in range(tap_count)
    ]
    pre_act = jnp.broadcast_to(conv_bias, (frame_count, width))
    for tap_index in range(tap_count):
        pre_act = pre_act + conv_kernel[tap_index] * jnp.where(
            same_taps[tap_index], conv_wide[tap_index : tap_index + frame_count], 0.0
        )
    gate_sig = jax.nn.sigmoid(pre_act)
    conv_out = (pre_act * gate_sig).astype(jnp.bfloat16)
    grad_pre = (
        cotangent[0].astype(jnp.float32) * gate_sig * (1.0 + pre_act * (1.0 - gate_sig))
    ).astype(jnp.bfloat16)
    grad_pre_f = grad_pre.astype(jnp.float32)
    bias_part = jnp.sum(grad_pre_f, 0)
    kernel_rows = []
    for tap_index in range(tap_count):
        kernel_rows.append(
            jnp.sum(
                jnp.where(
                    same_taps[tap_index],
                    conv_wide[tap_index : tap_index + frame_count] * grad_pre_f,
                    0.0,
                ),
                0,
            )
        )
    kernel_part = jnp.stack(kernel_rows, 0)
    grad_wide = with_halo(grad_pre, (("seq", 0),), half_taps).astype(jnp.float32)
    grad_in = jnp.zeros((frame_count, width), jnp.float32)
    for tap_index in range(tap_count):
        mirror = 2 * half_taps - tap_index
        grad_in = grad_in + conv_kernel[tap_index] * jnp.where(
            same_taps[mirror], grad_wide[mirror : mirror + frame_count], 0.0
        )
    gain_part = jnp.sum(grad_in * normed, 0)
    grad_norm = grad_in * norm_gain
    grad_context = (
        (
            grad_norm
            - jnp.mean(grad_norm, -1, keepdims=True)
            - normed * jnp.mean(grad_norm * normed, -1, keepdims=True)
        )
        * inv_std
    ).astype(jnp.bfloat16)
    row_delta = jnp.sum(
        (grad_context.astype(jnp.float32) * context_f).reshape(frame_count, HEADS, HEAD_DIM), -1
    )
    delta_groups = row_delta.T.reshape(group_count, block, frame_count)
    grad_groups = to_groups(grad_context.reshape(frame_count, HEADS, HEAD_DIM), block)

    def backward_group(operands):
        query_rows, key_rows, value_rows, grad_rows, log_total, delta_rows = operands
        prob_low, grad_logit = back_terms(
            query_rows, key_rows, value_rows, grad_rows, log_total, delta_rows, same_fwd
        )
        query_part = jnp.einsum(
            "hqk,khe->qhe", grad_logit, key_rows, preferred_element_type=jnp.float32
        )
        key_part = jnp.einsum(
            "hqk,qhe->khe", grad_logit, query_rows, preferred_element_type=jnp.float32
        )
        value_part = jnp.einsum(
            "hqk,qhe->khe", prob_low, grad_rows, preferred_element_type=jnp.float32
        )
        return (query_part, key_part, value_part)

    query_blocks, key_blocks, value_blocks = lax.map(
        backward_group,
        (query_groups, key_groups, value_groups, grad_groups, total_groups, delta_groups),
    )
    key_value_grad = jnp.stack((from_groups(key_blocks), from_groups(value_blocks)), 1)
    own_grad = key_value_grad[reach_rows : reach_rows + frame_count]
    hop = 1
    for offset_by in (hop, -hop):
        if offset_by > 0:
            moved_piece = key_value_grad[
                (REACH + hop) * frame_count : (REACH + hop + 1) * frame_count
            ]
        else:
            moved_piece = key_value_grad[
                (REACH - hop) * frame_count : (REACH - hop + 1) * frame_count
            ]
        own_grad = own_grad + shifted(moved_piece.astype(jnp.bfloat16), "seq", offset_by).astype(
            moved_piece.dtype
        )
    key_grad = own_grad[:, 0]
    value_grad = own_grad[:, 1]
    query_grad = from_groups(query_blocks)
    gain_sum, kernel_sum, bias_sum = lax.psum((gain_part, kernel_part, bias_part), ("dp", "seq"))
    norm_factor = (lax.axis_size("dp") * lax.axis_size("seq") * frame_count) ** (-0.5)
    return (
        conv_out[None],
        query_grad.astype(jnp.bfloat16)[None],
        key_grad.astype(jnp.bfloat16)[None],
        value_grad.astype(jnp.bfloat16)[None],
        gain_sum * norm_factor,
        kernel_sum * norm_factor,
        bias_sum * norm_factor,
    )


def solution(mesh):
    placed = (
        P("dp", "seq", None),
        P("dp", "seq", None),
        P("dp", "seq", None),
        P("dp", None),
        P(),
        P(),
        P(),
        P("dp", "seq", None),
    )
    return jax.shard_map(
        per_device,
        mesh=mesh,
        in_specs=placed,
        out_specs=(
            P("dp", "seq", None),
            P("dp", "seq", None),
            P("dp", "seq", None),
            P("dp", "seq", None),
            P(),
            P(),
            P(),
        ),
        check_vma=False,
    )
```

profile of v0, /device:TPU:12, one launch (start us, length us, event | category | flops | bytes accessed | tf_op | source)
XLA Modules:
  0.0 272.9 jit_solution(13279747715882612665)
XLA Ops:
  7.3 1.3 pad_maximum_fusion.2
  8.5 2.7 collective-permute-start.1
  11.3 1.9 collective-permute-start
  13.2 2.5 slice_reduce_fusion.30
  18.9 1.9 collective-permute-done.1
  20.8 4.8 %collective-permute-done = bf16[128,2,1536]{2,0,1:T(8,128)(2,1)S(1)} collective-permute-done((bf16[128,2,1536]{2,0,1:T(8,128)(2,1)S(1)}, bf16[128,2,1536]{2,0,1:T(8,128)(2,1)S(1)}, u32[]{:S(2)}, u32[]{:S(2)}) %collective-permute-start) | collective-permute-done | bytes 786464 | tf_op jit(solution)/shard_map/ppermute | solution.py:19
  26.6 1.4 copy.23
  28.1 21.4 %while.28 = (s32[]{:T(128)}, bf16[6,128,4,64]{1,3,2,0:T(8,128)(2,1)S(1)}, f32[6,4,128]{2,1,0:T(4,128)}, bf16[6,384,4,64]{1,3,2,0:T(8,128)(2,1)}, bf16[6,128,4,64...) while((s32[]{:T(128)}, ...), condition=%wide.region_3.4_spmd.clone, body=%wide.region_0.3_spmd.clone.sunk | while | flops 51953152 | bytes 3068009 | solution.py:117
  28.3 1.2 fusion.223
  29.8 1.3 fusion.225
  31.8 1.2 fusion.223
  33.4 1.3 fusion.225
  35.4 1.2 fusion.223
  36.9 1.3 fusion.225
  38.9 1.2 fusion.223
  40.5 1.3 fusion.225
  42.5 1.2 fusion.223
  44.0 1.3 fusion.225
  46.1 1.2 fusion.223
  47.6 1.3 fusion.225
  51.3 6.6 %collective-permute-start.2 = (bf16[15,1536]{0,1:T(8,128)(2,1)}, bf16[15,1536]{0,1:T(8,128)(2,1)}, u32[]{:S(2)}, u32[]{:S(2)}) collective-permute-start(bf16[15,1536]{0,1:T(8,128)(2,1)} %get-tuple-element.291), channel_id=1, source_target_pairs={{0,1},{1,2},{2,3},{3,4},{4,5},{5,6},{6,7},{7,8},{8,9},{9,10},{10,1... | collective-permute-start | bytes 138248 | tf_op jit(solution)/shard_map/ppermute | solution.py:30
  58.0 2.1 collective-permute-start.3
  60.1 2.1 slice_reduce_fusion.29
  63.8 1.7 collective-permute-done.3
  65.5 1.6 maximum_convert_fusion
  67.5 18.6 %fusion.110 = (f32[1536]{0:T(1024)S(1)}, f32[1536]{0:T(1024)S(1)}, f32[1536]{0:T(1024)S(1)}, f32[1536]{0:T(1024)S(1)}, f32[1536]{0:T(1024)S(1)}, /*index=5*/f32[...) fusion(f32[158,1536]{0,1:T(8,128)S(1)} %maximum_convert_fusion,, ...), kind=kLoop, calls=%fused_computation.158 | loop fusion | flops 25741824 | bytes 26208128 | tf_op jit(solution)/shard_map/reduce_sum | solution.py:145
  86.2 4.4 %fusion.112 = (f32[1536]{0:T(1024)S(1)}, f32[1536]{0:T(1024)S(1)}, f32[1536]{0:T(1024)S(1)}, f32[1536]{0:T(1024)S(1)}, f32[1536]{0:T(1024)S(1)}, /*index=5*/f32[...) fusion(bf16[128,1536]{0,1:T(8,128)(2,1)S(1)} %get-tuple-element.272, ...), kind=kLoop, calls=%fused_computation.160 | loop fusion | flops 5491200 | bytes 7527552 | tf_op jit(solution)/shard_map/reduce_sum | solution.py:145
  90.7 3.7 %fusion.114 = (f32[1536]{0:T(1024)S(1)}, f32[1536]{0:T(1024)S(1)}, f32[1536]{0:T(1024)S(1)}, f32[1536]{0:T(1024)S(1)}, f32[1536]{0:T(1024)S(1)}, /*index=5*/f32[...) fusion(bf16[128,1536]{0,1:T(8,128)(2,1)S(1)} %get-tuple-element.272, ...), kind=kLoop, calls=%fused_computation.162 | loop fusion | flops 5491200 | bytes 7527552 | tf_op jit(solution)/shard_map/reduce_sum | solution.py:145
  95.3 6.2 %collective-permute-start.4 = (bf16[15,1536]{0,1:T(8,128)(2,1)}, bf16[15,1536]{0,1:T(8,128)(2,1)}, u32[]{:S(2)}, u32[]{:S(2)}) collective-permute-start(bf16[15,1536]{0,1:T(8,128)(2,1)} %get-tuple-element.289), channel_id=1, source_target_pairs={{0,1},{1,2},{2,3},{3,4},{4,5},{5,6},{6,7},{7,8},{8,9},{9,10},{10,1... | collective-permute-start | bytes 138248 | tf_op jit(solution)/shard_map/ppermute | solution.py:30
  101.6 2.1 collective-permute-start.5
  103.8 2.2 fusion.108
  124.5 6.0 %stack.135 = f32[31,1536]{1,0:T(8,128)} concatenate(f32[1,1536]{1,0:T(1,128)} %stack.104, f32[1,1536]{1,0:T(1,128)} %stack.105, f32[1,1536]{1,0:T(1,128)} %stack.106, f32[1,1536]{1,0:T(1,128)} %stack.107, f32[1,1536]{1,0:T(1,128)} %stack.108, f32[1,1536]{1,0:T(1,128)} %stack.109, f32[1,1536]{1,0:T(1,128)} %stack.110, f32[1,1536]{1,0:T(1,128)} %stack.111, f32[1,1536]{1,0:T(1,128)} %stack.112, ...), dimensions={0} | concatenate | bytes 380928 | tf_op jit(solution)/shard_map/stack | solution.py:154
  130.5 1.6 maximum_convert_fusion.1
  132.0 19.2 %fusion.190 = (f32[1536]{0:T(1024)}, f32[128]{0:T(128)S(1)}, f32[128]{0:T(128)S(1)}, f32[128,1536]{0,1:T(8,128)S(1)}) fusion(bf16[6,128,4,64]{1,3,2,0:T(8,128)(2,1)S(1)} %get-tuple-element.104, f32[128]{0:T(128)} %copy-done.60, f32[128]{0:T(128)} %copy-done.58, f32[1536]{0:T(1024)} %param.16, f32[158,1536]{0,1:T(8,128)S(1)} %maximum_convert_fusion.1, ...), kind=kLoop, calls=%fused_computation.277 | loop fusion | flops 19855616 | bytes 25767808 | tf_op jit(solution)/shard_map/reduce_sum | solution.py:162
  153.1 45.3 %while.29 = (s32[]{:T(128)}, bf16[6,128,4,64]{1,3,2,0:T(8,128)(2,1)S(1)}, f32[6,384,4,64]{1,3,2,0:T(8,128)}, f32[6,384,4,64]{1,3,2,0:T(8,128)S(1)}, bf16[6,384,4...) while((s32[]{:T(128)}, ...), condition=%wide.region_10.11_spmd.clone, body=%wide.region_9.10_spmd.clone.sunk | while | flops 127451136 | bytes 5426313 | solution.py:194
  153.9 1.3 fusion.237
  155.2 1.3 fusion.238
  156.5 1.2 fusion.239
  158.8 1.8 fusion.240
  161.4 1.3 fusion.237
  162.7 1.3 fusion.238
  164.0 1.2 fusion.239
  166.3 1.8 fusion.240
  168.9 1.3 fusion.237
  170.3 1.3 fusion.238
  173.9 1.8 fusion.240
  176.5 1.3 fusion.237
  177.8 1.3 fusion.238
  179.1 1.2 fusion.239
  181.4 1.8 fusion.240
  184.0 1.3 fusion.237
  185.4 1.3 fusion.238
  189.0 1.8 fusion.240
  191.6 1.3 fusion.237
  192.9 1.3 fusion.238
  194.2 1.2 fusion.239
  196.5 1.8 fusion.240
  198.3 2.0 fusion.48
  200.4 1.5 fusion.196
  201.8 4.3 %collective-permute-start.6 = (bf16[128,2,1536]{0,2,1:T(8,128)(2,1)}, bf16[128,2,1536]{0,2,1:T(8,128)(2,1)}, u32[]{:S(2)}, u32[]{:S(2)}) collective-permute-start(bf16[128,2,1536]{0,2,1:T(8,128)(2,1)} %get-tuple-element.283), channel_id=1, source_target_pairs={{0,1},{1,2},{2,3},{3,4},{4,5},{5,6},{6,7},{7,8},{8,9},{9,10},{10,1... | collective-permute-start | bytes 2359304 | tf_op jit(solution)/shard_map/ppermute | solution.py:19
  206.2 2.2 collective-permute-start.7
  209.6 49.5 %all-reduce.1 = (f32[1536]{0:T(1024)S(1)}, f32[1536]{0:T(1024)S(1)}) all-reduce(f32[1536]{0:T(1024)S(1)} %copy-done.40, f32[1536]{0:T(1024)S(1)} %copy-done.39), channel_id=1, replica_groups=mesh['dp'=2,'seq'=16] {'dp','seq'}, use_global_device_ids=true, to_apply=%region_12.13 | all-reduce | flops 3072 | bytes 24576 | tf_op jit(solution)/shard_map/psum | solution.py:216
  260.7 1.6 broadcast_multiply_fusion
  262.3 1.9 fusion.52
  (233 shorter events, 52.9 us)
Async XLA Ops:
  7.2 18.4 %copy-start.2 = (bf16[1,128,1536]{2,1,0:T(8,128)(2,1)S(1)}, bf16[1,128,1536]{2,1,0:T(8,128)(2,1)}, u32[]{:S(2)}) copy-start(bf16[1,128,1536]{2,1,0:T(8,128)(2,1)} %param.14) | copy-start | bytes 1179652
  7.2 18.4 %copy-start.3 = (bf16[1,128,1536]{2,1,0:T(8,128)(2,1)S(1)}, bf16[1,128,1536]{2,1,0:T(8,128)(2,1)}, u32[]{:S(2)}) copy-start(bf16[1,128,1536]{2,1,0:T(8,128)(2,1)} %param.13) | copy-start | bytes 1179652
  7.2 8.5 %copy-start.38 = (s32[1,2048]{1,0:T(1,128)S(1)}, s32[1,2048]{1,0:T(1,128)}, u32[]{:S(2)}) copy-start(s32[1,2048]{1,0:T(1,128)} %param.15) | copy-start | bytes 24580
  7.2 8.6 %copy-start.4 = (bf16[1,128,1536]{2,1,0:T(8,128)(2,1)S(1)}, bf16[1,128,1536]{2,1,0:T(8,128)(2,1)}, u32[]{:S(2)}) copy-start(bf16[1,128,1536]{2,1,0:T(8,128)(2,1)} %param.12) | copy-start | bytes 1179652
  7.2 253.5 %all-reduce.4.cloned.1.call-start = ((), (), s32[]{:S(2)}) async-start(), calls=%async_computation | async-start | bytes 393216 | tf_op jit(solution)/shard_map/psum | solution.py:216
  8.5 12.3 %collective-permute-start.1 = (bf16[128,2,1536]{2,0,1:T(8,128)(2,1)S(1)}, bf16[128,2,1536]{2,0,1:T(8,128)(2,1)S(1)}, u32[]{:S(2)}, u32[]{:S(2)}) collective-permute-start(bf16[128,2,1536]{2,0,1:T(8,128)(2,1)S(1)} %pad_maximum_fusion.2), channel_id=1, source_target_pairs={{1,0},{2,1},{3,2},{4,3},{5,4},{6,5},{7,6},{8,7},{9,8},{10,9},{11,1... | collective-permute-start | bytes 2359304 | tf_op jit(solution)/shard_map/ppermute | solution.py:19
  11.3 14.3 %collective-permute-start = (bf16[128,2,1536]{2,0,1:T(8,128)(2,1)S(1)}, bf16[128,2,1536]{2,0,1:T(8,128)(2,1)S(1)}, u32[]{:S(2)}, u32[]{:S(2)}) collective-permute-start(bf16[128,2,1536]{2,0,1:T(8,128)(2,1)S(1)} %pad_maximum_fusion.2), channel_id=1, source_target_pairs={{0,1},{1,2},{2,3},{3,4},{4,5},{5,6},{6,7},{7,8},{8,9},{9,10},{10,1... | collective-permute-start | bytes 2359304 | tf_op jit(solution)/shard_map/ppermute | solution.py:19
  28.1 21.8 %copy-start.5 = (f32[1536]{0:T(1024)S(1)}, f32[1536]{0:T(1024)}, u32[]{:S(2)}) copy-start(f32[1536]{0:T(1024)} %param.16) | copy-start | bytes 18436
  49.7 10.3 %copy-start.58 = (f32[128]{0:T(128)}, f32[128]{0:T(128)S(1)}, u32[]{:S(2)}) copy-start(f32[128]{0:T(128)S(1)} %broadcast_multiply_fusion.5) | copy-start | bytes 1540
  50.0 10.1 %copy-start.60 = (f32[128]{0:T(128)}, f32[128]{0:T(128)S(1)}, u32[]{:S(2)}) copy-start(f32[128]{0:T(128)S(1)} %add_rsqrt_fusion) | copy-start | bytes 1540
  51.3 12.5 %collective-permute-start.2 = (bf16[15,1536]{0,1:T(8,128)(2,1)}, bf16[15,1536]{0,1:T(8,128)(2,1)}, u32[]{:S(2)}, u32[]{:S(2)}) collective-permute-start(bf16[15,1536]{0,1:T(8,128)(2,1)} %get-tuple-element.291), channel_id=1, source_target_pairs={{0,1},{1,2},{2,3},{3,4},{4,5},{5,6},{6,7},{7,8},{8,9},{9,10},{10,1... | collective-permute-start | bytes 138248 | tf_op jit(solution)/shard_map/ppermute | solution.py:30
  58.0 7.6 %collective-permute-start.3 = (bf16[15,1536]{0,1:T(8,128)(2,1)}, bf16[15,1536]{0,1:T(8,128)(2,1)}, u32[]{:S(2)}, u32[]{:S(2)}) collective-permute-start(bf16[15,1536]{0,1:T(8,128)(2,1)} %get-tuple-element.292), channel_id=1, source_target_pairs={{1,0},{2,1},{3,2},{4,3},{5,4},{6,5},{7,6},{8,7},{9,8},{10,9},{11,1... | collective-permute-start | bytes 138248 | tf_op jit(solution)/shard_map/ppermute | solution.py:32
  63.4 3.7 %copy-start.7 = (f32[1536]{0:T(1024)S(1)}, f32[1536]{0:T(1024)}, u32[]{:S(2)}) copy-start(f32[1536]{0:T(1024)} %get-tuple-element.199) | copy-start | bytes 18436
  63.4 3.7 %copy-start.8 = (f32[1536]{0:T(1024)S(1)}, f32[1536]{0:T(1024)}, u32[]{:S(2)}) copy-start(f32[1536]{0:T(1024)} %get-tuple-element.200) | copy-start | bytes 18436
  63.4 3.7 %copy-start.9 = (f32[1536]{0:T(1024)S(1)}, f32[1536]{0:T(1024)}, u32[]{:S(2)}) copy-start(f32[1536]{0:T(1024)} %get-tuple-element.201) | copy-start | bytes 18436
  63.4 3.7 %copy-start.10 = (f32[1536]{0:T(1024)S(1)}, f32[1536]{0:T(1024)}, u32[]{:S(2)}) copy-start(f32[1536]{0:T(1024)} %get-tuple-element.202) | copy-start | bytes 18436
  63.4 3.7 %copy-start.11 = (f32[1536]{0:T(1024)S(1)}, f32[1536]{0:T(1024)}, u32[]{:S(2)}) copy-start(f32[1536]{0:T(1024)} %get-tuple-element.203) | copy-start | bytes 18436
  63.4 3.7 %copy-start.12 = (f32[1536]{0:T(1024)S(1)}, f32[1536]{0:T(1024)}, u32[]{:S(2)}) copy-start(f32[1536]{0:T(1024)} %get-tuple-element.204) | copy-start | bytes 18436
  63.4 3.7 %copy-start.13 = (f32[1536]{0:T(1024)S(1)}, f32[1536]{0:T(1024)}, u32[]{:S(2)}) copy-start(f32[1536]{0:T(1024)} %get-tuple-element.205) | copy-start | bytes 18436
  63.4 3.7 %copy-start.14 = (f32[1536]{0:T(1024)S(1)}, f32[1536]{0:T(1024)}, u32[]{:S(2)}) copy-start(f32[1536]{0:T(1024)} %get-tuple-element.206) | copy-start | bytes 18436
  63.5 3.7 %copy-start.15 = (f32[1536]{0:T(1024)S(1)}, f32[1536]{0:T(1024)}, u32[]{:S(2)}) copy-start(f32[1536]{0:T(1024)} %get-tuple-element.207) | copy-start | bytes 18436
  63.5 3.7 %copy-start.16 = (f32[1536]{0:T(1024)S(1)}, f32[1536]{0:T(1024)}, u32[]{:S(2)}) copy-start(f32[1536]{0:T(1024)} %get-tuple-element.208) | copy-start | bytes 18436
  63.5 3.7 %copy-start.17 = (f32[1536]{0:T(1024)S(1)}, f32[1536]{0:T(1024)}, u32[]{:S(2)}) copy-start(f32[1536]{0:T(1024)} %get-tuple-element.209) | copy-start | bytes 18436
  63.5 3.7 %copy-start.18 = (f32[1536]{0:T(1024)S(1)}, f32[1536]{0:T(1024)}, u32[]{:S(2)}) copy-start(f32[1536]{0:T(1024)} %get-tuple-element.210) | copy-start | bytes 18436
  63.5 3.7 %copy-start.19 = (f32[1536]{0:T(1024)S(1)}, f32[1536]{0:T(1024)}, u32[]{:S(2)}) copy-start(f32[1536]{0:T(1024)} %get-tuple-element.211) | copy-start | bytes 18436
  63.5 3.7 %copy-start.20 = (f32[1536]{0:T(1024)S(1)}, f32[1536]{0:T(1024)}, u32[]{:S(2)}) copy-start(f32[1536]{0:T(1024)} %get-tuple-element.212) | copy-start | bytes 18436
  63.5 3.7 %copy-start.21 = (f32[1536]{0:T(1024)S(1)}, f32[1536]{0:T(1024)}, u32[]{:S(2)}) copy-start(f32[1536]{0:T(1024)} %get-tuple-element.213) | copy-start | bytes 18436
  63.5 3.7 %copy-start.22 = (f32[1536]{0:T(1024)S(1)}, f32[1536]{0:T(1024)}, u32[]{:S(2)}) copy-start(f32[1536]{0:T(1024)} %get-tuple-element.214) | copy-start | bytes 18436
  63.5 3.7 %copy-start.23 = (f32[1536]{0:T(1024)S(1)}, f32[1536]{0:T(1024)}, u32[]{:S(2)}) copy-start(f32[1536]{0:T(1024)} %get-tuple-element.215) | copy-start | bytes 18436
  63.5 3.7 %copy-start.24 = (f32[1536]{0:T(1024)S(1)}, f32[1536]{0:T(1024)}, u32[]{:S(2)}) copy-start(f32[1536]{0:T(1024)} %get-tuple-element.216) | copy-start | bytes 18436
  63.6 3.7 %copy-start.25 = (f32[1536]{0:T(1024)S(1)}, f32[1536]{0:T(1024)}, u32[]{:S(2)}) copy-start(f32[1536]{0:T(1024)} %get-tuple-element.217) | copy-start | bytes 18436
  63.6 3.7 %copy-start.26 = (f32[1536]{0:T(1024)S(1)}, f32[1536]{0:T(1024)}, u32[]{:S(2)}) copy-start(f32[1536]{0:T(1024)} %get-tuple-element.218) | copy-start | bytes 18436
  63.6 3.7 %copy-start.27 = (f32[1536]{0:T(1024)S(1)}, f32[1536]{0:T(1024)}, u32[]{:S(2)}) copy-start(f32[1536]{0:T(1024)} %get-tuple-element.219) | copy-start | bytes 18436
  63.6 3.7 %copy-start.28 = (f32[1536]{0:T(1024)S(1)}, f32[1536]{0:T(1024)}, u32[]{:S(2)}) copy-start(f32[1536]{0:T(1024)} %get-tuple-element.220) | copy-start | bytes 18436
  63.6 3.7 %copy-start.29 = (f32[1536]{0:T(1024)S(1)}, f32[1536]{0:T(1024)}, u32[]{:S(2)}) copy-start(f32[1536]{0:T(1024)} %get-tuple-element.221) | copy-start | bytes 18436
  63.6 3.7 %copy-start.30 = (f32[1536]{0:T(1024)S(1)}, f32[1536]{0:T(1024)}, u32[]{:S(2)}) copy-start(f32[1536]{0:T(1024)} %get-tuple-element.222) | copy-start | bytes 18436
  63.6 3.7 %copy-start.31 = (f32[1536]{0:T(1024)S(1)}, f32[1536]{0:T(1024)}, u32[]{:S(2)}) copy-start(f32[1536]{0:T(1024)} %get-tuple-element.223) | copy-start | bytes 18436
  63.6 3.7 %copy-start.32 = (f32[1536]{0:T(1024)S(1)}, f32[1536]{0:T(1024)}, u32[]{:S(2)}) copy-start(f32[1536]{0:T(1024)} %get-tuple-element.224) | copy-start | bytes 18436
  63.6 3.7 %copy-start.33 = (f32[1536]{0:T(1024)S(1)}, f32[1536]{0:T(1024)}, u32[]{:S(2)}) copy-start(f32[1536]{0:T(1024)} %get-tuple-element.225) | copy-start | bytes 18436
  63.6 3.7 %copy-start.34 = (f32[1536]{0:T(1024)S(1)}, f32[1536]{0:T(1024)}, u32[]{:S(2)}) copy-start(f32[1536]{0:T(1024)} %get-tuple-element.226) | copy-start | bytes 18436
  63.7 3.7 %copy-start.35 = (f32[1536]{0:T(1024)S(1)}, f32[1536]{0:T(1024)}, u32[]{:S(2)}) copy-start(f32[1536]{0:T(1024)} %get-tuple-element.227) | copy-start | bytes 18436
  63.7 3.7 %copy-start.36 = (f32[1536]{0:T(1024)S(1)}, f32[1536]{0:T(1024)}, u32[]{:S(2)}) copy-start(f32[1536]{0:T(1024)} %get-tuple-element.228) | copy-start | bytes 18436
  63.7 3.7 %copy-start.37 = (f32[1536]{0:T(1024)S(1)}, f32[1536]{0:T(1024)}, u32[]{:S(2)}) copy-start(f32[1536]{0:T(1024)} %get-tuple-element.229) | copy-start | bytes 18436
  63.7 3.7 %copy-start.41 = (pred[128]{0:T(512)(128)(4,1)S(1)}, pred[128]{0:T(512)(128)(4,1)}, u32[]{:S(2)}) copy-start(pred[128]{0:T(512)(128)(4,1)} %get-tuple-element.311) | copy-start | bytes 388
  63.7 3.7 %copy-start.42 = (pred[128]{0:T(512)(128)(4,1)S(1)}, pred[128]{0:T(512)(128)(4,1)}, u32[]{:S(2)}) copy-start(pred[128]{0:T(512)(128)(4,1)} %get-tuple-element.312) | copy-start | bytes 388
  63.7 3.7 %copy-start.43 = (pred[128]{0:T(512)(128)(4,1)S(1)}, pred[128]{0:T(512)(128)(4,1)}, u32[]{:S(2)}) copy-start(pred[128]{0:T(512)(128)(4,1)} %get-tuple-element.313) | copy-start | bytes 388
  86.1 4.5 %copy-start.50 = (pred[128]{0:T(512)(128)(4,1)S(1)}, pred[128]{0:T(512)(128)(4,1)}, u32[]{:S(2)}) copy-start(pred[128]{0:T(512)(128)(4,1)} %get-tuple-element.320) | copy-start | bytes 388
  86.1 4.5 %copy-start.51 = (pred[128]{0:T(512)(128)(4,1)S(1)}, pred[128]{0:T(512)(128)(4,1)}, u32[]{:S(2)}) copy-start(pred[128]{0:T(512)(128)(4,1)} %get-tuple-element.321) | copy-start | bytes 388
  86.1 4.5 %copy-start.52 = (pred[128]{0:T(512)(128)(4,1)S(1)}, pred[128]{0:T(512)(128)(4,1)}, u32[]{:S(2)}) copy-start(pred[128]{0:T(512)(128)(4,1)} %get-tuple-element.322) | copy-start | bytes 388
  86.2 4.5 %copy-start.53 = (pred[128]{0:T(512)(128)(4,1)S(1)}, pred[128]{0:T(512)(128)(4,1)}, u32[]{:S(2)}) copy-start(pred[128]{0:T(512)(128)(4,1)} %get-tuple-element.293) | copy-start | bytes 388
  86.2 4.5 %copy-start.54 = (pred[128]{0:T(512)(128)(4,1)S(1)}, pred[128]{0:T(512)(128)(4,1)}, u32[]{:S(2)}) copy-start(pred[128]{0:T(512)(128)(4,1)} %get-tuple-element.294) | copy-start | bytes 388
  94.4 9.3 %copy-start.55 = (pred[128]{0:T(512)(128)(4,1)S(1)}, pred[128]{0:T(512)(128)(4,1)}, u32[]{:S(2)}) copy-start(pred[128]{0:T(512)(128)(4,1)} %get-tuple-element.297) | copy-start | bytes 388
  94.4 9.3 %copy-start.56 = (pred[128]{0:T(512)(128)(4,1)S(1)}, pred[128]{0:T(512)(128)(4,1)}, u32[]{:S(2)}) copy-start(pred[128]{0:T(512)(128)(4,1)} %get-tuple-element.298) | copy-start | bytes 388
  94.4 9.3 %copy-start.57 = (pred[128]{0:T(512)(128)(4,1)S(1)}, pred[128]{0:T(512)(128)(4,1)}, u32[]{:S(2)}) copy-start(pred[128]{0:T(512)(128)(4,1)} %get-tuple-element.299) | copy-start | bytes 388
  95.3 35.1 %collective-permute-start.4 = (bf16[15,1536]{0,1:T(8,128)(2,1)}, bf16[15,1536]{0,1:T(8,128)(2,1)}, u32[]{:S(2)}, u32[]{:S(2)}) collective-permute-start(bf16[15,1536]{0,1:T(8,128)(2,1)} %get-tuple-element.289), channel_id=1, source_target_pairs={{0,1},{1,2},{2,3},{3,4},{4,5},{5,6},{6,7},{7,8},{8,9},{9,10},{10,1... | collective-permute-start | bytes 138248 | tf_op jit(solution)/shard_map/ppermute | solution.py:30
  101.6 28.9 %collective-permute-start.5 = (bf16[15,1536]{0,1:T(8,128)(2,1)S(1)}, bf16[15,1536]{0,1:T(8,128)(2,1)}, u32[]{:S(2)}, u32[]{:S(2)}) collective-permute-start(bf16[15,1536]{0,1:T(8,128)(2,1)S(1)} %get-tuple-element.290), channel_id=1, source_target_pairs={{1,0},{2,1},{3,2},{4,3},{5,4},{6,5},{7,6},{8,7},{9,8},{10,9},{11,1... | collective-permute-start | bytes 138248 | tf_op jit(solution)/shard_map/ppermute | solution.py:32
  132.0 19.2 %copy-start.6 = (f32[1536]{0:T(1024)S(1)}, f32[1536]{0:T(1024)}, u32[]{:S(2)}) copy-start(f32[1536]{0:T(1024)} %param.16) | copy-start | bytes 18436
  132.0 19.2 %copy-start.59 = (f32[128]{0:T(128)S(1)}, f32[128]{0:T(128)}, u32[]{:S(2)}) copy-start(f32[128]{0:T(128)} %copy-done.58) | copy-start | bytes 1540
  132.0 19.2 %copy-start.61 = (f32[128]{0:T(128)S(1)}, f32[128]{0:T(128)}, u32[]{:S(2)}) copy-start(f32[128]{0:T(128)} %copy-done.60) | copy-start | bytes 1540
  200.4 8.1 %copy-start.1 = (f32[128,1536]{0,1:T(8,128)S(1)}, f32[128,1536]{0,1:T(8,128)}, u32[]{:S(2)}) copy-start(f32[128,1536]{0,1:T(8,128)} %get-tuple-element.273) | copy-start | bytes 2359300
  201.8 7.8 %copy-start.39 = (f32[1536]{0:T(1024)S(1)}, f32[1536]{0:T(1024)}, u32[]{:S(2)}) copy-start(f32[1536]{0:T(1024)} %get-tuple-element.198) | copy-start | bytes 18436
  201.8 7.8 %copy-start.40 = (f32[1536]{0:T(1024)S(1)}, f32[1536]{0:T(1024)}, u32[]{:S(2)}) copy-start(f32[1536]{0:T(1024)} %get-tuple-element.195) | copy-start | bytes 18436
  201.8 60.4 %collective-permute-start.6 = (bf16[128,2,1536]{0,2,1:T(8,128)(2,1)}, bf16[128,2,1536]{0,2,1:T(8,128)(2,1)}, u32[]{:S(2)}, u32[]{:S(2)}) collective-permute-start(bf16[128,2,1536]{0,2,1:T(8,128)(2,1)} %get-tuple-element.283), channel_id=1, source_target_pairs={{0,1},{1,2},{2,3},{3,4},{4,5},{5,6},{6,7},{7,8},{8,9},{9,10},{10,1... | collective-permute-start | bytes 2359304 | tf_op jit(solution)/shard_map/ppermute | solution.py:19
  206.2 56.1 %collective-permute-start.7 = (bf16[128,2,1536]{0,2,1:T(8,128)(2,1)}, bf16[128,2,1536]{0,2,1:T(8,128)(2,1)}, u32[]{:S(2)}, u32[]{:S(2)}) collective-permute-start(bf16[128,2,1536]{0,2,1:T(8,128)(2,1)} %get-tuple-element.284), channel_id=1, source_target_pairs={{1,0},{2,1},{3,2},{4,3},{5,4},{6,5},{7,6},{8,7},{9,8},{10,9},{11,1... | collective-permute-start | bytes 2359304 | tf_op jit(solution)/shard_map/ppermute | solution.py:19
  (7 other events, 24.0 us)
Sparse Core Ops, SparseCore 0:
  130.6 127.3 all-reduce.3
where the time goes:
time: 277 us; the launch traced here: 273 us
  other arithmetic  70.1 us (25%)
  matrix products  55.6 us (20%)
  blocking collectives  49.5 us (18%)
  local copies, waits for them, and re-layouts  45.4 us (16%)
  starting transfers between devices  28.4 us (10%)
  between operations  15.1 us (5%)
  waiting for transfers between devices  8.47 us (3%)
    psum x1, blocking collectives, per_device(): lax.psum((gain_part, kernel_part, bias_part), ('dp', 'seq'))  49.5 us
    reduce_sum x4, other arithmetic, per_device(): jnp.sum(jnp.where(same_taps[tap_index], conv_wide[tap_index:tap_index + f...  29 us
    another operation x32, local copies, waits for them, and re-layouts, per_device(): kernel_part = jnp.stack(kernel_rows, 0)  24.4 us
    reduce_sum x1, other arithmetic, per_device(): gain_part = jnp.sum(grad_in * normed, 0)  19.2 us
    dot_general x12, matrix products, masked_logits(): jnp.einsum('qhe,khe->hqk', query_rows, key_rows, preferred_element_type=j...  15.4 us
    ppermute x2, starting transfers between devices, with_halo(): lax.ppermute(tail, axis, [(i, (i + 1) % count) for i in range(ends)])  12.9 us
    ppermute x4, starting transfers between devices, shifted(): return lax.ppermute(block, axis, route)  11.2 us
    dot_general x6, matrix products, backward_group(): jnp.einsum('hqk,qhe->khe', grad_logit, query_rows, preferred_element_type...  10.9 us
  transfers between devices with their start and end apart: 9, of which 3 were waited for; matrix products, arithmetic and copies ran while one was open for 41% of the time, Pallas kernels for 0%

commit v1 on v0

v1 whole, which is shorter than its diff:
```python
import functools

import jax
import jax.numpy as jnp
from jax import lax
from jax.experimental import pallas as pl
from jax.experimental.pallas import tpu as pltpu
from jax.sharding import PartitionSpec as P

HEAD_DIM = 64
EPS = 1e-05
NEG = -1e30
LANES = 128
PAD = 16
GROUPS = 3
VMEM = pl.BlockSpec(memory_space=pltpu.VMEM)
F32 = jnp.float32
BF16 = jnp.bfloat16


def dot(a, b, dims):
    return lax.dot_general(a, b, (dims, ((), ())), preferred_element_type=F32)


NN = ((1,), (0,))
NT = ((1,), (1,))
TN = ((0,), (0,))


def lanes_of(index):
    return pl.ds(pl.multiple_of(index * LANES, LANES), LANES)


def block_ids(seg_ref, frames):
    me = lax.axis_index("seq")
    count = seg_ref.shape[1] // frames
    own = seg_ref[0:1, pl.ds(pl.multiple_of(me * frames, frames), frames)].astype(F32)
    before = jnp.maximum(me - 1, 0)
    after = jnp.minimum(me + 1, count - 1)
    prev = seg_ref[0:1, pl.ds(pl.multiple_of(before * frames, frames), frames)].astype(F32)
    following = seg_ref[0:1, pl.ds(pl.multiple_of(after * frames, frames), frames)].astype(F32)
    prev_last = jnp.where(me > 0, prev[:, frames - 1 :], -1.0)
    following = jnp.where(me < count - 1, following, -1.0)
    return own, following, prev_last, following[:, 0:1]


def crossing(seg_ref, frames):
    own, following, _, edge = block_ids(seg_ref, frames)
    left = jnp.sum(jnp.where((own == edge) & (edge >= 0.0), 1.0, 0.0), 1, keepdims=True)
    right = jnp.sum(jnp.where(following == edge, 1.0, 0.0), 1, keepdims=True)
    length = jnp.where(left > 0.0, left + right, 0.0)
    return frames - left, length


def iota(shape, axis):
    return lax.broadcasted_iota(jnp.int32, shape, axis).astype(F32)


def gather_matrix(first, length, frames):
    shape = (frames, 2 * frames)
    row = iota(shape, 0)
    return jnp.where((iota(shape, 1) == row + first) & (row < length), 1.0, 0.0).astype(BF16)


def scatter_matrix(first, length, frames):
    shape = (2 * frames, frames)
    col = iota(shape, 1)
    return jnp.where((iota(shape, 0) == col + first) & (col < length), 1.0, 0.0).astype(BF16)


def pair_masks(rows):
    low = lax.broadcasted_iota(jnp.int32, (rows, LANES), 1) < HEAD_DIM
    return low


def stack_pair(pair, low):
    zero = jnp.zeros_like(pair)
    return jnp.concatenate([jnp.where(low, pair, zero), jnp.where(low, zero, pair)], 0)


def attend(query, key, value, bias, keep, low):
    frames = query.shape[0]
    logits = dot(query * jnp.asarray(HEAD_DIM**-0.5, BF16), stack_pair(key, low), NT)
    halves = []
    for half in range(2):
        part = logits[:, half * frames : (half + 1) * frames] + bias
        top = jnp.max(part, 1, keepdims=True)
        power = jnp.exp(part - top)
        total = jnp.sum(power, 1, keepdims=True)
        halves.append((power * (1.0 / total)).astype(BF16))
    prob = jnp.concatenate(halves, 1)
    context = dot(prob, stack_pair(value, low), NN)
    return prob, (context * keep).astype(BF16)


def attend_back(query, key, value, prob, context, grad, low):
    frames = query.shape[0]
    scale = HEAD_DIM**-0.5
    grad_prob = dot(grad, stack_pair(value, low), NT)
    product = grad.astype(F32) * context.astype(F32)
    zero = jnp.zeros_like(product)
    deltas = (
        jnp.sum(jnp.where(low, product, zero), 1, keepdims=True),
        jnp.sum(jnp.where(low, zero, product), 1, keepdims=True),
    )
    parts = []
    for half in range(2):
        cols = slice(half * frames, (half + 1) * frames)
        parts.append(
            (prob[:, cols].astype(F32) * (grad_prob[:, cols] - deltas[half]) * scale).astype(BF16)
        )
    query_grad = dot(jnp.concatenate(parts, 1), stack_pair(key, low), NN)
    key_grad = dot(jnp.concatenate(parts, 0), stack_pair(query, low), TN)
    prob_rows = jnp.concatenate([prob[:, :frames], prob[:, frames:]], 0)
    value_grad = dot(prob_rows, stack_pair(grad, low), TN)
    return query_grad, key_grad, value_grad


def normalize(context):
    context = context.astype(F32)
    centred = context - jnp.mean(context, -1, keepdims=True)
    inv_std = lax.rsqrt(jnp.mean(centred * centred, -1, keepdims=True) + EPS)
    return centred * inv_std, inv_std


CHUNK = 32


def chunks(frames):
    return [pl.ds(start, CHUNK) for start in range(0, frames, CHUNK)]


def clear_edges(pad_ref, frames):
    zero = jnp.zeros((PAD, pad_ref.shape[1]), F32)
    pad_ref[0:PAD, :] = zero
    pad_ref[PAD + frames : 2 * PAD + frames, :] = zero


def shifts(frames, taps):
    base = PAD - taps // 2
    for turn in range(8):
        for start in range(0, 2 * PAD + 1, 8):
            tap = start + turn - base
            if 0 <= tap < taps:
                yield turn, start, tap


def turned(block, turn):
    rows = block.shape[0]
    return block if turn == 0 else pltpu.roll(block, rows - turn, 0)


def conv_forward(pad_ref, kernel_ref, bias_ref, mask_ref, frames, lanes):
    taps = kernel_ref.shape[0]
    block = pad_ref[:, lanes]
    total = jnp.broadcast_to(bias_ref[0:1, lanes], (frames, LANES))
    at, view = None, None
    for turn, start, tap in shifts(frames, taps):
        if turn != at:
            at, view = turn, turned(block, turn)
        term = view[start : start + frames]
        if mask_ref is not None:
            term = term * mask_ref[tap * frames : (tap + 1) * frames, :]
        total = total + kernel_ref[tap : tap + 1, lanes] * term
    return total


def conv_backward(pad_ref, conv_in, kernel_ref, mask_ref, frames, lanes, store):
    taps = kernel_ref.shape[0]
    block = pad_ref[:, lanes]
    total = jnp.zeros((frames, LANES), F32)
    at, view = None, None
    for turn, start, mirror in shifts(frames, taps):
        if turn != at:
            at, view = turn, turned(block, turn)
        tap = taps - 1 - mirror
        term = view[start : start + frames]
        if mask_ref is not None:
            term = term * mask_ref[mirror * frames : (mirror + 1) * frames, :]
        total = total + kernel_ref[tap : tap + 1, lanes] * term
        store(tap, jnp.sum(conv_in * term, 0, keepdims=True))
    return total


def gate(pre_act):
    return 1.0 / (1.0 + jnp.exp(-pre_act))


def gate_grad(cotangent, pre_act, sig):
    return (cotangent * sig * (1.0 + pre_act * (1.0 - sig))).astype(BF16).astype(F32)


def norm_backward(context_ref, grad_ref, gain_ref, keep, out_ref, frames):
    for rows in chunks(frames):
        normed, inv_std = normalize(context_ref[rows, :])
        grad = grad_ref[rows, :] * gain_ref[0:1, :]
        centre = jnp.mean(grad, -1, keepdims=True)
        slope = jnp.mean(grad * normed, -1, keepdims=True)
        result = (grad - centre - normed * slope) * inv_std
        out_ref[rows, :] = jnp.where(keep[rows.start : rows.start + CHUNK, 0:1] > 0.0, result, 0.0).astype(BF16)


def own_kernel(
    q_ref, k_ref, v_ref, cot_ref, seg_ref, gain_ref, kernel_ref, bias_ref,
    out_ref, grad_ref, prob_ref, context_ref, sums_ref,
    pad_ref, normed_ref, pre_ref, mask_ref, keep_ref,
):
    frames, width = q_ref.shape
    taps = kernel_ref.shape[0]
    tiles = width // LANES
    own, _, prev_last, next_first = block_ids(seg_ref, frames)
    ids = jnp.where((own == prev_last) | (own == next_first), -5.0, own)
    ids_row = jnp.broadcast_to(ids, (frames, frames))
    ids_col = jnp.transpose(ids_row)
    bias = jnp.where(ids_row == ids_col, 0.0, NEG)
    keep = jnp.where(ids_col >= 0.0, 1.0, 0.0)
    keep_ref[...] = keep
    pad_ref[0:PAD, 0:LANES] = jnp.full((PAD, LANES), -9.0, F32)
    pad_ref[PAD + frames :, 0:LANES] = jnp.full((PAD, LANES), -9.0, F32)
    pad_ref[PAD : PAD + frames, 0:LANES] = ids_col
    ids_pad = pad_ref[:, 0:LANES]
    at, view = None, None
    for turn, start, tap in shifts(frames, taps):
        if turn != at:
            at, view = turn, turned(ids_pad, turn)
        mask_ref[tap * frames : (tap + 1) * frames, :] = jnp.where(
            view[start : start + frames] == ids_col, 1.0, 0.0
        )
    clear_edges(pad_ref, frames)
    low = pair_masks(frames)

    @pl.loop(0, tiles)
    def _(index):
        lanes = lanes_of(index)
        prob, context = attend(q_ref[:, lanes], k_ref[:, lanes], v_ref[:, lanes], bias, keep, low)
        prob_ref[index] = prob
        context_ref[:, lanes] = context

    for rows in chunks(frames):
        normed, _ = normalize(context_ref[rows, :])
        normed = jnp.where(keep[rows.start : rows.start + CHUNK, 0:1] > 0.0, normed, 0.0)
        normed_ref[rows, :] = normed
        pad_ref[pl.ds(PAD + rows.start, CHUNK), :] = (
            (normed * gain_ref[0:1, :]).astype(BF16).astype(F32)
        )

    @pl.loop(0, tiles)
    def _(index):
        lanes = lanes_of(index)
        pre_ref[:, lanes] = conv_forward(pad_ref, kernel_ref, bias_ref, mask_ref, frames, lanes)

    @pl.loop(0, tiles)
    def _(index):
        lanes = lanes_of(index)
        pre_act = pre_ref[:, lanes]
        sig = gate(pre_act)
        out_ref[:, lanes] = (pre_act * sig * keep_ref[...]).astype(BF16)
        grad_pre = gate_grad(cot_ref[:, lanes].astype(F32) * keep_ref[...], pre_act, sig)
        conv_in = pad_ref[PAD : PAD + frames, lanes]
        pad_ref[PAD : PAD + frames, lanes] = grad_pre
        sums_ref[taps : taps + 1, lanes] = jnp.sum(grad_pre, 0, keepdims=True)

        def store(tap, value):
            sums_ref[tap : tap + 1, lanes] = value

        grad_in = conv_backward(pad_ref, conv_in, kernel_ref, mask_ref, frames, lanes, store)
        sums_ref[taps + 1 : taps + 2, lanes] = jnp.sum(grad_in * normed_ref[:, lanes], 0, keepdims=True)
        pre_ref[:, lanes] = grad_in

    norm_backward(context_ref, pre_ref, gain_ref, keep, grad_ref, frames)


def cross_forward_kernel(
    q_ref, k_ref, v_ref, qn_ref, kn_ref, vn_ref, seg_ref, gain_ref, kernel_ref, bias_ref,
    own_ref, next_ref, qg_ref, kg_ref, vg_ref, prob_ref, context_ref, pre_ref,
    pad_ref,
):
    frames, width = q_ref.shape
    tiles = width // LANES
    first, length = crossing(seg_ref, frames)
    pick = gather_matrix(first, length, frames)
    place = scatter_matrix(first, length, frames)
    shape = (frames, frames)
    bias = jnp.where(iota(shape, 1) < length, 0.0, NEG)
    keep = jnp.where(iota(shape, 0) < length, 1.0, 0.0)
    low = pair_masks(frames)
    clear_edges(pad_ref, frames)

    @pl.loop(0, tiles)
    def _(index):
        lanes = lanes_of(index)

        def picked(own, other):
            both = jnp.concatenate([own[:, lanes], other[:, lanes]], 0)
            return dot(pick, both, NN).astype(BF16)

        query, key, value = picked(q_ref, qn_ref), picked(k_ref, kn_ref), picked(v_ref, vn_ref)
        qg_ref[:, lanes] = query
        kg_ref[:, lanes] = key
        vg_ref[:, lanes] = value
        prob, context = attend(query, key, value, bias, keep, low)
        prob_ref[index] = prob
        context_ref[:, lanes] = context

    for rows in chunks(frames):
        normed, _ = normalize(context_ref[rows, :])
        normed = jnp.where(keep[rows.start : rows.start + CHUNK, 0:1] > 0.0, normed, 0.0)
        pad_ref[pl.ds(PAD + rows.start, CHUNK), :] = (
            (normed * gain_ref[0:1, :]).astype(BF16).astype(F32)
        )

    @pl.loop(0, tiles)
    def _(index):
        lanes = lanes_of(index)
        pre_act = conv_forward(pad_ref, kernel_ref, bias_ref, None, frames, lanes)
        pre_ref[:, lanes] = pre_act
        placed = dot(place, (pre_act * gate(pre_act)).astype(BF16), NN).astype(BF16)
        own_ref[:, lanes] = placed[:frames]
        next_ref[:, lanes] = placed[frames:]


def cross_conv_kernel(
    cot_ref, cotn_ref, seg_ref, gain_ref, kernel_ref, context_ref, pre_ref, part_ref,
    grad_ref, sums_ref,
    pad_ref, in_ref, normed_ref, back_ref,
):
    frames, width = cot_ref.shape
    taps = kernel_ref.shape[0]
    tiles = width // LANES
    first, length = crossing(seg_ref, frames)
    pick = gather_matrix(first, length, frames)
    keep = jnp.where(iota((frames, frames), 0) < length, 1.0, 0.0)
    clear_edges(pad_ref, frames)
    for rows in chunks(frames):
        normed, _ = normalize(context_ref[rows, :])
        normed = jnp.where(keep[rows.start : rows.start + CHUNK, 0:1] > 0.0, normed, 0.0)
        normed_ref[rows, :] = normed
        in_ref[rows, :] = (normed * gain_ref[0:1, :]).astype(BF16).astype(F32)

    @pl.loop(0, tiles)
    def _(index):
        lanes = lanes_of(index)
        cotangent = dot(pick, jnp.concatenate([cot_ref[:, lanes], cotn_ref[:, lanes]], 0), NN)
        pre_act = pre_ref[:, lanes]
        grad_pre = gate_grad(cotangent, pre_act, gate(pre_act))
        pad_ref[PAD : PAD + frames, lanes] = grad_pre

        def store(row, value):
            sums_ref[row : row + 1, lanes] = part_ref[row : row + 1, lanes] + value

        store(taps, jnp.sum(grad_pre, 0, keepdims=True))
        grad_in = conv_backward(pad_ref, in_ref[:, lanes], kernel_ref, None, frames, lanes, store)
        store(taps + 1, jnp.sum(grad_in * normed_ref[:, lanes], 0, keepdims=True))
        back_ref[:, lanes] = grad_in

    norm_backward(context_ref, back_ref, gain_ref, keep, grad_ref, frames)


def cross_back_kernel(
    group, tiles, q_ref, k_ref, v_ref, prob_ref, context_ref, grad_ref, seg_ref, own_ref, next_ref
):
    frames = q_ref.shape[0]
    place = scatter_matrix(*crossing(seg_ref, frames), frames)
    low = pair_masks(frames)

    @pl.loop(0, tiles)
    def _(step):
        index = group * tiles + step
        lanes, dest = lanes_of(index), lanes_of(step)
        results = attend_back(
            q_ref[:, lanes], k_ref[:, lanes], v_ref[:, lanes], prob_ref[index],
            context_ref[:, lanes], grad_ref[:, lanes], low,
        )
        for which, result in enumerate(results):
            placed = dot(place, result.astype(BF16), NN).astype(BF16)
            own_ref[which, :, dest] = placed[:frames]
            next_ref[which, :, dest] = placed[frames:]


def own_back_kernel(q_ref, k_ref, v_ref, prob_ref, context_ref, grad_ref, *refs):
    cross, (out_ref,) = refs[:-1], refs[-1:]
    frames, width = q_ref.shape
    low = pair_masks(frames)
    tiles = width // LANES // len(cross)
    for group, cross_ref in enumerate(cross):

        @pl.loop(0, tiles)
        def _(step):
            index = group * tiles + step
            lanes, dest = lanes_of(index), lanes_of(step)
            results = attend_back(
                q_ref[:, lanes], k_ref[:, lanes], v_ref[:, lanes], prob_ref[index],
                context_ref[:, lanes], grad_ref[:, lanes], low,
            )
            for which, result in enumerate(results):
                out_ref[which, :, lanes] = result.astype(BF16) + cross_ref[which, :, dest]


def call(kernel, outs, scratch, flops, *args):
    size = sum(a.size * a.dtype.itemsize for a in args) + sum(o.size * o.dtype.itemsize for o in outs)
    return pl.pallas_call(
        kernel,
        out_shape=outs,
        in_specs=[VMEM] * len(args),
        out_specs=[VMEM] * len(outs),
        scratch_shapes=scratch,
        compiler_params=pltpu.CompilerParams(vmem_limit_bytes=40 * 1024 * 1024),
        cost_estimate=pl.CostEstimate(flops=flops, bytes_accessed=size, transcendentals=0),
    )(*args)


def total_over_devices(part, axes):
    total = part
    for axis in axes:
        count = lax.axis_size(axis)
        step = 1
        while step < count:
            sent = total.astype(BF16)
            came = lax.ppermute(sent, axis, [(i, i ^ step) for i in range(count)])
            total = sent.astype(F32) + came.astype(F32)
            step *= 2
    return total


def per_device(queries, keys, values, segment_ids, norm_gain, conv_kernel, conv_bias, cotangent):
    q, k, v, cot = queries[0], keys[0], values[0], cotangent[0]
    frames, width = q.shape
    taps = conv_kernel.shape[0]
    tiles = width // LANES
    count = lax.axis_size("seq")
    gain, bias = norm_gain[None], conv_bias[None]
    seg = segment_ids
    to_left = [(i + 1, i) for i in range(count - 1)]
    to_right = [(i, i + 1) for i in range(count - 1)]
    qn, kn, vn, cotn = (lax.ppermute(a, "seq", to_left) for a in (q, k, v, cot))

    def sds(shape, dtype):
        return jax.ShapeDtypeStruct(shape, dtype)

    rows16 = sds((frames, width), BF16)
    rows32 = sds((frames, width), F32)
    probs = sds((tiles, frames, 2 * frames), BF16)
    sums = sds((taps + 2, width), F32)
    padded = pltpu.VMEM((frames + 2 * PAD, width), F32)
    plain = pltpu.VMEM((frames, width), F32)

    out_own, grad_own, prob_own, context_own, sums_own = call(
        own_kernel,
        [rows16, rows16, probs, rows16, sums],
        [padded, plain, plain, pltpu.VMEM((taps * frames, LANES), F32), pltpu.VMEM((frames, LANES), F32)],
        10**10,
        q, k, v, cot, seg, gain, conv_kernel, bias,
    )
    out_cross, out_next, qg, kg, vg, prob_cross, context_cross, pre_cross = call(
        cross_forward_kernel,
        [rows16, rows16, rows16, rows16, rows16, probs, rows16, rows32],
        [padded],
        4 * 10**9,
        q, k, v, qn, kn, vn, seg, gain, conv_kernel, bias,
    )
    out_came = lax.ppermute(out_next, "seq", to_right)
    grad_cross, sums_both = call(
        cross_conv_kernel,
        [rows16, sums],
        [padded, plain, plain, plain],
        4 * 10**9,
        cot, cotn, seg, gain, conv_kernel, context_cross, pre_cross, sums_own,
    )
    per_group = tiles // GROUPS
    piece = sds((3, frames, per_group * LANES), BF16)
    own_parts, came_parts = [], []
    for group in range(GROUPS):
        own_part, next_part = call(
            functools.partial(cross_back_kernel, group, per_group),
            [piece, piece],
            [],
            10**9,
            qg, kg, vg, prob_cross, context_cross, grad_cross, seg,
        )
        own_parts.append(own_part)
        came_parts.append(lax.ppermute(next_part, "seq", to_right))
    (grads_own,) = call(
        own_back_kernel,
        [sds((3, frames, width), BF16)],
        [],
        3 * 10**9,
        q, k, v, prob_own, context_own, grad_own, *own_parts,
    )
    conv_out = out_own + out_cross + out_came
    grads = grads_own + jnp.concatenate(came_parts, 2)
    total = total_over_devices(sums_both, ("seq", "dp"))
    total = total * (lax.axis_size("dp") * count * frames) ** (-0.5)
    return (
        conv_out[None],
        grads[0][None],
        grads[1][None],
        grads[2][None],
        total[taps + 1],
        total[:taps],
        total[taps],
    )


def solution(mesh):
    rows = P("dp", "seq", None)
    return jax.shard_map(
        per_device,
        mesh=mesh,
        in_specs=(rows, rows, rows, P("dp", None), P(), P(), P(), rows),
        out_specs=(rows, rows, rows, rows, P(), P(), P()),
        check_vma=False,
    )
```

time: 277 us -> 97.9 us (0.35)
  the two profiles are of different devices: /device:TPU:12 before, /device:TPU:0 now
where the time goes in v1:
time: 97.9 us; the launch traced here: 97.2 us
  Pallas kernels  48.3 us (49%)
  starting transfers between devices  28.8 us (29%)
  local copies, waits for them, and re-layouts  9.4 us (10%)
  waiting for transfers between devices  8.53 us (9%)
  other arithmetic  1.28 us (1%)
    pallas_call x7, Pallas kernels, call(): pl.pallas_call(kernel, out_shape=outs, in_specs=[VMEM] * len(args), out_s...  48.3 us
    ppermute x3, starting transfers between devices, per_device(): came_parts.append(lax.ppermute(next_part, 'seq', to_right))  11 us
    ppermute x5, starting transfers between devices, total_over_devices(): came = lax.ppermute(sent, axis, [(i, i ^ step) for i in range(count)])  11 us
    ppermute x5, waiting for transfers between devices, total_over_devices(): came = lax.ppermute(sent, axis, [(i, i ^ step) for i in range(count)])  8.51 us
    unnamed x24, local copies, waits for them, and re-layouts  5.64 us
    ppermute x4, starting transfers between devices, per_device(): qn, kn, vn, cotn = (lax.ppermute(a, 'seq', to_left) for a in (q, k, v, cot))  5.17 us
  transfers between devices with their start and end apart: 13, of which 2 were waited for; matrix products, arithmetic and copies ran while one was open for 4% of the time, Pallas kernels for 42%

profile of v1, /device:TPU:0, one launch (start us, length us, event | category | flops | bytes accessed | tf_op | source)
XLA Modules:
  0.0 97.2 jit_solution(17942898759722448192)
XLA Ops:
  0.6 1.3 %collective-permute-start = (bf16[128,1536]{1,0:T(8,128)(2,1)}, bf16[128,1536]{1,0:T(8,128)(2,1)S(1)}, u32[]{:S(2)}, u32[]{:S(2)}) collective-permute-start(bf16[128,1536]{1,0:T(8,128)(2,1)} %bitcast.9), channel_id=1, source_target_pairs={{1,0},{2,1},{3,2},{4,3},{5,4},{6,5},{7,6},{8,7},{9,8},{10,9},{11,1... | collective-permute-start | bytes 1179656 | tf_op jit(solution)/shard_map/ppermute | solution.py:435
  1.9 1.3 %collective-permute-start.1 = (bf16[128,1536]{1,0:T(8,128)(2,1)}, bf16[128,1536]{1,0:T(8,128)(2,1)S(1)}, u32[]{:S(2)}, u32[]{:S(2)}) collective-permute-start(bf16[128,1536]{1,0:T(8,128)(2,1)} %bitcast.13), channel_id=1, source_target_pairs={{1,0},{2,1},{3,2},{4,3},{5,4},{6,5},{7,6},{8,7},{9,8},{10,9},{11,1... | collective-permute-start | bytes 1179656 | tf_op jit(solution)/shard_map/ppermute | solution.py:435
  3.2 1.3 %collective-permute-start.2 = (bf16[128,1536]{1,0:T(8,128)(2,1)}, bf16[128,1536]{1,0:T(8,128)(2,1)S(1)}, u32[]{:S(2)}, u32[]{:S(2)}) collective-permute-start(bf16[128,1536]{1,0:T(8,128)(2,1)} %bitcast.17), channel_id=1, source_target_pairs={{1,0},{2,1},{3,2},{4,3},{5,4},{6,5},{7,6},{8,7},{9,8},{10,9},{11,1... | collective-permute-start | bytes 1179656 | tf_op jit(solution)/shard_map/ppermute | solution.py:435
  4.5 1.3 %collective-permute-start.4 = (bf16[128,1536]{1,0:T(8,128)(2,1)}, bf16[128,1536]{1,0:T(8,128)(2,1)S(1)}, u32[]{:S(2)}, u32[]{:S(2)}) collective-permute-start(bf16[128,1536]{1,0:T(8,128)(2,1)} %bitcast.6), channel_id=1, source_target_pairs={{1,0},{2,1},{3,2},{4,3},{5,4},{6,5},{7,6},{8,7},{9,8},{10,9},{11,1... | collective-permute-start | bytes 1179656 | tf_op jit(solution)/shard_map/ppermute | solution.py:435
  5.8 0.7 broadcast_in_dim.9.gain_ref
  6.5 0.7 broadcast_in_dim.10.bias_ref
  7.2 0.0 copy-start
  7.2 1.0 %copy-done = bf16[1,128,1536]{2,1,0:T(8,128)(2,1)S(1)} copy-done((bf16[1,128,1536]{2,1,0:T(8,128)(2,1)S(1)}, bf16[1,128,1536]{2,1,0:T(8,128)(2,1)}, u32[]{:S(2)}) %copy-start) | copy-done | bytes 393240
  8.2 0.0 copy-start.2
  8.2 1.0 %copy-done.2 = bf16[1,128,1536]{2,1,0:T(8,128)(2,1)S(1)} copy-done((bf16[1,128,1536]{2,1,0:T(8,128)(2,1)S(1)}, bf16[1,128,1536]{2,1,0:T(8,128)(2,1)}, u32[]{:S(2)}) %copy-start.2) | copy-done | bytes 393240
  9.2 0.0 copy-start.4
  9.2 1.0 %copy-done.4 = bf16[1,128,1536]{2,1,0:T(8,128)(2,1)S(1)} copy-done((bf16[1,128,1536]{2,1,0:T(8,128)(2,1)S(1)}, bf16[1,128,1536]{2,1,0:T(8,128)(2,1)}, u32[]{:S(2)}) %copy-start.4) | copy-done | bytes 393240
  10.2 0.0 copy-start.6
  10.2 1.0 %copy-done.6 = bf16[1,128,1536]{2,1,0:T(8,128)(2,1)S(1)} copy-done((bf16[1,128,1536]{2,1,0:T(8,128)(2,1)S(1)}, bf16[1,128,1536]{2,1,0:T(8,128)(2,1)}, u32[]{:S(2)}) %copy-start.6) | copy-done | bytes 393240
  11.2 0.0 copy-start.8
  11.2 0.9 copy-done.8
  12.1 0.0 copy-start.10
  12.2 0.7 copy-done.10
  12.8 16.5 %shard_map.135 = (bf16[128,1536]{1,0:T(8,128)(2,1)S(1)}, bf16[128,1536]{1,0:T(8,128)(2,1)S(1)}, bf16[12,128,256]{2,1,0:T(8,128)(2,1)S(1)}, bf16[128,1536]{1,0:T(8,128)(2,1)S(1)}, f32[33,1536]{1,0:T(8,128)S(1)}) custom-call(bf16[128,1536]{1,0:T(8,128)(2,1)S(1)} %bitcast.10, bf16[128,1536]{1,0:T(8,128)(2,1)S(1)} %bitcast.14, bf16[128,1536]{1,0:T(8,128)(2,1)S(1)} %bitcast.18, ...), custom_call_target="tpu_custom_call" | custom-call | flops 10000000000 | bytes 3952640 | tf_op jit(solution)/shard_map/pallas_call | solution.py:401
  29.3 0.0 copy-start.1
  29.4 0.0 copy-start.9
  29.4 0.0 copy-start.11
  29.4 0.0 collective-permute-done.qn_ref
  29.4 0.0 collective-permute-done.1.kn_ref
  29.4 0.0 collective-permute-done.2.vn_ref
  29.4 12.4 %shard_map.136 = (bf16[128,1536]{1,0:T(8,128)(2,1)S(1)}, bf16[128,1536]{1,0:T(8,128)(2,1)S(1)}, bf16[128,1536]{1,0:T(8,128)(2,1)S(1)}, bf16[128,1536]{1,0:T(8,12...) custom-call(bf16[128,1536]{1,0:T(8,128)(2,1)S(1)} %bitcast.11, ...), custom_call_target="tpu_custom_call" | custom-call | flops 4000000000 | bytes 6502400 | tf_op jit(solution)/shard_map/pallas_call | solution.py:401
  41.9 0.0 collective-permute-done.4.cotn_ref
  41.9 0.0 copy-done.1
  41.9 0.0 copy-done.9
  41.9 0.0 copy-done.11
  41.9 7.5 %shard_map.137 = (bf16[128,1536]{1,0:T(8,128)(2,1)S(1)}, f32[33,1536]{1,0:T(8,128)S(1)}) custom-call(bf16[128,1536]{1,0:T(8,128)(2,1)S(1)} %bitcast.8, bf16[128,1536]{1,0:T(8,128)(2,1)S(1)} %collective-permute-done.4.cotn_ref, s32[1,2048]{1,0:T(1,128)S(1)} %copy-done.11, f32[1,1536]{1,0:T(1,128)S(1)} %broadcast_in_dim.9.gain_ref, f32[31,1536]{1,0:T(8,128)S(1)} %copy-done.9, ...), custom_call_target="tpu_custom_call" | custom-call | flops 4000000000 | bytes 2969600 | tf_op jit(solution)/shard_map/pallas_call | solution.py:401
  49.4 3.1 %collective-permute-start.8 = (bf16[33,1536]{1,0:T(8,128)(2,1)S(1)}, bf16[33,1536]{1,0:T(8,128)(2,1)S(1)}, u32[]{:S(2)}, u32[]{:S(2)}) collective-permute-start(bf16[33,1536]{1,0:T(8,128)(2,1)S(1)} %convert_element_type.45), channel_id=1, source_target_pairs={{0,1},{1,0},{2,3},{3,2},{4,5},{5,4},{6,7},{7,6},{8,9},{9,8},{10,11... | collective-permute-start | bytes 304136 | tf_op jit(solution)/shard_map/ppermute | solution.py:419
  52.5 2.4 %shard_map.139 = (bf16[3,128,512]{2,1,0:T(8,128)(2,1)S(1)}, bf16[3,128,512]{2,1,0:T(8,128)(2,1)S(1)}) custom-call(bf16[128,1536]{1,0:T(8,128)(2,1)S(1)} %get-tuple-element.34.q_ref, bf16[128,1536]{1,0:T(8,128)(2,1)S(1)} %get-tuple-element.35.k_ref, bf16[128,1536]{1,0:T(8,128)(2,1)S(1)} %get-tuple-element.36.v_ref, ...), custom_call_target="tpu_custom_call" | custom-call | flops 1000000000 | bytes 3547136 | tf_op jit(solution)/shard_map/pallas_call | solution.py:401
  54.9 0.0 collective-permute-done.8
  54.9 3.0 %collective-permute-start.9 = (bf16[33,1536]{1,0:T(8,128)(2,1)S(1)}, bf16[33,1536]{1,0:T(8,128)(2,1)S(1)}, u32[]{:S(2)}, u32[]{:S(2)}) collective-permute-start(bf16[33,1536]{1,0:T(8,128)(2,1)S(1)} %add_convert_fusion.3), channel_id=1, source_target_pairs={{0,2},{1,3},{2,0},{3,1},{4,6},{5,7},{6,4},{7,5},{8,10},{9,11},{10,... | collective-permute-start | bytes 304136 | tf_op jit(solution)/shard_map/ppermute | solution.py:419
  57.9 2.4 %shard_map.140 = (bf16[3,128,512]{2,1,0:T(8,128)(2,1)S(1)}, bf16[3,128,512]{2,1,0:T(8,128)(2,1)S(1)}) custom-call(bf16[128,1536]{1,0:T(8,128)(2,1)S(1)} %get-tuple-element.34.q_ref, bf16[128,1536]{1,0:T(8,128)(2,1)S(1)} %get-tuple-element.35.k_ref, bf16[128,1536]{1,0:T(8,128)(2,1)S(1)} %get-tuple-element.36.v_ref, ...), custom_call_target="tpu_custom_call" | custom-call | flops 1000000000 | bytes 3547136 | tf_op jit(solution)/shard_map/pallas_call | solution.py:401
  60.3 1.7 %collective-permute-start.3 = (bf16[128,1536]{1,0:T(8,128)(2,1)S(1)}, bf16[128,1536]{1,0:T(8,128)(2,1)S(1)}, u32[]{:S(2)}, u32[]{:S(2)}) collective-permute-start(bf16[128,1536]{1,0:T(8,128)(2,1)S(1)} %get-tuple-element.30), channel_id=1, source_target_pairs={{0,1},{1,2},{2,3},{3,4},{4,5},{5,6},{6,7},{7,8},{8,9},{9,10},{10,1... | collective-permute-start | bytes 1179656 | tf_op jit(solution)/shard_map/ppermute | solution.py:461
  62.0 2.3 %collective-permute-start.7 = (bf16[3,128,512]{2,1,0:T(8,128)(2,1)S(1)}, bf16[3,128,512]{2,1,0:T(8,128)(2,1)S(1)}, u32[]{:S(2)}, u32[]{:S(2)}) collective-permute-start(bf16[3,128,512]{2,1,0:T(8,128)(2,1)S(1)} %get-tuple-element.47), channel_id=1, source_target_pairs={{0,1},{1,2},{2,3},{3,4},{4,5},{5,6},{6,7},{7,8},{8,9},{9,10},{10,1... | collective-permute-start | bytes 1179656 | tf_op jit(solution)/shard_map/ppermute | solution.py:481
  64.3 0.0 copy-start.3
  64.3 0.0 copy-start.5
  64.3 0.0 copy-start.7
  64.3 2.1 %collective-permute-start.6 = (bf16[3,128,512]{2,1,0:T(8,128)(2,1)S(1)}, bf16[3,128,512]{2,1,0:T(8,128)(2,1)S(1)}, u32[]{:S(2)}, u32[]{:S(2)}) collective-permute-start(bf16[3,128,512]{2,1,0:T(8,128)(2,1)S(1)} %get-tuple-element.46), channel_id=1, source_target_pairs={{0,1},{1,2},{2,3},{3,4},{4,5},{5,6},{6,7},{7,8},{8,9},{9,10},{10,1... | collective-permute-start | bytes 1179656 | tf_op jit(solution)/shard_map/ppermute | solution.py:481
  66.4 2.4 %shard_map.138 = (bf16[3,128,512]{2,1,0:T(8,128)(2,1)S(1)}, bf16[3,128,512]{2,1,0:T(8,128)(2,1)S(1)}) custom-call(bf16[128,1536]{1,0:T(8,128)(2,1)S(1)} %get-tuple-element.34.q_ref, bf16[128,1536]{1,0:T(8,128)(2,1)S(1)} %get-tuple-element.35.k_ref, bf16[128,1536]{1,0:T(8,128)(2,1)S(1)} %get-tuple-element.36.v_ref, ...), custom_call_target="tpu_custom_call" | custom-call | flops 1000000000 | bytes 3547136 | tf_op jit(solution)/shard_map/pallas_call | solution.py:401
  68.7 6.6 %collective-permute-start.5 = (bf16[3,128,512]{2,1,0:T(8,128)(2,1)S(1)}, bf16[3,128,512]{2,1,0:T(8,128)(2,1)S(1)}, u32[]{:S(2)}, u32[]{:S(2)}) collective-permute-start(bf16[3,128,512]{2,1,0:T(8,128)(2,1)S(1)} %get-tuple-element.45), channel_id=1, source_target_pairs={{0,1},{1,2},{2,3},{3,4},{4,5},{5,6},{6,7},{7,8},{8,9},{9,10},{10,1... | collective-permute-start | bytes 1179656 | tf_op jit(solution)/shard_map/ppermute | solution.py:481
  75.4 0.0 collective-permute-done.9
  75.5 1.6 %collective-permute-start.10 = (bf16[33,1536]{1,0:T(8,128)(2,1)S(1)}, bf16[33,1536]{1,0:T(8,128)(2,1)S(1)}, u32[]{:S(2)}, u32[]{:S(2)}) collective-permute-start(bf16[33,1536]{1,0:T(8,128)(2,1)S(1)} %add_convert_fusion.2), channel_id=1, source_target_pairs={{0,4},{1,5},{2,6},{3,7},{4,0},{5,1},{6,2},{7,3},{8,12},{9,13},{10,... | collective-permute-start | bytes 304136 | tf_op jit(solution)/shard_map/ppermute | solution.py:419
  77.1 0.0 copy-done.3
  77.1 0.0 copy-done.5
  77.1 0.0 copy-done.7
  77.1 4.8 %shard_map.141 = bf16[3,128,1536]{2,1,0:T(8,128)(2,1)S(1)} custom-call(bf16[128,1536]{1,0:T(8,128)(2,1)S(1)} %bitcast.12, bf16[128,1536]{1,0:T(8,128)(2,1)S(1)} %bitcast.16, bf16[128,1536]{1,0:T(8,128)(2,1)S(1)} %bitcast.20, bf16[12,128,256]{2,1,0:T(8,128)(2,1)S(1)} %get-tuple-element.31.prob_ref, bf16[128,1536]{1,0:T(8,128)(2,1)S(1)} %get-tuple-element.32.context_ref, ...), custom_call_target="tpu_custom_call" | custom-call | flops 3000000000 | bytes 5111808 | tf_op jit(solution)/shard_map/pallas_call | solution.py:401
  81.8 0.0 collective-permute-done.10
  81.9 1.7 %collective-permute-start.11 = (bf16[33,1536]{1,0:T(8,128)(2,1)S(1)}, bf16[33,1536]{1,0:T(8,128)(2,1)S(1)}, u32[]{:S(2)}, u32[]{:S(2)}) collective-permute-start(bf16[33,1536]{1,0:T(8,128)(2,1)S(1)} %add_convert_fusion.1), channel_id=1, source_target_pairs={{0,8},{1,9},{2,10},{3,11},{4,12},{5,13},{6,14},{7,15},{8,0},{9,1},... | collective-permute-start | bytes 304136 | tf_op jit(solution)/shard_map/ppermute | solution.py:419
  83.6 0.0 collective-permute-done.7
  83.6 0.0 collective-permute-done.6
  83.6 0.0 collective-permute-done.5
  83.6 0.3 maximum_add_fusion
  83.9 1.0 %fusion = (bf16[1,128,1536]{2,1,0:T(8,128)(2,1)}, bf16[1,128,1536]{2,1,0:T(8,128)(2,1)}, bf16[1,128,1536]{2,1,0:T(8,128)(2,1)}) fusion(bf16[3,128,1536]{2,1,0:T(8,128)(2,1)S(1)} %maximum_add_fusion), kind=kLoop, calls=%fused_computation.9 | loop fusion | bytes 2359296 | tf_op jit(solution)/shard_map/slice | solution.py:497
  84.9 5.6 %collective-permute-done.11 = bf16[33,1536]{1,0:T(8,128)(2,1)S(1)} collective-permute-done((bf16[33,1536]{1,0:T(8,128)(2,1)S(1)}, bf16[33,1536]{1,0:T(8,128)(2,1)S(1)}, u32[]{:S(2)}, u32[]{:S(2)}) %collective-permute-start.11) | collective-permute-done | bytes 101408 | tf_op jit(solution)/shard_map/ppermute | solution.py:419
  90.6 1.6 %collective-permute-start.12 = (bf16[33,1536]{1,0:T(8,128)(2,1)S(1)}, bf16[33,1536]{1,0:T(8,128)(2,1)S(1)}, u32[]{:S(2)}, u32[]{:S(2)}) collective-permute-start(bf16[33,1536]{1,0:T(8,128)(2,1)S(1)} %add_convert_fusion), channel_id=1, source_target_pairs={{0,16},{16,0},{1,17},{17,1},{2,18},{18,2},{3,19},{19,3},{4,20},{20... | collective-permute-start | bytes 304136 | tf_op jit(solution)/shard_map/ppermute | solution.py:419
  92.2 0.0 collective-permute-done.3
  92.2 0.8 add_bitcast_fusion
  93.0 2.9 %collective-permute-done.12 = bf16[33,1536]{1,0:T(8,128)(2,1)S(1)} collective-permute-done((bf16[33,1536]{1,0:T(8,128)(2,1)S(1)}, bf16[33,1536]{1,0:T(8,128)(2,1)S(1)}, u32[]{:S(2)}, u32[]{:S(2)}) %collective-permute-start.12) | collective-permute-done | bytes 101408 | tf_op jit(solution)/shard_map/ppermute | solution.py:419
  95.9 0.6 slice_reduce_fusion
  96.6 0.7 slice.28
  (6 shorter events, 0.2 us)
Async XLA Ops:
  0.6 28.7 %collective-permute-start = (bf16[128,1536]{1,0:T(8,128)(2,1)}, bf16[128,1536]{1,0:T(8,128)(2,1)S(1)}, u32[]{:S(2)}, u32[]{:S(2)}) collective-permute-start(bf16[128,1536]{1,0:T(8,128)(2,1)} %bitcast.9), channel_id=1, source_target_pairs={{1,0},{2,1},{3,2},{4,3},{5,4},{6,5},{7,6},{8,7},{9,8},{10,9},{11,1... | collective-permute-start | bytes 1179656 | tf_op jit(solution)/shard_map/ppermute | solution.py:435
  1.9 27.5 %collective-permute-start.1 = (bf16[128,1536]{1,0:T(8,128)(2,1)}, bf16[128,1536]{1,0:T(8,128)(2,1)S(1)}, u32[]{:S(2)}, u32[]{:S(2)}) collective-permute-start(bf16[128,1536]{1,0:T(8,128)(2,1)} %bitcast.13), channel_id=1, source_target_pairs={{1,0},{2,1},{3,2},{4,3},{5,4},{6,5},{7,6},{8,7},{9,8},{10,9},{11,1... | collective-permute-start | bytes 1179656 | tf_op jit(solution)/shard_map/ppermute | solution.py:435
  3.2 26.2 %collective-permute-start.2 = (bf16[128,1536]{1,0:T(8,128)(2,1)}, bf16[128,1536]{1,0:T(8,128)(2,1)S(1)}, u32[]{:S(2)}, u32[]{:S(2)}) collective-permute-start(bf16[128,1536]{1,0:T(8,128)(2,1)} %bitcast.17), channel_id=1, source_target_pairs={{1,0},{2,1},{3,2},{4,3},{5,4},{6,5},{7,6},{8,7},{9,8},{10,9},{11,1... | collective-permute-start | bytes 1179656 | tf_op jit(solution)/shard_map/ppermute | solution.py:435
  4.5 37.3 %collective-permute-start.4 = (bf16[128,1536]{1,0:T(8,128)(2,1)}, bf16[128,1536]{1,0:T(8,128)(2,1)S(1)}, u32[]{:S(2)}, u32[]{:S(2)}) collective-permute-start(bf16[128,1536]{1,0:T(8,128)(2,1)} %bitcast.6), channel_id=1, source_target_pairs={{1,0},{2,1},{3,2},{4,3},{5,4},{6,5},{7,6},{8,7},{9,8},{10,9},{11,1... | collective-permute-start | bytes 1179656 | tf_op jit(solution)/shard_map/ppermute | solution.py:435
  7.2 1.0 %copy-start = (bf16[1,128,1536]{2,1,0:T(8,128)(2,1)S(1)}, bf16[1,128,1536]{2,1,0:T(8,128)(2,1)}, u32[]{:S(2)}) copy-start(bf16[1,128,1536]{2,1,0:T(8,128)(2,1)} %param.15) | copy-start | bytes 1179652
  8.2 1.0 %copy-start.2 = (bf16[1,128,1536]{2,1,0:T(8,128)(2,1)S(1)}, bf16[1,128,1536]{2,1,0:T(8,128)(2,1)}, u32[]{:S(2)}) copy-start(bf16[1,128,1536]{2,1,0:T(8,128)(2,1)} %param.8) | copy-start | bytes 1179652
  9.2 1.0 %copy-start.4 = (bf16[1,128,1536]{2,1,0:T(8,128)(2,1)S(1)}, bf16[1,128,1536]{2,1,0:T(8,128)(2,1)}, u32[]{:S(2)}) copy-start(bf16[1,128,1536]{2,1,0:T(8,128)(2,1)} %param.9) | copy-start | bytes 1179652
  10.2 1.0 %copy-start.6 = (bf16[1,128,1536]{2,1,0:T(8,128)(2,1)S(1)}, bf16[1,128,1536]{2,1,0:T(8,128)(2,1)}, u32[]{:S(2)}) copy-start(bf16[1,128,1536]{2,1,0:T(8,128)(2,1)} %param.10) | copy-start | bytes 1179652
  11.2 0.9 copy-start.8
  12.1 0.7 copy-start.10
  29.3 12.5 %copy-start.1 = (bf16[1,128,1536]{2,1,0:T(8,128)(2,1)S(1)}, bf16[1,128,1536]{2,1,0:T(8,128)(2,1)}, u32[]{:S(2)}) copy-start(bf16[1,128,1536]{2,1,0:T(8,128)(2,1)} %param.15) | copy-start | bytes 1179652
  29.4 12.5 %copy-start.9 = (f32[31,1536]{1,0:T(8,128)S(1)}, f32[31,1536]{1,0:T(8,128)}, u32[]{:S(2)}) copy-start(f32[31,1536]{1,0:T(8,128)} %kernel_ref.5) | copy-start | bytes 571396
  29.4 12.5 %copy-start.11 = (s32[1,2048]{1,0:T(1,128)S(1)}, s32[1,2048]{1,0:T(1,128)}, u32[]{:S(2)}) copy-start(s32[1,2048]{1,0:T(1,128)} %seg_ref.11) | copy-start | bytes 24580
  49.4 5.5 %collective-permute-start.8 = (bf16[33,1536]{1,0:T(8,128)(2,1)S(1)}, bf16[33,1536]{1,0:T(8,128)(2,1)S(1)}, u32[]{:S(2)}, u32[]{:S(2)}) collective-permute-start(bf16[33,1536]{1,0:T(8,128)(2,1)S(1)} %convert_element_type.45), channel_id=1, source_target_pairs={{0,1},{1,0},{2,3},{3,2},{4,5},{5,4},{6,7},{7,6},{8,9},{9,8},{10,11... | collective-permute-start | bytes 304136 | tf_op jit(solution)/shard_map/ppermute | solution.py:419
  54.9 20.5 %collective-permute-start.9 = (bf16[33,1536]{1,0:T(8,128)(2,1)S(1)}, bf16[33,1536]{1,0:T(8,128)(2,1)S(1)}, u32[]{:S(2)}, u32[]{:S(2)}) collective-permute-start(bf16[33,1536]{1,0:T(8,128)(2,1)S(1)} %add_convert_fusion.3), channel_id=1, source_target_pairs={{0,2},{1,3},{2,0},{3,1},{4,6},{5,7},{6,4},{7,5},{8,10},{9,11},{10,... | collective-permute-start | bytes 304136 | tf_op jit(solution)/shard_map/ppermute | solution.py:419
  60.3 31.9 %collective-permute-start.3 = (bf16[128,1536]{1,0:T(8,128)(2,1)S(1)}, bf16[128,1536]{1,0:T(8,128)(2,1)S(1)}, u32[]{:S(2)}, u32[]{:S(2)}) collective-permute-start(bf16[128,1536]{1,0:T(8,128)(2,1)S(1)} %get-tuple-element.30), channel_id=1, source_target_pairs={{0,1},{1,2},{2,3},{3,4},{4,5},{5,6},{6,7},{7,8},{8,9},{9,10},{10,1... | collective-permute-start | bytes 1179656 | tf_op jit(solution)/shard_map/ppermute | solution.py:461
  62.0 21.6 %collective-permute-start.7 = (bf16[3,128,512]{2,1,0:T(8,128)(2,1)S(1)}, bf16[3,128,512]{2,1,0:T(8,128)(2,1)S(1)}, u32[]{:S(2)}, u32[]{:S(2)}) collective-permute-start(bf16[3,128,512]{2,1,0:T(8,128)(2,1)S(1)} %get-tuple-element.47), channel_id=1, source_target_pairs={{0,1},{1,2},{2,3},{3,4},{4,5},{5,6},{6,7},{7,8},{8,9},{9,10},{10,1... | collective-permute-start | bytes 1179656 | tf_op jit(solution)/shard_map/ppermute | solution.py:481
  64.3 12.8 %copy-start.3 = (bf16[1,128,1536]{2,1,0:T(8,128)(2,1)S(1)}, bf16[1,128,1536]{2,1,0:T(8,128)(2,1)}, u32[]{:S(2)}) copy-start(bf16[1,128,1536]{2,1,0:T(8,128)(2,1)} %param.8) | copy-start | bytes 1179652
  64.3 12.8 %copy-start.5 = (bf16[1,128,1536]{2,1,0:T(8,128)(2,1)S(1)}, bf16[1,128,1536]{2,1,0:T(8,128)(2,1)}, u32[]{:S(2)}) copy-start(bf16[1,128,1536]{2,1,0:T(8,128)(2,1)} %param.9) | copy-start | bytes 1179652
  64.3 12.8 %copy-start.7 = (bf16[1,128,1536]{2,1,0:T(8,128)(2,1)S(1)}, bf16[1,128,1536]{2,1,0:T(8,128)(2,1)}, u32[]{:S(2)}) copy-start(bf16[1,128,1536]{2,1,0:T(8,128)(2,1)} %param.10) | copy-start | bytes 1179652
  64.3 19.3 %collective-permute-start.6 = (bf16[3,128,512]{2,1,0:T(8,128)(2,1)S(1)}, bf16[3,128,512]{2,1,0:T(8,128)(2,1)S(1)}, u32[]{:S(2)}, u32[]{:S(2)}) collective-permute-start(bf16[3,128,512]{2,1,0:T(8,128)(2,1)S(1)} %get-tuple-element.46), channel_id=1, source_target_pairs={{0,1},{1,2},{2,3},{3,4},{4,5},{5,6},{6,7},{7,8},{8,9},{9,10},{10,1... | collective-permute-start | bytes 1179656 | tf_op jit(solution)/shard_map/ppermute | solution.py:481
  68.7 14.9 %collective-permute-start.5 = (bf16[3,128,512]{2,1,0:T(8,128)(2,1)S(1)}, bf16[3,128,512]{2,1,0:T(8,128)(2,1)S(1)}, u32[]{:S(2)}, u32[]{:S(2)}) collective-permute-start(bf16[3,128,512]{2,1,0:T(8,128)(2,1)S(1)} %get-tuple-element.45), channel_id=1, source_target_pairs={{0,1},{1,2},{2,3},{3,4},{4,5},{5,6},{6,7},{7,8},{8,9},{9,10},{10,1... | collective-permute-start | bytes 1179656 | tf_op jit(solution)/shard_map/ppermute | solution.py:481
  75.5 6.4 %collective-permute-start.10 = (bf16[33,1536]{1,0:T(8,128)(2,1)S(1)}, bf16[33,1536]{1,0:T(8,128)(2,1)S(1)}, u32[]{:S(2)}, u32[]{:S(2)}) collective-permute-start(bf16[33,1536]{1,0:T(8,128)(2,1)S(1)} %add_convert_fusion.2), channel_id=1, source_target_pairs={{0,4},{1,5},{2,6},{3,7},{4,0},{5,1},{6,2},{7,3},{8,12},{9,13},{10,... | collective-permute-start | bytes 304136 | tf_op jit(solution)/shard_map/ppermute | solution.py:419
  81.9 8.6 %collective-permute-start.11 = (bf16[33,1536]{1,0:T(8,128)(2,1)S(1)}, bf16[33,1536]{1,0:T(8,128)(2,1)S(1)}, u32[]{:S(2)}, u32[]{:S(2)}) collective-permute-start(bf16[33,1536]{1,0:T(8,128)(2,1)S(1)} %add_convert_fusion.1), channel_id=1, source_target_pairs={{0,8},{1,9},{2,10},{3,11},{4,12},{5,13},{6,14},{7,15},{8,0},{9,1},... | collective-permute-start | bytes 304136 | tf_op jit(solution)/shard_map/ppermute | solution.py:419
  90.6 5.3 %collective-permute-start.12 = (bf16[33,1536]{1,0:T(8,128)(2,1)S(1)}, bf16[33,1536]{1,0:T(8,128)(2,1)S(1)}, u32[]{:S(2)}, u32[]{:S(2)}) collective-permute-start(bf16[33,1536]{1,0:T(8,128)(2,1)S(1)} %add_convert_fusion), channel_id=1, source_target_pairs={{0,16},{16,0},{1,17},{17,1},{2,18},{18,2},{3,19},{19,3},{4,20},{20... | collective-permute-start | bytes 304136 | tf_op jit(solution)/shard_map/ppermute | solution.py:419

commit v2 on v1

--- a/solution.py
+++ b/solution.py
@@ -12,7 +12,8 @@
 NEG = -1e30
 LANES = 128
 PAD = 16
-GROUPS = 3
+GROUPS = 2
+WIDE = 512
 VMEM = pl.BlockSpec(memory_space=pltpu.VMEM)
 F32 = jnp.float32
 BF16 = jnp.bfloat16
@@ -200,25 +201,40 @@
         out_ref[rows, :] = jnp.where(keep[rows.start : rows.start + CHUNK, 0:1] > 0.0, result, 0.0).astype(BF16)
 
 
-def own_kernel(
-    q_ref, k_ref, v_ref, cot_ref, seg_ref, gain_ref, kernel_ref, bias_ref,
-    out_ref, grad_ref, prob_ref, context_ref, sums_ref,
-    pad_ref, normed_ref, pre_ref, mask_ref, keep_ref,
-):
-    frames, width = q_ref.shape
-    taps = kernel_ref.shape[0]
-    tiles = width // LANES
+def wide(width):
+    return [slice(start, start + WIDE) for start in range(0, width, WIDE)]
+
+
+def forward_all(q_ref, k_ref, v_ref, prob_ref, context_ref, bias, keep, low):
+    for index in range(q_ref.shape[1] // LANES):
+        lanes = slice(index * LANES, (index + 1) * LANES)
+        prob, context = attend(q_ref[:, lanes], k_ref[:, lanes], v_ref[:, lanes], bias, keep, low)
+        prob_ref[index] = prob
+        context_ref[:, lanes] = context
+
+
+def normalize_all(context_ref, gain_ref, keep, normed_ref, in_ref, offset, frames):
+    for rows in chunks(frames):
+        normed, _ = normalize(context_ref[rows, :])
+        normed = jnp.where(keep[rows.start : rows.start + CHUNK, 0:1] > 0.0, normed, 0.0)
+        if normed_ref is not None:
+            normed_ref[rows, :] = normed
+        in_ref[pl.ds(offset + rows.start, CHUNK), :] = (
+            (normed * gain_ref[0:1, :]).astype(BF16).astype(F32)
+        )
+
+
+def mask_kernel(taps, seg_ref, bias_ref, keep_ref, mask_ref, pad_ref):
+    frames = bias_ref.shape[0]
     own, _, prev_last, next_first = block_ids(seg_ref, frames)
     ids = jnp.where((own == prev_last) | (own == next_first), -5.0, own)
     ids_row = jnp.broadcast_to(ids, (frames, frames))
     ids_col = jnp.transpose(ids_row)
-    bias = jnp.where(ids_row == ids_col, 0.0, NEG)
-    keep = jnp.where(ids_col >= 0.0, 1.0, 0.0)
-    keep_ref[...] = keep
-    pad_ref[0:PAD, 0:LANES] = jnp.full((PAD, LANES), -9.0, F32)
-    pad_ref[PAD + frames :, 0:LANES] = jnp.full((PAD, LANES), -9.0, F32)
-    pad_ref[PAD : PAD + frames, 0:LANES] = ids_col
-    ids_pad = pad_ref[:, 0:LANES]
+    bias_ref[...] = jnp.where(ids_row == ids_col, 0.0, NEG)
+    keep_ref[...] = jnp.where(ids_col >= 0.0, 1.0, 0.0)
+    pad_ref[...] = jnp.full(pad_ref.shape, -9.0, F32)
+    pad_ref[PAD : PAD + frames, :] = ids_col
+    ids_pad = pad_ref[...]
     at, view = None, None
     for turn, start, tap in shifts(frames, taps):
         if turn != at:
@@ -226,23 +242,23 @@
         mask_ref[tap * frames : (tap + 1) * frames, :] = jnp.where(
             view[start : start + frames] == ids_col, 1.0, 0.0
         )
+
+
+def own_kernel(
+    q_ref, k_ref, v_ref, cot_ref, gain_row, kernel_ref, bias_row, same_ref, keep_ref, mask_ref,
+    out_ref, grad_ref, prob_ref, context_ref, sums_ref, gain_ref, bias_ref,
+    pad_ref, normed_ref, pre_ref,
+):
+    frames, width = q_ref.shape
+    taps = kernel_ref.shape[0]
+    tiles = width // LANES
     clear_edges(pad_ref, frames)
     low = pair_masks(frames)
-
-    @pl.loop(0, tiles)
-    def _(index):
-        lanes = lanes_of(index)
-        prob, context = attend(q_ref[:, lanes], k_ref[:, lanes], v_ref[:, lanes], bias, keep, low)
-        prob_ref[index] = prob
-        context_ref[:, lanes] = context
-
-    for rows in chunks(frames):
-        normed, _ = normalize(context_ref[rows, :])
-        normed = jnp.where(keep[rows.start : rows.start + CHUNK, 0:1] > 0.0, normed, 0.0)
-        normed_ref[rows, :] = normed
-        pad_ref[pl.ds(PAD + rows.start, CHUNK), :] = (
-            (normed * gain_ref[0:1, :]).astype(BF16).astype(F32)
-        )
+    gain_ref[...] = gain_row[...].reshape(1, width)
+    bias_ref[...] = bias_row[...].reshape(1, width)
+    bias, keep = same_ref[...], keep_ref[...]
+    forward_all(q_ref, k_ref, v_ref, prob_ref, context_ref, bias, keep, low)
+    normalize_all(context_ref, gain_ref, keep, normed_ref, pad_ref, PAD, frames)
 
     @pl.loop(0, tiles)
     def _(index):
@@ -271,9 +287,9 @@
 
 
 def cross_forward_kernel(
-    q_ref, k_ref, v_ref, qn_ref, kn_ref, vn_ref, seg_ref, gain_ref, kernel_ref, bias_ref,
+    q_ref, k_ref, v_ref, qn_ref, kn_ref, vn_ref, seg_ref, gain_ref, kernel_ref, bias_ref, add_ref,
     own_ref, next_ref, qg_ref, kg_ref, vg_ref, prob_ref, context_ref, pre_ref,
-    pad_ref,
+    pad_ref, out_ref,
 ):
     frames, width = q_ref.shape
     tiles = width // LANES
@@ -285,44 +301,30 @@
     keep = jnp.where(iota(shape, 0) < length, 1.0, 0.0)
     low = pair_masks(frames)
     clear_edges(pad_ref, frames)
-
-    @pl.loop(0, tiles)
-    def _(index):
-        lanes = lanes_of(index)
-
-        def picked(own, other):
-            both = jnp.concatenate([own[:, lanes], other[:, lanes]], 0)
-            return dot(pick, both, NN).astype(BF16)
-
-        query, key, value = picked(q_ref, qn_ref), picked(k_ref, kn_ref), picked(v_ref, vn_ref)
-        qg_ref[:, lanes] = query
-        kg_ref[:, lanes] = key
-        vg_ref[:, lanes] = value
-        prob, context = attend(query, key, value, bias, keep, low)
-        prob_ref[index] = prob
-        context_ref[:, lanes] = context
-
-    for rows in chunks(frames):
-        normed, _ = normalize(context_ref[rows, :])
-        normed = jnp.where(keep[rows.start : rows.start + CHUNK, 0:1] > 0.0, normed, 0.0)
-        pad_ref[pl.ds(PAD + rows.start, CHUNK), :] = (
-            (normed * gain_ref[0:1, :]).astype(BF16).astype(F32)
-        )
+    for own, other, got in ((q_ref, qn_ref, qg_ref), (k_ref, kn_ref, kg_ref), (v_ref, vn_ref, vg_ref)):
+        for cols in wide(width):
+            both = jnp.concatenate([own[:, cols], other[:, cols]], 0)
+            got[:, cols] = dot(pick, both, NN).astype(BF16)
+    forward_all(qg_ref, kg_ref, vg_ref, prob_ref, context_ref, bias, keep, low)
+    normalize_all(context_ref, gain_ref, keep, None, pad_ref, PAD, frames)
 
     @pl.loop(0, tiles)
     def _(index):
         lanes = lanes_of(index)
         pre_act = conv_forward(pad_ref, kernel_ref, bias_ref, None, frames, lanes)
         pre_ref[:, lanes] = pre_act
-        placed = dot(place, (pre_act * gate(pre_act)).astype(BF16), NN).astype(BF16)
-        own_ref[:, lanes] = placed[:frames]
-        next_ref[:, lanes] = placed[frames:]
+        out_ref[:, lanes] = (pre_act * gate(pre_act)).astype(BF16)
+
+    for cols in wide(width):
+        placed = dot(place, out_ref[:, cols], NN).astype(BF16)
+        own_ref[:, cols] = placed[:frames] + add_ref[:, cols]
+        next_ref[:, cols] = placed[frames:]
 
 
 def cross_conv_kernel(
     cot_ref, cotn_ref, seg_ref, gain_ref, kernel_ref, context_ref, pre_ref, part_ref,
-    grad_ref, sums_ref,
-    pad_ref, in_ref, normed_ref, back_ref,
+    back_ref, sums_ref, sent_ref,
+    pad_ref, in_ref, normed_ref,
 ):
     frames, width = cot_ref.shape
     taps = kernel_ref.shape[0]
@@ -331,50 +333,54 @@
     pick = gather_matrix(first, length, frames)
     keep = jnp.where(iota((frames, frames), 0) < length, 1.0, 0.0)
     clear_edges(pad_ref, frames)
-    for rows in chunks(frames):
-        normed, _ = normalize(context_ref[rows, :])
-        normed = jnp.where(keep[rows.start : rows.start + CHUNK, 0:1] > 0.0, normed, 0.0)
-        normed_ref[rows, :] = normed
-        in_ref[rows, :] = (normed * gain_ref[0:1, :]).astype(BF16).astype(F32)
+    for cols in wide(width):
+        cotangent = dot(pick, jnp.concatenate([cot_ref[:, cols], cotn_ref[:, cols]], 0), NN)
+        pre_act = pre_ref[:, cols]
+        pad_ref[PAD : PAD + frames, cols] = gate_grad(cotangent, pre_act, gate(pre_act))
+    normalize_all(context_ref, gain_ref, keep, normed_ref, in_ref, 0, frames)
 
     @pl.loop(0, tiles)
     def _(index):
         lanes = lanes_of(index)
-        cotangent = dot(pick, jnp.concatenate([cot_ref[:, lanes], cotn_ref[:, lanes]], 0), NN)
-        pre_act = pre_ref[:, lanes]
-        grad_pre = gate_grad(cotangent, pre_act, gate(pre_act))
-        pad_ref[PAD : PAD + frames, lanes] = grad_pre
 
         def store(row, value):
             sums_ref[row : row + 1, lanes] = part_ref[row : row + 1, lanes] + value
 
-        store(taps, jnp.sum(grad_pre, 0, keepdims=True))
+        store(taps, jnp.sum(pad_ref[PAD : PAD + frames, lanes], 0, keepdims=True))
         grad_in = conv_backward(pad_ref, in_ref[:, lanes], kernel_ref, None, frames, lanes, store)
         store(taps + 1, jnp.sum(grad_in * normed_ref[:, lanes], 0, keepdims=True))
         back_ref[:, lanes] = grad_in
 
-    norm_backward(context_ref, back_ref, gain_ref, keep, grad_ref, frames)
+    sent_ref[...] = sums_ref[...].astype(BF16)
 
 
 def cross_back_kernel(
-    group, tiles, q_ref, k_ref, v_ref, prob_ref, context_ref, grad_ref, seg_ref, own_ref, next_ref
+    group, tiles, q_ref, k_ref, v_ref, prob_ref, context_ref, back_ref, gain_ref, seg_ref,
+    own_ref, next_ref, grad_ref=None,
 ):
     frames = q_ref.shape[0]
-    place = scatter_matrix(*crossing(seg_ref, frames), frames)
+    first, length = crossing(seg_ref, frames)
+    place = scatter_matrix(first, length, frames)
     low = pair_masks(frames)
-
-    @pl.loop(0, tiles)
-    def _(step):
+    if group == 0:
+        keep = jnp.where(iota((frames, frames), 0) < length, 1.0, 0.0)
+        norm_backward(context_ref, back_ref, gain_ref, keep, grad_ref, frames)
+    else:
+        grad_ref = back_ref
+    for step in range(tiles):
         index = group * tiles + step
-        lanes, dest = lanes_of(index), lanes_of(step)
+        lanes = slice(index * LANES, (index + 1) * LANES)
+        dest = slice(step * LANES, (step + 1) * LANES)
         results = attend_back(
             q_ref[:, lanes], k_ref[:, lanes], v_ref[:, lanes], prob_ref[index],
             context_ref[:, lanes], grad_ref[:, lanes], low,
         )
-        for which, result in enumerate(results):
-            placed = dot(place, result.astype(BF16), NN).astype(BF16)
-            own_ref[which, :, dest] = placed[:frames]
-            next_ref[which, :, dest] = placed[frames:]
+        joined = jnp.concatenate([result.astype(BF16) for result in results], 1)
+        placed = dot(place, joined, NN).astype(BF16)
+        for which in range(3):
+            cols = slice(which * LANES, (which + 1) * LANES)
+            own_ref[which, :, dest] = placed[:frames, cols]
+            next_ref[which, :, dest] = placed[frames:, cols]
 
 
 def own_back_kernel(q_ref, k_ref, v_ref, prob_ref, context_ref, grad_ref, *refs):
@@ -383,17 +389,24 @@
     low = pair_masks(frames)
     tiles = width // LANES // len(cross)
     for group, cross_ref in enumerate(cross):
-
-        @pl.loop(0, tiles)
-        def _(step):
+        for step in range(tiles):
             index = group * tiles + step
-            lanes, dest = lanes_of(index), lanes_of(step)
+            lanes = slice(index * LANES, (index + 1) * LANES)
+            dest = slice(step * LANES, (step + 1) * LANES)
             results = attend_back(
                 q_ref[:, lanes], k_ref[:, lanes], v_ref[:, lanes], prob_ref[index],
                 context_ref[:, lanes], grad_ref[:, lanes], low,
             )
             for which, result in enumerate(results):
                 out_ref[which, :, lanes] = result.astype(BF16) + cross_ref[which, :, dest]
+
+
+def finish_kernel(scale, sent_ref, came_ref, gain_ref, kernel_ref, bias_ref):
+    taps, width = kernel_ref.shape
+    total = (sent_ref[...].astype(F32) + came_ref[...].astype(F32)) * scale
+    kernel_ref[...] = total[:taps]
+    bias_ref[...] = total[taps : taps + 1].reshape(width)
+    gain_ref[...] = total[taps + 1 : taps + 2].reshape(width)
 
 
 def call(kernel, outs, scratch, flops, *args):
@@ -404,22 +417,31 @@
         in_specs=[VMEM] * len(args),
         out_specs=[VMEM] * len(outs),
         scratch_shapes=scratch,
-        compiler_params=pltpu.CompilerParams(vmem_limit_bytes=40 * 1024 * 1024),
+        compiler_params=pltpu.CompilerParams(vmem_limit_bytes=24 * 1024 * 1024),
         cost_estimate=pl.CostEstimate(flops=flops, bytes_accessed=size, transcendentals=0),
     )(*args)
 
 
-def total_over_devices(part, axes):
-    total = part
+def after(value, *others):
+    return lax.optimization_barrier((value,) + others)[0]
+
+
+def sum_steps(axes):
+    steps = []
     for axis in axes:
-        count = lax.axis_size(axis)
         step = 1
-        while step < count:
-            sent = total.astype(BF16)
-            came = lax.ppermute(sent, axis, [(i, i ^ step) for i in range(count)])
-            total = sent.astype(F32) + came.astype(F32)
+        while step < lax.axis_size(axis):
+            steps.append((axis, step))
             step *= 2
-    return total
+    return steps
+
+
+def exchange(sent, axis, step):
+    return lax.ppermute(sent, axis, [(i, i ^ step) for i in range(lax.axis_size(axis))])
+
+
+def added(sent, came):
+    return (sent.astype(F32) + came.astype(F32)).astype(BF16)
 
 
 def per_device(queries, keys, values, segment_ids, norm_gain, conv_kernel, conv_bias, cotangent):
@@ -428,8 +450,6 @@
     taps = conv_kernel.shape[0]
     tiles = width // LANES
     count = lax.axis_size("seq")
-    gain, bias = norm_gain[None], conv_bias[None]
-    seg = segment_ids
     to_left = [(i + 1, i) for i in range(count - 1)]
     to_right = [(i, i + 1) for i in range(count - 1)]
     qn, kn, vn, cotn = (lax.ppermute(a, "seq", to_left) for a in (q, k, v, cot))
@@ -441,63 +461,92 @@
     rows32 = sds((frames, width), F32)
     probs = sds((tiles, frames, 2 * frames), BF16)
     sums = sds((taps + 2, width), F32)
+    row = sds((1, width), F32)
     padded = pltpu.VMEM((frames + 2 * PAD, width), F32)
     plain = pltpu.VMEM((frames, width), F32)
 
-    out_own, grad_own, prob_own, context_own, sums_own = call(
+    square = sds((frames, frames), F32)
+    same, keep, masks = call(
+        functools.partial(mask_kernel, taps),
+        [square, square, sds((taps * frames, LANES), F32)],
+        [pltpu.VMEM((frames + 2 * PAD, LANES), F32)],
+        10**10,
+        segment_ids,
+    )
+    out_own, grad_own, prob_own, context_own, sums_own, gain, bias = call(
         own_kernel,
-        [rows16, rows16, probs, rows16, sums],
-        [padded, plain, plain, pltpu.VMEM((taps * frames, LANES), F32), pltpu.VMEM((frames, LANES), F32)],
+        [rows16, rows16, probs, rows16, sums, row, row],
+        [padded, plain, plain],
         10**10,
-        q, k, v, cot, seg, gain, conv_kernel, bias,
-    )
-    out_cross, out_next, qg, kg, vg, prob_cross, context_cross, pre_cross = call(
+        q, k, v, cot, norm_gain, conv_kernel, conv_bias, same, keep, masks,
+    )
+    out_both, out_next, qg, kg, vg, prob_cross, context_cross, pre_cross = call(
         cross_forward_kernel,
         [rows16, rows16, rows16, rows16, rows16, probs, rows16, rows32],
-        [padded],
+        [padded, pltpu.VMEM((frames, width), BF16)],
         4 * 10**9,
-        q, k, v, qn, kn, vn, seg, gain, conv_kernel, bias,
+        q, k, v, qn, kn, vn, segment_ids, gain, conv_kernel, bias, out_own,
     )
     out_came = lax.ppermute(out_next, "seq", to_right)
-    grad_cross, sums_both = call(
+    back_cross, _, sent = call(
         cross_conv_kernel,
-        [rows16, sums],
-        [padded, plain, plain, plain],
+        [rows32, sums, sds(sums.shape, BF16)],
+        [padded, plain, plain],
         4 * 10**9,
-        cot, cotn, seg, gain, conv_kernel, context_cross, pre_cross, sums_own,
-    )
+        cot, cotn, segment_ids, gain, conv_kernel, context_cross, pre_cross, sums_own,
+    )
+    steps = sum_steps(("seq", "dp"))
+    came = exchange(sent, *steps[0])
     per_group = tiles // GROUPS
     piece = sds((3, frames, per_group * LANES), BF16)
     own_parts, came_parts = [], []
+    grad_cross = back_cross
     for group in range(GROUPS):
-        own_part, next_part = call(
+        own_part, next_part, *rest = call(
             functools.partial(cross_back_kernel, group, per_group),
-            [piece, piece],
+            [piece, piece] + [rows16] * (group == 0),
             [],
-            10**9,
-            qg, kg, vg, prob_cross, context_cross, grad_cross, seg,
+            2 * 10**9,
+            qg, kg, vg, prob_cross, context_cross, grad_cross, gain, segment_ids,
         )
+        if group == 0:
+            (grad_cross,) = rest
         own_parts.append(own_part)
         came_parts.append(lax.ppermute(next_part, "seq", to_right))
+        if group == 0:
+            conv_out = out_both + after(out_came, own_part)
+            sent = added(sent, after(came, own_part, conv_out))
+        else:
+            sent = added(sent, after(came, own_part, came_parts[0]))
+        came = exchange(sent, *steps[group + 1])
     (grads_own,) = call(
         own_back_kernel,
         [sds((3, frames, width), BF16)],
         [],
-        3 * 10**9,
+        4 * 10**9,
         q, k, v, prob_own, context_own, grad_own, *own_parts,
     )
-    conv_out = out_own + out_cross + out_came
+    came = after(came, grads_own, *came_parts)
+    for step in steps[GROUPS + 1 :]:
+        sent = added(sent, came)
+        came = exchange(sent, *step)
     grads = grads_own + jnp.concatenate(came_parts, 2)
-    total = total_over_devices(sums_both, ("seq", "dp"))
-    total = total * (lax.axis_size("dp") * count * frames) ** (-0.5)
+    scale = (lax.axis_size("dp") * count * frames) ** (-0.5)
+    gain_grad, kernel_grad, bias_grad = call(
+        functools.partial(finish_kernel, scale),
+        [sds((width,), F32), sds(conv_kernel.shape, F32), sds((width,), F32)],
+        [],
+        10**6,
+        sent, came,
+    )
     return (
         conv_out[None],
         grads[0][None],
         grads[1][None],
         grads[2][None],
-        total[taps + 1],
-        total[:taps],
-        total[taps],
+        gain_grad,
+        kernel_grad,
+        bias_grad,
     )
 
 

time: 97.9 us -> 85 us (0.87)
  Pallas kernels: 48.3 us -> 33.7 us
  starting transfers between devices: 28.8 us -> 38.6 us
  local copies, waits for them, and re-layouts: 9.4 us -> 1.76 us
    pallas_call x7 -> x8, Pallas kernels: 48.3 us -> 33.7 us  [call(): pl.pallas_call(kernel, out_shape=outs, in_specs=[VMEM] * len(args), out_s...]
    ppermute x5, starting transfers between devices: 11 us -> 22.4 us  [exchange(): lax.ppermute(sent, axis, [(i, i ^ step) for i in range(lax.axis_size(axis...]
    ppermute x3 -> x2, starting transfers between devices: 11 us -> 6.02 us  [per_device(): came_parts.append(lax.ppermute(next_part, 'seq', to_right))]
    unnamed x24 -> x18, local copies, waits for them, and re-layouts: 5.64 us -> 0.73 us
    ppermute x1, starting transfers between devices: 1.66 us -> 4.94 us  [per_device(): out_came = lax.ppermute(out_next, 'seq', to_right)]
    broadcast_in_dim x2 -> x0, local copies, waits for them, and re-layouts: 1.4 us -> none  [per_device(): gain, bias = (norm_gain[None], conv_bias[None])]
    slice x2 -> x0, local copies, waits for them, and re-layouts: 1.32 us -> none  [the longest x1 0.69 us: per_device(): total[:taps]]
  transfers between devices with their start and end apart: 13 -> 12, of which waited for: 2 -> 3; matrix products, arithmetic and copies ran while one was open for 4% -> 3% of each run, Pallas kernels for 42% -> 39%
where the time goes in v2:
time: 85 us; the launch traced here: 84.6 us
  starting transfers between devices  38.6 us (45%)
  Pallas kernels  33.7 us (40%)
  waiting for transfers between devices  8.33 us (10%)
  local copies, waits for them, and re-layouts  1.76 us (2%)
  other arithmetic  1.28 us (2%)
  between operations  0.96 us (1%)
    pallas_call x8, Pallas kernels, call(): pl.pallas_call(kernel, out_shape=outs, in_specs=[VMEM] * len(args), out_s...  33.7 us
    ppermute x5, starting transfers between devices, exchange(): lax.ppermute(sent, axis, [(i, i ^ step) for i in range(lax.axis_size(axis...  22.4 us
    ppermute x5, waiting for transfers between devices, exchange(): lax.ppermute(sent, axis, [(i, i ^ step) for i in range(lax.axis_size(axis...  8.31 us
    ppermute x2, starting transfers between devices, per_device(): came_parts.append(lax.ppermute(next_part, 'seq', to_right))  6.02 us
    ppermute x4, starting transfers between devices, per_device(): qn, kn, vn, cotn = (lax.ppermute(a, 'seq', to_left) for a in (q, k, v, cot))  5.3 us
    ppermute x1, starting transfers between devices, per_device(): out_came = lax.ppermute(out_next, 'seq', to_right)  4.94 us
  transfers between devices with their start and end apart: 12, of which 3 were waited for; matrix products, arithmetic and copies ran while one was open for 3% of the time, Pallas kernels for 39%

profile of v2, /device:TPU:0, one launch (start us, length us, event | category | flops | bytes accessed | tf_op | source)
XLA Modules:
  0.0 84.6 jit_solution(16302008357677078992)
XLA Ops:
  0.6 1.3 %collective-permute-start = (bf16[128,1536]{1,0:T(8,128)(2,1)}, bf16[128,1536]{1,0:T(8,128)(2,1)S(1)}, u32[]{:S(2)}, u32[]{:S(2)}) collective-permute-start(bf16[128,1536]{1,0:T(8,128)(2,1)} %bitcast.8), channel_id=1, source_target_pairs={{1,0},{2,1},{3,2},{4,3},{5,4},{6,5},{7,6},{8,7},{9,8},{10,9},{11,1... | collective-permute-start | bytes 1179656 | tf_op jit(solution)/shard_map/ppermute | solution.py:455
  1.9 1.3 %collective-permute-start.1 = (bf16[128,1536]{1,0:T(8,128)(2,1)}, bf16[128,1536]{1,0:T(8,128)(2,1)S(1)}, u32[]{:S(2)}, u32[]{:S(2)}) collective-permute-start(bf16[128,1536]{1,0:T(8,128)(2,1)} %bitcast.12), channel_id=1, source_target_pairs={{1,0},{2,1},{3,2},{4,3},{5,4},{6,5},{7,6},{8,7},{9,8},{10,9},{11,1... | collective-permute-start | bytes 1179656 | tf_op jit(solution)/shard_map/ppermute | solution.py:455
  3.2 1.3 %collective-permute-start.2 = (bf16[128,1536]{1,0:T(8,128)(2,1)}, bf16[128,1536]{1,0:T(8,128)(2,1)S(1)}, u32[]{:S(2)}, u32[]{:S(2)}) collective-permute-start(bf16[128,1536]{1,0:T(8,128)(2,1)} %bitcast.16), channel_id=1, source_target_pairs={{1,0},{2,1},{3,2},{4,3},{5,4},{6,5},{7,6},{8,7},{9,8},{10,9},{11,1... | collective-permute-start | bytes 1179656 | tf_op jit(solution)/shard_map/ppermute | solution.py:455
  4.5 0.0 copy-start
  4.5 0.0 copy-start.1
  4.6 0.0 copy-start.2
  4.6 0.0 copy-start.3
  4.6 0.0 copy-start.4
  4.6 0.0 copy-start.5
  4.6 0.0 copy-start.6
  4.6 1.4 %collective-permute-start.4 = (bf16[128,1536]{1,0:T(8,128)(2,1)}, bf16[128,1536]{1,0:T(8,128)(2,1)S(1)}, u32[]{:S(2)}, u32[]{:S(2)}) collective-permute-start(bf16[128,1536]{1,0:T(8,128)(2,1)} %bitcast.5), channel_id=1, source_target_pairs={{1,0},{2,1},{3,2},{4,3},{5,4},{6,5},{7,6},{8,7},{9,8},{10,9},{11,1... | collective-permute-start | bytes 1179656 | tf_op jit(solution)/shard_map/ppermute | solution.py:455
  6.0 0.0 copy-start.7
  6.0 0.7 copy-done.7
  6.7 0.3 shard_map.135
  7.1 0.0 copy-done
  7.1 0.0 copy-done.1
  7.1 0.0 copy-done.2
  7.1 0.0 copy-done.3
  7.1 0.0 copy-done.4
  7.1 0.0 copy-done.5
  7.1 0.0 copy-done.6
  7.1 0.0 copy-start.8
  7.1 13.2 %shard_map.136 = (bf16[128,1536]{1,0:T(8,128)(2,1)S(1)}, bf16[128,1536]{1,0:T(8,128)(2,1)S(1)}, bf16[12,128,256]{2,1,0:T(8,128)(2,1)S(1)}, bf16[128,1536]{1,0:T(...) custom-call(bf16[128,1536]{1,0:T(8,128)(2,1)S(1)} %bitcast.9, ...), custom_call_target="tpu_custom_call" | custom-call | flops 10000000000 | bytes 6119424 | tf_op jit(solution)/shard_map/pallas_call | solution.py:414
  20.3 0.0 collective-permute-done.qn_ref
  20.3 0.0 collective-permute-done.1.kn_ref
  20.3 0.0 collective-permute-done.2.vn_ref
  20.4 0.0 copy-done.8
  20.4 5.2 %shard_map.137 = (bf16[128,1536]{1,0:T(8,128)(2,1)S(1)}, bf16[128,1536]{1,0:T(8,128)(2,1)S(1)}, bf16[128,1536]{1,0:T(8,128)(2,1)S(1)}, bf16[128,1536]{1,0:T(8,12...) custom-call(bf16[128,1536]{1,0:T(8,128)(2,1)S(1)} %bitcast.10, ...), custom_call_target="tpu_custom_call" | custom-call | flops 4000000000 | bytes 6895616 | tf_op jit(solution)/shard_map/pallas_call | solution.py:414
  25.6 4.9 %collective-permute-start.3 = (bf16[128,1536]{1,0:T(8,128)(2,1)S(1)}, bf16[128,1536]{1,0:T(8,128)(2,1)S(1)}, u32[]{:S(2)}, u32[]{:S(2)}) collective-permute-start(bf16[128,1536]{1,0:T(8,128)(2,1)S(1)} %get-tuple-element.46), channel_id=1, source_target_pairs={{0,1},{1,2},{2,3},{3,4},{4,5},{5,6},{6,7},{7,8},{8,9},{9,10},{10,1... | collective-permute-start | bytes 1179656 | tf_op jit(solution)/shard_map/ppermute | solution.py:490
  30.5 0.0 collective-permute-done.4.cotn_ref
  30.5 6.3 %shard_map.138 = (f32[128,1536]{1,0:T(8,128)S(1)}, f32[33,1536]{1,0:T(8,128)}, bf16[33,1536]{1,0:T(8,128)(2,1)S(1)}) custom-call(bf16[128,1536]{1,0:T(8,128)(2,1)S(1)} %bitcast.7, bf16[128,1536]{1,0:T(8,128)(2,1)S(1)} %collective-permute-done.4.cotn_ref, s32[1,2048]{1,0:T(1,128)S(1)} %copy-done.8, f32[1,1536]{1,0:T(1,128)S(1)} %get-tuple-element.42.gain_ref, ...), custom_call_target="tpu_custom_call" | custom-call | flops 4000000000 | bytes 3464192 | tf_op jit(solution)/shard_map/pallas_call | solution.py:414
  36.8 2.5 %collective-permute-start.7 = (bf16[33,1536]{1,0:T(8,128)(2,1)S(1)}, bf16[33,1536]{1,0:T(8,128)(2,1)S(1)}, u32[]{:S(2)}, u32[]{:S(2)}) collective-permute-start(bf16[33,1536]{1,0:T(8,128)(2,1)S(1)} %get-tuple-element.64), channel_id=1, source_target_pairs={{0,1},{1,0},{2,3},{3,2},{4,5},{5,4},{6,7},{7,6},{8,9},{9,8},{10,11... | collective-permute-start | bytes 304136 | tf_op jit(solution)/shard_map/ppermute | solution.py:440
  39.4 2.8 %shard_map.139 = (bf16[3,128,768]{2,1,0:T(8,128)(2,1)S(1)}, bf16[3,128,768]{2,1,0:T(8,128)(2,1)S(1)}, bf16[128,1536]{1,0:T(8,128)(2,1)S(1)}) custom-call(bf16[128,1536]{1,0:T(8,128)(2,1)S(1)} %get-tuple-element.47.q_ref, bf16[128,1536]{1,0:T(8,128)(2,1)S(1)} %get-tuple-element.48.k_ref, bf16[128,1536]{1,0:T(8,128)(2,1)S(1)} %get-tuple-element.49.v_ref, ...), custom_call_target="tpu_custom_call" | custom-call | flops 2000000000 | bytes 4732928 | tf_op jit(solution)/shard_map/pallas_call | solution.py:414
  42.1 2.0 %collective-permute-start.5 = (bf16[3,128,768]{2,1,0:T(8,128)(2,1)S(1)}, bf16[3,128,768]{2,1,0:T(8,128)(2,1)S(1)}, u32[]{:S(2)}, u32[]{:S(2)}) collective-permute-start(bf16[3,128,768]{2,1,0:T(8,128)(2,1)S(1)} %get-tuple-element.62), channel_id=1, source_target_pairs={{0,1},{1,2},{2,3},{3,4},{4,5},{5,6},{6,7},{7,8},{8,9},{9,10},{10,1... | collective-permute-start | bytes 1769480 | tf_op jit(solution)/shard_map/ppermute | solution.py:515
  44.1 0.0 collective-permute-done.3
  44.1 0.9 %add.18 = bf16[128,1536]{1,0:T(8,128)(2,1)} add(bf16[128,1536]{1,0:T(8,128)(2,1)S(1)} %get-tuple-element.45, bf16[128,1536]{1,0:T(8,128)(2,1)S(1)} %collective-permute-done.3) | non-fusion elementwise | flops 196608 | bytes 1179648 | tf_op jit(solution)/shard_map/add | solution.py:517
  45.0 0.0 collective-permute-done.7
  45.0 3.0 %collective-permute-start.8 = (bf16[33,1536]{1,0:T(8,128)(2,1)S(1)}, bf16[33,1536]{1,0:T(8,128)(2,1)S(1)}, u32[]{:S(2)}, u32[]{:S(2)}) collective-permute-start(bf16[33,1536]{1,0:T(8,128)(2,1)S(1)} %add_convert_fusion.3), channel_id=1, source_target_pairs={{0,2},{1,3},{2,0},{3,1},{4,6},{5,7},{6,4},{7,5},{8,10},{9,11},{10,... | collective-permute-start | bytes 304136 | tf_op jit(solution)/shard_map/ppermute | solution.py:440
  48.0 2.3 %shard_map.140 = (bf16[3,128,768]{2,1,0:T(8,128)(2,1)S(1)}, bf16[3,128,768]{2,1,0:T(8,128)(2,1)S(1)}) custom-call(bf16[128,1536]{1,0:T(8,128)(2,1)S(1)} %get-tuple-element.47.q_ref, bf16[128,1536]{1,0:T(8,128)(2,1)S(1)} %get-tuple-element.48.k_ref, bf16[128,1536]{1,0:T(8,128)(2,1)S(1)} %get-tuple-element.49.v_ref, ...), custom_call_target="tpu_custom_call" | custom-call | flops 2000000000 | bytes 3946496 | tf_op jit(solution)/shard_map/pallas_call | solution.py:414
  50.4 4.1 %collective-permute-start.6 = (bf16[3,128,768]{2,1,0:T(8,128)(2,1)S(1)}, bf16[3,128,768]{2,1,0:T(8,128)(2,1)S(1)}, u32[]{:S(2)}, u32[]{:S(2)}) collective-permute-start(bf16[3,128,768]{2,1,0:T(8,128)(2,1)S(1)} %get-tuple-element.63), channel_id=1, source_target_pairs={{0,1},{1,2},{2,3},{3,4},{4,5},{5,6},{6,7},{7,8},{8,9},{9,10},{10,1... | collective-permute-start | bytes 1769480 | tf_op jit(solution)/shard_map/ppermute | solution.py:515
  54.5 0.0 collective-permute-done.8
  54.5 0.0 collective-permute-done.5
  54.5 12.4 %collective-permute-start.9 = (bf16[33,1536]{1,0:T(8,128)(2,1)S(1)}, bf16[33,1536]{1,0:T(8,128)(2,1)S(1)}, u32[]{:S(2)}, u32[]{:S(2)}) collective-permute-start(bf16[33,1536]{1,0:T(8,128)(2,1)S(1)} %add_convert_fusion.2), channel_id=1, source_target_pairs={{0,4},{1,5},{2,6},{3,7},{4,0},{5,1},{6,2},{7,3},{8,12},{9,13},{10,... | collective-permute-start | bytes 304136 | tf_op jit(solution)/shard_map/ppermute | solution.py:440
  66.9 2.9 %shard_map.141 = bf16[3,128,1536]{2,1,0:T(8,128)(2,1)S(1)} custom-call(bf16[128,1536]{1,0:T(8,128)(2,1)S(1)} %bitcast.11, bf16[128,1536]{1,0:T(8,128)(2,1)S(1)} %bitcast.15, bf16[128,1536]{1,0:T(8,128)(2,1)S(1)} %bitcast.19, bf16[12,128,256]{2,1,0:T(8,128)(2,1)S(1)} %get-tuple-element.57.prob_ref, bf16[128,1536]{1,0:T(8,128)(2,1)S(1)} %get-tuple-element.58.context_ref, ...), custom_call_target="tpu_custom_call" | custom-call | flops 4000000000 | bytes 5111808 | tf_op jit(solution)/shard_map/pallas_call | solution.py:414
  69.8 0.0 collective-permute-done.6
  69.8 0.7 collective-permute-done.9
  70.5 2.8 %collective-permute-start.10 = (bf16[33,1536]{1,0:T(8,128)(2,1)S(1)}, bf16[33,1536]{1,0:T(8,128)(2,1)S(1)}, u32[]{:S(2)}, u32[]{:S(2)}) collective-permute-start(bf16[33,1536]{1,0:T(8,128)(2,1)S(1)} %add_convert_fusion.1), channel_id=1, source_target_pairs={{0,8},{1,9},{2,10},{3,11},{4,12},{5,13},{6,14},{7,15},{8,0},{9,1},... | collective-permute-start | bytes 304136 | tf_op jit(solution)/shard_map/ppermute | solution.py:440
  73.3 0.3 maximum_add_fusion
  73.6 5.3 %collective-permute-done.10 = bf16[33,1536]{1,0:T(8,128)(2,1)S(1)} collective-permute-done((bf16[33,1536]{1,0:T(8,128)(2,1)S(1)}, bf16[33,1536]{1,0:T(8,128)(2,1)S(1)}, u32[]{:S(2)}, u32[]{:S(2)}) %collective-permute-start.10) | collective-permute-done | bytes 101408 | tf_op jit(solution)/shard_map/ppermute | solution.py:440
  79.0 1.6 %collective-permute-start.11 = (bf16[33,1536]{1,0:T(8,128)(2,1)S(1)}, bf16[33,1536]{1,0:T(8,128)(2,1)S(1)}, u32[]{:S(2)}, u32[]{:S(2)}) collective-permute-start(bf16[33,1536]{1,0:T(8,128)(2,1)S(1)} %add_convert_fusion.sent_ref), channel_id=1, source_target_pairs={{0,16},{16,0},{1,17},{17,1},{2,18},{18,2},{3,19},{19,3},{4,20},{20... | collective-permute-start | bytes 304136 | tf_op jit(solution)/shard_map/ppermute | solution.py:440
  80.6 1.0 %fusion = (bf16[1,128,1536]{2,1,0:T(8,128)(2,1)}, bf16[1,128,1536]{2,1,0:T(8,128)(2,1)}, bf16[1,128,1536]{2,1,0:T(8,128)(2,1)}) fusion(bf16[3,128,1536]{2,1,0:T(8,128)(2,1)S(1)} %maximum_add_fusion), kind=kLoop, calls=%fused_computation.5 | loop fusion | bytes 2359296 | tf_op jit(solution)/shard_map/slice | solution.py:546
  81.6 2.3 %collective-permute-done.11.came_ref = bf16[33,1536]{1,0:T(8,128)(2,1)S(1)} collective-permute-done((bf16[33,1536]{1,0:T(8,128)(2,1)S(1)}, bf16[33,1536]{1,0:T(8,128)(2,1)S(1)}, u32[]{:S(2)}, u32[]{:S(2)}) %collective-permute-start.11) | collective-permute-done | bytes 101408 | tf_op jit(solution)/shard_map/ppermute | solution.py:440
  83.9 0.7 shard_map.142
  (4 shorter events, 0.1 us)
Async XLA Ops:
  0.6 19.7 %collective-permute-start = (bf16[128,1536]{1,0:T(8,128)(2,1)}, bf16[128,1536]{1,0:T(8,128)(2,1)S(1)}, u32[]{:S(2)}, u32[]{:S(2)}) collective-permute-start(bf16[128,1536]{1,0:T(8,128)(2,1)} %bitcast.8), channel_id=1, source_target_pairs={{1,0},{2,1},{3,2},{4,3},{5,4},{6,5},{7,6},{8,7},{9,8},{10,9},{11,1... | collective-permute-start | bytes 1179656 | tf_op jit(solution)/shard_map/ppermute | solution.py:455
  1.9 18.4 %collective-permute-start.1 = (bf16[128,1536]{1,0:T(8,128)(2,1)}, bf16[128,1536]{1,0:T(8,128)(2,1)S(1)}, u32[]{:S(2)}, u32[]{:S(2)}) collective-permute-start(bf16[128,1536]{1,0:T(8,128)(2,1)} %bitcast.12), channel_id=1, source_target_pairs={{1,0},{2,1},{3,2},{4,3},{5,4},{6,5},{7,6},{8,7},{9,8},{10,9},{11,1... | collective-permute-start | bytes 1179656 | tf_op jit(solution)/shard_map/ppermute | solution.py:455
  3.2 17.1 %collective-permute-start.2 = (bf16[128,1536]{1,0:T(8,128)(2,1)}, bf16[128,1536]{1,0:T(8,128)(2,1)S(1)}, u32[]{:S(2)}, u32[]{:S(2)}) collective-permute-start(bf16[128,1536]{1,0:T(8,128)(2,1)} %bitcast.16), channel_id=1, source_target_pairs={{1,0},{2,1},{3,2},{4,3},{5,4},{6,5},{7,6},{8,7},{9,8},{10,9},{11,1... | collective-permute-start | bytes 1179656 | tf_op jit(solution)/shard_map/ppermute | solution.py:455
  4.5 2.5 %copy-start = (bf16[1,128,1536]{2,1,0:T(8,128)(2,1)S(1)}, bf16[1,128,1536]{2,1,0:T(8,128)(2,1)}, u32[]{:S(2)}) copy-start(bf16[1,128,1536]{2,1,0:T(8,128)(2,1)} %param.15) | copy-start | bytes 1179652
  4.5 2.5 %copy-start.1 = (bf16[1,128,1536]{2,1,0:T(8,128)(2,1)S(1)}, bf16[1,128,1536]{2,1,0:T(8,128)(2,1)}, u32[]{:S(2)}) copy-start(bf16[1,128,1536]{2,1,0:T(8,128)(2,1)} %param.8) | copy-start | bytes 1179652
  4.6 2.5 %copy-start.2 = (bf16[1,128,1536]{2,1,0:T(8,128)(2,1)S(1)}, bf16[1,128,1536]{2,1,0:T(8,128)(2,1)}, u32[]{:S(2)}) copy-start(bf16[1,128,1536]{2,1,0:T(8,128)(2,1)} %param.9) | copy-start | bytes 1179652
  4.6 2.5 %copy-start.3 = (bf16[1,128,1536]{2,1,0:T(8,128)(2,1)S(1)}, bf16[1,128,1536]{2,1,0:T(8,128)(2,1)}, u32[]{:S(2)}) copy-start(bf16[1,128,1536]{2,1,0:T(8,128)(2,1)} %param.10) | copy-start | bytes 1179652
  4.6 2.5 %copy-start.4 = (f32[31,1536]{1,0:T(8,128)S(1)}, f32[31,1536]{1,0:T(8,128)}, u32[]{:S(2)}) copy-start(f32[31,1536]{1,0:T(8,128)} %kernel_ref.5) | copy-start | bytes 571396
  4.6 2.5 %copy-start.5 = (f32[1536]{0:T(1024)S(1)}, f32[1536]{0:T(1024)}, u32[]{:S(2)}) copy-start(f32[1536]{0:T(1024)} %gain_row.1) | copy-start | bytes 18436
  4.6 2.5 %copy-start.6 = (f32[1536]{0:T(1024)S(1)}, f32[1536]{0:T(1024)}, u32[]{:S(2)}) copy-start(f32[1536]{0:T(1024)} %bias_row.1) | copy-start | bytes 18436
  4.6 25.9 %collective-permute-start.4 = (bf16[128,1536]{1,0:T(8,128)(2,1)}, bf16[128,1536]{1,0:T(8,128)(2,1)S(1)}, u32[]{:S(2)}, u32[]{:S(2)}) collective-permute-start(bf16[128,1536]{1,0:T(8,128)(2,1)} %bitcast.5), channel_id=1, source_target_pairs={{1,0},{2,1},{3,2},{4,3},{5,4},{6,5},{7,6},{8,7},{9,8},{10,9},{11,1... | collective-permute-start | bytes 1179656 | tf_op jit(solution)/shard_map/ppermute | solution.py:455
  6.0 0.7 copy-start.7
  7.1 13.2 %copy-start.8 = (s32[1,2048]{1,0:T(1,128)S(1)}, s32[1,2048]{1,0:T(1,128)}, u32[]{:S(2)}) copy-start(s32[1,2048]{1,0:T(1,128)} %seg_ref.9) | copy-start | bytes 24580
  25.6 18.5 %collective-permute-start.3 = (bf16[128,1536]{1,0:T(8,128)(2,1)S(1)}, bf16[128,1536]{1,0:T(8,128)(2,1)S(1)}, u32[]{:S(2)}, u32[]{:S(2)}) collective-permute-start(bf16[128,1536]{1,0:T(8,128)(2,1)S(1)} %get-tuple-element.46), channel_id=1, source_target_pairs={{0,1},{1,2},{2,3},{3,4},{4,5},{5,6},{6,7},{7,8},{8,9},{9,10},{10,1... | collective-permute-start | bytes 1179656 | tf_op jit(solution)/shard_map/ppermute | solution.py:490
  36.8 8.1 %collective-permute-start.7 = (bf16[33,1536]{1,0:T(8,128)(2,1)S(1)}, bf16[33,1536]{1,0:T(8,128)(2,1)S(1)}, u32[]{:S(2)}, u32[]{:S(2)}) collective-permute-start(bf16[33,1536]{1,0:T(8,128)(2,1)S(1)} %get-tuple-element.64), channel_id=1, source_target_pairs={{0,1},{1,0},{2,3},{3,2},{4,5},{5,4},{6,7},{7,6},{8,9},{9,8},{10,11... | collective-permute-start | bytes 304136 | tf_op jit(solution)/shard_map/ppermute | solution.py:440
  42.1 12.3 %collective-permute-start.5 = (bf16[3,128,768]{2,1,0:T(8,128)(2,1)S(1)}, bf16[3,128,768]{2,1,0:T(8,128)(2,1)S(1)}, u32[]{:S(2)}, u32[]{:S(2)}) collective-permute-start(bf16[3,128,768]{2,1,0:T(8,128)(2,1)S(1)} %get-tuple-element.62), channel_id=1, source_target_pairs={{0,1},{1,2},{2,3},{3,4},{4,5},{5,6},{6,7},{7,8},{8,9},{9,10},{10,1... | collective-permute-start | bytes 1769480 | tf_op jit(solution)/shard_map/ppermute | solution.py:515
  45.0 9.5 %collective-permute-start.8 = (bf16[33,1536]{1,0:T(8,128)(2,1)S(1)}, bf16[33,1536]{1,0:T(8,128)(2,1)S(1)}, u32[]{:S(2)}, u32[]{:S(2)}) collective-permute-start(bf16[33,1536]{1,0:T(8,128)(2,1)S(1)} %add_convert_fusion.3), channel_id=1, source_target_pairs={{0,2},{1,3},{2,0},{3,1},{4,6},{5,7},{6,4},{7,5},{8,10},{9,11},{10,... | collective-permute-start | bytes 304136 | tf_op jit(solution)/shard_map/ppermute | solution.py:440
  50.4 19.5 %collective-permute-start.6 = (bf16[3,128,768]{2,1,0:T(8,128)(2,1)S(1)}, bf16[3,128,768]{2,1,0:T(8,128)(2,1)S(1)}, u32[]{:S(2)}, u32[]{:S(2)}) collective-permute-start(bf16[3,128,768]{2,1,0:T(8,128)(2,1)S(1)} %get-tuple-element.63), channel_id=1, source_target_pairs={{0,1},{1,2},{2,3},{3,4},{4,5},{5,6},{6,7},{7,8},{8,9},{9,10},{10,1... | collective-permute-start | bytes 1769480 | tf_op jit(solution)/shard_map/ppermute | solution.py:515
  54.5 16.0 %collective-permute-start.9 = (bf16[33,1536]{1,0:T(8,128)(2,1)S(1)}, bf16[33,1536]{1,0:T(8,128)(2,1)S(1)}, u32[]{:S(2)}, u32[]{:S(2)}) collective-permute-start(bf16[33,1536]{1,0:T(8,128)(2,1)S(1)} %add_convert_fusion.2), channel_id=1, source_target_pairs={{0,4},{1,5},{2,6},{3,7},{4,0},{5,1},{6,2},{7,3},{8,12},{9,13},{10,... | collective-permute-start | bytes 304136 | tf_op jit(solution)/shard_map/ppermute | solution.py:440
  70.5 8.4 %collective-permute-start.10 = (bf16[33,1536]{1,0:T(8,128)(2,1)S(1)}, bf16[33,1536]{1,0:T(8,128)(2,1)S(1)}, u32[]{:S(2)}, u32[]{:S(2)}) collective-permute-start(bf16[33,1536]{1,0:T(8,128)(2,1)S(1)} %add_convert_fusion.1), channel_id=1, source_target_pairs={{0,8},{1,9},{2,10},{3,11},{4,12},{5,13},{6,14},{7,15},{8,0},{9,1},... | collective-permute-start | bytes 304136 | tf_op jit(solution)/shard_map/ppermute | solution.py:440
  79.0 4.9 %collective-permute-start.11 = (bf16[33,1536]{1,0:T(8,128)(2,1)S(1)}, bf16[33,1536]{1,0:T(8,128)(2,1)S(1)}, u32[]{:S(2)}, u32[]{:S(2)}) collective-permute-start(bf16[33,1536]{1,0:T(8,128)(2,1)S(1)} %add_convert_fusion.sent_ref), channel_id=1, source_target_pairs={{0,16},{16,0},{1,17},{17,1},{2,18},{18,2},{3,19},{19,3},{4,20},{20... | collective-permute-start | bytes 304136 | tf_op jit(solution)/shard_map/ppermute | solution.py:440

commit v3 on v2

--- a/solution.py
+++ b/solution.py
@@ -244,11 +244,22 @@
         )
 
 
+def stack_kernel(q_ref, k_ref, v_ref, out_ref, sems):
+    copies = [
+        pltpu.make_async_copy(ref, out_ref.at[i], sems.at[i]) for i, ref in enumerate((q_ref, k_ref, v_ref))
+    ]
+    for copy in copies:
+        copy.start()
+    for copy in copies:
+        copy.wait()
+
+
 def own_kernel(
-    q_ref, k_ref, v_ref, cot_ref, gain_row, kernel_ref, bias_row, same_ref, keep_ref, mask_ref,
-    out_ref, grad_ref, prob_ref, context_ref, sums_ref, gain_ref, bias_ref,
-    pad_ref, normed_ref, pre_ref,
+    qkv_ref, cot_ref, gain_row, kernel_ref, bias_row, same_ref, keep_ref, mask_ref,
+    out_ref, back_ref, prob_ref, context_ref, sums_ref, gain_ref, bias_ref,
+    pad_ref, normed_ref,
 ):
+    q_ref, k_ref, v_ref = (qkv_ref.at[i] for i in range(3))
     frames, width = q_ref.shape
     taps = kernel_ref.shape[0]
     tiles = width // LANES
@@ -263,12 +274,12 @@
     @pl.loop(0, tiles)
     def _(index):
         lanes = lanes_of(index)
-        pre_ref[:, lanes] = conv_forward(pad_ref, kernel_ref, bias_ref, mask_ref, frames, lanes)
+        back_ref[:, lanes] = conv_forward(pad_ref, kernel_ref, bias_ref, mask_ref, frames, lanes)
 
     @pl.loop(0, tiles)
     def _(index):
         lanes = lanes_of(index)
-        pre_act = pre_ref[:, lanes]
+        pre_act = back_ref[:, lanes]
         sig = gate(pre_act)
         out_ref[:, lanes] = (pre_act * sig * keep_ref[...]).astype(BF16)
         grad_pre = gate_grad(cot_ref[:, lanes].astype(F32) * keep_ref[...], pre_act, sig)
@@ -281,17 +292,15 @@
 
         grad_in = conv_backward(pad_ref, conv_in, kernel_ref, mask_ref, frames, lanes, store)
         sums_ref[taps + 1 : taps + 2, lanes] = jnp.sum(grad_in * normed_ref[:, lanes], 0, keepdims=True)
-        pre_ref[:, lanes] = grad_in
-
-    norm_backward(context_ref, pre_ref, gain_ref, keep, grad_ref, frames)
+        back_ref[:, lanes] = grad_in
 
 
 def cross_forward_kernel(
-    q_ref, k_ref, v_ref, qn_ref, kn_ref, vn_ref, seg_ref, gain_ref, kernel_ref, bias_ref, add_ref,
-    own_ref, next_ref, qg_ref, kg_ref, vg_ref, prob_ref, context_ref, pre_ref,
+    qkv_ref, other_ref, seg_ref, gain_ref, kernel_ref, bias_ref, add_ref,
+    own_ref, next_ref, got_ref, prob_ref, context_ref, pre_ref,
     pad_ref, out_ref,
 ):
-    frames, width = q_ref.shape
+    frames, width = qkv_ref.shape[1:]
     tiles = width // LANES
     first, length = crossing(seg_ref, frames)
     pick = gather_matrix(first, length, frames)
@@ -301,11 +310,11 @@
     keep = jnp.where(iota(shape, 0) < length, 1.0, 0.0)
     low = pair_masks(frames)
     clear_edges(pad_ref, frames)
-    for own, other, got in ((q_ref, qn_ref, qg_ref), (k_ref, kn_ref, kg_ref), (v_ref, vn_ref, vg_ref)):
+    for which in range(3):
         for cols in wide(width):
-            both = jnp.concatenate([own[:, cols], other[:, cols]], 0)
-            got[:, cols] = dot(pick, both, NN).astype(BF16)
-    forward_all(qg_ref, kg_ref, vg_ref, prob_ref, context_ref, bias, keep, low)
+            both = jnp.concatenate([qkv_ref[which, :, cols], other_ref[which, :, cols]], 0)
+            got_ref[which, :, cols] = dot(pick, both, NN).astype(BF16)
+    forward_all(*(got_ref.at[i] for i in range(3)), prob_ref, context_ref, bias, keep, low)
     normalize_all(context_ref, gain_ref, keep, None, pad_ref, PAD, frames)
 
     @pl.loop(0, tiles)
@@ -323,8 +332,8 @@
 
 def cross_conv_kernel(
     cot_ref, cotn_ref, seg_ref, gain_ref, kernel_ref, context_ref, pre_ref, part_ref,
-    back_ref, sums_ref, sent_ref,
-    pad_ref, in_ref, normed_ref,
+    back_ref, mine_ref, other_ref,
+    pad_ref, in_ref, normed_ref, sums_ref,
 ):
     frames, width = cot_ref.shape
     taps = kernel_ref.shape[0]
@@ -351,13 +360,17 @@
         store(taps + 1, jnp.sum(grad_in * normed_ref[:, lanes], 0, keepdims=True))
         back_ref[:, lanes] = grad_in
 
-    sent_ref[...] = sums_ref[...].astype(BF16)
+    half = width // 2
+    mine = lax.rem(lax.axis_index("seq"), 2)
+    mine_ref[...] = sums_ref[:, pl.ds(pl.multiple_of(mine * half, LANES), half)].astype(BF16)
+    other_ref[...] = sums_ref[:, pl.ds(pl.multiple_of((1 - mine) * half, LANES), half)].astype(BF16)
 
 
 def cross_back_kernel(
-    group, tiles, q_ref, k_ref, v_ref, prob_ref, context_ref, back_ref, gain_ref, seg_ref,
+    group, tiles, qkv_ref, prob_ref, context_ref, back_ref, gain_ref, seg_ref,
     own_ref, next_ref, grad_ref=None,
 ):
+    q_ref, k_ref, v_ref = (qkv_ref.at[i] for i in range(3))
     frames = q_ref.shape[0]
     first, length = crossing(seg_ref, frames)
     place = scatter_matrix(first, length, frames)
@@ -383,41 +396,60 @@
             next_ref[which, :, dest] = placed[frames:, cols]
 
 
-def own_back_kernel(q_ref, k_ref, v_ref, prob_ref, context_ref, grad_ref, *refs):
-    cross, (out_ref,) = refs[:-1], refs[-1:]
-    frames, width = q_ref.shape
+def own_back_kernel(first, *refs):
+    if first:
+        qkv_ref, prob_ref, context_ref, back_ref, gain_ref, keep_ref, cross_ref, out_ref, grad_ref = refs
+        frames = keep_ref.shape[0]
+        norm_backward(context_ref, back_ref, gain_ref, keep_ref[...], grad_ref, frames)
+    else:
+        qkv_ref, prob_ref, context_ref, grad_ref, cross_ref, out_ref = refs
+    frames, part = out_ref.shape[1:]
     low = pair_masks(frames)
-    tiles = width // LANES // len(cross)
-    for group, cross_ref in enumerate(cross):
-        for step in range(tiles):
-            index = group * tiles + step
-            lanes = slice(index * LANES, (index + 1) * LANES)
-            dest = slice(step * LANES, (step + 1) * LANES)
-            results = attend_back(
-                q_ref[:, lanes], k_ref[:, lanes], v_ref[:, lanes], prob_ref[index],
-                context_ref[:, lanes], grad_ref[:, lanes], low,
-            )
-            for which, result in enumerate(results):
-                out_ref[which, :, lanes] = result.astype(BF16) + cross_ref[which, :, dest]
-
-
-def finish_kernel(scale, sent_ref, came_ref, gain_ref, kernel_ref, bias_ref):
+    tiles = part // LANES
+    for step in range(tiles):
+        index = step if first else step + prob_ref.shape[0] - tiles
+        lanes = slice(index * LANES, (index + 1) * LANES)
+        dest = slice(step * LANES, (step + 1) * LANES)
+        results = attend_back(
+            *(qkv_ref[i, :, lanes] for i in range(3)), prob_ref[index],
+            context_ref[:, lanes], grad_ref[:, lanes], low,
+        )
+        for which, result in enumerate(results):
+            out_ref[which, :, dest] = result.astype(BF16) + cross_ref[which, :, dest]
+
+
+def merge_kernel(*refs):
+    ins, outs = refs[:-6], refs[-4:-1]
+    out_both_ref, out_came_ref, conv_ref = refs[-6], refs[-5], refs[-1]
+    conv_ref[...] = out_both_ref[...] + out_came_ref[...]
+    half = len(ins) // 2
+    start = 0
+    for own_ref, came_ref in zip(ins[:half], ins[half:]):
+        part = own_ref.shape[2]
+        for which, out_ref in enumerate(outs):
+            out_ref[:, start : start + part] = own_ref[which] + came_ref[which]
+        start += part
+
+
+def finish_kernel(scale, mine_ref, came_ref, gain_ref, kernel_ref, bias_ref):
     taps, width = kernel_ref.shape
-    total = (sent_ref[...].astype(F32) + came_ref[...].astype(F32)) * scale
+    even = lax.rem(lax.axis_index("seq"), 2) == 0
+    mine, came = mine_ref[...].astype(F32) * scale, came_ref[...].astype(F32) * scale
+    total = jnp.concatenate([jnp.where(even, mine, came), jnp.where(even, came, mine)], 1)
     kernel_ref[...] = total[:taps]
     bias_ref[...] = total[taps : taps + 1].reshape(width)
     gain_ref[...] = total[taps + 1 : taps + 2].reshape(width)
 
 
-def call(kernel, outs, scratch, flops, *args):
+def call(kernel, outs, scratch, flops, *args, space=pltpu.VMEM, limit=24):
     size = sum(a.size * a.dtype.itemsize for a in args) + sum(o.size * o.dtype.itemsize for o in outs)
     return pl.pallas_call(
         kernel,
         out_shape=outs,
-        in_specs=[VMEM] * len(args),
-        out_specs=[VMEM] * len(outs),
+        in_specs=[pl.BlockSpec(memory_space=space)] * len(args),
+        out_specs=[pl.BlockSpec(memory_space=space)] * len(outs),
         scratch_shapes=scratch,
-        compiler_params=pltpu.CompilerParams(vmem_limit_bytes=24 * 1024 * 1024),
+        compiler_params=pltpu.CompilerParams(vmem_limit_bytes=limit * 1024 * 1024),
         cost_estimate=pl.CostEstimate(flops=flops, bytes_accessed=size, transcendentals=0),
     )(*args)
 
@@ -426,14 +458,14 @@
     return lax.optimization_barrier((value,) + others)[0]
 
 
-def sum_steps(axes):
-    steps = []
-    for axis in axes:
+def sum_steps():
+    steps = {"seq": [], "dp": []}
+    for axis, distances in steps.items():
         step = 1
         while step < lax.axis_size(axis):
-            steps.append((axis, step))
+            distances.append((axis, step))
             step *= 2
-    return steps
+    return steps["seq"][:-1] + steps["dp"] + steps["seq"][-1:]
 
 
 def exchange(sent, axis, step):
@@ -445,27 +477,38 @@
 
 
 def per_device(queries, keys, values, segment_ids, norm_gain, conv_kernel, conv_bias, cotangent):
-    q, k, v, cot = queries[0], keys[0], values[0], cotangent[0]
-    frames, width = q.shape
+    frames, width = queries.shape[1:]
+    cot = cotangent[0]
     taps = conv_kernel.shape[0]
     tiles = width // LANES
     count = lax.axis_size("seq")
     to_left = [(i + 1, i) for i in range(count - 1)]
     to_right = [(i, i + 1) for i in range(count - 1)]
-    qn, kn, vn, cotn = (lax.ppermute(a, "seq", to_left) for a in (q, k, v, cot))
+    (qkv,) = call(
+        stack_kernel,
+        [jax.ShapeDtypeStruct((3, frames, width), BF16)],
+        [pltpu.SemaphoreType.DMA((3,))],
+        10**6,
+        queries[0], keys[0], values[0],
+        space=pl.ANY,
+        limit=60,
+    )
+    qkv_next = lax.ppermute(qkv, "seq", to_left)
+    cot_next = lax.ppermute(cot, "seq", to_left)
 
     def sds(shape, dtype):
         return jax.ShapeDtypeStruct(shape, dtype)
 
     rows16 = sds((frames, width), BF16)
     rows32 = sds((frames, width), F32)
+    three = sds((3, frames, width), BF16)
     probs = sds((tiles, frames, 2 * frames), BF16)
-    sums = sds((taps + 2, width), F32)
+    half_sums = sds((taps + 2, width // 2), BF16)
     row = sds((1, width), F32)
+    square = sds((frames, frames), F32)
     padded = pltpu.VMEM((frames + 2 * PAD, width), F32)
     plain = pltpu.VMEM((frames, width), F32)
 
-    square = sds((frames, frames), F32)
     same, keep, masks = call(
         functools.partial(mask_kernel, taps),
         [square, square, sds((taps * frames, LANES), F32)],
@@ -473,64 +516,74 @@
         10**10,
         segment_ids,
     )
-    out_own, grad_own, prob_own, context_own, sums_own, gain, bias = call(
+    out_own, back_own, prob_own, context_own, sums_own, gain, bias = call(
         own_kernel,
-        [rows16, rows16, probs, rows16, sums, row, row],
-        [padded, plain, plain],
+        [rows16, rows32, probs, rows16, sds((taps + 2, width), F32), row, row],
+        [padded, plain],
         10**10,
-        q, k, v, cot, norm_gain, conv_kernel, conv_bias, same, keep, masks,
-    )
-    out_both, out_next, qg, kg, vg, prob_cross, context_cross, pre_cross = call(
+        qkv, cot, norm_gain, conv_kernel, conv_bias, same, keep, masks,
+    )
+    out_both, out_next, got, prob_cross, context_cross, pre_cross = call(
         cross_forward_kernel,
-        [rows16, rows16, rows16, rows16, rows16, probs, rows16, rows32],
+        [rows16, rows16, three, probs, rows16, rows32],
         [padded, pltpu.VMEM((frames, width), BF16)],
         4 * 10**9,
-        q, k, v, qn, kn, vn, segment_ids, gain, conv_kernel, bias, out_own,
-    )
-    out_came = lax.ppermute(out_next, "seq", to_right)
-    back_cross, _, sent = call(
+        qkv, qkv_next, segment_ids, gain, conv_kernel, bias, out_own,
+    )
+    back_cross, mine, other = call(
         cross_conv_kernel,
-        [rows32, sums, sds(sums.shape, BF16)],
-        [padded, plain, plain],
+        [rows32, half_sums, half_sums],
+        [padded, plain, plain, pltpu.VMEM((taps + 2, width), F32)],
         4 * 10**9,
-        cot, cotn, segment_ids, gain, conv_kernel, context_cross, pre_cross, sums_own,
-    )
-    steps = sum_steps(("seq", "dp"))
-    came = exchange(sent, *steps[0])
+        cot, cot_next, segment_ids, gain, conv_kernel, context_cross, pre_cross, sums_own,
+    )
+    steps = sum_steps()
+    came = exchange(other, *steps[0])
+    out_came = lax.ppermute(after(out_next, mine), "seq", to_right)
     per_group = tiles // GROUPS
     piece = sds((3, frames, per_group * LANES), BF16)
-    own_parts, came_parts = [], []
     grad_cross = back_cross
+    own_parts, came_parts, sent = [], [], mine
     for group in range(GROUPS):
         own_part, next_part, *rest = call(
             functools.partial(cross_back_kernel, group, per_group),
             [piece, piece] + [rows16] * (group == 0),
             [],
             2 * 10**9,
-            qg, kg, vg, prob_cross, context_cross, grad_cross, gain, segment_ids,
+            got, prob_cross, context_cross, grad_cross, gain, segment_ids,
         )
         if group == 0:
             (grad_cross,) = rest
         own_parts.append(own_part)
-        came_parts.append(lax.ppermute(next_part, "seq", to_right))
+        sent = added(sent, after(came, own_part))
+        if group == 1:
+            sent = after(sent, out_came)
+        came = exchange(sent, *steps[group + 1])
+        came_parts.append(lax.ppermute(after(next_part, sent), "seq", to_right))
+    grads = []
+    grad_own = back_own
+    for group in range(GROUPS):
+        extra = [gain, keep] if group == 0 else []
+        part, *rest = call(
+            functools.partial(own_back_kernel, group == 0),
+            [piece] + [rows16] * (group == 0),
+            [],
+            3 * 10**9,
+            qkv, prob_own, context_own, grad_own, *extra, own_parts[group],
+        )
         if group == 0:
-            conv_out = out_both + after(out_came, own_part)
-            sent = added(sent, after(came, own_part, conv_out))
-        else:
-            sent = added(sent, after(came, own_part, came_parts[0]))
-        came = exchange(sent, *steps[group + 1])
-    (grads_own,) = call(
-        own_back_kernel,
-        [sds((3, frames, width), BF16)],
-        [],
-        4 * 10**9,
-        q, k, v, prob_own, context_own, grad_own, *own_parts,
-    )
-    came = after(came, grads_own, *came_parts)
-    for step in steps[GROUPS + 1 :]:
+            (grad_own,) = rest
+        grads.append(part)
+        sent = added(sent, after(came, part, *came_parts[: group + 1]))
+        came = exchange(sent, *steps[group + GROUPS + 1])
+    for step in steps[2 * GROUPS + 1 :]:
         sent = added(sent, came)
         came = exchange(sent, *step)
-    grads = grads_own + jnp.concatenate(came_parts, 2)
+    query_grad, key_grad, value_grad, conv_out = call(
+        merge_kernel, [rows16] * 4, [], 10**9, *grads, *came_parts, out_both, out_came,
+    )
+    sent = added(sent, after(came, query_grad))
+    came = exchange(sent, *steps[0])
     scale = (lax.axis_size("dp") * count * frames) ** (-0.5)
     gain_grad, kernel_grad, bias_grad = call(
         functools.partial(finish_kernel, scale),
@@ -541,9 +594,9 @@
     )
     return (
         conv_out[None],
-        grads[0][None],
-        grads[1][None],
-        grads[2][None],
+        query_grad[None],
+        key_grad[None],
+        value_grad[None],
         gain_grad,
         kernel_grad,
         bias_grad,

time: 85 us -> 101 us (1.19)
  the two profiles are of different devices: /device:TPU:0 before, /device:TPU:12 now
where the time goes in v3:
time: 101 us
  Pallas kernels  70.2 us (70%)
  starting transfers between devices  15.9 us (16%)
  waiting for transfers between devices  13.6 us (13%)
    pallas_call x11, Pallas kernels, call(): pl.pallas_call(kernel, out_shape=outs, in_specs=[pl.BlockSpec(memory_spac...  70.2 us
    ppermute x6, waiting for transfers between devices, exchange(): lax.ppermute(sent, axis, [(i, i ^ step) for i in range(lax.axis_size(axis...  6.98 us
    ppermute x2, waiting for transfers between devices, per_device(): came_parts.append(lax.ppermute(after(next_part, sent), 'seq', to_right))  6.65 us
    ppermute x6, starting transfers between devices, exchange(): lax.ppermute(sent, axis, [(i, i ^ step) for i in range(lax.axis_size(axis...  4.35 us
    ppermute x2, starting transfers between devices, per_device(): came_parts.append(lax.ppermute(after(next_part, sent), 'seq', to_right))  4.06 us
    ppermute x1, starting transfers between devices, per_device(): qkv_next = lax.ppermute(qkv, 'seq', to_left)  2.72 us
    ppermute x1, starting transfers between devices, per_device(): cot_next = lax.ppermute(cot, 'seq', to_left)  2.72 us
    ppermute x1, starting transfers between devices, per_device(): out_came = lax.ppermute(after(out_next, mine), 'seq', to_right)  2.06 us
  transfers between devices with their start and end apart: 11, of which 5 were waited for; matrix products, arithmetic and copies ran while one was open for 0% of the time, Pallas kernels for 27%

profile of v3, /device:TPU:12, one launch (start us, length us, event | category | flops | bytes accessed | tf_op | source)
XLA Modules:
  0.0 100.8 jit_solution(8238033691455143908)
XLA Ops:
  0.6 0.0 copy-start.1
  0.6 0.0 copy-start.5
  0.7 36.9 %shard_map.135.qkv_ref.refs_0_ = bf16[3,128,1536]{2,1,0:T(8,128)(2,1)} custom-call(bf16[128,1536]{1,0:T(8,128)(2,1)} %bitcast.11, bf16[128,1536]{1,0:T(8,128)(2,1)} %bitcast.12, bf16[128,1536]{1,0:T(8,128)(2,1)} %bitcast.13), custom_call_target="tpu_custom_call" | custom-call | flops 1000000 | bytes 2359296 | tf_op jit(solution)/shard_map/pallas_call | solution.py:446
  37.5 2.7 %collective-permute-start = (bf16[3,128,1536]{2,1,0:T(8,128)(2,1)}, bf16[3,128,1536]{2,1,0:T(8,128)(2,1)S(1)}, u32[]{:S(2)}, u32[]{:S(2)}) collective-permute-start(bf16[3,128,1536]{2,1,0:T(8,128)(2,1)} %shard_map.135.qkv_ref.refs_0_), channel_id=1, source_target_pairs={{1,0},{2,1},{3,2},{4,3},{5,4},{6,5},{7,6},{8,7},{9,8},{10,9},{11,1... | collective-permute-start | bytes 3538952 | tf_op jit(solution)/shard_map/ppermute | solution.py:496
  40.3 0.0 copy-done.1
  40.3 0.0 copy-start
  40.3 0.0 copy-start.2
  40.3 0.0 copy-start.3
  40.3 0.0 copy-start.4
  40.3 2.7 %collective-permute-start.1 = (bf16[128,1536]{1,0:T(8,128)(2,1)S(1)}, bf16[128,1536]{1,0:T(8,128)(2,1)S(1)}, u32[]{:S(2)}, u32[]{:S(2)}) collective-permute-start(bf16[128,1536]{1,0:T(8,128)(2,1)S(1)} %bitcast.8), channel_id=1, source_target_pairs={{1,0},{2,1},{3,2},{4,3},{5,4},{6,5},{7,6},{8,7},{9,8},{10,9},{11,1... | collective-permute-start | bytes 1179656 | tf_op jit(solution)/shard_map/ppermute | solution.py:497
  43.0 0.0 copy-done.5
  43.0 0.3 shard_map.136
  43.4 0.0 copy-done
  43.4 0.0 copy-done.2
  43.4 0.0 copy-done.3
  43.4 0.0 copy-done.4
  43.4 11.5 %shard_map.137 = (bf16[128,1536]{1,0:T(8,128)(2,1)S(1)}, f32[128,1536]{1,0:T(8,128)S(1)}, bf16[12,128,256]{2,1,0:T(8,128)(2,1)S(1)}, bf16[128,1536]{1,0:T(8,128)...) custom-call(bf16[3,128,1536]{2,1,0:T(8,128)(2,1)S(1)} %copy-done, ...), custom_call_target="tpu_custom_call" | custom-call | flops 10000000000 | bytes 6512640 | tf_op jit(solution)/shard_map/pallas_call | solution.py:446
  55.0 0.0 collective-permute-done.other_ref
  55.0 5.2 %shard_map.138 = (bf16[128,1536]{1,0:T(8,128)(2,1)S(1)}, bf16[128,1536]{1,0:T(8,128)(2,1)S(1)}, bf16[3,128,1536]{2,1,0:T(8,128)(2,1)S(1)}, bf16[12,128,256]{2,1,...) custom-call(bf16[3,128,1536]{2,1,0:T(8,128)(2,1)S(1)} %copy-done, ...), custom_call_target="tpu_custom_call" | custom-call | flops 4000000000 | bytes 6895616 | tf_op jit(solution)/shard_map/pallas_call | solution.py:446
  60.2 0.0 collective-permute-done.1.cotn_ref
  60.2 5.6 %shard_map.139 = (f32[128,1536]{1,0:T(8,128)S(1)}, bf16[33,768]{1,0:T(8,128)(2,1)S(1)}, bf16[33,768]{1,0:T(8,128)(2,1)S(1)}) custom-call(bf16[128,1536]{1,0:T(8,128)(2,1)S(1)} %bitcast.10, bf16[128,1536]{1,0:T(8,128)(2,1)S(1)} %collective-permute-done.1.cotn_ref, s32[1,2048]{1,0:T(1,128)S(1)} %copy-done.5, f32[1,1536]{1,0:T(1,128)S(1)} %get-tuple-element.55.gain_ref.refs_4_, ...), custom_call_target="tpu_custom_call" | custom-call | flops 4000000000 | bytes 3261440 | tf_op jit(solution)/shard_map/pallas_call | solution.py:446
  65.8 2.1 %collective-permute-start.5 = (bf16[128,1536]{1,0:T(8,128)(2,1)S(1)}, bf16[128,1536]{1,0:T(8,128)(2,1)S(1)}, u32[]{:S(2)}, u32[]{:S(2)}) collective-permute-start(bf16[128,1536]{1,0:T(8,128)(2,1)S(1)} %get-tuple-element.77), channel_id=1, source_target_pairs={{0,1},{1,2},{2,3},{3,4},{4,5},{5,6},{6,7},{7,8},{8,9},{9,10},{10,1... | collective-permute-start | bytes 1179656 | tf_op jit(solution)/shard_map/ppermute | solution.py:542
  67.9 0.7 collective-permute-start.2
  68.5 2.8 %shard_map.140 = (bf16[3,128,768]{2,1,0:T(8,128)(2,1)S(1)}, bf16[3,128,768]{2,1,0:T(8,128)(2,1)S(1)}, bf16[128,1536]{1,0:T(8,128)(2,1)S(1)}) custom-call(bf16[3,128,1536]{2,1,0:T(8,128)(2,1)S(1)} %get-tuple-element.58.qkv_ref, bf16[12,128,256]{2,1,0:T(8,128)(2,1)S(1)} %get-tuple-element.59.prob_ref, bf16[128,1536]{1,0:T(8,128)(2,1)S(1)} %get-tuple-element.60.context_ref, ...), custom_call_target="tpu_custom_call" | custom-call | flops 2000000000 | bytes 4732928 | tf_op jit(solution)/shard_map/pallas_call | solution.py:446
  71.3 0.0 collective-permute-done.2
  71.3 2.5 %collective-permute-start.4 = (bf16[33,768]{1,0:T(8,128)(2,1)S(1)}, bf16[33,768]{1,0:T(8,128)(2,1)S(1)}, u32[]{:S(2)}, u32[]{:S(2)}) collective-permute-start(bf16[33,768]{1,0:T(8,128)(2,1)S(1)} %add_convert_fusion.4), channel_id=1, source_target_pairs={{0,2},{1,3},{2,0},{3,1},{4,6},{5,7},{6,4},{7,5},{8,10},{9,11},{10,... | collective-permute-start | bytes 152072 | tf_op jit(solution)/shard_map/ppermute | solution.py:472
  73.8 1.9 %collective-permute-start.3 = (bf16[3,128,768]{2,1,0:T(8,128)(2,1)S(1)}, bf16[3,128,768]{2,1,0:T(8,128)(2,1)S(1)}, u32[]{:S(2)}, u32[]{:S(2)}) collective-permute-start(bf16[3,128,768]{2,1,0:T(8,128)(2,1)S(1)} %get-tuple-element.73), channel_id=1, source_target_pairs={{0,1},{1,2},{2,3},{3,4},{4,5},{5,6},{6,7},{7,8},{8,9},{9,10},{10,1... | collective-permute-start | bytes 1769480 | tf_op jit(solution)/shard_map/ppermute | solution.py:562
  75.7 2.3 %shard_map.142 = (bf16[3,128,768]{2,1,0:T(8,128)(2,1)S(1)}, bf16[3,128,768]{2,1,0:T(8,128)(2,1)S(1)}) custom-call(bf16[3,128,1536]{2,1,0:T(8,128)(2,1)S(1)} %get-tuple-element.58.qkv_ref, bf16[12,128,256]{2,1,0:T(8,128)(2,1)S(1)} %get-tuple-element.59.prob_ref, bf16[128,1536]{1,0:T(8,128)(2,1)S(1)} %get-tuple-element.60.context_ref, ...), custom_call_target="tpu_custom_call" | custom-call | flops 2000000000 | bytes 3946496 | tf_op jit(solution)/shard_map/pallas_call | solution.py:446
  78.0 0.0 collective-permute-done.4
  78.1 0.0 collective-permute-done.5.refs_5_
  78.1 0.3 collective-permute-start.7
  78.4 2.1 %collective-permute-start.6 = (bf16[3,128,768]{2,1,0:T(8,128)(2,1)S(1)}, bf16[3,128,768]{2,1,0:T(8,128)(2,1)S(1)}, u32[]{:S(2)}, u32[]{:S(2)}) collective-permute-start(bf16[3,128,768]{2,1,0:T(8,128)(2,1)S(1)} %get-tuple-element.79), channel_id=1, source_target_pairs={{0,1},{1,2},{2,3},{3,4},{4,5},{5,6},{6,7},{7,8},{8,9},{9,10},{10,1... | collective-permute-start | bytes 1769480 | tf_op jit(solution)/shard_map/ppermute | solution.py:562
  80.5 2.0 %shard_map.141 = (bf16[3,128,768]{2,1,0:T(8,128)(2,1)S(1)}, bf16[128,1536]{1,0:T(8,128)(2,1)S(1)}) custom-call(bf16[3,128,1536]{2,1,0:T(8,128)(2,1)S(1)} %copy-done, bf16[12,128,256]{2,1,0:T(8,128)(2,1)S(1)} %get-tuple-element.52.refs_1_, bf16[128,1536]{1,0:T(8,128)(2,1)S(1)} %get-tuple-element.53.refs_2_, f32[128,1536]{1,0:T(8,128)S(1)} %get-tuple-element.54.refs_3_, ...), custom_call_target="tpu_custom_call" | custom-call | flops 3000000000 | bytes 4790272 | tf_op jit(solution)/shard_map/pallas_call | solution.py:446
  82.6 0.0 collective-permute-done.7
  82.6 4.0 %collective-permute-done.3.refs_2_ = bf16[3,128,768]{2,1,0:T(8,128)(2,1)S(1)} collective-permute-done((bf16[3,128,768]{2,1,0:T(8,128)(2,1)S(1)}, bf16[3,128,768]{2,1,0:T(8,128)(2,1)S(1)}, u32[]{:S(2)}, u32[]{:S(2)}) %collective-permute-start.3) | collective-permute-done | bytes 589856 | tf_op jit(solution)/shard_map/ppermute | solution.py:562
  86.6 0.6 collective-permute-start.8
  87.1 1.5 %shard_map.143.refs_1_ = bf16[3,128,768]{2,1,0:T(8,128)(2,1)S(1)} custom-call(bf16[3,128,1536]{2,1,0:T(8,128)(2,1)S(1)} %copy-done, bf16[12,128,256]{2,1,0:T(8,128)(2,1)S(1)} %get-tuple-element.52.refs_1_, bf16[128,1536]{1,0:T(8,128)(2,1)S(1)} %get-tuple-element.53.refs_2_, bf16[128,1536]{1,0:T(8,128)(2,1)S(1)} %get-tuple-element.66.refs_3_, ...), custom_call_target="tpu_custom_call" | custom-call | flops 3000000000 | bytes 3932160 | tf_op jit(solution)/shard_map/pallas_call | solution.py:446
  88.7 2.2 %collective-permute-done.8 = bf16[33,768]{1,0:T(8,128)(2,1)S(1)} collective-permute-done((bf16[33,768]{1,0:T(8,128)(2,1)S(1)}, bf16[33,768]{1,0:T(8,128)(2,1)S(1)}, u32[]{:S(2)}, u32[]{:S(2)}) %collective-permute-start.8) | collective-permute-done | bytes 50720 | tf_op jit(solution)/shard_map/ppermute | solution.py:472
  90.9 2.7 %collective-permute-done.6.refs_3_ = bf16[3,128,768]{2,1,0:T(8,128)(2,1)S(1)} collective-permute-done((bf16[3,128,768]{2,1,0:T(8,128)(2,1)S(1)}, bf16[3,128,768]{2,1,0:T(8,128)(2,1)S(1)}, u32[]{:S(2)}, u32[]{:S(2)}) %collective-permute-start.6) | collective-permute-done | bytes 589856 | tf_op jit(solution)/shard_map/ppermute | solution.py:562
  93.5 0.3 collective-permute-start.9
  93.8 1.3 %shard_map.144 = (bf16[128,1536]{1,0:T(8,128)(2,1)}, bf16[128,1536]{1,0:T(8,128)(2,1)}, bf16[128,1536]{1,0:T(8,128)(2,1)}, bf16[128,1536]{1,0:T(8,128)(2,1)}) custom-call(bf16[3,128,768]{2,1,0:T(8,128)(2,1)S(1)} %get-tuple-element.65.refs_0_, bf16[3,128,768]{2,1,0:T(8,128)(2,1)S(1)} %shard_map.143.refs_1_, ...), custom_call_target="tpu_custom_call" | custom-call | flops 1000000000 | bytes 4718592 | tf_op jit(solution)/shard_map/pallas_call | solution.py:446
  95.2 3.6 %collective-permute-done.9 = bf16[33,768]{1,0:T(8,128)(2,1)S(1)} collective-permute-done((bf16[33,768]{1,0:T(8,128)(2,1)S(1)}, bf16[33,768]{1,0:T(8,128)(2,1)S(1)}, u32[]{:S(2)}, u32[]{:S(2)}) %collective-permute-start.9) | collective-permute-done | bytes 50720 | tf_op jit(solution)/shard_map/ppermute | solution.py:472
  98.8 0.1 collective-permute-start.10
  98.8 1.2 %collective-permute-done.10.came_ref = bf16[33,768]{1,0:T(8,128)(2,1)S(1)} collective-permute-done((bf16[33,768]{1,0:T(8,128)(2,1)S(1)}, bf16[33,768]{1,0:T(8,128)(2,1)S(1)}, u32[]{:S(2)}, u32[]{:S(2)}) %collective-permute-start.10) | collective-permute-done | bytes 50720 | tf_op jit(solution)/shard_map/ppermute | solution.py:472
  100.1 0.7 shard_map.145
  (5 shorter events, 0.1 us)
Async XLA Ops:
  0.6 39.6 %copy-start.1 = (bf16[1,128,1536]{2,1,0:T(8,128)(2,1)S(1)}, bf16[1,128,1536]{2,1,0:T(8,128)(2,1)}, u32[]{:S(2)}) copy-start(bf16[1,128,1536]{2,1,0:T(8,128)(2,1)} %param.15) | copy-start | bytes 1179652
  0.6 42.4 %copy-start.5 = (s32[1,2048]{1,0:T(1,128)S(1)}, s32[1,2048]{1,0:T(1,128)}, u32[]{:S(2)}) copy-start(s32[1,2048]{1,0:T(1,128)} %seg_ref.9) | copy-start | bytes 24580
  37.5 17.4 %collective-permute-start = (bf16[3,128,1536]{2,1,0:T(8,128)(2,1)}, bf16[3,128,1536]{2,1,0:T(8,128)(2,1)S(1)}, u32[]{:S(2)}, u32[]{:S(2)}) collective-permute-start(bf16[3,128,1536]{2,1,0:T(8,128)(2,1)} %shard_map.135.qkv_ref.refs_0_), channel_id=1, source_target_pairs={{1,0},{2,1},{3,2},{4,3},{5,4},{6,5},{7,6},{8,7},{9,8},{10,9},{11,1... | collective-permute-start | bytes 3538952 | tf_op jit(solution)/shard_map/ppermute | solution.py:496
  40.3 3.1 %copy-start = (bf16[3,128,1536]{2,1,0:T(8,128)(2,1)S(1)}, bf16[3,128,1536]{2,1,0:T(8,128)(2,1)}, u32[]{:S(2)}) copy-start(bf16[3,128,1536]{2,1,0:T(8,128)(2,1)} %shard_map.135.qkv_ref.refs_0_) | copy-start | bytes 3538948
  40.3 3.1 %copy-start.2 = (f32[31,1536]{1,0:T(8,128)S(1)}, f32[31,1536]{1,0:T(8,128)}, u32[]{:S(2)}) copy-start(f32[31,1536]{1,0:T(8,128)} %kernel_ref.5) | copy-start | bytes 571396
  40.3 3.1 %copy-start.3 = (f32[1536]{0:T(1024)S(1)}, f32[1536]{0:T(1024)}, u32[]{:S(2)}) copy-start(f32[1536]{0:T(1024)} %gain_row.1) | copy-start | bytes 18436
  40.3 3.1 %copy-start.4 = (f32[1536]{0:T(1024)S(1)}, f32[1536]{0:T(1024)}, u32[]{:S(2)}) copy-start(f32[1536]{0:T(1024)} %bias_row.1) | copy-start | bytes 18436
  40.3 19.9 %collective-permute-start.1 = (bf16[128,1536]{1,0:T(8,128)(2,1)S(1)}, bf16[128,1536]{1,0:T(8,128)(2,1)S(1)}, u32[]{:S(2)}, u32[]{:S(2)}) collective-permute-start(bf16[128,1536]{1,0:T(8,128)(2,1)S(1)} %bitcast.8), channel_id=1, source_target_pairs={{1,0},{2,1},{3,2},{4,3},{5,4},{6,5},{7,6},{8,7},{9,8},{10,9},{11,1... | collective-permute-start | bytes 1179656 | tf_op jit(solution)/shard_map/ppermute | solution.py:497
  65.8 12.3 %collective-permute-start.5 = (bf16[128,1536]{1,0:T(8,128)(2,1)S(1)}, bf16[128,1536]{1,0:T(8,128)(2,1)S(1)}, u32[]{:S(2)}, u32[]{:S(2)}) collective-permute-start(bf16[128,1536]{1,0:T(8,128)(2,1)S(1)} %get-tuple-element.77), channel_id=1, source_target_pairs={{0,1},{1,2},{2,3},{3,4},{4,5},{5,6},{6,7},{7,8},{8,9},{9,10},{10,1... | collective-permute-start | bytes 1179656 | tf_op jit(solution)/shard_map/ppermute | solution.py:542
  67.9 3.5 %collective-permute-start.2 = (bf16[33,768]{1,0:T(8,128)(2,1)S(1)}, bf16[33,768]{1,0:T(8,128)(2,1)S(1)}, u32[]{:S(2)}, u32[]{:S(2)}) collective-permute-start(bf16[33,768]{1,0:T(8,128)(2,1)S(1)} %get-tuple-element.71), channel_id=1, source_target_pairs={{0,1},{1,0},{2,3},{3,2},{4,5},{5,4},{6,7},{7,6},{8,9},{9,8},{10,11... | collective-permute-start | bytes 152072 | tf_op jit(solution)/shard_map/ppermute | solution.py:472
  71.3 6.7 %collective-permute-start.4 = (bf16[33,768]{1,0:T(8,128)(2,1)S(1)}, bf16[33,768]{1,0:T(8,128)(2,1)S(1)}, u32[]{:S(2)}, u32[]{:S(2)}) collective-permute-start(bf16[33,768]{1,0:T(8,128)(2,1)S(1)} %add_convert_fusion.4), channel_id=1, source_target_pairs={{0,2},{1,3},{2,0},{3,1},{4,6},{5,7},{6,4},{7,5},{8,10},{9,11},{10,... | collective-permute-start | bytes 152072 | tf_op jit(solution)/shard_map/ppermute | solution.py:472
  73.8 12.7 %collective-permute-start.3 = (bf16[3,128,768]{2,1,0:T(8,128)(2,1)S(1)}, bf16[3,128,768]{2,1,0:T(8,128)(2,1)S(1)}, u32[]{:S(2)}, u32[]{:S(2)}) collective-permute-start(bf16[3,128,768]{2,1,0:T(8,128)(2,1)S(1)} %get-tuple-element.73), channel_id=1, source_target_pairs={{0,1},{1,2},{2,3},{3,4},{4,5},{5,6},{6,7},{7,8},{8,9},{9,10},{10,1... | collective-permute-start | bytes 1769480 | tf_op jit(solution)/shard_map/ppermute | solution.py:562
  78.1 4.5 %collective-permute-start.7 = (bf16[33,768]{1,0:T(8,128)(2,1)S(1)}, bf16[33,768]{1,0:T(8,128)(2,1)S(1)}, u32[]{:S(2)}, u32[]{:S(2)}) collective-permute-start(bf16[33,768]{1,0:T(8,128)(2,1)S(1)} %add_convert_fusion.3), channel_id=1, source_target_pairs={{0,4},{1,5},{2,6},{3,7},{4,0},{5,1},{6,2},{7,3},{8,12},{9,13},{10,... | collective-permute-start | bytes 152072 | tf_op jit(solution)/shard_map/ppermute | solution.py:472
  78.4 15.2 %collective-permute-start.6 = (bf16[3,128,768]{2,1,0:T(8,128)(2,1)S(1)}, bf16[3,128,768]{2,1,0:T(8,128)(2,1)S(1)}, u32[]{:S(2)}, u32[]{:S(2)}) collective-permute-start(bf16[3,128,768]{2,1,0:T(8,128)(2,1)S(1)} %get-tuple-element.79), channel_id=1, source_target_pairs={{0,1},{1,2},{2,3},{3,4},{4,5},{5,6},{6,7},{7,8},{8,9},{9,10},{10,1... | collective-permute-start | bytes 1769480 | tf_op jit(solution)/shard_map/ppermute | solution.py:562
  86.6 4.3 %collective-permute-start.8 = (bf16[33,768]{1,0:T(8,128)(2,1)S(1)}, bf16[33,768]{1,0:T(8,128)(2,1)S(1)}, u32[]{:S(2)}, u32[]{:S(2)}) collective-permute-start(bf16[33,768]{1,0:T(8,128)(2,1)S(1)} %add_convert_fusion.2), channel_id=1, source_target_pairs={{0,16},{16,0},{1,17},{17,1},{2,18},{18,2},{3,19},{19,3},{4,20},{20... | collective-permute-start | bytes 152072 | tf_op jit(solution)/shard_map/ppermute | solution.py:472
  93.5 5.2 %collective-permute-start.9 = (bf16[33,768]{1,0:T(8,128)(2,1)S(1)}, bf16[33,768]{1,0:T(8,128)(2,1)S(1)}, u32[]{:S(2)}, u32[]{:S(2)}) collective-permute-start(bf16[33,768]{1,0:T(8,128)(2,1)S(1)} %add_convert_fusion.1), channel_id=1, source_target_pairs={{0,8},{1,9},{2,10},{3,11},{4,12},{5,13},{6,14},{7,15},{8,0},{9,1},... | collective-permute-start | bytes 152072 | tf_op jit(solution)/shard_map/ppermute | solution.py:472
  98.8 1.3 %collective-permute-start.10 = (bf16[33,768]{1,0:T(8,128)(2,1)S(1)}, bf16[33,768]{1,0:T(8,128)(2,1)S(1)}, u32[]{:S(2)}, u32[]{:S(2)}) collective-permute-start(bf16[33,768]{1,0:T(8,128)(2,1)S(1)} %add_convert_fusion.mine_ref), channel_id=1, source_target_pairs={{0,1},{1,0},{2,3},{3,2},{4,5},{5,4},{6,7},{7,6},{8,9},{9,8},{10,11... | collective-permute-start | bytes 152072 | tf_op jit(solution)/shard_map/ppermute | solution.py:472

commit v4 on v3

--- a/solution.py
+++ b/solution.py
@@ -57,15 +57,21 @@
     return lax.broadcasted_iota(jnp.int32, shape, axis).astype(F32)
 
 
+def frame_of(shape, axis):
+    place = lax.broadcasted_iota(jnp.int32, shape, axis)
+    tiles = shape[axis] // 8
+    return (lax.rem(place, 8) * tiles + lax.div(place, 8)).astype(F32)
+
+
 def gather_matrix(first, length, frames):
     shape = (frames, 2 * frames)
-    row = iota(shape, 0)
+    row = frame_of(shape, 0)
     return jnp.where((iota(shape, 1) == row + first) & (row < length), 1.0, 0.0).astype(BF16)
 
 
 def scatter_matrix(first, length, frames):
     shape = (2 * frames, frames)
-    col = iota(shape, 1)
+    col = frame_of(shape, 1)
     return jnp.where((iota(shape, 0) == col + first) & (col < length), 1.0, 0.0).astype(BF16)
 
 
@@ -183,6 +189,82 @@
     return total
 
 
+def phase_views(block, half_taps):
+    tiles = block.shape[0] // 8
+    row = lax.broadcasted_iota(jnp.int32, (8, LANES), 0)
+    views = {}
+    for j in range(tiles):
+        tile = block[8 * j : 8 * j + 8]
+        views[j] = tile
+        if j - tiles >= -half_taps:
+            views[j - tiles] = jnp.where(row >= 1, pltpu.roll(tile, 1, 0), 0.0)
+        if j < half_taps:
+            views[j + tiles] = jnp.where(row < 7, pltpu.roll(tile, 7, 0), 0.0)
+    return views
+
+
+def half_rate(views, taps, tiles):
+    reach = tiles // 2 + (taps + 1) // 2 - 1
+    low = -(taps // 2)
+    middle = [views[low + 2 * n + 1] if low + 2 * n + 1 in views else None for n in range(reach)]
+    before = [views[low + 2 * n] for n in range(reach)]
+    after_ = [views.get(low + 2 * n + 2) for n in range(reach)]
+    return middle, before, after_
+
+
+def minus(a, b):
+    if b is None:
+        return a
+    return -b if a is None else a - b
+
+
+def phase_conv(block, weight, taps, start):
+    tiles = block.shape[0] // 8
+    middle, before, behind = half_rate(phase_views(block, taps // 2), taps, tiles)
+    pairs = tiles // 2
+
+    def run(values, weights, total):
+        for s, w in enumerate(weights):
+            for a in range(pairs):
+                if values[a + s] is not None:
+                    term = w * values[a + s]
+                    total[a] = term if total[a] is None else total[a] + term
+        return total
+
+    even = [weight(t) for t in range(0, taps, 2)]
+    odd = [weight(t) for t in range(1, taps, 2)]
+    both = [e + o for e, o in zip(even, odd)] + even[len(odd) :]
+    shared = run(middle, both, [start] * pairs)
+    first = run([minus(b, m) for b, m in zip(before, middle)], even, list(shared))
+    second = run([minus(b, m) for b, m in zip(behind, middle)], odd, list(shared))
+    return jnp.concatenate([tile for pair in zip(first, second) for tile in pair], 0)
+
+
+def phase_products(block, rows, taps, store):
+    tiles = block.shape[0] // 8
+    middle, before, behind = half_rate(phase_views(block, taps // 2), taps, tiles)
+    pairs = tiles // 2
+    even = [rows[16 * a : 16 * a + 8] for a in range(pairs)]
+    odd = [rows[16 * a + 8 : 16 * a + 16] for a in range(pairs)]
+    both = [e + o for e, o in zip(even, odd)]
+    first = [minus(b, m) for b, m in zip(before, middle)]
+    second = [minus(b, m) for b, m in zip(behind, middle)]
+
+    def run(values, tiles_of, s):
+        total = None
+        for a in range(pairs):
+            if values[a + s] is not None:
+                term = tiles_of[a] * values[a + s]
+                total = term if total is None else total + term
+        return total
+
+    for s in range((taps + 1) // 2):
+        shared = run(middle, both, s)
+        store(2 * s, jnp.sum(shared + run(first, even, s), 0, keepdims=True))
+        if 2 * s + 1 < taps:
+            store(2 * s + 1, jnp.sum(shared + run(second, odd, s), 0, keepdims=True))
+
+
 def gate(pre_act):
     return 1.0 / (1.0 + jnp.exp(-pre_act))
 
@@ -213,12 +295,10 @@
         context_ref[:, lanes] = context
 
 
-def normalize_all(context_ref, gain_ref, keep, normed_ref, in_ref, offset, frames):
+def normalize_all(context_ref, gain_ref, keep, in_ref, offset, frames):
     for rows in chunks(frames):
         normed, _ = normalize(context_ref[rows, :])
         normed = jnp.where(keep[rows.start : rows.start + CHUNK, 0:1] > 0.0, normed, 0.0)
-        if normed_ref is not None:
-            normed_ref[rows, :] = normed
         in_ref[pl.ds(offset + rows.start, CHUNK), :] = (
             (normed * gain_ref[0:1, :]).astype(BF16).astype(F32)
         )
@@ -244,20 +324,10 @@
         )
 
 
-def stack_kernel(q_ref, k_ref, v_ref, out_ref, sems):
-    copies = [
-        pltpu.make_async_copy(ref, out_ref.at[i], sems.at[i]) for i, ref in enumerate((q_ref, k_ref, v_ref))
-    ]
-    for copy in copies:
-        copy.start()
-    for copy in copies:
-        copy.wait()
-
-
 def own_kernel(
     qkv_ref, cot_ref, gain_row, kernel_ref, bias_row, same_ref, keep_ref, mask_ref,
     out_ref, back_ref, prob_ref, context_ref, sums_ref, gain_ref, bias_ref,
-    pad_ref, normed_ref,
+    pad_ref,
 ):
     q_ref, k_ref, v_ref = (qkv_ref.at[i] for i in range(3))
     frames, width = q_ref.shape
@@ -269,7 +339,7 @@
     bias_ref[...] = bias_row[...].reshape(1, width)
     bias, keep = same_ref[...], keep_ref[...]
     forward_all(q_ref, k_ref, v_ref, prob_ref, context_ref, bias, keep, low)
-    normalize_all(context_ref, gain_ref, keep, normed_ref, pad_ref, PAD, frames)
+    normalize_all(context_ref, gain_ref, keep, pad_ref, PAD, frames)
 
     @pl.loop(0, tiles)
     def _(index):
@@ -291,36 +361,36 @@
             sums_ref[tap : tap + 1, lanes] = value
 
         grad_in = conv_backward(pad_ref, conv_in, kernel_ref, mask_ref, frames, lanes, store)
-        sums_ref[taps + 1 : taps + 2, lanes] = jnp.sum(grad_in * normed_ref[:, lanes], 0, keepdims=True)
         back_ref[:, lanes] = grad_in
 
 
 def cross_forward_kernel(
     qkv_ref, other_ref, seg_ref, gain_ref, kernel_ref, bias_ref, add_ref,
-    own_ref, next_ref, got_ref, prob_ref, context_ref, pre_ref,
-    pad_ref, out_ref,
+    own_ref, next_ref, got_ref, prob_ref, context_ref, pre_ref, in_ref,
+    out_ref,
 ):
     frames, width = qkv_ref.shape[1:]
+    taps = kernel_ref.shape[0]
     tiles = width // LANES
     first, length = crossing(seg_ref, frames)
     pick = gather_matrix(first, length, frames)
     place = scatter_matrix(first, length, frames)
     shape = (frames, frames)
-    bias = jnp.where(iota(shape, 1) < length, 0.0, NEG)
-    keep = jnp.where(iota(shape, 0) < length, 1.0, 0.0)
+    bias = jnp.where(frame_of(shape, 1) < length, 0.0, NEG)
+    keep = jnp.where(frame_of(shape, 0) < length, 1.0, 0.0)
     low = pair_masks(frames)
-    clear_edges(pad_ref, frames)
     for which in range(3):
         for cols in wide(width):
             both = jnp.concatenate([qkv_ref[which, :, cols], other_ref[which, :, cols]], 0)
             got_ref[which, :, cols] = dot(pick, both, NN).astype(BF16)
     forward_all(*(got_ref.at[i] for i in range(3)), prob_ref, context_ref, bias, keep, low)
-    normalize_all(context_ref, gain_ref, keep, None, pad_ref, PAD, frames)
+    normalize_all(context_ref, gain_ref, keep, in_ref, 0, frames)
 
     @pl.loop(0, tiles)
     def _(index):
         lanes = lanes_of(index)
-        pre_act = conv_forward(pad_ref, kernel_ref, bias_ref, None, frames, lanes)
+        start = jnp.broadcast_to(bias_ref[0:1, lanes], (8, LANES))
+        pre_act = phase_conv(in_ref[:, lanes], lambda t: kernel_ref[t : t + 1, lanes], taps, start)
         pre_ref[:, lanes] = pre_act
         out_ref[:, lanes] = (pre_act * gate(pre_act)).astype(BF16)
 
@@ -330,35 +400,32 @@
         next_ref[:, cols] = placed[frames:]
 
 
-def cross_conv_kernel(
-    cot_ref, cotn_ref, seg_ref, gain_ref, kernel_ref, context_ref, pre_ref, part_ref,
-    back_ref, mine_ref, other_ref,
-    pad_ref, in_ref, normed_ref, sums_ref,
+def cross_sums_kernel(
+    cot_ref, cotn_ref, seg_ref, pre_ref, in_ref, part_ref,
+    grad_ref, mine_ref, other_ref,
+    sums_ref,
 ):
     frames, width = cot_ref.shape
-    taps = kernel_ref.shape[0]
-    tiles = width // LANES
+    taps = part_ref.shape[0] - 1
     first, length = crossing(seg_ref, frames)
     pick = gather_matrix(first, length, frames)
-    keep = jnp.where(iota((frames, frames), 0) < length, 1.0, 0.0)
-    clear_edges(pad_ref, frames)
     for cols in wide(width):
         cotangent = dot(pick, jnp.concatenate([cot_ref[:, cols], cotn_ref[:, cols]], 0), NN)
         pre_act = pre_ref[:, cols]
-        pad_ref[PAD : PAD + frames, cols] = gate_grad(cotangent, pre_act, gate(pre_act))
-    normalize_all(context_ref, gain_ref, keep, normed_ref, in_ref, 0, frames)
-
-    @pl.loop(0, tiles)
+        grad_ref[:, cols] = gate_grad(cotangent, pre_act, gate(pre_act))
+
+    @pl.loop(0, width // LANES)
     def _(index):
         lanes = lanes_of(index)
 
         def store(row, value):
             sums_ref[row : row + 1, lanes] = part_ref[row : row + 1, lanes] + value
 
-        store(taps, jnp.sum(pad_ref[PAD : PAD + frames, lanes], 0, keepdims=True))
-        grad_in = conv_backward(pad_ref, in_ref[:, lanes], kernel_ref, None, frames, lanes, store)
-        store(taps + 1, jnp.sum(grad_in * normed_ref[:, lanes], 0, keepdims=True))
-        back_ref[:, lanes] = grad_in
+        grad_pre = grad_ref[:, lanes]
+        store(taps, jnp.sum(grad_pre, 0, keepdims=True))
+        phase_products(
+            grad_pre, in_ref[:, lanes], taps, lambda shift, value: store(taps - 1 - shift, value)
+        )
 
     half = width // 2
     mine = lax.rem(lax.axis_index("seq"), 2)
@@ -366,20 +433,27 @@
     other_ref[...] = sums_ref[:, pl.ds(pl.multiple_of((1 - mine) * half, LANES), half)].astype(BF16)
 
 
-def cross_back_kernel(
-    group, tiles, qkv_ref, prob_ref, context_ref, back_ref, gain_ref, seg_ref,
-    own_ref, next_ref, grad_ref=None,
-):
+def cross_back_kernel(group, tiles, qkv_ref, prob_ref, context_ref, seg_ref, *refs):
     q_ref, k_ref, v_ref = (qkv_ref.at[i] for i in range(3))
-    frames = q_ref.shape[0]
+    frames, width = q_ref.shape
     first, length = crossing(seg_ref, frames)
     place = scatter_matrix(first, length, frames)
     low = pair_masks(frames)
     if group == 0:
-        keep = jnp.where(iota((frames, frames), 0) < length, 1.0, 0.0)
+        gain_ref, kernel_ref, pre_ref, own_ref, next_ref, grad_ref, back_ref = refs
+        taps = kernel_ref.shape[0]
+
+        @pl.loop(0, width // LANES)
+        def _(index):
+            lanes = lanes_of(index)
+            back_ref[:, lanes] = phase_conv(
+                pre_ref[:, lanes], lambda t: kernel_ref[taps - 1 - t : taps - t, lanes], taps, None
+            )
+
+        keep = jnp.where(frame_of((frames, frames), 0) < length, 1.0, 0.0)
         norm_backward(context_ref, back_ref, gain_ref, keep, grad_ref, frames)
     else:
-        grad_ref = back_ref
+        grad_ref, own_ref, next_ref = refs
     for step in range(tiles):
         index = group * tiles + step
         lanes = slice(index * LANES, (index + 1) * LANES)
@@ -431,25 +505,26 @@
         start += part
 
 
-def finish_kernel(scale, mine_ref, came_ref, gain_ref, kernel_ref, bias_ref):
+def finish_kernel(scale, mine_ref, came_ref, weight_ref, norm_ref, gain_ref, kernel_ref, bias_ref):
     taps, width = kernel_ref.shape
     even = lax.rem(lax.axis_index("seq"), 2) == 0
     mine, came = mine_ref[...].astype(F32) * scale, came_ref[...].astype(F32) * scale
     total = jnp.concatenate([jnp.where(even, mine, came), jnp.where(even, came, mine)], 1)
     kernel_ref[...] = total[:taps]
     bias_ref[...] = total[taps : taps + 1].reshape(width)
-    gain_ref[...] = total[taps + 1 : taps + 2].reshape(width)
-
-
-def call(kernel, outs, scratch, flops, *args, space=pltpu.VMEM, limit=24):
+    gain = jnp.sum(total[:taps] * weight_ref[...], 0, keepdims=True) / norm_ref[...]
+    gain_ref[...] = gain.reshape(width)
+
+
+def call(kernel, outs, scratch, flops, *args):
     size = sum(a.size * a.dtype.itemsize for a in args) + sum(o.size * o.dtype.itemsize for o in outs)
     return pl.pallas_call(
         kernel,
         out_shape=outs,
-        in_specs=[pl.BlockSpec(memory_space=space)] * len(args),
-        out_specs=[pl.BlockSpec(memory_space=space)] * len(outs),
+        in_specs=[VMEM] * len(args),
+        out_specs=[VMEM] * len(outs),
         scratch_shapes=scratch,
-        compiler_params=pltpu.CompilerParams(vmem_limit_bytes=limit * 1024 * 1024),
+        compiler_params=pltpu.CompilerParams(vmem_limit_bytes=24 * 1024 * 1024),
         cost_estimate=pl.CostEstimate(flops=flops, bytes_accessed=size, transcendentals=0),
     )(*args)
 
@@ -484,16 +559,9 @@
     count = lax.axis_size("seq")
     to_left = [(i + 1, i) for i in range(count - 1)]
     to_right = [(i, i + 1) for i in range(count - 1)]
-    (qkv,) = call(
-        stack_kernel,
-        [jax.ShapeDtypeStruct((3, frames, width), BF16)],
-        [pltpu.SemaphoreType.DMA((3,))],
-        10**6,
-        queries[0], keys[0], values[0],
-        space=pl.ANY,
-        limit=60,
-    )
-    qkv_next = lax.ppermute(qkv, "seq", to_left)
+    qkv = jnp.concatenate([queries[0], keys[0], values[0]], 0)
+    qkv_next = lax.ppermute(qkv, "seq", to_left).reshape(3, frames, width)
+    qkv = qkv.reshape(3, frames, width)
     cot_next = lax.ppermute(cot, "seq", to_left)
 
     def sds(shape, dtype):
@@ -503,7 +571,7 @@
     rows32 = sds((frames, width), F32)
     three = sds((3, frames, width), BF16)
     probs = sds((tiles, frames, 2 * frames), BF16)
-    half_sums = sds((taps + 2, width // 2), BF16)
+    half_sums = sds((taps + 1, width // 2), BF16)
     row = sds((1, width), F32)
     square = sds((frames, frames), F32)
     padded = pltpu.VMEM((frames + 2 * PAD, width), F32)
@@ -518,39 +586,42 @@
     )
     out_own, back_own, prob_own, context_own, sums_own, gain, bias = call(
         own_kernel,
-        [rows16, rows32, probs, rows16, sds((taps + 2, width), F32), row, row],
-        [padded, plain],
+        [rows16, rows32, probs, rows16, sds((taps + 1, width), F32), row, row],
+        [padded],
         10**10,
         qkv, cot, norm_gain, conv_kernel, conv_bias, same, keep, masks,
     )
-    out_both, out_next, got, prob_cross, context_cross, pre_cross = call(
+    out_both, out_next, got, prob_cross, context_cross, pre_cross, in_cross = call(
         cross_forward_kernel,
-        [rows16, rows16, three, probs, rows16, rows32],
-        [padded, pltpu.VMEM((frames, width), BF16)],
+        [rows16, rows16, three, probs, rows16, rows32, rows32],
+        [pltpu.VMEM((frames, width), BF16)],
         4 * 10**9,
         qkv, qkv_next, segment_ids, gain, conv_kernel, bias, out_own,
     )
-    back_cross, mine, other = call(
-        cross_conv_kernel,
+    grad_pre, mine, other = call(
+        cross_sums_kernel,
         [rows32, half_sums, half_sums],
-        [padded, plain, plain, pltpu.VMEM((taps + 2, width), F32)],
-        4 * 10**9,
-        cot, cot_next, segment_ids, gain, conv_kernel, context_cross, pre_cross, sums_own,
+        [pltpu.VMEM((taps + 1, width), F32)],
+        3 * 10**9,
+        cot, cot_next, segment_ids, pre_cross, in_cross, sums_own,
     )
     steps = sum_steps()
     came = exchange(other, *steps[0])
     out_came = lax.ppermute(after(out_next, mine), "seq", to_right)
+    sent = added(mine, came)
+    came = exchange(sent, *steps[1])
     per_group = tiles // GROUPS
     piece = sds((3, frames, per_group * LANES), BF16)
-    grad_cross = back_cross
-    own_parts, came_parts, sent = [], [], mine
+    own_parts, came_parts = [], []
+    grad_pre = after(grad_pre, sent)
     for group in range(GROUPS):
+        extra = [gain, conv_kernel, grad_pre] if group == 0 else [grad_cross]
         own_part, next_part, *rest = call(
             functools.partial(cross_back_kernel, group, per_group),
             [piece, piece] + [rows16] * (group == 0),
-            [],
-            2 * 10**9,
-            got, prob_cross, context_cross, grad_cross, gain, segment_ids,
+            [plain] * (group == 0),
+            2 * 10**9 + 3 * 10**9 * (group == 0),
+            got, prob_cross, context_cross, segment_ids, *extra,
         )
         if group == 0:
             (grad_cross,) = rest
@@ -558,7 +629,7 @@
         sent = added(sent, after(came, own_part))
         if group == 1:
             sent = after(sent, out_came)
-        came = exchange(sent, *steps[group + 1])
+        came = exchange(sent, *steps[group + 2])
         came_parts.append(lax.ppermute(after(next_part, sent), "seq", to_right))
     grads = []
     grad_own = back_own
@@ -569,28 +640,26 @@
             [piece] + [rows16] * (group == 0),
             [],
             3 * 10**9,
-            qkv, prob_own, context_own, grad_own, *extra, own_parts[group],
+            qkv, prob_own, context_own, after(grad_own, sent), *extra, own_parts[group],
         )
         if group == 0:
             (grad_own,) = rest
+            for step in steps[4:]:
+                sent = added(sent, after(came, part, came_parts[0]))
+                came = exchange(sent, *step)
         grads.append(part)
-        sent = added(sent, after(came, part, *came_parts[: group + 1]))
-        came = exchange(sent, *steps[group + GROUPS + 1])
-    for step in steps[2 * GROUPS + 1 :]:
-        sent = added(sent, came)
-        came = exchange(sent, *step)
+    sent = added(sent, after(came, *grads, *came_parts))
+    came = exchange(sent, *steps[0])
     query_grad, key_grad, value_grad, conv_out = call(
         merge_kernel, [rows16] * 4, [], 10**9, *grads, *came_parts, out_both, out_came,
     )
-    sent = added(sent, after(came, query_grad))
-    came = exchange(sent, *steps[0])
     scale = (lax.axis_size("dp") * count * frames) ** (-0.5)
     gain_grad, kernel_grad, bias_grad = call(
         functools.partial(finish_kernel, scale),
         [sds((width,), F32), sds(conv_kernel.shape, F32), sds((width,), F32)],
         [],
         10**6,
-        sent, came,
+        sent, came, conv_kernel, gain,
     )
     return (
         conv_out[None],

time: 101 us -> 63 us (0.62)
  the two profiles are of different devices: /device:TPU:12 before, /device:TPU:17 now
where the time goes in v4:
time: 63 us; the launch traced here: 62.7 us
  Pallas kernels  32.6 us (52%)
  starting transfers between devices  23.5 us (37%)
  waiting for transfers between devices  4.26 us (7%)
  other arithmetic  1.44 us (2%)
  between operations  0.9 us (1%)
    pallas_call x10, Pallas kernels, call(): pl.pallas_call(kernel, out_shape=outs, in_specs=[VMEM] * len(args), out_s...  32.6 us
    ppermute x6, starting transfers between devices, exchange(): lax.ppermute(sent, axis, [(i, i ^ step) for i in range(lax.axis_size(axis...  10.7 us
    ppermute x2, starting transfers between devices, per_device(): came_parts.append(lax.ppermute(after(next_part, sent), 'seq', to_right))  4.74 us
    ppermute x6, waiting for transfers between devices, exchange(): lax.ppermute(sent, axis, [(i, i ^ step) for i in range(lax.axis_size(axis...  3.58 us
    ppermute x1, starting transfers between devices, per_device(): cot_next = lax.ppermute(cot, 'seq', to_left)  2.86 us
    ppermute x1, starting transfers between devices, per_device(): out_came = lax.ppermute(after(out_next, mine), 'seq', to_right)  2.71 us
    ppermute x1, starting transfers between devices, per_device(): qkv_next = lax.ppermute(qkv, 'seq', to_left).reshape(3, frames, width)  2.58 us
    concatenate x1, other arithmetic, per_device(): qkv = jnp.concatenate([queries[0], keys[0], values[0]], 0)  1.36 us
  transfers between devices with their start and end apart: 11, of which 3 were waited for; matrix products, arithmetic and copies ran while one was open for 0% of the time, Pallas kernels for 47%

profile of v4, /device:TPU:17, one launch (start us, length us, event | category | flops | bytes accessed | tf_op | source)
XLA Modules:
  0.0 62.7 jit_solution(13427113410345307927)
XLA Ops:
  0.6 0.0 copy-start.1
  0.6 0.0 copy-start.4
  0.7 1.4 %pad_maximum_fusion = bf16[384,1536]{1,0:T(8,128)(2,1)S(1)} fusion(bf16[128,1536]{1,0:T(8,128)(2,1)} %bitcast.18, bf16[128,1536]{1,0:T(8,128)(2,1)} %bitcast.19, bf16[128,1536]{1,0:T(8,128)(2,1)} %bitcast.20), kind=kLoop, calls=%fused_computation | loop fusion | flops 3538944 | bytes 2359296 | tf_op jit(solution)/shard_map/concatenate | solution.py:562
  2.0 2.6 %collective-permute-start.1 = (bf16[384,1536]{1,0:T(8,128)(2,1)S(1)}, bf16[384,1536]{1,0:T(8,128)(2,1)S(1)}, u32[]{:S(2)}, u32[]{:S(2)}) collective-permute-start(bf16[384,1536]{1,0:T(8,128)(2,1)S(1)} %pad_maximum_fusion), channel_id=1, source_target_pairs={{1,0},{2,1},{3,2},{4,3},{5,4},{6,5},{7,6},{8,7},{9,8},{10,9},{11,1... | collective-permute-start | bytes 3538952 | tf_op jit(solution)/shard_map/ppermute | solution.py:563
  4.6 0.0 copy-done.1
  4.6 0.0 copy-start
  4.6 0.0 copy-start.2
  4.6 0.0 copy-start.3
  4.7 2.9 %collective-permute-start = (bf16[128,1536]{1,0:T(8,128)(2,1)S(1)}, bf16[128,1536]{1,0:T(8,128)(2,1)S(1)}, u32[]{:S(2)}, u32[]{:S(2)}) collective-permute-start(bf16[128,1536]{1,0:T(8,128)(2,1)S(1)} %bitcast.15), channel_id=1, source_target_pairs={{1,0},{2,1},{3,2},{4,3},{5,4},{6,5},{7,6},{8,7},{9,8},{10,9},{11,1... | collective-permute-start | bytes 1179656 | tf_op jit(solution)/shard_map/ppermute | solution.py:565
  7.5 0.0 copy-done.4
  7.5 0.3 shard_map.135
  7.9 0.0 copy-done
  7.9 0.0 copy-done.2
  7.9 0.0 copy-done.3
  7.9 12.6 %shard_map.136 = (bf16[128,1536]{1,0:T(8,128)(2,1)S(1)}, f32[128,1536]{1,0:T(8,128)S(1)}, bf16[12,128,256]{2,1,0:T(8,128)(2,1)S(1)}, bf16[128,1536]{1,0:T(8,128)...) custom-call(bf16[3,128,1536]{2,1,0:T(8,128)(2,1)S(1)} %bitcast.10, ...), custom_call_target="tpu_custom_call" | custom-call | flops 10000000000 | bytes 6506496 | tf_op jit(solution)/shard_map/pallas_call | solution.py:521
  20.5 0.0 collective-permute-done.1
  20.6 4.5 %shard_map.137 = (bf16[128,1536]{1,0:T(8,128)(2,1)S(1)}, bf16[128,1536]{1,0:T(8,128)(2,1)S(1)}, bf16[3,128,1536]{2,1,0:T(8,128)(2,1)S(1)}, bf16[12,128,256]{2,1,...) custom-call(bf16[3,128,1536]{2,1,0:T(8,128)(2,1)S(1)} %bitcast.11, ...), custom_call_target="tpu_custom_call" | custom-call | flops 4000000000 | bytes 7682048 | tf_op jit(solution)/shard_map/pallas_call | solution.py:521
  25.0 0.0 collective-permute-done.cotn_ref
  25.0 2.5 %shard_map.138 = (f32[128,1536]{1,0:T(8,128)S(1)}, bf16[32,768]{1,0:T(8,128)(2,1)S(1)}, bf16[32,768]{1,0:T(8,128)(2,1)S(1)}) custom-call(bf16[128,1536]{1,0:T(8,128)(2,1)S(1)} %bitcast.17, bf16[128,1536]{1,0:T(8,128)(2,1)S(1)} %collective-permute-done.cotn_ref, s32[1,2048]{1,0:T(1,128)S(1)} %copy-done.4, f32[128,1536]{1,0:T(8,128)S(1)} %get-tuple-element.61.pre_ref, ...), custom_call_target="tpu_custom_call" | custom-call | flops 3000000000 | bytes 3448832 | tf_op jit(solution)/shard_map/pallas_call | solution.py:521
  27.6 0.7 %collective-permute-start.2 = (bf16[32,768]{1,0:T(8,128)(2,1)S(1)}, bf16[32,768]{1,0:T(8,128)(2,1)S(1)}, u32[]{:S(2)}, u32[]{:S(2)}) collective-permute-start(bf16[32,768]{1,0:T(8,128)(2,1)S(1)} %get-tuple-element.65), channel_id=1, source_target_pairs={{0,1},{1,0},{2,3},{3,2},{4,5},{5,4},{6,7},{7,6},{8,9},{9,8},{10,11... | collective-permute-start | bytes 147464 | tf_op jit(solution)/shard_map/ppermute | solution.py:547
  28.3 2.7 %collective-permute-start.5 = (bf16[128,1536]{1,0:T(8,128)(2,1)S(1)}, bf16[128,1536]{1,0:T(8,128)(2,1)S(1)}, u32[]{:S(2)}, u32[]{:S(2)}) collective-permute-start(bf16[128,1536]{1,0:T(8,128)(2,1)S(1)} %get-tuple-element.77), channel_id=1, source_target_pairs={{0,1},{1,2},{2,3},{3,4},{4,5},{5,6},{6,7},{7,8},{8,9},{9,10},{10,1... | collective-permute-start | bytes 1179656 | tf_op jit(solution)/shard_map/ppermute | solution.py:610
  31.0 0.0 collective-permute-done.2
  31.1 1.7 %collective-permute-start.3 = (bf16[32,768]{1,0:T(8,128)(2,1)S(1)}, bf16[32,768]{1,0:T(8,128)(2,1)S(1)}, u32[]{:S(2)}, u32[]{:S(2)}) collective-permute-start(bf16[32,768]{1,0:T(8,128)(2,1)S(1)} %add_convert_fusion.4), channel_id=1, source_target_pairs={{0,2},{1,3},{2,0},{3,1},{4,6},{5,7},{6,4},{7,5},{8,10},{9,11},{10,... | collective-permute-start | bytes 147464 | tf_op jit(solution)/shard_map/ppermute | solution.py:547
  32.7 4.7 %shard_map.139 = (bf16[3,128,768]{2,1,0:T(8,128)(2,1)S(1)}, bf16[3,128,768]{2,1,0:T(8,128)(2,1)S(1)}, bf16[128,1536]{1,0:T(8,128)(2,1)S(1)}) custom-call(bf16[3,128,1536]{2,1,0:T(8,128)(2,1)S(1)} %get-tuple-element.66.qkv_ref, bf16[12,128,256]{2,1,0:T(8,128)(2,1)S(1)} %get-tuple-element.67.prob_ref, bf16[128,1536]{1,0:T(8,128)(2,1)S(1)} %get-tuple-element.68.context_ref, ...), custom_call_target="tpu_custom_call" | custom-call | flops 5000000000 | bytes 4923392 | tf_op jit(solution)/shard_map/pallas_call | solution.py:521
  37.4 1.6 %collective-permute-done.3 = bf16[32,768]{1,0:T(8,128)(2,1)S(1)} collective-permute-done((bf16[32,768]{1,0:T(8,128)(2,1)S(1)}, bf16[32,768]{1,0:T(8,128)(2,1)S(1)}, u32[]{:S(2)}, u32[]{:S(2)}) %collective-permute-start.3) | collective-permute-done | bytes 49184 | tf_op jit(solution)/shard_map/ppermute | solution.py:547
  39.0 0.5 collective-permute-start.4
  39.5 2.2 %collective-permute-start.7 = (bf16[3,128,768]{2,1,0:T(8,128)(2,1)S(1)}, bf16[3,128,768]{2,1,0:T(8,128)(2,1)S(1)}, u32[]{:S(2)}, u32[]{:S(2)}) collective-permute-start(bf16[3,128,768]{2,1,0:T(8,128)(2,1)S(1)} %get-tuple-element.83), channel_id=1, source_target_pairs={{0,1},{1,2},{2,3},{3,4},{4,5},{5,6},{6,7},{7,8},{8,9},{9,10},{10,1... | collective-permute-start | bytes 1769480 | tf_op jit(solution)/shard_map/ppermute | solution.py:633
  41.7 2.3 %shard_map.140 = (bf16[3,128,768]{2,1,0:T(8,128)(2,1)S(1)}, bf16[3,128,768]{2,1,0:T(8,128)(2,1)S(1)}) custom-call(bf16[3,128,1536]{2,1,0:T(8,128)(2,1)S(1)} %get-tuple-element.66.qkv_ref, bf16[12,128,256]{2,1,0:T(8,128)(2,1)S(1)} %get-tuple-element.67.prob_ref, bf16[128,1536]{1,0:T(8,128)(2,1)S(1)} %get-tuple-element.68.context_ref, ...), custom_call_target="tpu_custom_call" | custom-call | flops 2000000000 | bytes 3940352 | tf_op jit(solution)/shard_map/pallas_call | solution.py:521
  44.0 0.0 collective-permute-done.4
  44.1 0.0 collective-permute-done.5.refs_5_
  44.1 1.3 %collective-permute-start.6 = (bf16[32,768]{1,0:T(8,128)(2,1)S(1)}, bf16[32,768]{1,0:T(8,128)(2,1)S(1)}, u32[]{:S(2)}, u32[]{:S(2)}) collective-permute-start(bf16[32,768]{1,0:T(8,128)(2,1)S(1)} %add_convert_fusion.2), channel_id=1, source_target_pairs={{0,16},{16,0},{1,17},{17,1},{2,18},{18,2},{3,19},{19,3},{4,20},{20... | collective-permute-start | bytes 147464 | tf_op jit(solution)/shard_map/ppermute | solution.py:547
  45.4 2.5 %collective-permute-start.8 = (bf16[3,128,768]{2,1,0:T(8,128)(2,1)S(1)}, bf16[3,128,768]{2,1,0:T(8,128)(2,1)S(1)}, u32[]{:S(2)}, u32[]{:S(2)}) collective-permute-start(bf16[3,128,768]{2,1,0:T(8,128)(2,1)S(1)} %get-tuple-element.87), channel_id=1, source_target_pairs={{0,1},{1,2},{2,3},{3,4},{4,5},{5,6},{6,7},{7,8},{8,9},{9,10},{10,1... | collective-permute-start | bytes 1769480 | tf_op jit(solution)/shard_map/ppermute | solution.py:633
  47.9 2.0 %shard_map.141 = (bf16[3,128,768]{2,1,0:T(8,128)(2,1)S(1)}, bf16[128,1536]{1,0:T(8,128)(2,1)S(1)}) custom-call(bf16[3,128,1536]{2,1,0:T(8,128)(2,1)S(1)} %bitcast.12, bf16[12,128,256]{2,1,0:T(8,128)(2,1)S(1)} %get-tuple-element.55.refs_1_, bf16[128,1536]{1,0:T(8,128)(2,1)S(1)} %get-tuple-element.56.refs_2_, f32[128,1536]{1,0:T(8,128)S(1)} %get-tuple-element.79.refs_3_, ...), custom_call_target="tpu_custom_call" | custom-call | flops 3000000000 | bytes 4790272 | tf_op jit(solution)/shard_map/pallas_call | solution.py:521
  49.9 0.0 collective-permute-done.6
  49.9 0.0 collective-permute-done.7.refs_2_
  50.0 0.6 %collective-permute-start.9 = (bf16[32,768]{1,0:T(8,128)(2,1)S(1)}, bf16[32,768]{1,0:T(8,128)(2,1)S(1)}, u32[]{:S(2)}, u32[]{:S(2)}) collective-permute-start(bf16[32,768]{1,0:T(8,128)(2,1)S(1)} %add_convert_fusion.1), channel_id=1, source_target_pairs={{0,8},{1,9},{2,10},{3,11},{4,12},{5,13},{6,14},{7,15},{8,0},{9,1},... | collective-permute-start | bytes 147464 | tf_op jit(solution)/shard_map/ppermute | solution.py:547
  50.6 1.5 %shard_map.142.refs_1_ = bf16[3,128,768]{2,1,0:T(8,128)(2,1)S(1)} custom-call(bf16[3,128,1536]{2,1,0:T(8,128)(2,1)S(1)} %bitcast.13, bf16[12,128,256]{2,1,0:T(8,128)(2,1)S(1)} %get-tuple-element.55.refs_1_, bf16[128,1536]{1,0:T(8,128)(2,1)S(1)} %get-tuple-element.56.refs_2_, bf16[128,1536]{1,0:T(8,128)(2,1)S(1)} %get-tuple-element.85.refs_3_, ...), custom_call_target="tpu_custom_call" | custom-call | flops 3000000000 | bytes 3932160 | tf_op jit(solution)/shard_map/pallas_call | solution.py:521
  52.2 2.0 %collective-permute-done.9 = bf16[32,768]{1,0:T(8,128)(2,1)S(1)} collective-permute-done((bf16[32,768]{1,0:T(8,128)(2,1)S(1)}, bf16[32,768]{1,0:T(8,128)(2,1)S(1)}, u32[]{:S(2)}, u32[]{:S(2)}) %collective-permute-start.9) | collective-permute-done | bytes 49184 | tf_op jit(solution)/shard_map/ppermute | solution.py:547
  54.2 0.7 %collective-permute-done.8.refs_3_ = bf16[3,128,768]{2,1,0:T(8,128)(2,1)S(1)} collective-permute-done((bf16[3,128,768]{2,1,0:T(8,128)(2,1)S(1)}, bf16[3,128,768]{2,1,0:T(8,128)(2,1)S(1)}, u32[]{:S(2)}, u32[]{:S(2)}) %collective-permute-start.8) | collective-permute-done | bytes 589856 | tf_op jit(solution)/shard_map/ppermute | solution.py:633
  54.9 5.8 %collective-permute-start.10 = (bf16[32,768]{1,0:T(8,128)(2,1)S(1)}, bf16[32,768]{1,0:T(8,128)(2,1)S(1)}, u32[]{:S(2)}, u32[]{:S(2)}) collective-permute-start(bf16[32,768]{1,0:T(8,128)(2,1)S(1)} %add_convert_fusion.mine_ref), channel_id=1, source_target_pairs={{0,1},{1,0},{2,3},{3,2},{4,5},{5,4},{6,7},{7,6},{8,9},{9,8},{10,11... | collective-permute-start | bytes 147464 | tf_op jit(solution)/shard_map/ppermute | solution.py:547
  60.7 1.3 %shard_map.143 = (bf16[128,1536]{1,0:T(8,128)(2,1)}, bf16[128,1536]{1,0:T(8,128)(2,1)}, bf16[128,1536]{1,0:T(8,128)(2,1)}, bf16[128,1536]{1,0:T(8,128)(2,1)}) custom-call(bf16[3,128,768]{2,1,0:T(8,128)(2,1)S(1)} %get-tuple-element.80.refs_0_, bf16[3,128,768]{2,1,0:T(8,128)(2,1)S(1)} %shard_map.142.refs_1_, ...), custom_call_target="tpu_custom_call" | custom-call | flops 1000000000 | bytes 4718592 | tf_op jit(solution)/shard_map/pallas_call | solution.py:521
  62.0 0.0 collective-permute-done.10.came_ref
  62.0 0.7 %shard_map.144 = (f32[1536]{0:T(1024)}, f32[31,1536]{1,0:T(8,128)}, f32[1536]{0:T(1024)}) custom-call(bf16[32,768]{1,0:T(8,128)(2,1)S(1)} %add_convert_fusion.mine_ref, bf16[32,768]{1,0:T(8,128)(2,1)S(1)} %collective-permute-done.10.came_ref, f32[31,1536]{1,0:T(8,128)S(1)} %copy-done, f32[1,1536]{1,0:T(1,128)S(1)} %get-tuple-element.58.gain_ref.refs_0_.refs_4_.norm_ref), custom_call_target="tpu_custom_call" | custom-call | flops 1000000 | bytes 497664 | tf_op jit(solution)/shard_map/pallas_call | solution.py:521
  (5 shorter events, 0.1 us)
Async XLA Ops:
  0.6 4.0 %copy-start.1 = (bf16[1,128,1536]{2,1,0:T(8,128)(2,1)S(1)}, bf16[1,128,1536]{2,1,0:T(8,128)(2,1)}, u32[]{:S(2)}) copy-start(bf16[1,128,1536]{2,1,0:T(8,128)(2,1)} %param.15) | copy-start | bytes 1179652
  0.6 6.9 %copy-start.4 = (s32[1,2048]{1,0:T(1,128)S(1)}, s32[1,2048]{1,0:T(1,128)}, u32[]{:S(2)}) copy-start(s32[1,2048]{1,0:T(1,128)} %seg_ref.9) | copy-start | bytes 24580
  2.0 18.5 %collective-permute-start.1 = (bf16[384,1536]{1,0:T(8,128)(2,1)S(1)}, bf16[384,1536]{1,0:T(8,128)(2,1)S(1)}, u32[]{:S(2)}, u32[]{:S(2)}) collective-permute-start(bf16[384,1536]{1,0:T(8,128)(2,1)S(1)} %pad_maximum_fusion), channel_id=1, source_target_pairs={{1,0},{2,1},{3,2},{4,3},{5,4},{6,5},{7,6},{8,7},{9,8},{10,9},{11,1... | collective-permute-start | bytes 3538952 | tf_op jit(solution)/shard_map/ppermute | solution.py:563
  4.6 3.2 %copy-start = (f32[31,1536]{1,0:T(8,128)S(1)}, f32[31,1536]{1,0:T(8,128)}, u32[]{:S(2)}) copy-start(f32[31,1536]{1,0:T(8,128)} %weight_ref.1) | copy-start | bytes 571396
  4.6 3.2 %copy-start.2 = (f32[1536]{0:T(1024)S(1)}, f32[1536]{0:T(1024)}, u32[]{:S(2)}) copy-start(f32[1536]{0:T(1024)} %gain_row.1) | copy-start | bytes 18436
  4.6 3.2 %copy-start.3 = (f32[1536]{0:T(1024)S(1)}, f32[1536]{0:T(1024)}, u32[]{:S(2)}) copy-start(f32[1536]{0:T(1024)} %bias_row.1) | copy-start | bytes 18436
  4.7 20.4 %collective-permute-start = (bf16[128,1536]{1,0:T(8,128)(2,1)S(1)}, bf16[128,1536]{1,0:T(8,128)(2,1)S(1)}, u32[]{:S(2)}, u32[]{:S(2)}) collective-permute-start(bf16[128,1536]{1,0:T(8,128)(2,1)S(1)} %bitcast.15), channel_id=1, source_target_pairs={{1,0},{2,1},{3,2},{4,3},{5,4},{6,5},{7,6},{8,7},{9,8},{10,9},{11,1... | collective-permute-start | bytes 1179656 | tf_op jit(solution)/shard_map/ppermute | solution.py:565
  27.6 3.5 %collective-permute-start.2 = (bf16[32,768]{1,0:T(8,128)(2,1)S(1)}, bf16[32,768]{1,0:T(8,128)(2,1)S(1)}, u32[]{:S(2)}, u32[]{:S(2)}) collective-permute-start(bf16[32,768]{1,0:T(8,128)(2,1)S(1)} %get-tuple-element.65), channel_id=1, source_target_pairs={{0,1},{1,0},{2,3},{3,2},{4,5},{5,4},{6,7},{7,6},{8,9},{9,8},{10,11... | collective-permute-start | bytes 147464 | tf_op jit(solution)/shard_map/ppermute | solution.py:547
  28.3 15.8 %collective-permute-start.5 = (bf16[128,1536]{1,0:T(8,128)(2,1)S(1)}, bf16[128,1536]{1,0:T(8,128)(2,1)S(1)}, u32[]{:S(2)}, u32[]{:S(2)}) collective-permute-start(bf16[128,1536]{1,0:T(8,128)(2,1)S(1)} %get-tuple-element.77), channel_id=1, source_target_pairs={{0,1},{1,2},{2,3},{3,4},{4,5},{5,6},{6,7},{7,8},{8,9},{9,10},{10,1... | collective-permute-start | bytes 1179656 | tf_op jit(solution)/shard_map/ppermute | solution.py:610
  31.1 7.9 %collective-permute-start.3 = (bf16[32,768]{1,0:T(8,128)(2,1)S(1)}, bf16[32,768]{1,0:T(8,128)(2,1)S(1)}, u32[]{:S(2)}, u32[]{:S(2)}) collective-permute-start(bf16[32,768]{1,0:T(8,128)(2,1)S(1)} %add_convert_fusion.4), channel_id=1, source_target_pairs={{0,2},{1,3},{2,0},{3,1},{4,6},{5,7},{6,4},{7,5},{8,10},{9,11},{10,... | collective-permute-start | bytes 147464 | tf_op jit(solution)/shard_map/ppermute | solution.py:547
  39.0 5.0 %collective-permute-start.4 = (bf16[32,768]{1,0:T(8,128)(2,1)S(1)}, bf16[32,768]{1,0:T(8,128)(2,1)S(1)}, u32[]{:S(2)}, u32[]{:S(2)}) collective-permute-start(bf16[32,768]{1,0:T(8,128)(2,1)S(1)} %add_convert_fusion.3), channel_id=1, source_target_pairs={{0,4},{1,5},{2,6},{3,7},{4,0},{5,1},{6,2},{7,3},{8,12},{9,13},{10,... | collective-permute-start | bytes 147464 | tf_op jit(solution)/shard_map/ppermute | solution.py:547
  39.5 10.5 %collective-permute-start.7 = (bf16[3,128,768]{2,1,0:T(8,128)(2,1)S(1)}, bf16[3,128,768]{2,1,0:T(8,128)(2,1)S(1)}, u32[]{:S(2)}, u32[]{:S(2)}) collective-permute-start(bf16[3,128,768]{2,1,0:T(8,128)(2,1)S(1)} %get-tuple-element.83), channel_id=1, source_target_pairs={{0,1},{1,2},{2,3},{3,4},{4,5},{5,6},{6,7},{7,8},{8,9},{9,10},{10,1... | collective-permute-start | bytes 1769480 | tf_op jit(solution)/shard_map/ppermute | solution.py:633
  44.1 5.8 %collective-permute-start.6 = (bf16[32,768]{1,0:T(8,128)(2,1)S(1)}, bf16[32,768]{1,0:T(8,128)(2,1)S(1)}, u32[]{:S(2)}, u32[]{:S(2)}) collective-permute-start(bf16[32,768]{1,0:T(8,128)(2,1)S(1)} %add_convert_fusion.2), channel_id=1, source_target_pairs={{0,16},{16,0},{1,17},{17,1},{2,18},{18,2},{3,19},{19,3},{4,20},{20... | collective-permute-start | bytes 147464 | tf_op jit(solution)/shard_map/ppermute | solution.py:547
  45.4 9.5 %collective-permute-start.8 = (bf16[3,128,768]{2,1,0:T(8,128)(2,1)S(1)}, bf16[3,128,768]{2,1,0:T(8,128)(2,1)S(1)}, u32[]{:S(2)}, u32[]{:S(2)}) collective-permute-start(bf16[3,128,768]{2,1,0:T(8,128)(2,1)S(1)} %get-tuple-element.87), channel_id=1, source_target_pairs={{0,1},{1,2},{2,3},{3,4},{4,5},{5,6},{6,7},{7,8},{8,9},{9,10},{10,1... | collective-permute-start | bytes 1769480 | tf_op jit(solution)/shard_map/ppermute | solution.py:633
  50.0 4.2 %collective-permute-start.9 = (bf16[32,768]{1,0:T(8,128)(2,1)S(1)}, bf16[32,768]{1,0:T(8,128)(2,1)S(1)}, u32[]{:S(2)}, u32[]{:S(2)}) collective-permute-start(bf16[32,768]{1,0:T(8,128)(2,1)S(1)} %add_convert_fusion.1), channel_id=1, source_target_pairs={{0,8},{1,9},{2,10},{3,11},{4,12},{5,13},{6,14},{7,15},{8,0},{9,1},... | collective-permute-start | bytes 147464 | tf_op jit(solution)/shard_map/ppermute | solution.py:547
  54.9 7.2 %collective-permute-start.10 = (bf16[32,768]{1,0:T(8,128)(2,1)S(1)}, bf16[32,768]{1,0:T(8,128)(2,1)S(1)}, u32[]{:S(2)}, u32[]{:S(2)}) collective-permute-start(bf16[32,768]{1,0:T(8,128)(2,1)S(1)} %add_convert_fusion.mine_ref), channel_id=1, source_target_pairs={{0,1},{1,0},{2,3},{3,2},{4,5},{5,4},{6,7},{7,6},{8,9},{9,8},{10,11... | collective-permute-start | bytes 147464 | tf_op jit(solution)/shard_map/ppermute | solution.py:547

commit v5 on v4

--- a/solution.py
+++ b/solution.py
@@ -14,6 +14,7 @@
 PAD = 16
 GROUPS = 2
 WIDE = 512
+BATCH = 6
 VMEM = pl.BlockSpec(memory_space=pltpu.VMEM)
 F32 = jnp.float32
 BF16 = jnp.bfloat16
@@ -100,27 +101,57 @@
     return prob, (context * keep).astype(BF16)
 
 
-def attend_back(query, key, value, prob, context, grad, low):
-    frames = query.shape[0]
+def attend_back(query, key, value, prob, context, grad, pairs, store):
+    frames = context(0).shape[0]
+    low = pair_masks(frames)
     scale = HEAD_DIM**-0.5
-    grad_prob = dot(grad, stack_pair(value, low), NT)
-    product = grad.astype(F32) * context.astype(F32)
-    zero = jnp.zeros_like(product)
-    deltas = (
-        jnp.sum(jnp.where(low, product, zero), 1, keepdims=True),
-        jnp.sum(jnp.where(low, zero, product), 1, keepdims=True),
-    )
-    parts = []
-    for half in range(2):
-        cols = slice(half * frames, (half + 1) * frames)
-        parts.append(
-            (prob[:, cols].astype(F32) * (grad_prob[:, cols] - deltas[half]) * scale).astype(BF16)
+    grad_probs = [dot(grad(p), stack_pair(value(p), low), NT) for p in pairs]
+    deltas = []
+    for p in pairs:
+        product = grad(p).astype(F32) * context(p).astype(F32)
+        zero = jnp.zeros_like(product)
+        deltas.append(
+            (
+                jnp.sum(jnp.where(low, product, zero), 1, keepdims=True),
+                jnp.sum(jnp.where(low, zero, product), 1, keepdims=True),
+            )
         )
-    query_grad = dot(jnp.concatenate(parts, 1), stack_pair(key, low), NN)
-    key_grad = dot(jnp.concatenate(parts, 0), stack_pair(query, low), TN)
-    prob_rows = jnp.concatenate([prob[:, :frames], prob[:, frames:]], 0)
-    value_grad = dot(prob_rows, stack_pair(grad, low), TN)
-    return query_grad, key_grad, value_grad
+    grad_logits = []
+    for p, grad_prob, delta in zip(pairs, grad_probs, deltas):
+        both = prob(p)
+        halves = []
+        for half in range(2):
+            cols = slice(half * frames, (half + 1) * frames)
+            halves.append(
+                (both[:, cols].astype(F32) * (grad_prob[:, cols] - delta[half]) * scale).astype(BF16)
+            )
+        grad_logits.append(halves)
+    for p, halves in zip(pairs, grad_logits):
+        store(0, p, dot(jnp.concatenate(halves, 1), stack_pair(key(p), low), NN).astype(BF16))
+    for p, halves in zip(pairs, grad_logits):
+        store(1, p, dot(jnp.concatenate(halves, 0), stack_pair(query(p), low), TN).astype(BF16))
+    for p in pairs:
+        both = prob(p)
+        rows = jnp.concatenate([both[:, :frames], both[:, frames:]], 0)
+        store(2, p, dot(rows, stack_pair(grad(p), low), TN).astype(BF16))
+
+
+def lanes_at(index):
+    return slice(index * LANES, (index + 1) * LANES)
+
+
+def back_all(qkv_ref, prob_ref, context_ref, grad_ref, first, pairs, store):
+    for start in range(0, pairs, BATCH):
+        attend_back(
+            lambda p: qkv_ref[0, :, lanes_at(first + p)],
+            lambda p: qkv_ref[1, :, lanes_at(first + p)],
+            lambda p: qkv_ref[2, :, lanes_at(first + p)],
+            lambda p: prob_ref[first + p],
+            lambda p: context_ref[:, lanes_at(first + p)],
+            lambda p: grad_ref[:, lanes_at(first + p)],
+            range(start, min(start + BATCH, pairs)),
+            store,
+        )
 
 
 def normalize(context):
@@ -434,13 +465,11 @@
 
 
 def cross_back_kernel(group, tiles, qkv_ref, prob_ref, context_ref, seg_ref, *refs):
-    q_ref, k_ref, v_ref = (qkv_ref.at[i] for i in range(3))
-    frames, width = q_ref.shape
+    frames, width = context_ref.shape
     first, length = crossing(seg_ref, frames)
     place = scatter_matrix(first, length, frames)
-    low = pair_masks(frames)
     if group == 0:
-        gain_ref, kernel_ref, pre_ref, own_ref, next_ref, grad_ref, back_ref = refs
+        gain_ref, kernel_ref, pre_ref, own_ref, next_ref, grad_ref, result_ref, back_ref = refs
         taps = kernel_ref.shape[0]
 
         @pl.loop(0, width // LANES)
@@ -453,56 +482,39 @@
         keep = jnp.where(frame_of((frames, frames), 0) < length, 1.0, 0.0)
         norm_backward(context_ref, back_ref, gain_ref, keep, grad_ref, frames)
     else:
-        grad_ref, own_ref, next_ref = refs
-    for step in range(tiles):
-        index = group * tiles + step
-        lanes = slice(index * LANES, (index + 1) * LANES)
-        dest = slice(step * LANES, (step + 1) * LANES)
-        results = attend_back(
-            q_ref[:, lanes], k_ref[:, lanes], v_ref[:, lanes], prob_ref[index],
-            context_ref[:, lanes], grad_ref[:, lanes], low,
-        )
-        joined = jnp.concatenate([result.astype(BF16) for result in results], 1)
-        placed = dot(place, joined, NN).astype(BF16)
+        grad_ref, own_ref, next_ref, result_ref = refs
+
+    def store(which, pair, result):
+        result_ref[which, :, lanes_at(pair)] = result
+
+    back_all(qkv_ref, prob_ref, context_ref, grad_ref, group * tiles, tiles, store)
+    for which in range(3):
+        placed = dot(place, result_ref[which], NN).astype(BF16)
+        own_ref[which] = placed[:frames]
+        next_ref[which] = placed[frames:]
+
+
+def own_back_kernel(
+    qkv_ref, prob_ref, context_ref, back_ref, gain_ref, keep_ref, out_ref, grad_ref
+):
+    frames, width = context_ref.shape
+    norm_backward(context_ref, back_ref, gain_ref, keep_ref[...], grad_ref, frames)
+
+    def store(which, pair, result):
+        out_ref[which, :, lanes_at(pair)] = result
+
+    back_all(qkv_ref, prob_ref, context_ref, grad_ref, 0, width // LANES, store)
+
+
+def merge_kernel(grads_ref, out_both_ref, out_came_ref, *refs):
+    parts, outs = refs[:-4], refs[-4:]
+    outs[3][...] = out_both_ref[...] + out_came_ref[...]
+    start = 0
+    for cross_ref, came_ref in zip(parts[::2], parts[1::2]):
+        cols = slice(start, start + came_ref.shape[2])
         for which in range(3):
-            cols = slice(which * LANES, (which + 1) * LANES)
-            own_ref[which, :, dest] = placed[:frames, cols]
-            next_ref[which, :, dest] = placed[frames:, cols]
-
-
-def own_back_kernel(first, *refs):
-    if first:
-        qkv_ref, prob_ref, context_ref, back_ref, gain_ref, keep_ref, cross_ref, out_ref, grad_ref = refs
-        frames = keep_ref.shape[0]
-        norm_backward(context_ref, back_ref, gain_ref, keep_ref[...], grad_ref, frames)
-    else:
-        qkv_ref, prob_ref, context_ref, grad_ref, cross_ref, out_ref = refs
-    frames, part = out_ref.shape[1:]
-    low = pair_masks(frames)
-    tiles = part // LANES
-    for step in range(tiles):
-        index = step if first else step + prob_ref.shape[0] - tiles
-        lanes = slice(index * LANES, (index + 1) * LANES)
-        dest = slice(step * LANES, (step + 1) * LANES)
-        results = attend_back(
-            *(qkv_ref[i, :, lanes] for i in range(3)), prob_ref[index],
-            context_ref[:, lanes], grad_ref[:, lanes], low,
-        )
-        for which, result in enumerate(results):
-            out_ref[which, :, dest] = result.astype(BF16) + cross_ref[which, :, dest]
-
-
-def merge_kernel(*refs):
-    ins, outs = refs[:-6], refs[-4:-1]
-    out_both_ref, out_came_ref, conv_ref = refs[-6], refs[-5], refs[-1]
-    conv_ref[...] = out_both_ref[...] + out_came_ref[...]
-    half = len(ins) // 2
-    start = 0
-    for own_ref, came_ref in zip(ins[:half], ins[half:]):
-        part = own_ref.shape[2]
-        for which, out_ref in enumerate(outs):
-            out_ref[:, start : start + part] = own_ref[which] + came_ref[which]
-        start += part
+            outs[which][:, cols] = grads_ref[which, :, cols] + cross_ref[which] + came_ref[which]
+        start = cols.stop
 
 
 def finish_kernel(scale, mine_ref, came_ref, weight_ref, norm_ref, gain_ref, kernel_ref, bias_ref):
@@ -607,51 +619,43 @@
     )
     steps = sum_steps()
     came = exchange(other, *steps[0])
-    out_came = lax.ppermute(after(out_next, mine), "seq", to_right)
-    sent = added(mine, came)
+    (grads_own,) = call(
+        own_back_kernel,
+        [three],
+        [pltpu.VMEM((frames, width), BF16)],
+        4 * 10**9,
+        qkv, prob_own, context_own, after(back_own, mine), gain, keep,
+    )
+    sent = added(mine, after(came, grads_own))
     came = exchange(sent, *steps[1])
+    out_came = lax.ppermute(after(out_next, sent), "seq", to_right)
     per_group = tiles // GROUPS
     piece = sds((3, frames, per_group * LANES), BF16)
-    own_parts, came_parts = [], []
+    parts = []
     grad_pre = after(grad_pre, sent)
     for group in range(GROUPS):
         extra = [gain, conv_kernel, grad_pre] if group == 0 else [grad_cross]
         own_part, next_part, *rest = call(
             functools.partial(cross_back_kernel, group, per_group),
             [piece, piece] + [rows16] * (group == 0),
-            [plain] * (group == 0),
+            [pltpu.VMEM(piece.shape, BF16)] + [plain] * (group == 0),
             2 * 10**9 + 3 * 10**9 * (group == 0),
             got, prob_cross, context_cross, segment_ids, *extra,
         )
         if group == 0:
             (grad_cross,) = rest
-        own_parts.append(own_part)
         sent = added(sent, after(came, own_part))
         if group == 1:
             sent = after(sent, out_came)
         came = exchange(sent, *steps[group + 2])
-        came_parts.append(lax.ppermute(after(next_part, sent), "seq", to_right))
-    grads = []
-    grad_own = back_own
-    for group in range(GROUPS):
-        extra = [gain, keep] if group == 0 else []
-        part, *rest = call(
-            functools.partial(own_back_kernel, group == 0),
-            [piece] + [rows16] * (group == 0),
-            [],
-            3 * 10**9,
-            qkv, prob_own, context_own, after(grad_own, sent), *extra, own_parts[group],
-        )
-        if group == 0:
-            (grad_own,) = rest
-            for step in steps[4:]:
-                sent = added(sent, after(came, part, came_parts[0]))
-                came = exchange(sent, *step)
-        grads.append(part)
-    sent = added(sent, after(came, *grads, *came_parts))
+        parts += [own_part, lax.ppermute(after(next_part, sent), "seq", to_right)]
+    for step in steps[GROUPS + 2 :]:
+        sent = added(sent, after(came, parts[1]))
+        came = exchange(sent, *step)
+    sent = added(sent, after(came, parts[3]))
     came = exchange(sent, *steps[0])
     query_grad, key_grad, value_grad, conv_out = call(
-        merge_kernel, [rows16] * 4, [], 10**9, *grads, *came_parts, out_both, out_came,
+        merge_kernel, [rows16] * 4, [], 10**9, grads_own, out_both, out_came, *parts,
     )
     scale = (lax.axis_size("dp") * count * frames) ** (-0.5)
     gain_grad, kernel_grad, bias_grad = call(

time: 63 us -> 59.5 us (0.944)
  the two profiles are of different devices: /device:TPU:17 before, /device:TPU:12 now
where the time goes in v5:
time: 59.5 us; the launch traced here: 58.6 us
  Pallas kernels  27.3 us (46%)
  starting transfers between devices  16.4 us (28%)
  waiting for transfers between devices  12.6 us (21%)
  other arithmetic  1.43 us (2%)
  between operations  0.88 us (1%)
    pallas_call x9, Pallas kernels, call(): pl.pallas_call(kernel, out_shape=outs, in_specs=[VMEM] * len(args), out_s...  27.3 us
    ppermute x6, waiting for transfers between devices, exchange(): lax.ppermute(sent, axis, [(i, i ^ step) for i in range(lax.axis_size(axis...  7.71 us
    ppermute x6, starting transfers between devices, exchange(): lax.ppermute(sent, axis, [(i, i ^ step) for i in range(lax.axis_size(axis...  5.15 us
    ppermute x2, waiting for transfers between devices, per_device(): parts += [own_part, lax.ppermute(after(next_part, sent), 'seq', to_right)]  3.96 us
    ppermute x2, starting transfers between devices, per_device(): parts += [own_part, lax.ppermute(after(next_part, sent), 'seq', to_right)]  3.89 us
    ppermute x1, starting transfers between devices, per_device(): qkv_next = lax.ppermute(qkv, 'seq', to_left).reshape(3, frames, width)  2.72 us
    ppermute x1, starting transfers between devices, per_device(): cot_next = lax.ppermute(cot, 'seq', to_left)  2.72 us
    ppermute x1, starting transfers between devices, per_device(): out_came = lax.ppermute(after(out_next, sent), 'seq', to_right)  1.91 us
  transfers between devices with their start and end apart: 11, of which 6 were waited for; matrix products, arithmetic and copies ran while one was open for 0% of the time, Pallas kernels for 41%

profile of v5, /device:TPU:12, one launch (start us, length us, event | category | flops | bytes accessed | tf_op | source)
XLA Modules:
  0.0 58.6 jit_solution(16072472407463857978)
XLA Ops:
  0.6 0.0 copy-start.1
  0.6 0.0 copy-start.4
  0.7 1.4 %pad_maximum_fusion = bf16[384,1536]{1,0:T(8,128)(2,1)S(1)} fusion(bf16[128,1536]{1,0:T(8,128)(2,1)} %bitcast.17, bf16[128,1536]{1,0:T(8,128)(2,1)} %bitcast.18, bf16[128,1536]{1,0:T(8,128)(2,1)} %bitcast.19), kind=kLoop, calls=%fused_computation | loop fusion | flops 3538944 | bytes 2359296 | tf_op jit(solution)/shard_map/concatenate | solution.py:574
  2.0 2.7 %collective-permute-start.1 = (bf16[384,1536]{1,0:T(8,128)(2,1)S(1)}, bf16[384,1536]{1,0:T(8,128)(2,1)S(1)}, u32[]{:S(2)}, u32[]{:S(2)}) collective-permute-start(bf16[384,1536]{1,0:T(8,128)(2,1)S(1)} %pad_maximum_fusion), channel_id=1, source_target_pairs={{1,0},{2,1},{3,2},{4,3},{5,4},{6,5},{7,6},{8,7},{9,8},{10,9},{11,1... | collective-permute-start | bytes 3538952 | tf_op jit(solution)/shard_map/ppermute | solution.py:575
  4.7 0.0 copy-done.1
  4.8 0.0 copy-start
  4.8 0.0 copy-start.2
  4.8 0.0 copy-start.3
  4.8 2.7 %collective-permute-start = (bf16[128,1536]{1,0:T(8,128)(2,1)S(1)}, bf16[128,1536]{1,0:T(8,128)(2,1)S(1)}, u32[]{:S(2)}, u32[]{:S(2)}) collective-permute-start(bf16[128,1536]{1,0:T(8,128)(2,1)S(1)} %bitcast.14), channel_id=1, source_target_pairs={{1,0},{2,1},{3,2},{4,3},{5,4},{6,5},{7,6},{8,7},{9,8},{10,9},{11,1... | collective-permute-start | bytes 1179656 | tf_op jit(solution)/shard_map/ppermute | solution.py:577
  7.5 0.0 copy-done.4
  7.5 0.3 shard_map.135
  7.9 0.0 copy-done
  7.9 0.0 copy-done.2
  7.9 0.0 copy-done.3
  7.9 11.6 %shard_map.136 = (bf16[128,1536]{1,0:T(8,128)(2,1)S(1)}, f32[128,1536]{1,0:T(8,128)S(1)}, bf16[12,128,256]{2,1,0:T(8,128)(2,1)S(1)}, bf16[128,1536]{1,0:T(8,128)...) custom-call(bf16[3,128,1536]{2,1,0:T(8,128)(2,1)S(1)} %bitcast.10, ...), custom_call_target="tpu_custom_call" | custom-call | flops 10000000000 | bytes 6506496 | tf_op jit(solution)/shard_map/pallas_call | solution.py:533
  19.5 0.0 collective-permute-done.1
  19.5 4.4 %shard_map.137 = (bf16[128,1536]{1,0:T(8,128)(2,1)S(1)}, bf16[128,1536]{1,0:T(8,128)(2,1)S(1)}, bf16[3,128,1536]{2,1,0:T(8,128)(2,1)S(1)}, bf16[12,128,256]{2,1,...) custom-call(bf16[3,128,1536]{2,1,0:T(8,128)(2,1)S(1)} %bitcast.11, ...), custom_call_target="tpu_custom_call" | custom-call | flops 4000000000 | bytes 7682048 | tf_op jit(solution)/shard_map/pallas_call | solution.py:533
  23.9 0.0 collective-permute-done.cotn_ref
  23.9 2.5 %shard_map.138 = (f32[128,1536]{1,0:T(8,128)S(1)}, bf16[32,768]{1,0:T(8,128)(2,1)S(1)}, bf16[32,768]{1,0:T(8,128)(2,1)S(1)}) custom-call(bf16[128,1536]{1,0:T(8,128)(2,1)S(1)} %bitcast.16, bf16[128,1536]{1,0:T(8,128)(2,1)S(1)} %collective-permute-done.cotn_ref, s32[1,2048]{1,0:T(1,128)S(1)} %copy-done.4, f32[128,1536]{1,0:T(8,128)S(1)} %get-tuple-element.59.pre_ref, ...), custom_call_target="tpu_custom_call" | custom-call | flops 3000000000 | bytes 3448832 | tf_op jit(solution)/shard_map/pallas_call | solution.py:533
  26.5 0.1 collective-permute-start.2
  26.6 1.8 %shard_map.139.grads_ref = bf16[3,128,1536]{2,1,0:T(8,128)(2,1)S(1)} custom-call(bf16[3,128,1536]{2,1,0:T(8,128)(2,1)S(1)} %bitcast.12, bf16[12,128,256]{2,1,0:T(8,128)(2,1)S(1)} %get-tuple-element.53.prob_ref, bf16[128,1536]{1,0:T(8,128)(2,1)S(1)} %get-tuple-element.54.context_ref, f32[128,1536]{1,0:T(8,128)S(1)} %get-tuple-element.63.back_ref, ...), custom_call_target="tpu_custom_call" | custom-call | flops 4000000000 | bytes 4397056 | tf_op jit(solution)/shard_map/pallas_call | solution.py:533
  28.3 0.0 collective-permute-done.2
  28.4 2.3 %collective-permute-start.4 = (bf16[32,768]{1,0:T(8,128)(2,1)S(1)}, bf16[32,768]{1,0:T(8,128)(2,1)S(1)}, u32[]{:S(2)}, u32[]{:S(2)}) collective-permute-start(bf16[32,768]{1,0:T(8,128)(2,1)S(1)} %add_convert_fusion.4), channel_id=1, source_target_pairs={{0,2},{1,3},{2,0},{3,1},{4,6},{5,7},{6,4},{7,5},{8,10},{9,11},{10,... | collective-permute-start | bytes 147464 | tf_op jit(solution)/shard_map/ppermute | solution.py:559
  30.7 1.9 %collective-permute-start.3 = (bf16[128,1536]{1,0:T(8,128)(2,1)S(1)}, bf16[128,1536]{1,0:T(8,128)(2,1)S(1)}, u32[]{:S(2)}, u32[]{:S(2)}) collective-permute-start(bf16[128,1536]{1,0:T(8,128)(2,1)S(1)} %get-tuple-element.68), channel_id=1, source_target_pairs={{0,1},{1,2},{2,3},{3,4},{4,5},{5,6},{6,7},{7,8},{8,9},{9,10},{10,1... | collective-permute-start | bytes 1179656 | tf_op jit(solution)/shard_map/ppermute | solution.py:631
  32.6 3.5 %shard_map.140 = (bf16[3,128,768]{2,1,0:T(8,128)(2,1)S(1)}, bf16[3,128,768]{2,1,0:T(8,128)(2,1)S(1)}, bf16[128,1536]{1,0:T(8,128)(2,1)S(1)}) custom-call(bf16[3,128,1536]{2,1,0:T(8,128)(2,1)S(1)} %get-tuple-element.69.qkv_ref, bf16[12,128,256]{2,1,0:T(8,128)(2,1)S(1)} %get-tuple-element.70.prob_ref, bf16[128,1536]{1,0:T(8,128)(2,1)S(1)} %get-tuple-element.71.context_ref, ...), custom_call_target="tpu_custom_call" | custom-call | flops 5000000000 | bytes 4923392 | tf_op jit(solution)/shard_map/pallas_call | solution.py:533
  36.1 0.0 collective-permute-done.4
  36.1 0.3 collective-permute-start.6
  36.4 2.0 %collective-permute-start.5 = (bf16[3,128,768]{2,1,0:T(8,128)(2,1)S(1)}, bf16[3,128,768]{2,1,0:T(8,128)(2,1)S(1)}, u32[]{:S(2)}, u32[]{:S(2)}) collective-permute-start(bf16[3,128,768]{2,1,0:T(8,128)(2,1)S(1)} %get-tuple-element.77), channel_id=1, source_target_pairs={{0,1},{1,2},{2,3},{3,4},{4,5},{5,6},{6,7},{7,8},{8,9},{9,10},{10,1... | collective-permute-start | bytes 1769480 | tf_op jit(solution)/shard_map/ppermute | solution.py:651
  38.4 1.1 %shard_map.141 = (bf16[3,128,768]{2,1,0:T(8,128)(2,1)S(1)}, bf16[3,128,768]{2,1,0:T(8,128)(2,1)S(1)}) custom-call(bf16[3,128,1536]{2,1,0:T(8,128)(2,1)S(1)} %get-tuple-element.69.qkv_ref, bf16[12,128,256]{2,1,0:T(8,128)(2,1)S(1)} %get-tuple-element.70.prob_ref, bf16[128,1536]{1,0:T(8,128)(2,1)S(1)} %get-tuple-element.71.context_ref, ...), custom_call_target="tpu_custom_call" | custom-call | flops 2000000000 | bytes 3940352 | tf_op jit(solution)/shard_map/pallas_call | solution.py:533
  39.5 0.8 %collective-permute-done.6 = bf16[32,768]{1,0:T(8,128)(2,1)S(1)} collective-permute-done((bf16[32,768]{1,0:T(8,128)(2,1)S(1)}, bf16[32,768]{1,0:T(8,128)(2,1)S(1)}, u32[]{:S(2)}, u32[]{:S(2)}) %collective-permute-start.6) | collective-permute-done | bytes 49184 | tf_op jit(solution)/shard_map/ppermute | solution.py:559
  40.3 0.9 %collective-permute-done.3.out_came_ref = bf16[128,1536]{1,0:T(8,128)(2,1)S(1)} collective-permute-done((bf16[128,1536]{1,0:T(8,128)(2,1)S(1)}, bf16[128,1536]{1,0:T(8,128)(2,1)S(1)}, u32[]{:S(2)}, u32[]{:S(2)}) %collective-permute-start.3) | collective-permute-done | bytes 393248 | tf_op jit(solution)/shard_map/ppermute | solution.py:631
  41.2 1.9 %collective-permute-start.7 = (bf16[3,128,768]{2,1,0:T(8,128)(2,1)S(1)}, bf16[3,128,768]{2,1,0:T(8,128)(2,1)S(1)}, u32[]{:S(2)}, u32[]{:S(2)}) collective-permute-start(bf16[3,128,768]{2,1,0:T(8,128)(2,1)S(1)} %get-tuple-element.83), channel_id=1, source_target_pairs={{0,1},{1,2},{2,3},{3,4},{4,5},{5,6},{6,7},{7,8},{8,9},{9,10},{10,1... | collective-permute-start | bytes 1769480 | tf_op jit(solution)/shard_map/ppermute | solution.py:651
  43.1 0.6 collective-permute-start.8
  43.7 3.7 %collective-permute-done.8 = bf16[32,768]{1,0:T(8,128)(2,1)S(1)} collective-permute-done((bf16[32,768]{1,0:T(8,128)(2,1)S(1)}, bf16[32,768]{1,0:T(8,128)(2,1)S(1)}, u32[]{:S(2)}, u32[]{:S(2)}) %collective-permute-start.8) | collective-permute-done | bytes 49184 | tf_op jit(solution)/shard_map/ppermute | solution.py:559
  47.4 2.2 %collective-permute-done.5.refs_1_ = bf16[3,128,768]{2,1,0:T(8,128)(2,1)S(1)} collective-permute-done((bf16[3,128,768]{2,1,0:T(8,128)(2,1)S(1)}, bf16[3,128,768]{2,1,0:T(8,128)(2,1)S(1)}, u32[]{:S(2)}, u32[]{:S(2)}) %collective-permute-start.5) | collective-permute-done | bytes 589856 | tf_op jit(solution)/shard_map/ppermute | solution.py:651
  49.6 1.8 %collective-permute-start.9 = (bf16[32,768]{1,0:T(8,128)(2,1)S(1)}, bf16[32,768]{1,0:T(8,128)(2,1)S(1)}, u32[]{:S(2)}, u32[]{:S(2)}) collective-permute-start(bf16[32,768]{1,0:T(8,128)(2,1)S(1)} %add_convert_fusion.1), channel_id=1, source_target_pairs={{0,8},{1,9},{2,10},{3,11},{4,12},{5,13},{6,14},{7,15},{8,0},{9,1},... | collective-permute-start | bytes 147464 | tf_op jit(solution)/shard_map/ppermute | solution.py:559
  51.4 3.2 %collective-permute-done.9 = bf16[32,768]{1,0:T(8,128)(2,1)S(1)} collective-permute-done((bf16[32,768]{1,0:T(8,128)(2,1)S(1)}, bf16[32,768]{1,0:T(8,128)(2,1)S(1)}, u32[]{:S(2)}, u32[]{:S(2)}) %collective-permute-start.9) | collective-permute-done | bytes 49184 | tf_op jit(solution)/shard_map/ppermute | solution.py:559
  54.6 1.8 %collective-permute-done.7.refs_3_ = bf16[3,128,768]{2,1,0:T(8,128)(2,1)S(1)} collective-permute-done((bf16[3,128,768]{2,1,0:T(8,128)(2,1)S(1)}, bf16[3,128,768]{2,1,0:T(8,128)(2,1)S(1)}, u32[]{:S(2)}, u32[]{:S(2)}) %collective-permute-start.7) | collective-permute-done | bytes 589856 | tf_op jit(solution)/shard_map/ppermute | solution.py:651
  56.4 0.1 collective-permute-start.10
  56.5 1.4 %shard_map.142 = (bf16[128,1536]{1,0:T(8,128)(2,1)}, bf16[128,1536]{1,0:T(8,128)(2,1)}, bf16[128,1536]{1,0:T(8,128)(2,1)}, bf16[128,1536]{1,0:T(8,128)(2,1)}) custom-call(bf16[3,128,1536]{2,1,0:T(8,128)(2,1)S(1)} %shard_map.139.grads_ref, bf16[128,1536]{1,0:T(8,128)(2,1)S(1)} %get-tuple-element.64.out_both_ref, ...), custom_call_target="tpu_custom_call" | custom-call | flops 1000000000 | bytes 5898240 | tf_op jit(solution)/shard_map/pallas_call | solution.py:533
  57.9 0.0 collective-permute-done.10.came_ref
  57.9 0.7 %shard_map.143 = (f32[1536]{0:T(1024)}, f32[31,1536]{1,0:T(8,128)}, f32[1536]{0:T(1024)}) custom-call(bf16[32,768]{1,0:T(8,128)(2,1)S(1)} %add_convert_fusion.mine_ref, bf16[32,768]{1,0:T(8,128)(2,1)S(1)} %collective-permute-done.10.came_ref, f32[31,1536]{1,0:T(8,128)S(1)} %copy-done, f32[1,1536]{1,0:T(1,128)S(1)} %get-tuple-element.56.gain_ref.refs_0_.norm_ref), custom_call_target="tpu_custom_call" | custom-call | flops 1000000 | bytes 497664 | tf_op jit(solution)/shard_map/pallas_call | solution.py:533
  (5 shorter events, 0.1 us)
Async XLA Ops:
  0.6 4.1 %copy-start.1 = (bf16[1,128,1536]{2,1,0:T(8,128)(2,1)S(1)}, bf16[1,128,1536]{2,1,0:T(8,128)(2,1)}, u32[]{:S(2)}) copy-start(bf16[1,128,1536]{2,1,0:T(8,128)(2,1)} %param.15) | copy-start | bytes 1179652
  0.6 6.9 %copy-start.4 = (s32[1,2048]{1,0:T(1,128)S(1)}, s32[1,2048]{1,0:T(1,128)}, u32[]{:S(2)}) copy-start(s32[1,2048]{1,0:T(1,128)} %seg_ref.9) | copy-start | bytes 24580
  2.0 17.4 %collective-permute-start.1 = (bf16[384,1536]{1,0:T(8,128)(2,1)S(1)}, bf16[384,1536]{1,0:T(8,128)(2,1)S(1)}, u32[]{:S(2)}, u32[]{:S(2)}) collective-permute-start(bf16[384,1536]{1,0:T(8,128)(2,1)S(1)} %pad_maximum_fusion), channel_id=1, source_target_pairs={{1,0},{2,1},{3,2},{4,3},{5,4},{6,5},{7,6},{8,7},{9,8},{10,9},{11,1... | collective-permute-start | bytes 3538952 | tf_op jit(solution)/shard_map/ppermute | solution.py:575
  4.8 3.1 %copy-start = (f32[31,1536]{1,0:T(8,128)S(1)}, f32[31,1536]{1,0:T(8,128)}, u32[]{:S(2)}) copy-start(f32[31,1536]{1,0:T(8,128)} %weight_ref.1) | copy-start | bytes 571396
  4.8 3.1 %copy-start.2 = (f32[1536]{0:T(1024)S(1)}, f32[1536]{0:T(1024)}, u32[]{:S(2)}) copy-start(f32[1536]{0:T(1024)} %gain_row.1) | copy-start | bytes 18436
  4.8 3.1 %copy-start.3 = (f32[1536]{0:T(1024)S(1)}, f32[1536]{0:T(1024)}, u32[]{:S(2)}) copy-start(f32[1536]{0:T(1024)} %bias_row.1) | copy-start | bytes 18436
  4.8 19.1 %collective-permute-start = (bf16[128,1536]{1,0:T(8,128)(2,1)S(1)}, bf16[128,1536]{1,0:T(8,128)(2,1)S(1)}, u32[]{:S(2)}, u32[]{:S(2)}) collective-permute-start(bf16[128,1536]{1,0:T(8,128)(2,1)S(1)} %bitcast.14), channel_id=1, source_target_pairs={{1,0},{2,1},{3,2},{4,3},{5,4},{6,5},{7,6},{8,7},{9,8},{10,9},{11,1... | collective-permute-start | bytes 1179656 | tf_op jit(solution)/shard_map/ppermute | solution.py:577
  26.5 1.9 %collective-permute-start.2 = (bf16[32,768]{1,0:T(8,128)(2,1)S(1)}, bf16[32,768]{1,0:T(8,128)(2,1)S(1)}, u32[]{:S(2)}, u32[]{:S(2)}) collective-permute-start(bf16[32,768]{1,0:T(8,128)(2,1)S(1)} %get-tuple-element.66), channel_id=1, source_target_pairs={{0,1},{1,0},{2,3},{3,2},{4,5},{5,4},{6,7},{7,6},{8,9},{9,8},{10,11... | collective-permute-start | bytes 147464 | tf_op jit(solution)/shard_map/ppermute | solution.py:559
  28.4 7.7 %collective-permute-start.4 = (bf16[32,768]{1,0:T(8,128)(2,1)S(1)}, bf16[32,768]{1,0:T(8,128)(2,1)S(1)}, u32[]{:S(2)}, u32[]{:S(2)}) collective-permute-start(bf16[32,768]{1,0:T(8,128)(2,1)S(1)} %add_convert_fusion.4), channel_id=1, source_target_pairs={{0,2},{1,3},{2,0},{3,1},{4,6},{5,7},{6,4},{7,5},{8,10},{9,11},{10,... | collective-permute-start | bytes 147464 | tf_op jit(solution)/shard_map/ppermute | solution.py:559
  30.7 10.5 %collective-permute-start.3 = (bf16[128,1536]{1,0:T(8,128)(2,1)S(1)}, bf16[128,1536]{1,0:T(8,128)(2,1)S(1)}, u32[]{:S(2)}, u32[]{:S(2)}) collective-permute-start(bf16[128,1536]{1,0:T(8,128)(2,1)S(1)} %get-tuple-element.68), channel_id=1, source_target_pairs={{0,1},{1,2},{2,3},{3,4},{4,5},{5,6},{6,7},{7,8},{8,9},{9,10},{10,1... | collective-permute-start | bytes 1179656 | tf_op jit(solution)/shard_map/ppermute | solution.py:631
  36.1 4.2 %collective-permute-start.6 = (bf16[32,768]{1,0:T(8,128)(2,1)S(1)}, bf16[32,768]{1,0:T(8,128)(2,1)S(1)}, u32[]{:S(2)}, u32[]{:S(2)}) collective-permute-start(bf16[32,768]{1,0:T(8,128)(2,1)S(1)} %add_convert_fusion.3), channel_id=1, source_target_pairs={{0,4},{1,5},{2,6},{3,7},{4,0},{5,1},{6,2},{7,3},{8,12},{9,13},{10,... | collective-permute-start | bytes 147464 | tf_op jit(solution)/shard_map/ppermute | solution.py:559
  36.4 13.2 %collective-permute-start.5 = (bf16[3,128,768]{2,1,0:T(8,128)(2,1)S(1)}, bf16[3,128,768]{2,1,0:T(8,128)(2,1)S(1)}, u32[]{:S(2)}, u32[]{:S(2)}) collective-permute-start(bf16[3,128,768]{2,1,0:T(8,128)(2,1)S(1)} %get-tuple-element.77), channel_id=1, source_target_pairs={{0,1},{1,2},{2,3},{3,4},{4,5},{5,6},{6,7},{7,8},{8,9},{9,10},{10,1... | collective-permute-start | bytes 1769480 | tf_op jit(solution)/shard_map/ppermute | solution.py:651
  41.2 15.2 %collective-permute-start.7 = (bf16[3,128,768]{2,1,0:T(8,128)(2,1)S(1)}, bf16[3,128,768]{2,1,0:T(8,128)(2,1)S(1)}, u32[]{:S(2)}, u32[]{:S(2)}) collective-permute-start(bf16[3,128,768]{2,1,0:T(8,128)(2,1)S(1)} %get-tuple-element.83), channel_id=1, source_target_pairs={{0,1},{1,2},{2,3},{3,4},{4,5},{5,6},{6,7},{7,8},{8,9},{9,10},{10,1... | collective-permute-start | bytes 1769480 | tf_op jit(solution)/shard_map/ppermute | solution.py:651
  43.1 4.3 %collective-permute-start.8 = (bf16[32,768]{1,0:T(8,128)(2,1)S(1)}, bf16[32,768]{1,0:T(8,128)(2,1)S(1)}, u32[]{:S(2)}, u32[]{:S(2)}) collective-permute-start(bf16[32,768]{1,0:T(8,128)(2,1)S(1)} %add_convert_fusion.2), channel_id=1, source_target_pairs={{0,16},{16,0},{1,17},{17,1},{2,18},{18,2},{3,19},{19,3},{4,20},{20... | collective-permute-start | bytes 147464 | tf_op jit(solution)/shard_map/ppermute | solution.py:559
  49.6 5.1 %collective-permute-start.9 = (bf16[32,768]{1,0:T(8,128)(2,1)S(1)}, bf16[32,768]{1,0:T(8,128)(2,1)S(1)}, u32[]{:S(2)}, u32[]{:S(2)}) collective-permute-start(bf16[32,768]{1,0:T(8,128)(2,1)S(1)} %add_convert_fusion.1), channel_id=1, source_target_pairs={{0,8},{1,9},{2,10},{3,11},{4,12},{5,13},{6,14},{7,15},{8,0},{9,1},... | collective-permute-start | bytes 147464 | tf_op jit(solution)/shard_map/ppermute | solution.py:559
  56.4 1.4 %collective-permute-start.10 = (bf16[32,768]{1,0:T(8,128)(2,1)S(1)}, bf16[32,768]{1,0:T(8,128)(2,1)S(1)}, u32[]{:S(2)}, u32[]{:S(2)}) collective-permute-start(bf16[32,768]{1,0:T(8,128)(2,1)S(1)} %add_convert_fusion.mine_ref), channel_id=1, source_target_pairs={{0,1},{1,0},{2,3},{3,2},{4,5},{5,4},{6,7},{7,6},{8,9},{9,8},{10,11... | collective-permute-start | bytes 147464 | tf_op jit(solution)/shard_map/ppermute | solution.py:559

commit v6 on v5

--- a/solution.py
+++ b/solution.py
@@ -140,12 +140,12 @@
     return slice(index * LANES, (index + 1) * LANES)
 
 
-def back_all(qkv_ref, prob_ref, context_ref, grad_ref, first, pairs, store):
+def back_all(q_ref, k_ref, v_ref, prob_ref, context_ref, grad_ref, first, pairs, store):
     for start in range(0, pairs, BATCH):
         attend_back(
-            lambda p: qkv_ref[0, :, lanes_at(first + p)],
-            lambda p: qkv_ref[1, :, lanes_at(first + p)],
-            lambda p: qkv_ref[2, :, lanes_at(first + p)],
+            lambda p: q_ref[:, lanes_at(first + p)],
+            lambda p: k_ref[:, lanes_at(first + p)],
+            lambda p: v_ref[:, lanes_at(first + p)],
             lambda p: prob_ref[first + p],
             lambda p: context_ref[:, lanes_at(first + p)],
             lambda p: grad_ref[:, lanes_at(first + p)],
@@ -188,35 +188,18 @@
     return block if turn == 0 else pltpu.roll(block, rows - turn, 0)
 
 
-def conv_forward(pad_ref, kernel_ref, bias_ref, mask_ref, frames, lanes):
-    taps = kernel_ref.shape[0]
+def masked_conv(pad_ref, mask_ref, weight, taps, start, lanes, keep_view=None):
+    frames = start.shape[0]
     block = pad_ref[:, lanes]
-    total = jnp.broadcast_to(bias_ref[0:1, lanes], (frames, LANES))
+    total = start
     at, view = None, None
-    for turn, start, tap in shifts(frames, taps):
+    for turn, row, tap in shifts(frames, taps):
         if turn != at:
             at, view = turn, turned(block, turn)
-        term = view[start : start + frames]
-        if mask_ref is not None:
-            term = term * mask_ref[tap * frames : (tap + 1) * frames, :]
-        total = total + kernel_ref[tap : tap + 1, lanes] * term
-    return total
-
-
-def conv_backward(pad_ref, conv_in, kernel_ref, mask_ref, frames, lanes, store):
-    taps = kernel_ref.shape[0]
-    block = pad_ref[:, lanes]
-    total = jnp.zeros((frames, LANES), F32)
-    at, view = None, None
-    for turn, start, mirror in shifts(frames, taps):
-        if turn != at:
-            at, view = turn, turned(block, turn)
-        tap = taps - 1 - mirror
-        term = view[start : start + frames]
-        if mask_ref is not None:
-            term = term * mask_ref[mirror * frames : (mirror + 1) * frames, :]
-        total = total + kernel_ref[tap : tap + 1, lanes] * term
-        store(tap, jnp.sum(conv_in * term, 0, keepdims=True))
+        term = view[row : row + frames] * mask_ref[tap * frames : (tap + 1) * frames, :]
+        if keep_view is not None:
+            keep_view(tap, term)
+        total = total + weight(tap) * term
     return total
 
 
@@ -356,51 +339,64 @@
 
 
 def own_kernel(
-    qkv_ref, cot_ref, gain_row, kernel_ref, bias_row, same_ref, keep_ref, mask_ref,
-    out_ref, back_ref, prob_ref, context_ref, sums_ref, gain_ref, bias_ref,
-    pad_ref,
+    q_ref, kv_ref, cot_ref, gain_row, kernel_ref, bias_row, same_ref, keep_ref, mask_ref,
+    out_ref, grad_ref, prob_ref, context_ref, sums_ref, gain_ref, bias_ref,
+    pad_ref, view_ref,
 ):
-    q_ref, k_ref, v_ref = (qkv_ref.at[i] for i in range(3))
     frames, width = q_ref.shape
     taps = kernel_ref.shape[0]
-    tiles = width // LANES
     clear_edges(pad_ref, frames)
+    clear_edges(grad_ref, frames)
     low = pair_masks(frames)
     gain_ref[...] = gain_row[...].reshape(1, width)
     bias_ref[...] = bias_row[...].reshape(1, width)
     bias, keep = same_ref[...], keep_ref[...]
-    forward_all(q_ref, k_ref, v_ref, prob_ref, context_ref, bias, keep, low)
+    forward_all(q_ref, kv_ref.at[0], kv_ref.at[1], prob_ref, context_ref, bias, keep, low)
     normalize_all(context_ref, gain_ref, keep, pad_ref, PAD, frames)
 
-    @pl.loop(0, tiles)
+    @pl.loop(0, width // LANES)
     def _(index):
         lanes = lanes_of(index)
-        back_ref[:, lanes] = conv_forward(pad_ref, kernel_ref, bias_ref, mask_ref, frames, lanes)
-
-    @pl.loop(0, tiles)
-    def _(index):
-        lanes = lanes_of(index)
-        pre_act = back_ref[:, lanes]
+
+        def keep_view(tap, term):
+            view_ref[tap] = term
+
+        pre_act = masked_conv(
+            pad_ref, mask_ref, lambda t: kernel_ref[t : t + 1, lanes], taps,
+            jnp.broadcast_to(bias_ref[0:1, lanes], (frames, LANES)), lanes, keep_view,
+        )
         sig = gate(pre_act)
         out_ref[:, lanes] = (pre_act * sig * keep_ref[...]).astype(BF16)
         grad_pre = gate_grad(cot_ref[:, lanes].astype(F32) * keep_ref[...], pre_act, sig)
-        conv_in = pad_ref[PAD : PAD + frames, lanes]
-        pad_ref[PAD : PAD + frames, lanes] = grad_pre
+        grad_ref[PAD : PAD + frames, lanes] = grad_pre
         sums_ref[taps : taps + 1, lanes] = jnp.sum(grad_pre, 0, keepdims=True)
-
-        def store(tap, value):
-            sums_ref[tap : tap + 1, lanes] = value
-
-        grad_in = conv_backward(pad_ref, conv_in, kernel_ref, mask_ref, frames, lanes, store)
-        back_ref[:, lanes] = grad_in
+        for tap in range(taps):
+            sums_ref[tap : tap + 1, lanes] = jnp.sum(grad_pre * view_ref[tap], 0, keepdims=True)
+
+
+def own_grad_kernel(
+    pad_ref, context_ref, mask_ref, keep_ref, gain_ref, kernel_ref, grad_ref, back_ref
+):
+    frames, width = context_ref.shape
+    taps = kernel_ref.shape[0]
+
+    @pl.loop(0, width // LANES)
+    def _(index):
+        lanes = lanes_of(index)
+        back_ref[:, lanes] = masked_conv(
+            pad_ref, mask_ref, lambda t: kernel_ref[taps - 1 - t : taps - t, lanes], taps,
+            jnp.zeros((frames, LANES), F32), lanes,
+        )
+
+    norm_backward(context_ref, back_ref, gain_ref, keep_ref[...], grad_ref, frames)
 
 
 def cross_forward_kernel(
-    qkv_ref, other_ref, seg_ref, gain_ref, kernel_ref, bias_ref, add_ref,
+    q_ref, kv_ref, qn_ref, kvn_ref, seg_ref, gain_ref, kernel_ref, bias_ref, add_ref,
     own_ref, next_ref, got_ref, prob_ref, context_ref, pre_ref, in_ref,
     out_ref,
 ):
-    frames, width = qkv_ref.shape[1:]
+    frames, width = q_ref.shape
     taps = kernel_ref.shape[0]
     tiles = width // LANES
     first, length = crossing(seg_ref, frames)
@@ -410,9 +406,10 @@
     bias = jnp.where(frame_of(shape, 1) < length, 0.0, NEG)
     keep = jnp.where(frame_of(shape, 0) < length, 1.0, 0.0)
     low = pair_masks(frames)
-    for which in range(3):
+    sources = ((q_ref, qn_ref), (kv_ref.at[0], kvn_ref.at[0]), (kv_ref.at[1], kvn_ref.at[1]))
+    for which, (own, other) in enumerate(sources):
         for cols in wide(width):
-            both = jnp.concatenate([qkv_ref[which, :, cols], other_ref[which, :, cols]], 0)
+            both = jnp.concatenate([own[:, cols], other[:, cols]], 0)
             got_ref[which, :, cols] = dot(pick, both, NN).astype(BF16)
     forward_all(*(got_ref.at[i] for i in range(3)), prob_ref, context_ref, bias, keep, low)
     normalize_all(context_ref, gain_ref, keep, in_ref, 0, frames)
@@ -487,23 +484,22 @@
     def store(which, pair, result):
         result_ref[which, :, lanes_at(pair)] = result
 
-    back_all(qkv_ref, prob_ref, context_ref, grad_ref, group * tiles, tiles, store)
+    got = [qkv_ref.at[i] for i in range(3)]
+    back_all(*got, prob_ref, context_ref, grad_ref, group * tiles, tiles, store)
     for which in range(3):
         placed = dot(place, result_ref[which], NN).astype(BF16)
         own_ref[which] = placed[:frames]
         next_ref[which] = placed[frames:]
 
 
-def own_back_kernel(
-    qkv_ref, prob_ref, context_ref, back_ref, gain_ref, keep_ref, out_ref, grad_ref
-):
-    frames, width = context_ref.shape
-    norm_backward(context_ref, back_ref, gain_ref, keep_ref[...], grad_ref, frames)
-
+def own_back_kernel(q_ref, kv_ref, prob_ref, context_ref, grad_ref, out_ref):
     def store(which, pair, result):
         out_ref[which, :, lanes_at(pair)] = result
 
-    back_all(qkv_ref, prob_ref, context_ref, grad_ref, 0, width // LANES, store)
+    back_all(
+        q_ref, kv_ref.at[0], kv_ref.at[1], prob_ref, context_ref, grad_ref,
+        0, q_ref.shape[1] // LANES, store,
+    )
 
 
 def merge_kernel(grads_ref, out_both_ref, out_came_ref, *refs):
@@ -528,7 +524,7 @@
     gain_ref[...] = gain.reshape(width)
 
 
-def call(kernel, outs, scratch, flops, *args):
+def call(kernel, outs, scratch, flops, *args, limit=24):
     size = sum(a.size * a.dtype.itemsize for a in args) + sum(o.size * o.dtype.itemsize for o in outs)
     return pl.pallas_call(
         kernel,
@@ -536,7 +532,7 @@
         in_specs=[VMEM] * len(args),
         out_specs=[VMEM] * len(outs),
         scratch_shapes=scratch,
-        compiler_params=pltpu.CompilerParams(vmem_limit_bytes=24 * 1024 * 1024),
+        compiler_params=pltpu.CompilerParams(vmem_limit_bytes=limit * 1024 * 1024),
         cost_estimate=pl.CostEstimate(flops=flops, bytes_accessed=size, transcendentals=0),
     )(*args)
 
@@ -552,7 +548,8 @@
         while step < lax.axis_size(axis):
             distances.append((axis, step))
             step *= 2
-    return steps["seq"][:-1] + steps["dp"] + steps["seq"][-1:]
+    core, x, *rest = steps["seq"]
+    return [core, x] + rest[1:] + steps["dp"] + rest[:1]
 
 
 def exchange(sent, axis, step):
@@ -565,15 +562,16 @@
 
 def per_device(queries, keys, values, segment_ids, norm_gain, conv_kernel, conv_bias, cotangent):
     frames, width = queries.shape[1:]
-    cot = cotangent[0]
+    q, cot = queries[0], cotangent[0]
     taps = conv_kernel.shape[0]
     tiles = width // LANES
     count = lax.axis_size("seq")
     to_left = [(i + 1, i) for i in range(count - 1)]
     to_right = [(i, i + 1) for i in range(count - 1)]
-    qkv = jnp.concatenate([queries[0], keys[0], values[0]], 0)
-    qkv_next = lax.ppermute(qkv, "seq", to_left).reshape(3, frames, width)
-    qkv = qkv.reshape(3, frames, width)
+    q_next = lax.ppermute(q, "seq", to_left)
+    kv = jnp.concatenate([keys[0], values[0]], 0)
+    kv_next = lax.ppermute(kv, "seq", to_left).reshape(2, frames, width)
+    kv = kv.reshape(2, frames, width)
     cot_next = lax.ppermute(cot, "seq", to_left)
 
     def sds(shape, dtype):
@@ -596,19 +594,19 @@
         10**10,
         segment_ids,
     )
-    out_own, back_own, prob_own, context_own, sums_own, gain, bias = call(
+    out_own, pre_own, prob_own, context_own, sums_own, gain, bias = call(
         own_kernel,
-        [rows16, rows32, probs, rows16, sds((taps + 1, width), F32), row, row],
-        [padded],
+        [rows16, sds((frames + 2 * PAD, width), F32), probs, rows16, sds((taps + 1, width), F32), row, row],
+        [padded, pltpu.VMEM((taps, frames, LANES), F32)],
         10**10,
-        qkv, cot, norm_gain, conv_kernel, conv_bias, same, keep, masks,
+        q, kv, cot, norm_gain, conv_kernel, conv_bias, same, keep, masks,
     )
     out_both, out_next, got, prob_cross, context_cross, pre_cross, in_cross = call(
         cross_forward_kernel,
         [rows16, rows16, three, probs, rows16, rows32, rows32],
         [pltpu.VMEM((frames, width), BF16)],
         4 * 10**9,
-        qkv, qkv_next, segment_ids, gain, conv_kernel, bias, out_own,
+        q, kv, q_next, kv_next, segment_ids, gain, conv_kernel, bias, out_own,
     )
     grad_pre, mine, other = call(
         cross_sums_kernel,
@@ -619,16 +617,9 @@
     )
     steps = sum_steps()
     came = exchange(other, *steps[0])
-    (grads_own,) = call(
-        own_back_kernel,
-        [three],
-        [pltpu.VMEM((frames, width), BF16)],
-        4 * 10**9,
-        qkv, prob_own, context_own, after(back_own, mine), gain, keep,
-    )
-    sent = added(mine, after(came, grads_own))
+    out_came = lax.ppermute(after(out_next, mine), "seq", to_right)
+    sent = added(mine, came)
     came = exchange(sent, *steps[1])
-    out_came = lax.ppermute(after(out_next, sent), "seq", to_right)
     per_group = tiles // GROUPS
     piece = sds((3, frames, per_group * LANES), BF16)
     parts = []
@@ -645,14 +636,28 @@
         if group == 0:
             (grad_cross,) = rest
         sent = added(sent, after(came, own_part))
-        if group == 1:
+        if group == 0:
             sent = after(sent, out_came)
         came = exchange(sent, *steps[group + 2])
         parts += [own_part, lax.ppermute(after(next_part, sent), "seq", to_right)]
+    (grad_own,) = call(
+        own_grad_kernel,
+        [rows16],
+        [plain],
+        4 * 10**9,
+        after(pre_own, sent), context_own, masks, keep, gain, conv_kernel,
+    )
     for step in steps[GROUPS + 2 :]:
-        sent = added(sent, after(came, parts[1]))
+        sent = added(sent, after(came, grad_own, parts[1]))
         came = exchange(sent, *step)
-    sent = added(sent, after(came, parts[3]))
+    (grads_own,) = call(
+        own_back_kernel,
+        [three],
+        [],
+        4 * 10**9,
+        q, kv, prob_own, context_own, after(grad_own, sent),
+    )
+    sent = added(sent, after(came, grads_own, parts[3]))
     came = exchange(sent, *steps[0])
     query_grad, key_grad, value_grad, conv_out = call(
         merge_kernel, [rows16] * 4, [], 10**9, grads_own, out_both, out_came, *parts,

time: 59.5 us -> 61.8 us (1.039)
  starting transfers between devices: 16.4 us -> 19.6 us
    ppermute x2, waiting for transfers between devices: 3.96 us -> 9.24 us  [per_device(): parts += [own_part, lax.ppermute(after(next_part, sent), 'seq', to_right)]]
    ppermute x6, waiting for transfers between devices: 7.71 us -> 3.09 us  [exchange(): lax.ppermute(sent, axis, [(i, i ^ step) for i in range(lax.axis_size(axis...]
    ppermute x2 -> x3, starting transfers between devices: 4.63 us -> 7.36 us  [the longest x1 2.86 us: per_device(): q_next = lax.ppermute(q, 'seq', to_left)]
    ppermute x6, starting transfers between devices: 5.15 us -> 6.32 us  [exchange(): lax.ppermute(sent, axis, [(i, i ^ step) for i in range(lax.axis_size(axis...]
    ppermute x2 -> x3, waiting for transfers between devices: 0.92 us -> 0.08 us  [the longest x1 0.07 us: per_device(): kv_next = lax.ppermute(kv, 'seq', to_left).reshape(2, frames, width)]
    ppermute x1, starting transfers between devices: 2.72 us -> 2.05 us  [per_device(): cot_next = lax.ppermute(cot, 'seq', to_left)]
    pallas_call x9 -> x10, Pallas kernels: 27.3 us -> 26.7 us  [call(): pl.pallas_call(kernel, out_shape=outs, in_specs=[VMEM] * len(args), out_s...]
  transfers between devices with their start and end apart: 11 -> 12, of which waited for: 6 -> 4; matrix products, arithmetic and copies ran while one was open for 0% -> 2% of each run, Pallas kernels for 41% -> 38%
where the time goes in v6:
time: 61.8 us; the launch traced here: 60.9 us
  Pallas kernels  26.7 us (43%)
  starting transfers between devices  19.6 us (32%)
  waiting for transfers between devices  12.4 us (20%)
  other arithmetic  1.24 us (2%)
  between operations  0.93 us (2%)
    pallas_call x10, Pallas kernels, call(): pl.pallas_call(kernel, out_shape=outs, in_specs=[VMEM] * len(args), out_s...  26.7 us
    ppermute x2, waiting for transfers between devices, per_device(): parts += [own_part, lax.ppermute(after(next_part, sent), 'seq', to_right)]  9.24 us
    ppermute x6, starting transfers between devices, exchange(): lax.ppermute(sent, axis, [(i, i ^ step) for i in range(lax.axis_size(axis...  6.32 us
    ppermute x2, starting transfers between devices, per_device(): parts += [own_part, lax.ppermute(after(next_part, sent), 'seq', to_right)]  3.83 us
    ppermute x6, waiting for transfers between devices, exchange(): lax.ppermute(sent, axis, [(i, i ^ step) for i in range(lax.axis_size(axis...  3.09 us
    ppermute x1, starting transfers between devices, per_device(): q_next = lax.ppermute(q, 'seq', to_left)  2.86 us
    ppermute x1, starting transfers between devices, per_device(): kv_next = lax.ppermute(kv, 'seq', to_left).reshape(2, frames, width)  2.58 us
    ppermute x1, starting transfers between devices, per_device(): cot_next = lax.ppermute(cot, 'seq', to_left)  2.05 us
  transfers between devices with their start and end apart: 12, of which 4 were waited for; matrix products, arithmetic and copies ran while one was open for 2% of the time, Pallas kernels for 38%

profile of v6, /device:TPU:12, one launch (start us, length us, event | category | flops | bytes accessed | tf_op | source)
XLA Modules:
  0.0 60.9 jit_solution(2637039792353928012)
XLA Ops:
  0.6 0.0 copy-start.1
  0.6 0.0 copy-start.5
  0.7 2.9 %collective-permute-start.1 = (bf16[128,1536]{1,0:T(8,128)(2,1)}, bf16[128,1536]{1,0:T(8,128)(2,1)S(1)}, u32[]{:S(2)}, u32[]{:S(2)}) collective-permute-start(bf16[128,1536]{1,0:T(8,128)(2,1)} %bitcast.17), channel_id=1, source_target_pairs={{1,0},{2,1},{3,2},{4,3},{5,4},{6,5},{7,6},{8,7},{9,8},{10,9},{11,1... | collective-permute-start | bytes 1179656 | tf_op jit(solution)/shard_map/ppermute | solution.py:571
  3.5 1.2 %pad_maximum_fusion = bf16[256,1536]{1,0:T(8,128)(2,1)S(1)} fusion(bf16[128,1536]{1,0:T(8,128)(2,1)} %bitcast.21, bf16[128,1536]{1,0:T(8,128)(2,1)} %bitcast.22), kind=kLoop, calls=%fused_computation | loop fusion | flops 1572864 | bytes 1572864 | tf_op jit(solution)/shard_map/concatenate | solution.py:572
  4.7 2.6 %collective-permute-start.2 = (bf16[256,1536]{1,0:T(8,128)(2,1)S(1)}, bf16[256,1536]{1,0:T(8,128)(2,1)S(1)}, u32[]{:S(2)}, u32[]{:S(2)}) collective-permute-start(bf16[256,1536]{1,0:T(8,128)(2,1)S(1)} %pad_maximum_fusion), channel_id=1, source_target_pairs={{1,0},{2,1},{3,2},{4,3},{5,4},{6,5},{7,6},{8,7},{9,8},{10,9},{11,1... | collective-permute-start | bytes 2359304 | tf_op jit(solution)/shard_map/ppermute | solution.py:573
  7.3 0.0 copy-done.1
  7.3 0.0 copy-start
  7.3 0.0 copy-start.2
  7.3 0.0 copy-start.3
  7.3 0.0 copy-start.4
  7.3 2.1 %collective-permute-start = (bf16[128,1536]{1,0:T(8,128)(2,1)S(1)}, bf16[128,1536]{1,0:T(8,128)(2,1)S(1)}, u32[]{:S(2)}, u32[]{:S(2)}) collective-permute-start(bf16[128,1536]{1,0:T(8,128)(2,1)S(1)} %bitcast.14), channel_id=1, source_target_pairs={{1,0},{2,1},{3,2},{4,3},{5,4},{6,5},{7,6},{8,7},{9,8},{10,9},{11,1... | collective-permute-start | bytes 1179656 | tf_op jit(solution)/shard_map/ppermute | solution.py:575
  9.4 0.0 copy-done.5
  9.4 0.3 shard_map.135
  9.7 0.0 copy-done
  9.8 0.0 copy-done.2
  9.8 0.0 copy-done.3
  9.8 0.0 copy-done.4
  9.8 7.6 %shard_map.136 = (bf16[128,1536]{1,0:T(8,128)(2,1)S(1)}, f32[160,1536]{1,0:T(8,128)S(1)}, bf16[12,128,256]{2,1,0:T(8,128)(2,1)S(1)}, bf16[128,1536]{1,0:T(8,128)...) custom-call(bf16[128,1536]{1,0:T(8,128)(2,1)S(1)} %bitcast.18, ...), custom_call_target="tpu_custom_call" | custom-call | flops 10000000000 | bytes 6703104 | tf_op jit(solution)/shard_map/pallas_call | solution.py:529
  17.3 0.0 collective-permute-done.1.qn_ref
  17.4 0.1 collective-permute-done.2
  17.4 4.4 %shard_map.137 = (bf16[128,1536]{1,0:T(8,128)(2,1)S(1)}, bf16[128,1536]{1,0:T(8,128)(2,1)S(1)}, bf16[3,128,1536]{2,1,0:T(8,128)(2,1)S(1)}, bf16[12,128,256]{2,1,...) custom-call(bf16[128,1536]{1,0:T(8,128)(2,1)S(1)} %bitcast.19, ...), custom_call_target="tpu_custom_call" | custom-call | flops 4000000000 | bytes 7682048 | tf_op jit(solution)/shard_map/pallas_call | solution.py:529
  21.9 0.0 collective-permute-done.cotn_ref
  21.9 2.5 %shard_map.138 = (f32[128,1536]{1,0:T(8,128)S(1)}, bf16[32,768]{1,0:T(8,128)(2,1)S(1)}, bf16[32,768]{1,0:T(8,128)(2,1)S(1)}) custom-call(bf16[128,1536]{1,0:T(8,128)(2,1)S(1)} %bitcast.16, bf16[128,1536]{1,0:T(8,128)(2,1)S(1)} %collective-permute-done.cotn_ref, s32[1,2048]{1,0:T(1,128)S(1)} %copy-done.5, f32[128,1536]{1,0:T(8,128)S(1)} %get-tuple-element.59.pre_ref, ...), custom_call_target="tpu_custom_call" | custom-call | flops 3000000000 | bytes 3448832 | tf_op jit(solution)/shard_map/pallas_call | solution.py:529
  24.4 1.0 %collective-permute-start.3 = (bf16[32,768]{1,0:T(8,128)(2,1)S(1)}, bf16[32,768]{1,0:T(8,128)(2,1)S(1)}, u32[]{:S(2)}, u32[]{:S(2)}) collective-permute-start(bf16[32,768]{1,0:T(8,128)(2,1)S(1)} %get-tuple-element.63), channel_id=1, source_target_pairs={{0,1},{1,0},{2,3},{3,2},{4,5},{5,4},{6,7},{7,6},{8,9},{9,8},{10,11... | collective-permute-start | bytes 147464 | tf_op jit(solution)/shard_map/ppermute | solution.py:556
  25.5 1.9 %collective-permute-start.5 = (bf16[128,1536]{1,0:T(8,128)(2,1)S(1)}, bf16[128,1536]{1,0:T(8,128)(2,1)S(1)}, u32[]{:S(2)}, u32[]{:S(2)}) collective-permute-start(bf16[128,1536]{1,0:T(8,128)(2,1)S(1)} %get-tuple-element.72), channel_id=1, source_target_pairs={{0,1},{1,2},{2,3},{3,4},{4,5},{5,6},{6,7},{7,8},{8,9},{9,10},{10,1... | collective-permute-start | bytes 1179656 | tf_op jit(solution)/shard_map/ppermute | solution.py:620
  27.4 0.0 collective-permute-done.3
  27.4 2.4 %collective-permute-start.4 = (bf16[32,768]{1,0:T(8,128)(2,1)S(1)}, bf16[32,768]{1,0:T(8,128)(2,1)S(1)}, u32[]{:S(2)}, u32[]{:S(2)}) collective-permute-start(bf16[32,768]{1,0:T(8,128)(2,1)S(1)} %add_convert_fusion.4), channel_id=1, source_target_pairs={{0,2},{1,3},{2,0},{3,1},{4,6},{5,7},{6,4},{7,5},{8,10},{9,11},{10,... | collective-permute-start | bytes 147464 | tf_op jit(solution)/shard_map/ppermute | solution.py:556
  29.8 3.5 %shard_map.139 = (bf16[3,128,768]{2,1,0:T(8,128)(2,1)S(1)}, bf16[3,128,768]{2,1,0:T(8,128)(2,1)S(1)}, bf16[128,1536]{1,0:T(8,128)(2,1)S(1)}) custom-call(bf16[3,128,1536]{2,1,0:T(8,128)(2,1)S(1)} %get-tuple-element.64.qkv_ref, bf16[12,128,256]{2,1,0:T(8,128)(2,1)S(1)} %get-tuple-element.65.prob_ref, bf16[128,1536]{1,0:T(8,128)(2,1)S(1)} %get-tuple-element.66.context_ref, ...), custom_call_target="tpu_custom_call" | custom-call | flops 5000000000 | bytes 4923392 | tf_op jit(solution)/shard_map/pallas_call | solution.py:529
  33.3 3.1 %collective-permute-done.4 = bf16[32,768]{1,0:T(8,128)(2,1)S(1)} collective-permute-done((bf16[32,768]{1,0:T(8,128)(2,1)S(1)}, bf16[32,768]{1,0:T(8,128)(2,1)S(1)}, u32[]{:S(2)}, u32[]{:S(2)}) %collective-permute-start.4) | collective-permute-done | bytes 49184 | tf_op jit(solution)/shard_map/ppermute | solution.py:556
  36.4 0.0 collective-permute-done.5.out_came_ref
  36.4 2.2 %collective-permute-start.6 = (bf16[32,768]{1,0:T(8,128)(2,1)S(1)}, bf16[32,768]{1,0:T(8,128)(2,1)S(1)}, u32[]{:S(2)}, u32[]{:S(2)}) collective-permute-start(bf16[32,768]{1,0:T(8,128)(2,1)S(1)} %add_convert_fusion.3), channel_id=1, source_target_pairs={{0,8},{1,9},{2,10},{3,11},{4,12},{5,13},{6,14},{7,15},{8,0},{9,1},... | collective-permute-start | bytes 147464 | tf_op jit(solution)/shard_map/ppermute | solution.py:556
  38.6 1.1 %shard_map.140 = (bf16[3,128,768]{2,1,0:T(8,128)(2,1)S(1)}, bf16[3,128,768]{2,1,0:T(8,128)(2,1)S(1)}) custom-call(bf16[3,128,1536]{2,1,0:T(8,128)(2,1)S(1)} %get-tuple-element.64.qkv_ref, bf16[12,128,256]{2,1,0:T(8,128)(2,1)S(1)} %get-tuple-element.65.prob_ref, bf16[128,1536]{1,0:T(8,128)(2,1)S(1)} %get-tuple-element.66.context_ref, ...), custom_call_target="tpu_custom_call" | custom-call | flops 2000000000 | bytes 3940352 | tf_op jit(solution)/shard_map/pallas_call | solution.py:529
  39.7 1.9 %collective-permute-start.8 = (bf16[3,128,768]{2,1,0:T(8,128)(2,1)S(1)}, bf16[3,128,768]{2,1,0:T(8,128)(2,1)S(1)}, u32[]{:S(2)}, u32[]{:S(2)}) collective-permute-start(bf16[3,128,768]{2,1,0:T(8,128)(2,1)S(1)} %get-tuple-element.79), channel_id=1, source_target_pairs={{0,1},{1,2},{2,3},{3,4},{4,5},{5,6},{6,7},{7,8},{8,9},{9,10},{10,1... | collective-permute-start | bytes 1769480 | tf_op jit(solution)/shard_map/ppermute | solution.py:642
  41.6 0.0 collective-permute-done.6
  41.7 0.6 collective-permute-start.7
  42.2 1.9 %collective-permute-start.9 = (bf16[3,128,768]{2,1,0:T(8,128)(2,1)S(1)}, bf16[3,128,768]{2,1,0:T(8,128)(2,1)S(1)}, u32[]{:S(2)}, u32[]{:S(2)}) collective-permute-start(bf16[3,128,768]{2,1,0:T(8,128)(2,1)S(1)} %get-tuple-element.84), channel_id=1, source_target_pairs={{0,1},{1,2},{2,3},{3,4},{4,5},{5,6},{6,7},{7,8},{8,9},{9,10},{10,1... | collective-permute-start | bytes 1769480 | tf_op jit(solution)/shard_map/ppermute | solution.py:642
  44.2 3.8 %shard_map.141.grad_ref = bf16[128,1536]{1,0:T(8,128)(2,1)S(1)} custom-call(f32[160,1536]{1,0:T(8,128)S(1)} %get-tuple-element.77.pad_ref, bf16[128,1536]{1,0:T(8,128)(2,1)S(1)} %get-tuple-element.54.context_ref, f32[3968,128]{1,0:T(8,128)S(1)} %get-tuple-element.52.mask_ref, f32[128,128]{1,0:T(8,128)S(1)} %get-tuple-element.51.keep_ref, ...), custom_call_target="tpu_custom_call" | custom-call | flops 4000000000 | bytes 4063232 | tf_op jit(solution)/shard_map/pallas_call | solution.py:529
  48.0 0.0 collective-permute-done.7
  48.0 3.8 %collective-permute-done.8.refs_1_ = bf16[3,128,768]{2,1,0:T(8,128)(2,1)S(1)} collective-permute-done((bf16[3,128,768]{2,1,0:T(8,128)(2,1)S(1)}, bf16[3,128,768]{2,1,0:T(8,128)(2,1)S(1)}, u32[]{:S(2)}, u32[]{:S(2)}) %collective-permute-start.8) | collective-permute-done | bytes 589856 | tf_op jit(solution)/shard_map/ppermute | solution.py:642
  51.8 0.1 collective-permute-start.10
  51.9 1.3 %shard_map.142.grads_ref = bf16[3,128,1536]{2,1,0:T(8,128)(2,1)S(1)} custom-call(bf16[128,1536]{1,0:T(8,128)(2,1)S(1)} %bitcast.20, bf16[2,128,1536]{2,1,0:T(8,128)(2,1)S(1)} %bitcast.12, bf16[12,128,256]{2,1,0:T(8,128)(2,1)S(1)} %get-tuple-element.53.prob_ref, bf16[128,1536]{1,0:T(8,128)(2,1)S(1)} %get-tuple-element.54.context_ref, ...), custom_call_target="tpu_custom_call" | custom-call | flops 4000000000 | bytes 3932160 | tf_op jit(solution)/shard_map/pallas_call | solution.py:529
  53.2 5.4 %collective-permute-done.9.refs_3_ = bf16[3,128,768]{2,1,0:T(8,128)(2,1)S(1)} collective-permute-done((bf16[3,128,768]{2,1,0:T(8,128)(2,1)S(1)}, bf16[3,128,768]{2,1,0:T(8,128)(2,1)S(1)}, u32[]{:S(2)}, u32[]{:S(2)}) %collective-permute-start.9) | collective-permute-done | bytes 589856 | tf_op jit(solution)/shard_map/ppermute | solution.py:642
  58.7 0.0 collective-permute-done.10
  58.7 0.1 collective-permute-start.11
  58.8 1.4 %shard_map.143 = (bf16[128,1536]{1,0:T(8,128)(2,1)}, bf16[128,1536]{1,0:T(8,128)(2,1)}, bf16[128,1536]{1,0:T(8,128)(2,1)}, bf16[128,1536]{1,0:T(8,128)(2,1)}) custom-call(bf16[3,128,1536]{2,1,0:T(8,128)(2,1)S(1)} %shard_map.142.grads_ref, bf16[128,1536]{1,0:T(8,128)(2,1)S(1)} %get-tuple-element.82.out_both_ref, ...), custom_call_target="tpu_custom_call" | custom-call | flops 1000000000 | bytes 5898240 | tf_op jit(solution)/shard_map/pallas_call | solution.py:529
  60.2 0.0 collective-permute-done.11.came_ref
  60.2 0.7 %shard_map.144 = (f32[1536]{0:T(1024)}, f32[31,1536]{1,0:T(8,128)}, f32[1536]{0:T(1024)}) custom-call(bf16[32,768]{1,0:T(8,128)(2,1)S(1)} %add_convert_fusion.mine_ref, bf16[32,768]{1,0:T(8,128)(2,1)S(1)} %collective-permute-done.11.came_ref, f32[31,1536]{1,0:T(8,128)S(1)} %copy-done, f32[1,1536]{1,0:T(1,128)S(1)} %get-tuple-element.56.gain_ref.refs_0_.norm_ref), custom_call_target="tpu_custom_call" | custom-call | flops 1000000 | bytes 497664 | tf_op jit(solution)/shard_map/pallas_call | solution.py:529
  (5 shorter events, 0.1 us)
Async XLA Ops:
  0.6 6.7 %copy-start.1 = (bf16[1,128,1536]{2,1,0:T(8,128)(2,1)S(1)}, bf16[1,128,1536]{2,1,0:T(8,128)(2,1)}, u32[]{:S(2)}) copy-start(bf16[1,128,1536]{2,1,0:T(8,128)(2,1)} %param.15) | copy-start | bytes 1179652
  0.6 8.8 %copy-start.5 = (s32[1,2048]{1,0:T(1,128)S(1)}, s32[1,2048]{1,0:T(1,128)}, u32[]{:S(2)}) copy-start(s32[1,2048]{1,0:T(1,128)} %seg_ref.9) | copy-start | bytes 24580
  0.7 16.7 %collective-permute-start.1 = (bf16[128,1536]{1,0:T(8,128)(2,1)}, bf16[128,1536]{1,0:T(8,128)(2,1)S(1)}, u32[]{:S(2)}, u32[]{:S(2)}) collective-permute-start(bf16[128,1536]{1,0:T(8,128)(2,1)} %bitcast.17), channel_id=1, source_target_pairs={{1,0},{2,1},{3,2},{4,3},{5,4},{6,5},{7,6},{8,7},{9,8},{10,9},{11,1... | collective-permute-start | bytes 1179656 | tf_op jit(solution)/shard_map/ppermute | solution.py:571
  4.7 12.7 %collective-permute-start.2 = (bf16[256,1536]{1,0:T(8,128)(2,1)S(1)}, bf16[256,1536]{1,0:T(8,128)(2,1)S(1)}, u32[]{:S(2)}, u32[]{:S(2)}) collective-permute-start(bf16[256,1536]{1,0:T(8,128)(2,1)S(1)} %pad_maximum_fusion), channel_id=1, source_target_pairs={{1,0},{2,1},{3,2},{4,3},{5,4},{6,5},{7,6},{8,7},{9,8},{10,9},{11,1... | collective-permute-start | bytes 2359304 | tf_op jit(solution)/shard_map/ppermute | solution.py:573
  7.3 2.5 %copy-start = (f32[31,1536]{1,0:T(8,128)S(1)}, f32[31,1536]{1,0:T(8,128)}, u32[]{:S(2)}) copy-start(f32[31,1536]{1,0:T(8,128)} %weight_ref.1) | copy-start | bytes 571396
  7.3 2.5 %copy-start.2 = (bf16[1,128,1536]{2,1,0:T(8,128)(2,1)S(1)}, bf16[1,128,1536]{2,1,0:T(8,128)(2,1)}, u32[]{:S(2)}) copy-start(bf16[1,128,1536]{2,1,0:T(8,128)(2,1)} %param.8) | copy-start | bytes 1179652
  7.3 2.5 %copy-start.3 = (f32[1536]{0:T(1024)S(1)}, f32[1536]{0:T(1024)}, u32[]{:S(2)}) copy-start(f32[1536]{0:T(1024)} %gain_row.1) | copy-start | bytes 18436
  7.3 2.4 %copy-start.4 = (f32[1536]{0:T(1024)S(1)}, f32[1536]{0:T(1024)}, u32[]{:S(2)}) copy-start(f32[1536]{0:T(1024)} %bias_row.1) | copy-start | bytes 18436
  7.3 14.5 %collective-permute-start = (bf16[128,1536]{1,0:T(8,128)(2,1)S(1)}, bf16[128,1536]{1,0:T(8,128)(2,1)S(1)}, u32[]{:S(2)}, u32[]{:S(2)}) collective-permute-start(bf16[128,1536]{1,0:T(8,128)(2,1)S(1)} %bitcast.14), channel_id=1, source_target_pairs={{1,0},{2,1},{3,2},{4,3},{5,4},{6,5},{7,6},{8,7},{9,8},{10,9},{11,1... | collective-permute-start | bytes 1179656 | tf_op jit(solution)/shard_map/ppermute | solution.py:575
  24.4 3.0 %collective-permute-start.3 = (bf16[32,768]{1,0:T(8,128)(2,1)S(1)}, bf16[32,768]{1,0:T(8,128)(2,1)S(1)}, u32[]{:S(2)}, u32[]{:S(2)}) collective-permute-start(bf16[32,768]{1,0:T(8,128)(2,1)S(1)} %get-tuple-element.63), channel_id=1, source_target_pairs={{0,1},{1,0},{2,3},{3,2},{4,5},{5,4},{6,7},{7,6},{8,9},{9,8},{10,11... | collective-permute-start | bytes 147464 | tf_op jit(solution)/shard_map/ppermute | solution.py:556
  25.5 11.0 %collective-permute-start.5 = (bf16[128,1536]{1,0:T(8,128)(2,1)S(1)}, bf16[128,1536]{1,0:T(8,128)(2,1)S(1)}, u32[]{:S(2)}, u32[]{:S(2)}) collective-permute-start(bf16[128,1536]{1,0:T(8,128)(2,1)S(1)} %get-tuple-element.72), channel_id=1, source_target_pairs={{0,1},{1,2},{2,3},{3,4},{4,5},{5,6},{6,7},{7,8},{8,9},{9,10},{10,1... | collective-permute-start | bytes 1179656 | tf_op jit(solution)/shard_map/ppermute | solution.py:620
  27.4 9.0 %collective-permute-start.4 = (bf16[32,768]{1,0:T(8,128)(2,1)S(1)}, bf16[32,768]{1,0:T(8,128)(2,1)S(1)}, u32[]{:S(2)}, u32[]{:S(2)}) collective-permute-start(bf16[32,768]{1,0:T(8,128)(2,1)S(1)} %add_convert_fusion.4), channel_id=1, source_target_pairs={{0,2},{1,3},{2,0},{3,1},{4,6},{5,7},{6,4},{7,5},{8,10},{9,11},{10,... | collective-permute-start | bytes 147464 | tf_op jit(solution)/shard_map/ppermute | solution.py:556
  36.4 5.2 %collective-permute-start.6 = (bf16[32,768]{1,0:T(8,128)(2,1)S(1)}, bf16[32,768]{1,0:T(8,128)(2,1)S(1)}, u32[]{:S(2)}, u32[]{:S(2)}) collective-permute-start(bf16[32,768]{1,0:T(8,128)(2,1)S(1)} %add_convert_fusion.3), channel_id=1, source_target_pairs={{0,8},{1,9},{2,10},{3,11},{4,12},{5,13},{6,14},{7,15},{8,0},{9,1},... | collective-permute-start | bytes 147464 | tf_op jit(solution)/shard_map/ppermute | solution.py:556
  39.7 12.1 %collective-permute-start.8 = (bf16[3,128,768]{2,1,0:T(8,128)(2,1)S(1)}, bf16[3,128,768]{2,1,0:T(8,128)(2,1)S(1)}, u32[]{:S(2)}, u32[]{:S(2)}) collective-permute-start(bf16[3,128,768]{2,1,0:T(8,128)(2,1)S(1)} %get-tuple-element.79), channel_id=1, source_target_pairs={{0,1},{1,2},{2,3},{3,4},{4,5},{5,6},{6,7},{7,8},{8,9},{9,10},{10,1... | collective-permute-start | bytes 1769480 | tf_op jit(solution)/shard_map/ppermute | solution.py:642
  41.7 6.3 %collective-permute-start.7 = (bf16[32,768]{1,0:T(8,128)(2,1)S(1)}, bf16[32,768]{1,0:T(8,128)(2,1)S(1)}, u32[]{:S(2)}, u32[]{:S(2)}) collective-permute-start(bf16[32,768]{1,0:T(8,128)(2,1)S(1)} %add_convert_fusion.2), channel_id=1, source_target_pairs={{0,16},{16,0},{1,17},{17,1},{2,18},{18,2},{3,19},{19,3},{4,20},{20... | collective-permute-start | bytes 147464 | tf_op jit(solution)/shard_map/ppermute | solution.py:556
  42.2 16.4 %collective-permute-start.9 = (bf16[3,128,768]{2,1,0:T(8,128)(2,1)S(1)}, bf16[3,128,768]{2,1,0:T(8,128)(2,1)S(1)}, u32[]{:S(2)}, u32[]{:S(2)}) collective-permute-start(bf16[3,128,768]{2,1,0:T(8,128)(2,1)S(1)} %get-tuple-element.84), channel_id=1, source_target_pairs={{0,1},{1,2},{2,3},{3,4},{4,5},{5,6},{6,7},{7,8},{8,9},{9,10},{10,1... | collective-permute-start | bytes 1769480 | tf_op jit(solution)/shard_map/ppermute | solution.py:642
  51.8 6.8 %collective-permute-start.10 = (bf16[32,768]{1,0:T(8,128)(2,1)S(1)}, bf16[32,768]{1,0:T(8,128)(2,1)S(1)}, u32[]{:S(2)}, u32[]{:S(2)}) collective-permute-start(bf16[32,768]{1,0:T(8,128)(2,1)S(1)} %add_convert_fusion.1), channel_id=1, source_target_pairs={{0,4},{1,5},{2,6},{3,7},{4,0},{5,1},{6,2},{7,3},{8,12},{9,13},{10,... | collective-permute-start | bytes 147464 | tf_op jit(solution)/shard_map/ppermute | solution.py:556
  58.7 1.5 %collective-permute-start.11 = (bf16[32,768]{1,0:T(8,128)(2,1)S(1)}, bf16[32,768]{1,0:T(8,128)(2,1)S(1)}, u32[]{:S(2)}, u32[]{:S(2)}) collective-permute-start(bf16[32,768]{1,0:T(8,128)(2,1)S(1)} %add_convert_fusion.mine_ref), channel_id=1, source_target_pairs={{0,1},{1,0},{2,3},{3,2},{4,5},{5,4},{6,7},{7,6},{8,9},{9,8},{10,11... | collective-permute-start | bytes 147464 | tf_op jit(solution)/shard_map/ppermute | solution.py:556

commit v7 on v6

--- a/solution.py
+++ b/solution.py
@@ -549,7 +549,7 @@
             distances.append((axis, step))
             step *= 2
     core, x, *rest = steps["seq"]
-    return [core, x] + rest[1:] + steps["dp"] + rest[:1]
+    return [core, x] + rest[::-1] + steps["dp"]
 
 
 def exchange(sent, axis, step):
@@ -615,10 +615,10 @@
         3 * 10**9,
         cot, cot_next, segment_ids, pre_cross, in_cross, sums_own,
     )
+    out_came = lax.ppermute(out_next, "seq", to_right)
     steps = sum_steps()
     came = exchange(other, *steps[0])
-    out_came = lax.ppermute(after(out_next, mine), "seq", to_right)
-    sent = added(mine, came)
+    sent = added(mine, after(came, out_came))
     came = exchange(sent, *steps[1])
     per_group = tiles // GROUPS
     piece = sds((3, frames, per_group * LANES), BF16)
@@ -636,8 +636,6 @@
         if group == 0:
             (grad_cross,) = rest
         sent = added(sent, after(came, own_part))
-        if group == 0:
-            sent = after(sent, out_came)
         came = exchange(sent, *steps[group + 2])
         parts += [own_part, lax.ppermute(after(next_part, sent), "seq", to_right)]
     (grad_own,) = call(
@@ -657,7 +655,7 @@
         4 * 10**9,
         q, kv, prob_own, context_own, after(grad_own, sent),
     )
-    sent = added(sent, after(came, grads_own, parts[3]))
+    sent = added(sent, after(came, grads_own))
     came = exchange(sent, *steps[0])
     query_grad, key_grad, value_grad, conv_out = call(
         merge_kernel, [rows16] * 4, [], 10**9, grads_own, out_both, out_came, *parts,

time: 61.8 us -> 61.9 us (level); the launches traced: 60.9 us -> 61.6 us
    ppermute x2, waiting for transfers between devices: 9.24 us -> 5.72 us  [per_device(): parts += [own_part, lax.ppermute(after(next_part, sent), 'seq', to_right)]]
    ppermute x1, waiting for transfers between devices: 0.01 us -> 3.23 us  [per_device(): out_came = lax.ppermute(out_next, 'seq', to_right)]
    ppermute x6, starting transfers between devices: 6.32 us -> 4.36 us  [exchange(): lax.ppermute(sent, axis, [(i, i ^ step) for i in range(lax.axis_size(axis...]
    ppermute x2, starting transfers between devices: 3.83 us -> 5.5 us  [per_device(): parts += [own_part, lax.ppermute(after(next_part, sent), 'seq', to_right)]]
    ppermute x1, starting transfers between devices: 1.92 us -> 2.87 us  [per_device(): out_came = lax.ppermute(out_next, 'seq', to_right)]
  transfers between devices with their start and end apart: 12 -> 12, of which waited for: 4 -> 7; matrix products, arithmetic and copies ran while one was open for 2% -> 2% of each run, Pallas kernels for 38% -> 42%
where the time goes in v7:
time: 61.9 us; the launch traced here: 61.6 us
  Pallas kernels  26.7 us (43%)
  starting transfers between devices  20.2 us (33%)
  waiting for transfers between devices  12.5 us (20%)
  other arithmetic  1.24 us (2%)
  between operations  0.91 us (1%)
    pallas_call x10, Pallas kernels, call(): pl.pallas_call(kernel, out_shape=outs, in_specs=[VMEM] * len(args), out_s...  26.7 us
    ppermute x2, waiting for transfers between devices, per_device(): parts += [own_part, lax.ppermute(after(next_part, sent), 'seq', to_right)]  5.72 us
    ppermute x2, starting transfers between devices, per_device(): parts += [own_part, lax.ppermute(after(next_part, sent), 'seq', to_right)]  5.5 us
    ppermute x6, starting transfers between devices, exchange(): lax.ppermute(sent, axis, [(i, i ^ step) for i in range(lax.axis_size(axis...  4.36 us
    ppermute x6, waiting for transfers between devices, exchange(): lax.ppermute(sent, axis, [(i, i ^ step) for i in range(lax.axis_size(axis...  3.45 us
    ppermute x1, waiting for transfers between devices, per_device(): out_came = lax.ppermute(out_next, 'seq', to_right)  3.23 us
    ppermute x1, starting transfers between devices, per_device(): out_came = lax.ppermute(out_next, 'seq', to_right)  2.87 us
    ppermute x1, starting transfers between devices, per_device(): q_next = lax.ppermute(q, 'seq', to_left)  2.86 us
  transfers between devices with their start and end apart: 12, of which 7 were waited for; matrix products, arithmetic and copies ran while one was open for 2% of the time, Pallas kernels for 42%

profile of v7, /device:TPU:12, one launch (start us, length us, event | category | flops | bytes accessed | tf_op | source)
XLA Modules:
  0.0 61.6 jit_solution(9981682119128492701)
XLA Ops:
  0.6 0.0 copy-start.1
  0.6 0.0 copy-start.5
  0.7 2.9 %collective-permute-start.1 = (bf16[128,1536]{1,0:T(8,128)(2,1)}, bf16[128,1536]{1,0:T(8,128)(2,1)S(1)}, u32[]{:S(2)}, u32[]{:S(2)}) collective-permute-start(bf16[128,1536]{1,0:T(8,128)(2,1)} %bitcast.17), channel_id=1, source_target_pairs={{1,0},{2,1},{3,2},{4,3},{5,4},{6,5},{7,6},{8,7},{9,8},{10,9},{11,1... | collective-permute-start | bytes 1179656 | tf_op jit(solution)/shard_map/ppermute | solution.py:571
  3.5 1.2 %pad_maximum_fusion = bf16[256,1536]{1,0:T(8,128)(2,1)S(1)} fusion(bf16[128,1536]{1,0:T(8,128)(2,1)} %bitcast.21, bf16[128,1536]{1,0:T(8,128)(2,1)} %bitcast.22), kind=kLoop, calls=%fused_computation | loop fusion | flops 1572864 | bytes 1572864 | tf_op jit(solution)/shard_map/concatenate | solution.py:572
  4.7 2.6 %collective-permute-start.2 = (bf16[256,1536]{1,0:T(8,128)(2,1)S(1)}, bf16[256,1536]{1,0:T(8,128)(2,1)S(1)}, u32[]{:S(2)}, u32[]{:S(2)}) collective-permute-start(bf16[256,1536]{1,0:T(8,128)(2,1)S(1)} %pad_maximum_fusion), channel_id=1, source_target_pairs={{1,0},{2,1},{3,2},{4,3},{5,4},{6,5},{7,6},{8,7},{9,8},{10,9},{11,1... | collective-permute-start | bytes 2359304 | tf_op jit(solution)/shard_map/ppermute | solution.py:573
  7.3 0.0 copy-done.1
  7.3 0.0 copy-start
  7.3 0.0 copy-start.2
  7.3 0.0 copy-start.3
  7.3 0.0 copy-start.4
  7.3 2.1 %collective-permute-start = (bf16[128,1536]{1,0:T(8,128)(2,1)S(1)}, bf16[128,1536]{1,0:T(8,128)(2,1)S(1)}, u32[]{:S(2)}, u32[]{:S(2)}) collective-permute-start(bf16[128,1536]{1,0:T(8,128)(2,1)S(1)} %bitcast.14), channel_id=1, source_target_pairs={{1,0},{2,1},{3,2},{4,3},{5,4},{6,5},{7,6},{8,7},{9,8},{10,9},{11,1... | collective-permute-start | bytes 1179656 | tf_op jit(solution)/shard_map/ppermute | solution.py:575
  9.4 0.0 copy-done.5
  9.4 0.3 shard_map.135
  9.7 0.0 copy-done
  9.8 0.0 copy-done.2
  9.8 0.0 copy-done.3
  9.8 0.0 copy-done.4
  9.8 7.6 %shard_map.136 = (bf16[128,1536]{1,0:T(8,128)(2,1)S(1)}, f32[160,1536]{1,0:T(8,128)S(1)}, bf16[12,128,256]{2,1,0:T(8,128)(2,1)S(1)}, bf16[128,1536]{1,0:T(8,128)...) custom-call(bf16[128,1536]{1,0:T(8,128)(2,1)S(1)} %bitcast.18, ...), custom_call_target="tpu_custom_call" | custom-call | flops 10000000000 | bytes 6703104 | tf_op jit(solution)/shard_map/pallas_call | solution.py:529
  17.3 0.0 collective-permute-done.1.qn_ref
  17.4 0.1 collective-permute-done.2
  17.4 4.4 %shard_map.137 = (bf16[128,1536]{1,0:T(8,128)(2,1)S(1)}, bf16[128,1536]{1,0:T(8,128)(2,1)S(1)}, bf16[3,128,1536]{2,1,0:T(8,128)(2,1)S(1)}, bf16[12,128,256]{2,1,...) custom-call(bf16[128,1536]{1,0:T(8,128)(2,1)S(1)} %bitcast.19, ...), custom_call_target="tpu_custom_call" | custom-call | flops 4000000000 | bytes 7682048 | tf_op jit(solution)/shard_map/pallas_call | solution.py:529
  21.9 2.9 %collective-permute-start.4 = (bf16[128,1536]{1,0:T(8,128)(2,1)S(1)}, bf16[128,1536]{1,0:T(8,128)(2,1)S(1)}, u32[]{:S(2)}, u32[]{:S(2)}) collective-permute-start(bf16[128,1536]{1,0:T(8,128)(2,1)S(1)} %get-tuple-element.63), channel_id=1, source_target_pairs={{0,1},{1,2},{2,3},{3,4},{4,5},{5,6},{6,7},{7,8},{8,9},{9,10},{10,1... | collective-permute-start | bytes 1179656 | tf_op jit(solution)/shard_map/ppermute | solution.py:618
  24.8 0.0 collective-permute-done.cotn_ref
  24.8 2.5 %shard_map.138 = (f32[128,1536]{1,0:T(8,128)S(1)}, bf16[32,768]{1,0:T(8,128)(2,1)S(1)}, bf16[32,768]{1,0:T(8,128)(2,1)S(1)}) custom-call(bf16[128,1536]{1,0:T(8,128)(2,1)S(1)} %bitcast.16, bf16[128,1536]{1,0:T(8,128)(2,1)S(1)} %collective-permute-done.cotn_ref, s32[1,2048]{1,0:T(1,128)S(1)} %copy-done.5, f32[128,1536]{1,0:T(8,128)S(1)} %get-tuple-element.58.pre_ref, ...), custom_call_target="tpu_custom_call" | custom-call | flops 3000000000 | bytes 3448832 | tf_op jit(solution)/shard_map/pallas_call | solution.py:529
  27.3 0.6 collective-permute-start.3
  27.9 0.9 %collective-permute-done.3 = bf16[32,768]{1,0:T(8,128)(2,1)S(1)} collective-permute-done((bf16[32,768]{1,0:T(8,128)(2,1)S(1)}, bf16[32,768]{1,0:T(8,128)(2,1)S(1)}, u32[]{:S(2)}, u32[]{:S(2)}) %collective-permute-start.3) | collective-permute-done | bytes 49184 | tf_op jit(solution)/shard_map/ppermute | solution.py:556
  28.8 3.2 %collective-permute-done.4.out_came_ref = bf16[128,1536]{1,0:T(8,128)(2,1)S(1)} collective-permute-done((bf16[128,1536]{1,0:T(8,128)(2,1)S(1)}, bf16[128,1536]{1,0:T(8,128)(2,1)S(1)}, u32[]{:S(2)}, u32[]{:S(2)}) %collective-permute-start.4) | collective-permute-done | bytes 393248 | tf_op jit(solution)/shard_map/ppermute | solution.py:618
  32.1 0.4 collective-permute-start.5
  32.4 3.5 %shard_map.139 = (bf16[3,128,768]{2,1,0:T(8,128)(2,1)S(1)}, bf16[3,128,768]{2,1,0:T(8,128)(2,1)S(1)}, bf16[128,1536]{1,0:T(8,128)(2,1)S(1)}) custom-call(bf16[3,128,1536]{2,1,0:T(8,128)(2,1)S(1)} %get-tuple-element.65.qkv_ref, bf16[12,128,256]{2,1,0:T(8,128)(2,1)S(1)} %get-tuple-element.66.prob_ref, bf16[128,1536]{1,0:T(8,128)(2,1)S(1)} %get-tuple-element.67.context_ref, ...), custom_call_target="tpu_custom_call" | custom-call | flops 5000000000 | bytes 4923392 | tf_op jit(solution)/shard_map/pallas_call | solution.py:529
  35.9 0.3 collective-permute-done.5
  36.2 2.7 %collective-permute-start.6 = (bf16[32,768]{1,0:T(8,128)(2,1)S(1)}, bf16[32,768]{1,0:T(8,128)(2,1)S(1)}, u32[]{:S(2)}, u32[]{:S(2)}) collective-permute-start(bf16[32,768]{1,0:T(8,128)(2,1)S(1)} %add_convert_fusion.3), channel_id=1, source_target_pairs={{0,8},{1,9},{2,10},{3,11},{4,12},{5,13},{6,14},{7,15},{8,0},{9,1},... | collective-permute-start | bytes 147464 | tf_op jit(solution)/shard_map/ppermute | solution.py:556
  38.9 1.1 %shard_map.140 = (bf16[3,128,768]{2,1,0:T(8,128)(2,1)S(1)}, bf16[3,128,768]{2,1,0:T(8,128)(2,1)S(1)}) custom-call(bf16[3,128,1536]{2,1,0:T(8,128)(2,1)S(1)} %get-tuple-element.65.qkv_ref, bf16[12,128,256]{2,1,0:T(8,128)(2,1)S(1)} %get-tuple-element.66.prob_ref, bf16[128,1536]{1,0:T(8,128)(2,1)S(1)} %get-tuple-element.67.context_ref, ...), custom_call_target="tpu_custom_call" | custom-call | flops 2000000000 | bytes 3940352 | tf_op jit(solution)/shard_map/pallas_call | solution.py:529
  40.0 1.9 %collective-permute-start.8 = (bf16[3,128,768]{2,1,0:T(8,128)(2,1)S(1)}, bf16[3,128,768]{2,1,0:T(8,128)(2,1)S(1)}, u32[]{:S(2)}, u32[]{:S(2)}) collective-permute-start(bf16[3,128,768]{2,1,0:T(8,128)(2,1)S(1)} %get-tuple-element.77), channel_id=1, source_target_pairs={{0,1},{1,2},{2,3},{3,4},{4,5},{5,6},{6,7},{7,8},{8,9},{9,10},{10,1... | collective-permute-start | bytes 1769480 | tf_op jit(solution)/shard_map/ppermute | solution.py:640
  42.0 0.0 collective-permute-done.6
  42.0 0.1 collective-permute-start.7
  42.1 3.6 %collective-permute-start.9 = (bf16[3,128,768]{2,1,0:T(8,128)(2,1)S(1)}, bf16[3,128,768]{2,1,0:T(8,128)(2,1)S(1)}, u32[]{:S(2)}, u32[]{:S(2)}) collective-permute-start(bf16[3,128,768]{2,1,0:T(8,128)(2,1)S(1)} %get-tuple-element.82), channel_id=1, source_target_pairs={{0,1},{1,2},{2,3},{3,4},{4,5},{5,6},{6,7},{7,8},{8,9},{9,10},{10,1... | collective-permute-start | bytes 1769480 | tf_op jit(solution)/shard_map/ppermute | solution.py:640
  45.7 3.8 %shard_map.141.grad_ref = bf16[128,1536]{1,0:T(8,128)(2,1)S(1)} custom-call(f32[160,1536]{1,0:T(8,128)S(1)} %get-tuple-element.75.pad_ref, bf16[128,1536]{1,0:T(8,128)(2,1)S(1)} %get-tuple-element.53.context_ref, f32[3968,128]{1,0:T(8,128)S(1)} %get-tuple-element.51.mask_ref, f32[128,128]{1,0:T(8,128)S(1)} %get-tuple-element.50.keep_ref, ...), custom_call_target="tpu_custom_call" | custom-call | flops 4000000000 | bytes 4063232 | tf_op jit(solution)/shard_map/pallas_call | solution.py:529
  49.5 0.0 collective-permute-done.7
  49.5 3.1 %collective-permute-done.8.refs_1_ = bf16[3,128,768]{2,1,0:T(8,128)(2,1)S(1)} collective-permute-done((bf16[3,128,768]{2,1,0:T(8,128)(2,1)S(1)}, bf16[3,128,768]{2,1,0:T(8,128)(2,1)S(1)}, u32[]{:S(2)}, u32[]{:S(2)}) %collective-permute-start.8) | collective-permute-done | bytes 589856 | tf_op jit(solution)/shard_map/ppermute | solution.py:640
  52.7 0.6 collective-permute-start.10
  53.2 1.3 %shard_map.142.grads_ref = bf16[3,128,1536]{2,1,0:T(8,128)(2,1)S(1)} custom-call(bf16[128,1536]{1,0:T(8,128)(2,1)S(1)} %bitcast.20, bf16[2,128,1536]{2,1,0:T(8,128)(2,1)S(1)} %bitcast.12, bf16[12,128,256]{2,1,0:T(8,128)(2,1)S(1)} %get-tuple-element.52.prob_ref, bf16[128,1536]{1,0:T(8,128)(2,1)S(1)} %get-tuple-element.53.context_ref, ...), custom_call_target="tpu_custom_call" | custom-call | flops 4000000000 | bytes 3932160 | tf_op jit(solution)/shard_map/pallas_call | solution.py:529
  54.6 2.3 %collective-permute-done.10 = bf16[32,768]{1,0:T(8,128)(2,1)S(1)} collective-permute-done((bf16[32,768]{1,0:T(8,128)(2,1)S(1)}, bf16[32,768]{1,0:T(8,128)(2,1)S(1)}, u32[]{:S(2)}, u32[]{:S(2)}) %collective-permute-start.10) | collective-permute-done | bytes 49184 | tf_op jit(solution)/shard_map/ppermute | solution.py:556
  56.8 0.1 collective-permute-start.11
  56.9 2.6 %collective-permute-done.9.refs_3_ = bf16[3,128,768]{2,1,0:T(8,128)(2,1)S(1)} collective-permute-done((bf16[3,128,768]{2,1,0:T(8,128)(2,1)S(1)}, bf16[3,128,768]{2,1,0:T(8,128)(2,1)S(1)}, u32[]{:S(2)}, u32[]{:S(2)}) %collective-permute-start.9) | collective-permute-done | bytes 589856 | tf_op jit(solution)/shard_map/ppermute | solution.py:640
  59.5 1.4 %shard_map.143 = (bf16[128,1536]{1,0:T(8,128)(2,1)}, bf16[128,1536]{1,0:T(8,128)(2,1)}, bf16[128,1536]{1,0:T(8,128)(2,1)}, bf16[128,1536]{1,0:T(8,128)(2,1)}) custom-call(bf16[3,128,1536]{2,1,0:T(8,128)(2,1)S(1)} %shard_map.142.grads_ref, bf16[128,1536]{1,0:T(8,128)(2,1)S(1)} %get-tuple-element.80.out_both_ref, ...), custom_call_target="tpu_custom_call" | custom-call | flops 1000000000 | bytes 5898240 | tf_op jit(solution)/shard_map/pallas_call | solution.py:529
  60.9 0.0 collective-permute-done.11.came_ref
  60.9 0.7 %shard_map.144 = (f32[1536]{0:T(1024)}, f32[31,1536]{1,0:T(8,128)}, f32[1536]{0:T(1024)}) custom-call(bf16[32,768]{1,0:T(8,128)(2,1)S(1)} %add_convert_fusion.mine_ref, bf16[32,768]{1,0:T(8,128)(2,1)S(1)} %collective-permute-done.11.came_ref, f32[31,1536]{1,0:T(8,128)S(1)} %copy-done, f32[1,1536]{1,0:T(1,128)S(1)} %get-tuple-element.55.gain_ref.refs_0_.norm_ref), custom_call_target="tpu_custom_call" | custom-call | flops 1000000 | bytes 497664 | tf_op jit(solution)/shard_map/pallas_call | solution.py:529
  (5 shorter events, 0.1 us)
Async XLA Ops:
  0.6 6.7 %copy-start.1 = (bf16[1,128,1536]{2,1,0:T(8,128)(2,1)S(1)}, bf16[1,128,1536]{2,1,0:T(8,128)(2,1)}, u32[]{:S(2)}) copy-start(bf16[1,128,1536]{2,1,0:T(8,128)(2,1)} %param.15) | copy-start | bytes 1179652
  0.6 8.8 %copy-start.5 = (s32[1,2048]{1,0:T(1,128)S(1)}, s32[1,2048]{1,0:T(1,128)}, u32[]{:S(2)}) copy-start(s32[1,2048]{1,0:T(1,128)} %seg_ref.9) | copy-start | bytes 24580
  0.7 16.7 %collective-permute-start.1 = (bf16[128,1536]{1,0:T(8,128)(2,1)}, bf16[128,1536]{1,0:T(8,128)(2,1)S(1)}, u32[]{:S(2)}, u32[]{:S(2)}) collective-permute-start(bf16[128,1536]{1,0:T(8,128)(2,1)} %bitcast.17), channel_id=1, source_target_pairs={{1,0},{2,1},{3,2},{4,3},{5,4},{6,5},{7,6},{8,7},{9,8},{10,9},{11,1... | collective-permute-start | bytes 1179656 | tf_op jit(solution)/shard_map/ppermute | solution.py:571
  4.7 12.7 %collective-permute-start.2 = (bf16[256,1536]{1,0:T(8,128)(2,1)S(1)}, bf16[256,1536]{1,0:T(8,128)(2,1)S(1)}, u32[]{:S(2)}, u32[]{:S(2)}) collective-permute-start(bf16[256,1536]{1,0:T(8,128)(2,1)S(1)} %pad_maximum_fusion), channel_id=1, source_target_pairs={{1,0},{2,1},{3,2},{4,3},{5,4},{6,5},{7,6},{8,7},{9,8},{10,9},{11,1... | collective-permute-start | bytes 2359304 | tf_op jit(solution)/shard_map/ppermute | solution.py:573
  7.3 2.5 %copy-start = (f32[31,1536]{1,0:T(8,128)S(1)}, f32[31,1536]{1,0:T(8,128)}, u32[]{:S(2)}) copy-start(f32[31,1536]{1,0:T(8,128)} %weight_ref.1) | copy-start | bytes 571396
  7.3 2.5 %copy-start.2 = (bf16[1,128,1536]{2,1,0:T(8,128)(2,1)S(1)}, bf16[1,128,1536]{2,1,0:T(8,128)(2,1)}, u32[]{:S(2)}) copy-start(bf16[1,128,1536]{2,1,0:T(8,128)(2,1)} %param.8) | copy-start | bytes 1179652
  7.3 2.5 %copy-start.3 = (f32[1536]{0:T(1024)S(1)}, f32[1536]{0:T(1024)}, u32[]{:S(2)}) copy-start(f32[1536]{0:T(1024)} %gain_row.1) | copy-start | bytes 18436
  7.3 2.4 %copy-start.4 = (f32[1536]{0:T(1024)S(1)}, f32[1536]{0:T(1024)}, u32[]{:S(2)}) copy-start(f32[1536]{0:T(1024)} %bias_row.1) | copy-start | bytes 18436
  7.3 17.4 %collective-permute-start = (bf16[128,1536]{1,0:T(8,128)(2,1)S(1)}, bf16[128,1536]{1,0:T(8,128)(2,1)S(1)}, u32[]{:S(2)}, u32[]{:S(2)}) collective-permute-start(bf16[128,1536]{1,0:T(8,128)(2,1)S(1)} %bitcast.14), channel_id=1, source_target_pairs={{1,0},{2,1},{3,2},{4,3},{5,4},{6,5},{7,6},{8,7},{9,8},{10,9},{11,1... | collective-permute-start | bytes 1179656 | tf_op jit(solution)/shard_map/ppermute | solution.py:575
  21.9 10.2 %collective-permute-start.4 = (bf16[128,1536]{1,0:T(8,128)(2,1)S(1)}, bf16[128,1536]{1,0:T(8,128)(2,1)S(1)}, u32[]{:S(2)}, u32[]{:S(2)}) collective-permute-start(bf16[128,1536]{1,0:T(8,128)(2,1)S(1)} %get-tuple-element.63), channel_id=1, source_target_pairs={{0,1},{1,2},{2,3},{3,4},{4,5},{5,6},{6,7},{7,8},{8,9},{9,10},{10,1... | collective-permute-start | bytes 1179656 | tf_op jit(solution)/shard_map/ppermute | solution.py:618
  27.3 1.5 %collective-permute-start.3 = (bf16[32,768]{1,0:T(8,128)(2,1)S(1)}, bf16[32,768]{1,0:T(8,128)(2,1)S(1)}, u32[]{:S(2)}, u32[]{:S(2)}) collective-permute-start(bf16[32,768]{1,0:T(8,128)(2,1)S(1)} %get-tuple-element.62), channel_id=1, source_target_pairs={{0,1},{1,0},{2,3},{3,2},{4,5},{5,4},{6,7},{7,6},{8,9},{9,8},{10,11... | collective-permute-start | bytes 147464 | tf_op jit(solution)/shard_map/ppermute | solution.py:556
  32.1 4.2 %collective-permute-start.5 = (bf16[32,768]{1,0:T(8,128)(2,1)S(1)}, bf16[32,768]{1,0:T(8,128)(2,1)S(1)}, u32[]{:S(2)}, u32[]{:S(2)}) collective-permute-start(bf16[32,768]{1,0:T(8,128)(2,1)S(1)} %add_convert_fusion.4), channel_id=1, source_target_pairs={{0,2},{1,3},{2,0},{3,1},{4,6},{5,7},{6,4},{7,5},{8,10},{9,11},{10,... | collective-permute-start | bytes 147464 | tf_op jit(solution)/shard_map/ppermute | solution.py:556
  36.2 5.7 %collective-permute-start.6 = (bf16[32,768]{1,0:T(8,128)(2,1)S(1)}, bf16[32,768]{1,0:T(8,128)(2,1)S(1)}, u32[]{:S(2)}, u32[]{:S(2)}) collective-permute-start(bf16[32,768]{1,0:T(8,128)(2,1)S(1)} %add_convert_fusion.3), channel_id=1, source_target_pairs={{0,8},{1,9},{2,10},{3,11},{4,12},{5,13},{6,14},{7,15},{8,0},{9,1},... | collective-permute-start | bytes 147464 | tf_op jit(solution)/shard_map/ppermute | solution.py:556
  40.0 12.6 %collective-permute-start.8 = (bf16[3,128,768]{2,1,0:T(8,128)(2,1)S(1)}, bf16[3,128,768]{2,1,0:T(8,128)(2,1)S(1)}, u32[]{:S(2)}, u32[]{:S(2)}) collective-permute-start(bf16[3,128,768]{2,1,0:T(8,128)(2,1)S(1)} %get-tuple-element.77), channel_id=1, source_target_pairs={{0,1},{1,2},{2,3},{3,4},{4,5},{5,6},{6,7},{7,8},{8,9},{9,10},{10,1... | collective-permute-start | bytes 1769480 | tf_op jit(solution)/shard_map/ppermute | solution.py:640
  42.0 7.5 %collective-permute-start.7 = (bf16[32,768]{1,0:T(8,128)(2,1)S(1)}, bf16[32,768]{1,0:T(8,128)(2,1)S(1)}, u32[]{:S(2)}, u32[]{:S(2)}) collective-permute-start(bf16[32,768]{1,0:T(8,128)(2,1)S(1)} %add_convert_fusion.2), channel_id=1, source_target_pairs={{0,4},{1,5},{2,6},{3,7},{4,0},{5,1},{6,2},{7,3},{8,12},{9,13},{10,... | collective-permute-start | bytes 147464 | tf_op jit(solution)/shard_map/ppermute | solution.py:556
  42.1 17.4 %collective-permute-start.9 = (bf16[3,128,768]{2,1,0:T(8,128)(2,1)S(1)}, bf16[3,128,768]{2,1,0:T(8,128)(2,1)S(1)}, u32[]{:S(2)}, u32[]{:S(2)}) collective-permute-start(bf16[3,128,768]{2,1,0:T(8,128)(2,1)S(1)} %get-tuple-element.82), channel_id=1, source_target_pairs={{0,1},{1,2},{2,3},{3,4},{4,5},{5,6},{6,7},{7,8},{8,9},{9,10},{10,1... | collective-permute-start | bytes 1769480 | tf_op jit(solution)/shard_map/ppermute | solution.py:640
  52.7 4.2 %collective-permute-start.10 = (bf16[32,768]{1,0:T(8,128)(2,1)S(1)}, bf16[32,768]{1,0:T(8,128)(2,1)S(1)}, u32[]{:S(2)}, u32[]{:S(2)}) collective-permute-start(bf16[32,768]{1,0:T(8,128)(2,1)S(1)} %add_convert_fusion.1), channel_id=1, source_target_pairs={{0,16},{16,0},{1,17},{17,1},{2,18},{18,2},{3,19},{19,3},{4,20},{20... | collective-permute-start | bytes 147464 | tf_op jit(solution)/shard_map/ppermute | solution.py:556
  56.8 4.0 %collective-permute-start.11 = (bf16[32,768]{1,0:T(8,128)(2,1)S(1)}, bf16[32,768]{1,0:T(8,128)(2,1)S(1)}, u32[]{:S(2)}, u32[]{:S(2)}) collective-permute-start(bf16[32,768]{1,0:T(8,128)(2,1)S(1)} %add_convert_fusion.mine_ref), channel_id=1, source_target_pairs={{0,1},{1,0},{2,3},{3,2},{4,5},{5,4},{6,7},{7,6},{8,9},{9,8},{10,11... | collective-permute-start | bytes 147464 | tf_op jit(solution)/shard_map/ppermute | solution.py:556

commit v8 on v7

--- a/solution.py
+++ b/solution.py
@@ -374,26 +374,36 @@
             sums_ref[tap : tap + 1, lanes] = jnp.sum(grad_pre * view_ref[tap], 0, keepdims=True)
 
 
-def own_grad_kernel(
-    pad_ref, context_ref, mask_ref, keep_ref, gain_ref, kernel_ref, grad_ref, back_ref
-):
-    frames, width = context_ref.shape
+def own_conv_back(pad_ref, mask_ref, kernel_ref, back_ref, first, tiles):
+    frames = back_ref.shape[0]
     taps = kernel_ref.shape[0]
 
-    @pl.loop(0, width // LANES)
+    @pl.loop(first, first + tiles)
     def _(index):
         lanes = lanes_of(index)
-        back_ref[:, lanes] = masked_conv(
+        back_ref[:, lanes_of(index)] = masked_conv(
             pad_ref, mask_ref, lambda t: kernel_ref[taps - 1 - t : taps - t, lanes], taps,
             jnp.zeros((frames, LANES), F32), lanes,
         )
 
+
+def own_half_kernel(pad_ref, mask_ref, kernel_ref, back_ref):
+    own_conv_back(pad_ref, mask_ref, kernel_ref, back_ref, 0, back_ref.shape[1] // LANES)
+
+
+def own_grad_kernel(
+    pad_ref, context_ref, mask_ref, keep_ref, gain_ref, kernel_ref, half_ref, grad_ref, back_ref
+):
+    frames, width = context_ref.shape
+    half = half_ref.shape[1]
+    back_ref[:, :half] = half_ref[...]
+    own_conv_back(pad_ref, mask_ref, kernel_ref, back_ref, half // LANES, (width - half) // LANES)
     norm_backward(context_ref, back_ref, gain_ref, keep_ref[...], grad_ref, frames)
 
 
 def cross_forward_kernel(
     q_ref, kv_ref, qn_ref, kvn_ref, seg_ref, gain_ref, kernel_ref, bias_ref, add_ref,
-    own_ref, next_ref, got_ref, prob_ref, context_ref, pre_ref, in_ref,
+    own_ref, next_ref, got_ref, prob_ref, context_ref, slope_ref, in_ref,
     out_ref,
 ):
     frames, width = q_ref.shape
@@ -419,8 +429,9 @@
         lanes = lanes_of(index)
         start = jnp.broadcast_to(bias_ref[0:1, lanes], (8, LANES))
         pre_act = phase_conv(in_ref[:, lanes], lambda t: kernel_ref[t : t + 1, lanes], taps, start)
-        pre_ref[:, lanes] = pre_act
-        out_ref[:, lanes] = (pre_act * gate(pre_act)).astype(BF16)
+        sig = gate(pre_act)
+        slope_ref[:, lanes] = sig * (1.0 + pre_act * (1.0 - sig))
+        out_ref[:, lanes] = (pre_act * sig).astype(BF16)
 
     for cols in wide(width):
         placed = dot(place, out_ref[:, cols], NN).astype(BF16)
@@ -429,7 +440,7 @@
 
 
 def cross_sums_kernel(
-    cot_ref, cotn_ref, seg_ref, pre_ref, in_ref, part_ref,
+    cot_ref, cotn_ref, seg_ref, slope_ref, in_ref, part_ref,
     grad_ref, mine_ref, other_ref,
     sums_ref,
 ):
@@ -439,8 +450,7 @@
     pick = gather_matrix(first, length, frames)
     for cols in wide(width):
         cotangent = dot(pick, jnp.concatenate([cot_ref[:, cols], cotn_ref[:, cols]], 0), NN)
-        pre_act = pre_ref[:, cols]
-        grad_ref[:, cols] = gate_grad(cotangent, pre_act, gate(pre_act))
+        grad_ref[:, cols] = (cotangent * slope_ref[:, cols]).astype(BF16).astype(F32)
 
     @pl.loop(0, width // LANES)
     def _(index):
@@ -601,7 +611,7 @@
         10**10,
         q, kv, cot, norm_gain, conv_kernel, conv_bias, same, keep, masks,
     )
-    out_both, out_next, got, prob_cross, context_cross, pre_cross, in_cross = call(
+    out_both, out_next, got, prob_cross, context_cross, slope_cross, in_cross = call(
         cross_forward_kernel,
         [rows16, rows16, three, probs, rows16, rows32, rows32],
         [pltpu.VMEM((frames, width), BF16)],
@@ -613,19 +623,29 @@
         [rows32, half_sums, half_sums],
         [pltpu.VMEM((taps + 1, width), F32)],
         3 * 10**9,
-        cot, cot_next, segment_ids, pre_cross, in_cross, sums_own,
-    )
-    out_came = lax.ppermute(out_next, "seq", to_right)
+        cot, cot_next, segment_ids, slope_cross, in_cross, sums_own,
+    )
     steps = sum_steps()
     came = exchange(other, *steps[0])
-    sent = added(mine, after(came, out_came))
+    (half_own,) = call(
+        own_half_kernel,
+        [sds((frames, width // 2), F32)],
+        [],
+        2 * 10**9,
+        after(pre_own, mine), masks, conv_kernel,
+    )
+    sent = added(mine, after(came, half_own))
     came = exchange(sent, *steps[1])
+    out_came = lax.ppermute(after(out_next, sent), "seq", to_right)
     per_group = tiles // GROUPS
     piece = sds((3, frames, per_group * LANES), BF16)
     parts = []
     grad_pre = after(grad_pre, sent)
     for group in range(GROUPS):
-        extra = [gain, conv_kernel, grad_pre] if group == 0 else [grad_cross]
+        if group == 1:
+            sent = added(sent, after(came, out_came, grad_own))
+            came = exchange(sent, *steps[3])
+        extra = [gain, conv_kernel, grad_pre] if group == 0 else [after(grad_cross, sent)]
         own_part, next_part, *rest = call(
             functools.partial(cross_back_kernel, group, per_group),
             [piece, piece] + [rows16] * (group == 0),
@@ -635,18 +655,18 @@
         )
         if group == 0:
             (grad_cross,) = rest
-        sent = added(sent, after(came, own_part))
-        came = exchange(sent, *steps[group + 2])
+            sent = added(sent, after(came, own_part))
+            came = exchange(sent, *steps[2])
+            (grad_own,) = call(
+                own_grad_kernel,
+                [rows16],
+                [plain],
+                3 * 10**9,
+                after(pre_own, sent), context_own, masks, keep, gain, conv_kernel, half_own,
+            )
         parts += [own_part, lax.ppermute(after(next_part, sent), "seq", to_right)]
-    (grad_own,) = call(
-        own_grad_kernel,
-        [rows16],
-        [plain],
-        4 * 10**9,
-        after(pre_own, sent), context_own, masks, keep, gain, conv_kernel,
-    )
     for step in steps[GROUPS + 2 :]:
-        sent = added(sent, after(came, grad_own, parts[1]))
+        sent = added(sent, came)
         came = exchange(sent, *step)
     (grads_own,) = call(
         own_back_kernel,

time: 61.9 us -> 57 us (0.921)
  waiting for transfers between devices: 12.5 us -> 7.44 us
    ppermute x1, waiting for transfers between devices: 3.23 us -> 0.01 us  [per_device(): out_came = lax.ppermute(after(out_next, sent), 'seq', to_right)]
    ppermute x2, waiting for transfers between devices: 5.72 us -> 3.23 us  [per_device(): parts += [own_part, lax.ppermute(after(next_part, sent), 'seq', to_right)]]
    ppermute x6, starting transfers between devices: 4.36 us -> 6.06 us  [exchange(): lax.ppermute(sent, axis, [(i, i ^ step) for i in range(lax.axis_size(axis...]
    ppermute x1, starting transfers between devices: 2.87 us -> 1.91 us  [per_device(): out_came = lax.ppermute(after(out_next, sent), 'seq', to_right)]
    ppermute x6, waiting for transfers between devices: 3.45 us -> 4.13 us  [exchange(): lax.ppermute(sent, axis, [(i, i ^ step) for i in range(lax.axis_size(axis...]
    pallas_call x10 -> x11, Pallas kernels: 26.7 us -> 26.6 us  [call(): pl.pallas_call(kernel, out_shape=outs, in_specs=[VMEM] * len(args), out_s...]
  transfers between devices with their start and end apart: 12 -> 12, of which waited for: 7 -> 5; matrix products, arithmetic and copies ran while one was open for 2% -> 2% of each run, Pallas kernels for 42% -> 40%
where the time goes in v8:
time: 57 us; the launch traced here: 56.7 us
  Pallas kernels  26.6 us (47%)
  starting transfers between devices  20.5 us (36%)
  waiting for transfers between devices  7.44 us (13%)
  other arithmetic  1.25 us (2%)
  between operations  0.92 us (2%)
    pallas_call x11, Pallas kernels, call(): pl.pallas_call(kernel, out_shape=outs, in_specs=[VMEM] * len(args), out_s...  26.6 us
    ppermute x6, starting transfers between devices, exchange(): lax.ppermute(sent, axis, [(i, i ^ step) for i in range(lax.axis_size(axis...  6.06 us
    ppermute x2, starting transfers between devices, per_device(): parts += [own_part, lax.ppermute(after(next_part, sent), 'seq', to_right)]  5.02 us
    ppermute x6, waiting for transfers between devices, exchange(): lax.ppermute(sent, axis, [(i, i ^ step) for i in range(lax.axis_size(axis...  4.13 us
    ppermute x2, waiting for transfers between devices, per_device(): parts += [own_part, lax.ppermute(after(next_part, sent), 'seq', to_right)]  3.23 us
    ppermute x1, starting transfers between devices, per_device(): q_next = lax.ppermute(q, 'seq', to_left)  2.86 us
    ppermute x1, starting transfers between devices, per_device(): kv_next = lax.ppermute(kv, 'seq', to_left).reshape(2, frames, width)  2.58 us
    ppermute x1, starting transfers between devices, per_device(): cot_next = lax.ppermute(cot, 'seq', to_left)  2.05 us
  transfers between devices with their start and end apart: 12, of which 5 were waited for; matrix products, arithmetic and copies ran while one was open for 2% of the time, Pallas kernels for 40%

profile of v8, /device:TPU:12, one launch (start us, length us, event | category | flops | bytes accessed | tf_op | source)
XLA Modules:
  0.0 56.7 jit_solution(5625014965203577953)
XLA Ops:
  0.6 0.0 copy-start.1
  0.6 0.0 copy-start.5
  0.7 2.9 %collective-permute-start.1 = (bf16[128,1536]{1,0:T(8,128)(2,1)}, bf16[128,1536]{1,0:T(8,128)(2,1)S(1)}, u32[]{:S(2)}, u32[]{:S(2)}) collective-permute-start(bf16[128,1536]{1,0:T(8,128)(2,1)} %bitcast.17), channel_id=1, source_target_pairs={{1,0},{2,1},{3,2},{4,3},{5,4},{6,5},{7,6},{8,7},{9,8},{10,9},{11,1... | collective-permute-start | bytes 1179656 | tf_op jit(solution)/shard_map/ppermute | solution.py:581
  3.5 1.2 %pad_maximum_fusion = bf16[256,1536]{1,0:T(8,128)(2,1)S(1)} fusion(bf16[128,1536]{1,0:T(8,128)(2,1)} %bitcast.21, bf16[128,1536]{1,0:T(8,128)(2,1)} %bitcast.22), kind=kLoop, calls=%fused_computation | loop fusion | flops 1572864 | bytes 1572864 | tf_op jit(solution)/shard_map/concatenate | solution.py:582
  4.7 2.6 %collective-permute-start.2 = (bf16[256,1536]{1,0:T(8,128)(2,1)S(1)}, bf16[256,1536]{1,0:T(8,128)(2,1)S(1)}, u32[]{:S(2)}, u32[]{:S(2)}) collective-permute-start(bf16[256,1536]{1,0:T(8,128)(2,1)S(1)} %pad_maximum_fusion), channel_id=1, source_target_pairs={{1,0},{2,1},{3,2},{4,3},{5,4},{6,5},{7,6},{8,7},{9,8},{10,9},{11,1... | collective-permute-start | bytes 2359304 | tf_op jit(solution)/shard_map/ppermute | solution.py:583
  7.3 0.0 copy-done.1
  7.3 0.0 copy-start
  7.3 0.0 copy-start.2
  7.3 0.0 copy-start.3
  7.3 0.0 copy-start.4
  7.3 2.1 %collective-permute-start = (bf16[128,1536]{1,0:T(8,128)(2,1)S(1)}, bf16[128,1536]{1,0:T(8,128)(2,1)S(1)}, u32[]{:S(2)}, u32[]{:S(2)}) collective-permute-start(bf16[128,1536]{1,0:T(8,128)(2,1)S(1)} %bitcast.14), channel_id=1, source_target_pairs={{1,0},{2,1},{3,2},{4,3},{5,4},{6,5},{7,6},{8,7},{9,8},{10,9},{11,1... | collective-permute-start | bytes 1179656 | tf_op jit(solution)/shard_map/ppermute | solution.py:585
  9.4 0.0 copy-done.5
  9.4 0.3 shard_map.135
  9.7 0.0 copy-done
  9.8 0.0 copy-done.2
  9.8 0.0 copy-done.3
  9.8 0.0 copy-done.4
  9.8 7.6 %shard_map.136 = (bf16[128,1536]{1,0:T(8,128)(2,1)S(1)}, f32[160,1536]{1,0:T(8,128)S(1)}, bf16[12,128,256]{2,1,0:T(8,128)(2,1)S(1)}, bf16[128,1536]{1,0:T(8,128)...) custom-call(bf16[128,1536]{1,0:T(8,128)(2,1)S(1)} %bitcast.18, ...), custom_call_target="tpu_custom_call" | custom-call | flops 10000000000 | bytes 6703104 | tf_op jit(solution)/shard_map/pallas_call | solution.py:539
  17.3 0.0 collective-permute-done.1.qn_ref
  17.4 0.1 collective-permute-done.2
  17.4 4.5 %shard_map.137 = (bf16[128,1536]{1,0:T(8,128)(2,1)S(1)}, bf16[128,1536]{1,0:T(8,128)(2,1)S(1)}, bf16[3,128,1536]{2,1,0:T(8,128)(2,1)S(1)}, bf16[12,128,256]{2,1,...) custom-call(bf16[128,1536]{1,0:T(8,128)(2,1)S(1)} %bitcast.19, ...), custom_call_target="tpu_custom_call" | custom-call | flops 4000000000 | bytes 7682048 | tf_op jit(solution)/shard_map/pallas_call | solution.py:539
  21.9 0.0 collective-permute-done.cotn_ref
  21.9 2.4 %shard_map.138 = (f32[128,1536]{1,0:T(8,128)S(1)}, bf16[32,768]{1,0:T(8,128)(2,1)S(1)}, bf16[32,768]{1,0:T(8,128)(2,1)S(1)}) custom-call(bf16[128,1536]{1,0:T(8,128)(2,1)S(1)} %bitcast.16, bf16[128,1536]{1,0:T(8,128)(2,1)S(1)} %collective-permute-done.cotn_ref, s32[1,2048]{1,0:T(1,128)S(1)} %copy-done.5, f32[128,1536]{1,0:T(8,128)S(1)} %get-tuple-element.60.slope_ref, ...), custom_call_target="tpu_custom_call" | custom-call | flops 3000000000 | bytes 3448832 | tf_op jit(solution)/shard_map/pallas_call | solution.py:539
  24.3 1.0 %collective-permute-start.3 = (bf16[32,768]{1,0:T(8,128)(2,1)S(1)}, bf16[32,768]{1,0:T(8,128)(2,1)S(1)}, u32[]{:S(2)}, u32[]{:S(2)}) collective-permute-start(bf16[32,768]{1,0:T(8,128)(2,1)S(1)} %get-tuple-element.64), channel_id=1, source_target_pairs={{0,1},{1,0},{2,3},{3,2},{4,5},{5,4},{6,7},{7,6},{8,9},{9,8},{10,11... | collective-permute-start | bytes 147464 | tf_op jit(solution)/shard_map/ppermute | solution.py:566
  25.4 1.7 %shard_map.139.half_ref = f32[128,768]{1,0:T(8,128)S(1)} custom-call(f32[160,1536]{1,0:T(8,128)S(1)} %get-tuple-element.74.pad_ref, f32[3968,128]{1,0:T(8,128)S(1)} %get-tuple-element.53.mask_ref, f32[31,1536]{1,0:T(8,128)S(1)} %copy-done), custom_call_target="tpu_custom_call" | custom-call | flops 2000000000 | bytes 3598336 | tf_op jit(solution)/shard_map/pallas_call | solution.py:539
  27.0 0.0 collective-permute-done.3
  27.1 2.4 %collective-permute-start.4 = (bf16[32,768]{1,0:T(8,128)(2,1)S(1)}, bf16[32,768]{1,0:T(8,128)(2,1)S(1)}, u32[]{:S(2)}, u32[]{:S(2)}) collective-permute-start(bf16[32,768]{1,0:T(8,128)(2,1)S(1)} %add_convert_fusion.4), channel_id=1, source_target_pairs={{0,2},{1,3},{2,0},{3,1},{4,6},{5,7},{6,4},{7,5},{8,10},{9,11},{10,... | collective-permute-start | bytes 147464 | tf_op jit(solution)/shard_map/ppermute | solution.py:566
  29.5 1.9 %collective-permute-start.6 = (bf16[128,1536]{1,0:T(8,128)(2,1)S(1)}, bf16[128,1536]{1,0:T(8,128)(2,1)S(1)}, u32[]{:S(2)}, u32[]{:S(2)}) collective-permute-start(bf16[128,1536]{1,0:T(8,128)(2,1)S(1)} %get-tuple-element.76), channel_id=1, source_target_pairs={{0,1},{1,2},{2,3},{3,4},{4,5},{5,6},{6,7},{7,8},{8,9},{9,10},{10,1... | collective-permute-start | bytes 1179656 | tf_op jit(solution)/shard_map/ppermute | solution.py:639
  31.4 3.5 %shard_map.140 = (bf16[3,128,768]{2,1,0:T(8,128)(2,1)S(1)}, bf16[3,128,768]{2,1,0:T(8,128)(2,1)S(1)}, bf16[128,1536]{1,0:T(8,128)(2,1)S(1)}) custom-call(bf16[3,128,1536]{2,1,0:T(8,128)(2,1)S(1)} %get-tuple-element.67.qkv_ref, bf16[12,128,256]{2,1,0:T(8,128)(2,1)S(1)} %get-tuple-element.68.prob_ref, bf16[128,1536]{1,0:T(8,128)(2,1)S(1)} %get-tuple-element.69.context_ref, ...), custom_call_target="tpu_custom_call" | custom-call | flops 5000000000 | bytes 4923392 | tf_op jit(solution)/shard_map/pallas_call | solution.py:539
  34.9 0.0 collective-permute-done.4
  34.9 0.9 %collective-permute-start.5 = (bf16[32,768]{1,0:T(8,128)(2,1)S(1)}, bf16[32,768]{1,0:T(8,128)(2,1)S(1)}, u32[]{:S(2)}, u32[]{:S(2)}) collective-permute-start(bf16[32,768]{1,0:T(8,128)(2,1)S(1)} %add_convert_fusion.3), channel_id=1, source_target_pairs={{0,8},{1,9},{2,10},{3,11},{4,12},{5,13},{6,14},{7,15},{8,0},{9,1},... | collective-permute-start | bytes 147464 | tf_op jit(solution)/shard_map/ppermute | solution.py:566
  35.9 3.1 %collective-permute-start.8 = (bf16[3,128,768]{2,1,0:T(8,128)(2,1)S(1)}, bf16[3,128,768]{2,1,0:T(8,128)(2,1)S(1)}, u32[]{:S(2)}, u32[]{:S(2)}) collective-permute-start(bf16[3,128,768]{2,1,0:T(8,128)(2,1)S(1)} %get-tuple-element.81), channel_id=1, source_target_pairs={{0,1},{1,2},{2,3},{3,4},{4,5},{5,6},{6,7},{7,8},{8,9},{9,10},{10,1... | collective-permute-start | bytes 1769480 | tf_op jit(solution)/shard_map/ppermute | solution.py:667
  39.0 2.2 %shard_map.141.grad_ref = bf16[128,1536]{1,0:T(8,128)(2,1)S(1)} custom-call(f32[160,1536]{1,0:T(8,128)S(1)} %get-tuple-element.74.pad_ref, bf16[128,1536]{1,0:T(8,128)(2,1)S(1)} %get-tuple-element.55.context_ref, f32[3968,128]{1,0:T(8,128)S(1)} %get-tuple-element.53.mask_ref, f32[128,128]{1,0:T(8,128)S(1)} %get-tuple-element.52.keep_ref, ...), custom_call_target="tpu_custom_call" | custom-call | flops 3000000000 | bytes 4456448 | tf_op jit(solution)/shard_map/pallas_call | solution.py:539
  41.2 0.0 collective-permute-done.5
  41.2 0.0 collective-permute-done.6.out_came_ref
  41.2 0.9 %collective-permute-start.7 = (bf16[32,768]{1,0:T(8,128)(2,1)S(1)}, bf16[32,768]{1,0:T(8,128)(2,1)S(1)}, u32[]{:S(2)}, u32[]{:S(2)}) collective-permute-start(bf16[32,768]{1,0:T(8,128)(2,1)S(1)} %add_convert_fusion.2), channel_id=1, source_target_pairs={{0,4},{1,5},{2,6},{3,7},{4,0},{5,1},{6,2},{7,3},{8,12},{9,13},{10,... | collective-permute-start | bytes 147464 | tf_op jit(solution)/shard_map/ppermute | solution.py:566
  42.1 1.1 %shard_map.143 = (bf16[3,128,768]{2,1,0:T(8,128)(2,1)S(1)}, bf16[3,128,768]{2,1,0:T(8,128)(2,1)S(1)}) custom-call(bf16[3,128,1536]{2,1,0:T(8,128)(2,1)S(1)} %get-tuple-element.67.qkv_ref, bf16[12,128,256]{2,1,0:T(8,128)(2,1)S(1)} %get-tuple-element.68.prob_ref, bf16[128,1536]{1,0:T(8,128)(2,1)S(1)} %get-tuple-element.69.context_ref, ...), custom_call_target="tpu_custom_call" | custom-call | flops 2000000000 | bytes 3940352 | tf_op jit(solution)/shard_map/pallas_call | solution.py:539
  43.2 1.9 %collective-permute-start.9 = (bf16[3,128,768]{2,1,0:T(8,128)(2,1)S(1)}, bf16[3,128,768]{2,1,0:T(8,128)(2,1)S(1)}, u32[]{:S(2)}, u32[]{:S(2)}) collective-permute-start(bf16[3,128,768]{2,1,0:T(8,128)(2,1)S(1)} %get-tuple-element.86), channel_id=1, source_target_pairs={{0,1},{1,2},{2,3},{3,4},{4,5},{5,6},{6,7},{7,8},{8,9},{9,10},{10,1... | collective-permute-start | bytes 1769480 | tf_op jit(solution)/shard_map/ppermute | solution.py:667
  45.2 0.2 collective-permute-done.7
  45.4 0.6 %collective-permute-start.10 = (bf16[32,768]{1,0:T(8,128)(2,1)S(1)}, bf16[32,768]{1,0:T(8,128)(2,1)S(1)}, u32[]{:S(2)}, u32[]{:S(2)}) collective-permute-start(bf16[32,768]{1,0:T(8,128)(2,1)S(1)} %add_convert_fusion.1), channel_id=1, source_target_pairs={{0,16},{16,0},{1,17},{17,1},{2,18},{18,2},{3,19},{19,3},{4,20},{20... | collective-permute-start | bytes 147464 | tf_op jit(solution)/shard_map/ppermute | solution.py:566
  46.0 1.3 %shard_map.142.grads_ref = bf16[3,128,1536]{2,1,0:T(8,128)(2,1)S(1)} custom-call(bf16[128,1536]{1,0:T(8,128)(2,1)S(1)} %bitcast.20, bf16[2,128,1536]{2,1,0:T(8,128)(2,1)S(1)} %bitcast.12, bf16[12,128,256]{2,1,0:T(8,128)(2,1)S(1)} %get-tuple-element.54.prob_ref, bf16[128,1536]{1,0:T(8,128)(2,1)S(1)} %get-tuple-element.55.context_ref, ...), custom_call_target="tpu_custom_call" | custom-call | flops 4000000000 | bytes 3932160 | tf_op jit(solution)/shard_map/pallas_call | solution.py:539
  47.3 2.8 %collective-permute-done.10 = bf16[32,768]{1,0:T(8,128)(2,1)S(1)} collective-permute-done((bf16[32,768]{1,0:T(8,128)(2,1)S(1)}, bf16[32,768]{1,0:T(8,128)(2,1)S(1)}, u32[]{:S(2)}, u32[]{:S(2)}) %collective-permute-start.10) | collective-permute-done | bytes 49184 | tf_op jit(solution)/shard_map/ppermute | solution.py:566
  50.1 0.2 collective-permute-start.11
  50.3 1.1 %collective-permute-done.11.came_ref = bf16[32,768]{1,0:T(8,128)(2,1)S(1)} collective-permute-done((bf16[32,768]{1,0:T(8,128)(2,1)S(1)}, bf16[32,768]{1,0:T(8,128)(2,1)S(1)}, u32[]{:S(2)}, u32[]{:S(2)}) %collective-permute-start.11) | collective-permute-done | bytes 49184 | tf_op jit(solution)/shard_map/ppermute | solution.py:566
  51.4 0.7 %shard_map.145 = (f32[1536]{0:T(1024)}, f32[31,1536]{1,0:T(8,128)}, f32[1536]{0:T(1024)}) custom-call(bf16[32,768]{1,0:T(8,128)(2,1)S(1)} %add_convert_fusion.mine_ref, bf16[32,768]{1,0:T(8,128)(2,1)S(1)} %collective-permute-done.11.came_ref, f32[31,1536]{1,0:T(8,128)S(1)} %copy-done, f32[1,1536]{1,0:T(1,128)S(1)} %get-tuple-element.57.gain_ref.refs_0_.norm_ref), custom_call_target="tpu_custom_call" | custom-call | flops 1000000 | bytes 497664 | tf_op jit(solution)/shard_map/pallas_call | solution.py:539
  52.1 0.0 collective-permute-done.8.refs_1_
  52.1 3.2 %collective-permute-done.9.refs_3_ = bf16[3,128,768]{2,1,0:T(8,128)(2,1)S(1)} collective-permute-done((bf16[3,128,768]{2,1,0:T(8,128)(2,1)S(1)}, bf16[3,128,768]{2,1,0:T(8,128)(2,1)S(1)}, u32[]{:S(2)}, u32[]{:S(2)}) %collective-permute-start.9) | collective-permute-done | bytes 589856 | tf_op jit(solution)/shard_map/ppermute | solution.py:667
  55.3 1.3 %shard_map.144 = (bf16[128,1536]{1,0:T(8,128)(2,1)}, bf16[128,1536]{1,0:T(8,128)(2,1)}, bf16[128,1536]{1,0:T(8,128)(2,1)}, bf16[128,1536]{1,0:T(8,128)(2,1)}) custom-call(bf16[3,128,1536]{2,1,0:T(8,128)(2,1)S(1)} %shard_map.142.grads_ref, bf16[128,1536]{1,0:T(8,128)(2,1)S(1)} %get-tuple-element.79.out_both_ref, ...), custom_call_target="tpu_custom_call" | custom-call | flops 1000000000 | bytes 5898240 | tf_op jit(solution)/shard_map/pallas_call | solution.py:539
  (5 shorter events, 0.1 us)
Async XLA Ops:
  0.6 6.7 %copy-start.1 = (bf16[1,128,1536]{2,1,0:T(8,128)(2,1)S(1)}, bf16[1,128,1536]{2,1,0:T(8,128)(2,1)}, u32[]{:S(2)}) copy-start(bf16[1,128,1536]{2,1,0:T(8,128)(2,1)} %param.15) | copy-start | bytes 1179652
  0.6 8.8 %copy-start.5 = (s32[1,2048]{1,0:T(1,128)S(1)}, s32[1,2048]{1,0:T(1,128)}, u32[]{:S(2)}) copy-start(s32[1,2048]{1,0:T(1,128)} %seg_ref.9) | copy-start | bytes 24580
  0.7 16.7 %collective-permute-start.1 = (bf16[128,1536]{1,0:T(8,128)(2,1)}, bf16[128,1536]{1,0:T(8,128)(2,1)S(1)}, u32[]{:S(2)}, u32[]{:S(2)}) collective-permute-start(bf16[128,1536]{1,0:T(8,128)(2,1)} %bitcast.17), channel_id=1, source_target_pairs={{1,0},{2,1},{3,2},{4,3},{5,4},{6,5},{7,6},{8,7},{9,8},{10,9},{11,1... | collective-permute-start | bytes 1179656 | tf_op jit(solution)/shard_map/ppermute | solution.py:581
  4.7 12.7 %collective-permute-start.2 = (bf16[256,1536]{1,0:T(8,128)(2,1)S(1)}, bf16[256,1536]{1,0:T(8,128)(2,1)S(1)}, u32[]{:S(2)}, u32[]{:S(2)}) collective-permute-start(bf16[256,1536]{1,0:T(8,128)(2,1)S(1)} %pad_maximum_fusion), channel_id=1, source_target_pairs={{1,0},{2,1},{3,2},{4,3},{5,4},{6,5},{7,6},{8,7},{9,8},{10,9},{11,1... | collective-permute-start | bytes 2359304 | tf_op jit(solution)/shard_map/ppermute | solution.py:583
  7.3 2.5 %copy-start = (f32[31,1536]{1,0:T(8,128)S(1)}, f32[31,1536]{1,0:T(8,128)}, u32[]{:S(2)}) copy-start(f32[31,1536]{1,0:T(8,128)} %weight_ref.1) | copy-start | bytes 571396
  7.3 2.5 %copy-start.2 = (bf16[1,128,1536]{2,1,0:T(8,128)(2,1)S(1)}, bf16[1,128,1536]{2,1,0:T(8,128)(2,1)}, u32[]{:S(2)}) copy-start(bf16[1,128,1536]{2,1,0:T(8,128)(2,1)} %param.8) | copy-start | bytes 1179652
  7.3 2.5 %copy-start.3 = (f32[1536]{0:T(1024)S(1)}, f32[1536]{0:T(1024)}, u32[]{:S(2)}) copy-start(f32[1536]{0:T(1024)} %gain_row.1) | copy-start | bytes 18436
  7.3 2.4 %copy-start.4 = (f32[1536]{0:T(1024)S(1)}, f32[1536]{0:T(1024)}, u32[]{:S(2)}) copy-start(f32[1536]{0:T(1024)} %bias_row.1) | copy-start | bytes 18436
  7.3 14.6 %collective-permute-start = (bf16[128,1536]{1,0:T(8,128)(2,1)S(1)}, bf16[128,1536]{1,0:T(8,128)(2,1)S(1)}, u32[]{:S(2)}, u32[]{:S(2)}) collective-permute-start(bf16[128,1536]{1,0:T(8,128)(2,1)S(1)} %bitcast.14), channel_id=1, source_target_pairs={{1,0},{2,1},{3,2},{4,3},{5,4},{6,5},{7,6},{8,7},{9,8},{10,9},{11,1... | collective-permute-start | bytes 1179656 | tf_op jit(solution)/shard_map/ppermute | solution.py:585
  24.3 2.7 %collective-permute-start.3 = (bf16[32,768]{1,0:T(8,128)(2,1)S(1)}, bf16[32,768]{1,0:T(8,128)(2,1)S(1)}, u32[]{:S(2)}, u32[]{:S(2)}) collective-permute-start(bf16[32,768]{1,0:T(8,128)(2,1)S(1)} %get-tuple-element.64), channel_id=1, source_target_pairs={{0,1},{1,0},{2,3},{3,2},{4,5},{5,4},{6,7},{7,6},{8,9},{9,8},{10,11... | collective-permute-start | bytes 147464 | tf_op jit(solution)/shard_map/ppermute | solution.py:566
  27.1 7.8 %collective-permute-start.4 = (bf16[32,768]{1,0:T(8,128)(2,1)S(1)}, bf16[32,768]{1,0:T(8,128)(2,1)S(1)}, u32[]{:S(2)}, u32[]{:S(2)}) collective-permute-start(bf16[32,768]{1,0:T(8,128)(2,1)S(1)} %add_convert_fusion.4), channel_id=1, source_target_pairs={{0,2},{1,3},{2,0},{3,1},{4,6},{5,7},{6,4},{7,5},{8,10},{9,11},{10,... | collective-permute-start | bytes 147464 | tf_op jit(solution)/shard_map/ppermute | solution.py:566
  29.5 11.7 %collective-permute-start.6 = (bf16[128,1536]{1,0:T(8,128)(2,1)S(1)}, bf16[128,1536]{1,0:T(8,128)(2,1)S(1)}, u32[]{:S(2)}, u32[]{:S(2)}) collective-permute-start(bf16[128,1536]{1,0:T(8,128)(2,1)S(1)} %get-tuple-element.76), channel_id=1, source_target_pairs={{0,1},{1,2},{2,3},{3,4},{4,5},{5,6},{6,7},{7,8},{8,9},{9,10},{10,1... | collective-permute-start | bytes 1179656 | tf_op jit(solution)/shard_map/ppermute | solution.py:639
  34.9 6.3 %collective-permute-start.5 = (bf16[32,768]{1,0:T(8,128)(2,1)S(1)}, bf16[32,768]{1,0:T(8,128)(2,1)S(1)}, u32[]{:S(2)}, u32[]{:S(2)}) collective-permute-start(bf16[32,768]{1,0:T(8,128)(2,1)S(1)} %add_convert_fusion.3), channel_id=1, source_target_pairs={{0,8},{1,9},{2,10},{3,11},{4,12},{5,13},{6,14},{7,15},{8,0},{9,1},... | collective-permute-start | bytes 147464 | tf_op jit(solution)/shard_map/ppermute | solution.py:566
  35.9 16.2 %collective-permute-start.8 = (bf16[3,128,768]{2,1,0:T(8,128)(2,1)S(1)}, bf16[3,128,768]{2,1,0:T(8,128)(2,1)S(1)}, u32[]{:S(2)}, u32[]{:S(2)}) collective-permute-start(bf16[3,128,768]{2,1,0:T(8,128)(2,1)S(1)} %get-tuple-element.81), channel_id=1, source_target_pairs={{0,1},{1,2},{2,3},{3,4},{4,5},{5,6},{6,7},{7,8},{8,9},{9,10},{10,1... | collective-permute-start | bytes 1769480 | tf_op jit(solution)/shard_map/ppermute | solution.py:667
  41.2 4.2 %collective-permute-start.7 = (bf16[32,768]{1,0:T(8,128)(2,1)S(1)}, bf16[32,768]{1,0:T(8,128)(2,1)S(1)}, u32[]{:S(2)}, u32[]{:S(2)}) collective-permute-start(bf16[32,768]{1,0:T(8,128)(2,1)S(1)} %add_convert_fusion.2), channel_id=1, source_target_pairs={{0,4},{1,5},{2,6},{3,7},{4,0},{5,1},{6,2},{7,3},{8,12},{9,13},{10,... | collective-permute-start | bytes 147464 | tf_op jit(solution)/shard_map/ppermute | solution.py:566
  43.2 12.1 %collective-permute-start.9 = (bf16[3,128,768]{2,1,0:T(8,128)(2,1)S(1)}, bf16[3,128,768]{2,1,0:T(8,128)(2,1)S(1)}, u32[]{:S(2)}, u32[]{:S(2)}) collective-permute-start(bf16[3,128,768]{2,1,0:T(8,128)(2,1)S(1)} %get-tuple-element.86), channel_id=1, source_target_pairs={{0,1},{1,2},{2,3},{3,4},{4,5},{5,6},{6,7},{7,8},{8,9},{9,10},{10,1... | collective-permute-start | bytes 1769480 | tf_op jit(solution)/shard_map/ppermute | solution.py:667
  45.4 4.7 %collective-permute-start.10 = (bf16[32,768]{1,0:T(8,128)(2,1)S(1)}, bf16[32,768]{1,0:T(8,128)(2,1)S(1)}, u32[]{:S(2)}, u32[]{:S(2)}) collective-permute-start(bf16[32,768]{1,0:T(8,128)(2,1)S(1)} %add_convert_fusion.1), channel_id=1, source_target_pairs={{0,16},{16,0},{1,17},{17,1},{2,18},{18,2},{3,19},{19,3},{4,20},{20... | collective-permute-start | bytes 147464 | tf_op jit(solution)/shard_map/ppermute | solution.py:566
  50.1 1.3 %collective-permute-start.11 = (bf16[32,768]{1,0:T(8,128)(2,1)S(1)}, bf16[32,768]{1,0:T(8,128)(2,1)S(1)}, u32[]{:S(2)}, u32[]{:S(2)}) collective-permute-start(bf16[32,768]{1,0:T(8,128)(2,1)S(1)} %add_convert_fusion.mine_ref), channel_id=1, source_target_pairs={{0,1},{1,0},{2,3},{3,2},{4,5},{5,4},{6,7},{7,6},{8,9},{9,8},{10,11... | collective-permute-start | bytes 147464 | tf_op jit(solution)/shard_map/ppermute | solution.py:566

commit v9 on v8

--- a/solution.py
+++ b/solution.py
@@ -339,11 +339,11 @@
 
 
 def own_kernel(
-    q_ref, kv_ref, cot_ref, gain_row, kernel_ref, bias_row, same_ref, keep_ref, mask_ref,
+    qkv_ref, cot_ref, gain_row, kernel_ref, bias_row, same_ref, keep_ref, mask_ref,
     out_ref, grad_ref, prob_ref, context_ref, sums_ref, gain_ref, bias_ref,
     pad_ref, view_ref,
 ):
-    frames, width = q_ref.shape
+    frames, width = cot_ref.shape
     taps = kernel_ref.shape[0]
     clear_edges(pad_ref, frames)
     clear_edges(grad_ref, frames)
@@ -351,7 +351,7 @@
     gain_ref[...] = gain_row[...].reshape(1, width)
     bias_ref[...] = bias_row[...].reshape(1, width)
     bias, keep = same_ref[...], keep_ref[...]
-    forward_all(q_ref, kv_ref.at[0], kv_ref.at[1], prob_ref, context_ref, bias, keep, low)
+    forward_all(qkv_ref.at[0], qkv_ref.at[1], qkv_ref.at[2], prob_ref, context_ref, bias, keep, low)
     normalize_all(context_ref, gain_ref, keep, pad_ref, PAD, frames)
 
     @pl.loop(0, width // LANES)
@@ -402,24 +402,21 @@
 
 
 def cross_forward_kernel(
-    q_ref, kv_ref, qn_ref, kvn_ref, seg_ref, gain_ref, kernel_ref, bias_ref, add_ref,
-    own_ref, next_ref, got_ref, prob_ref, context_ref, slope_ref, in_ref,
-    out_ref,
+    qkv_ref, other_ref, seg_ref, gain_ref, kernel_ref, bias_ref,
+    out_ref, got_ref, prob_ref, context_ref, slope_ref, in_ref,
 ):
-    frames, width = q_ref.shape
+    frames, width = qkv_ref.shape[1:]
     taps = kernel_ref.shape[0]
     tiles = width // LANES
     first, length = crossing(seg_ref, frames)
     pick = gather_matrix(first, length, frames)
-    place = scatter_matrix(first, length, frames)
     shape = (frames, frames)
     bias = jnp.where(frame_of(shape, 1) < length, 0.0, NEG)
     keep = jnp.where(frame_of(shape, 0) < length, 1.0, 0.0)
     low = pair_masks(frames)
-    sources = ((q_ref, qn_ref), (kv_ref.at[0], kvn_ref.at[0]), (kv_ref.at[1], kvn_ref.at[1]))
-    for which, (own, other) in enumerate(sources):
+    for which in range(3):
         for cols in wide(width):
-            both = jnp.concatenate([own[:, cols], other[:, cols]], 0)
+            both = jnp.concatenate([qkv_ref[which, :, cols], other_ref[which, :, cols]], 0)
             got_ref[which, :, cols] = dot(pick, both, NN).astype(BF16)
     forward_all(*(got_ref.at[i] for i in range(3)), prob_ref, context_ref, bias, keep, low)
     normalize_all(context_ref, gain_ref, keep, in_ref, 0, frames)
@@ -433,6 +430,10 @@
         slope_ref[:, lanes] = sig * (1.0 + pre_act * (1.0 - sig))
         out_ref[:, lanes] = (pre_act * sig).astype(BF16)
 
+
+def cross_place_kernel(out_ref, add_ref, seg_ref, own_ref, next_ref):
+    frames, width = out_ref.shape
+    place = scatter_matrix(*crossing(seg_ref, frames), frames)
     for cols in wide(width):
         placed = dot(place, out_ref[:, cols], NN).astype(BF16)
         own_ref[:, cols] = placed[:frames] + add_ref[:, cols]
@@ -502,13 +503,13 @@
         next_ref[which] = placed[frames:]
 
 
-def own_back_kernel(q_ref, kv_ref, prob_ref, context_ref, grad_ref, out_ref):
+def own_back_kernel(qkv_ref, prob_ref, context_ref, grad_ref, out_ref):
     def store(which, pair, result):
         out_ref[which, :, lanes_at(pair)] = result
 
     back_all(
-        q_ref, kv_ref.at[0], kv_ref.at[1], prob_ref, context_ref, grad_ref,
-        0, q_ref.shape[1] // LANES, store,
+        qkv_ref.at[0], qkv_ref.at[1], qkv_ref.at[2], prob_ref, context_ref, grad_ref,
+        0, context_ref.shape[1] // LANES, store,
     )
 
 
@@ -572,16 +573,15 @@
 
 def per_device(queries, keys, values, segment_ids, norm_gain, conv_kernel, conv_bias, cotangent):
     frames, width = queries.shape[1:]
-    q, cot = queries[0], cotangent[0]
+    cot = cotangent[0]
     taps = conv_kernel.shape[0]
     tiles = width // LANES
     count = lax.axis_size("seq")
     to_left = [(i + 1, i) for i in range(count - 1)]
     to_right = [(i, i + 1) for i in range(count - 1)]
-    q_next = lax.ppermute(q, "seq", to_left)
-    kv = jnp.concatenate([keys[0], values[0]], 0)
-    kv_next = lax.ppermute(kv, "seq", to_left).reshape(2, frames, width)
-    kv = kv.reshape(2, frames, width)
+    qkv = jnp.concatenate([queries[0], keys[0], values[0]], 0)
+    qkv_next = lax.ppermute(qkv, "seq", to_left).reshape(3, frames, width)
+    qkv = qkv.reshape(3, frames, width)
     cot_next = lax.ppermute(cot, "seq", to_left)
 
     def sds(shape, dtype):
@@ -609,14 +609,21 @@
         [rows16, sds((frames + 2 * PAD, width), F32), probs, rows16, sds((taps + 1, width), F32), row, row],
         [padded, pltpu.VMEM((taps, frames, LANES), F32)],
         10**10,
-        q, kv, cot, norm_gain, conv_kernel, conv_bias, same, keep, masks,
-    )
-    out_both, out_next, got, prob_cross, context_cross, slope_cross, in_cross = call(
+        qkv, cot, norm_gain, conv_kernel, conv_bias, same, keep, masks,
+    )
+    (half_own,) = call(
+        own_half_kernel,
+        [sds((frames, width // 2), F32)],
+        [],
+        2 * 10**9,
+        pre_own, masks, conv_kernel,
+    )
+    out_cross, got, prob_cross, context_cross, slope_cross, in_cross = call(
         cross_forward_kernel,
-        [rows16, rows16, three, probs, rows16, rows32, rows32],
-        [pltpu.VMEM((frames, width), BF16)],
+        [rows16, three, probs, rows16, rows32, rows32],
+        [],
         4 * 10**9,
-        q, kv, q_next, kv_next, segment_ids, gain, conv_kernel, bias, out_own,
+        after(qkv, half_own), qkv_next, segment_ids, gain, conv_kernel, bias,
     )
     grad_pre, mine, other = call(
         cross_sums_kernel,
@@ -627,14 +634,10 @@
     )
     steps = sum_steps()
     came = exchange(other, *steps[0])
-    (half_own,) = call(
-        own_half_kernel,
-        [sds((frames, width // 2), F32)],
-        [],
-        2 * 10**9,
-        after(pre_own, mine), masks, conv_kernel,
-    )
-    sent = added(mine, after(came, half_own))
+    out_both, out_next = call(
+        cross_place_kernel, [rows16, rows16], [], 10**9, after(out_cross, mine), out_own, segment_ids,
+    )
+    sent = added(mine, after(came, out_next))
     came = exchange(sent, *steps[1])
     out_came = lax.ppermute(after(out_next, sent), "seq", to_right)
     per_group = tiles // GROUPS
@@ -643,7 +646,7 @@
     grad_pre = after(grad_pre, sent)
     for group in range(GROUPS):
         if group == 1:
-            sent = added(sent, after(came, out_came, grad_own))
+            sent = added(sent, after(came, out_came))
             came = exchange(sent, *steps[3])
         extra = [gain, conv_kernel, grad_pre] if group == 0 else [after(grad_cross, sent)]
         own_part, next_part, *rest = call(
@@ -657,23 +660,23 @@
             (grad_cross,) = rest
             sent = added(sent, after(came, own_part))
             came = exchange(sent, *steps[2])
-            (grad_own,) = call(
-                own_grad_kernel,
-                [rows16],
-                [plain],
-                3 * 10**9,
-                after(pre_own, sent), context_own, masks, keep, gain, conv_kernel, half_own,
-            )
         parts += [own_part, lax.ppermute(after(next_part, sent), "seq", to_right)]
+    (grad_own,) = call(
+        own_grad_kernel,
+        [rows16],
+        [plain],
+        3 * 10**9,
+        after(pre_own, sent), context_own, masks, keep, gain, conv_kernel, half_own,
+    )
     for step in steps[GROUPS + 2 :]:
-        sent = added(sent, came)
+        sent = added(sent, after(came, grad_own))
         came = exchange(sent, *step)
     (grads_own,) = call(
         own_back_kernel,
         [three],
         [],
         4 * 10**9,
-        q, kv, prob_own, context_own, after(grad_own, sent),
+        qkv, prob_own, context_own, after(grad_own, sent),
     )
     sent = added(sent, after(came, grads_own))
     came = exchange(sent, *steps[0])

time: 57 us -> 56.7 us (level)
  starting transfers between devices: 20.5 us -> 19 us
  Pallas kernels: 26.6 us -> 27.5 us
    ppermute x2 -> x1, starting transfers between devices: 5.44 us -> 2.72 us  [per_device(): qkv_next = lax.ppermute(qkv, 'seq', to_left).reshape(3, frames, width)]
    ppermute x2, waiting for transfers between devices: 3.23 us -> 1.72 us  [per_device(): parts += [own_part, lax.ppermute(after(next_part, sent), 'seq', to_right)]]
    pallas_call x11 -> x12, Pallas kernels: 26.6 us -> 27.5 us  [call(): pl.pallas_call(kernel, out_shape=outs, in_specs=[VMEM] * len(args), out_s...]
    ppermute x6, waiting for transfers between devices: 4.13 us -> 4.91 us  [exchange(): lax.ppermute(sent, axis, [(i, i ^ step) for i in range(lax.axis_size(axis...]
    ppermute x2 -> x1, waiting for transfers between devices: 0.07 us -> 0.85 us  [per_device(): qkv_next = lax.ppermute(qkv, 'seq', to_left).reshape(3, frames, width)]
    ppermute x1, starting transfers between devices: 2.05 us -> 2.72 us  [per_device(): cot_next = lax.ppermute(cot, 'seq', to_left)]
  transfers between devices with their start and end apart: 12 -> 11, of which waited for: 5 -> 6; matrix products, arithmetic and copies ran while one was open for 2% -> 0% of each run, Pallas kernels for 40% -> 42%
where the time goes in v9:
time: 56.7 us; the launch traced here: 56.4 us
  Pallas kernels  27.5 us (49%)
  starting transfers between devices  19 us (34%)
  waiting for transfers between devices  7.51 us (13%)
  other arithmetic  1.43 us (3%)
  between operations  0.88 us (2%)
    pallas_call x12, Pallas kernels, call(): pl.pallas_call(kernel, out_shape=outs, in_specs=[VMEM] * len(args), out_s...  27.5 us
    ppermute x6, starting transfers between devices, exchange(): lax.ppermute(sent, axis, [(i, i ^ step) for i in range(lax.axis_size(axis...  6.29 us
    ppermute x2, starting transfers between devices, per_device(): parts += [own_part, lax.ppermute(after(next_part, sent), 'seq', to_right)]  5.31 us
    ppermute x6, waiting for transfers between devices, exchange(): lax.ppermute(sent, axis, [(i, i ^ step) for i in range(lax.axis_size(axis...  4.91 us
    ppermute x1, starting transfers between devices, per_device(): qkv_next = lax.ppermute(qkv, 'seq', to_left).reshape(3, frames, width)  2.72 us
    ppermute x1, starting transfers between devices, per_device(): cot_next = lax.ppermute(cot, 'seq', to_left)  2.72 us
    ppermute x1, starting transfers between devices, per_device(): out_came = lax.ppermute(after(out_next, sent), 'seq', to_right)  1.97 us
    ppermute x2, waiting for transfers between devices, per_device(): parts += [own_part, lax.ppermute(after(next_part, sent), 'seq', to_right)]  1.72 us
  transfers between devices with their start and end apart: 11, of which 6 were waited for; matrix products, arithmetic and copies ran while one was open for 0% of the time, Pallas kernels for 42%

profile of v9, /device:TPU:12, one launch (start us, length us, event | category | flops | bytes accessed | tf_op | source)
XLA Modules:
  0.0 56.4 jit_solution(1965204765343566972)
XLA Ops:
  0.6 0.0 copy-start.1
  0.6 0.0 copy-start.4
  0.7 1.4 %pad_maximum_fusion = bf16[384,1536]{1,0:T(8,128)(2,1)S(1)} fusion(bf16[128,1536]{1,0:T(8,128)(2,1)} %bitcast.17, bf16[128,1536]{1,0:T(8,128)(2,1)} %bitcast.18, bf16[128,1536]{1,0:T(8,128)(2,1)} %bitcast.19), kind=kLoop, calls=%fused_computation | loop fusion | flops 3538944 | bytes 2359296 | tf_op jit(solution)/shard_map/concatenate | solution.py:582
  2.0 2.7 %collective-permute-start.1 = (bf16[384,1536]{1,0:T(8,128)(2,1)S(1)}, bf16[384,1536]{1,0:T(8,128)(2,1)S(1)}, u32[]{:S(2)}, u32[]{:S(2)}) collective-permute-start(bf16[384,1536]{1,0:T(8,128)(2,1)S(1)} %pad_maximum_fusion), channel_id=1, source_target_pairs={{1,0},{2,1},{3,2},{4,3},{5,4},{6,5},{7,6},{8,7},{9,8},{10,9},{11,1... | collective-permute-start | bytes 3538952 | tf_op jit(solution)/shard_map/ppermute | solution.py:583
  4.7 0.0 copy-done.1
  4.8 0.0 copy-start
  4.8 0.0 copy-start.2
  4.8 0.0 copy-start.3
  4.8 2.7 %collective-permute-start = (bf16[128,1536]{1,0:T(8,128)(2,1)S(1)}, bf16[128,1536]{1,0:T(8,128)(2,1)S(1)}, u32[]{:S(2)}, u32[]{:S(2)}) collective-permute-start(bf16[128,1536]{1,0:T(8,128)(2,1)S(1)} %bitcast.14), channel_id=1, source_target_pairs={{1,0},{2,1},{3,2},{4,3},{5,4},{6,5},{7,6},{8,7},{9,8},{10,9},{11,1... | collective-permute-start | bytes 1179656 | tf_op jit(solution)/shard_map/ppermute | solution.py:585
  7.5 0.0 copy-done.4
  7.5 0.3 shard_map.135
  7.9 0.0 copy-done
  7.9 0.0 copy-done.2
  7.9 0.0 copy-done.3
  7.9 7.8 %shard_map.136 = (bf16[128,1536]{1,0:T(8,128)(2,1)S(1)}, f32[160,1536]{1,0:T(8,128)S(1)}, bf16[12,128,256]{2,1,0:T(8,128)(2,1)S(1)}, bf16[128,1536]{1,0:T(8,128)...) custom-call(bf16[3,128,1536]{2,1,0:T(8,128)(2,1)S(1)} %bitcast.10, ...), custom_call_target="tpu_custom_call" | custom-call | flops 10000000000 | bytes 6703104 | tf_op jit(solution)/shard_map/pallas_call | solution.py:540
  15.7 1.9 %shard_map.137.half_ref = f32[128,768]{1,0:T(8,128)S(1)} custom-call(f32[160,1536]{1,0:T(8,128)S(1)} %get-tuple-element.82.pad_ref, f32[3968,128]{1,0:T(8,128)S(1)} %get-tuple-element.56.mask_ref, f32[31,1536]{1,0:T(8,128)S(1)} %copy-done), custom_call_target="tpu_custom_call" | custom-call | flops 2000000000 | bytes 3598336 | tf_op jit(solution)/shard_map/pallas_call | solution.py:540
  17.6 0.8 %collective-permute-done.1 = bf16[384,1536]{1,0:T(8,128)(2,1)S(1)} collective-permute-done((bf16[384,1536]{1,0:T(8,128)(2,1)S(1)}, bf16[384,1536]{1,0:T(8,128)(2,1)S(1)}, u32[]{:S(2)}, u32[]{:S(2)}) %collective-permute-start.1) | collective-permute-done | bytes 1179680 | tf_op jit(solution)/shard_map/ppermute | solution.py:583
  18.4 4.2 %shard_map.138 = (bf16[128,1536]{1,0:T(8,128)(2,1)S(1)}, bf16[3,128,1536]{2,1,0:T(8,128)(2,1)S(1)}, bf16[12,128,256]{2,1,0:T(8,128)(2,1)S(1)}, bf16[128,1536]{1,...) custom-call(bf16[3,128,1536]{2,1,0:T(8,128)(2,1)S(1)} %bitcast.11, ...), custom_call_target="tpu_custom_call" | custom-call | flops 4000000000 | bytes 6895616 | tf_op jit(solution)/shard_map/pallas_call | solution.py:540
  22.6 0.0 collective-permute-done.cotn_ref
  22.7 2.4 %shard_map.139 = (f32[128,1536]{1,0:T(8,128)S(1)}, bf16[32,768]{1,0:T(8,128)(2,1)S(1)}, bf16[32,768]{1,0:T(8,128)(2,1)S(1)}) custom-call(bf16[128,1536]{1,0:T(8,128)(2,1)S(1)} %bitcast.16, bf16[128,1536]{1,0:T(8,128)(2,1)S(1)} %collective-permute-done.cotn_ref, s32[1,2048]{1,0:T(1,128)S(1)} %copy-done.4, f32[128,1536]{1,0:T(8,128)S(1)} %get-tuple-element.63.slope_ref, ...), custom_call_target="tpu_custom_call" | custom-call | flops 3000000000 | bytes 3448832 | tf_op jit(solution)/shard_map/pallas_call | solution.py:540
  25.1 1.0 %collective-permute-start.2 = (bf16[32,768]{1,0:T(8,128)(2,1)S(1)}, bf16[32,768]{1,0:T(8,128)(2,1)S(1)}, u32[]{:S(2)}, u32[]{:S(2)}) collective-permute-start(bf16[32,768]{1,0:T(8,128)(2,1)S(1)} %get-tuple-element.67), channel_id=1, source_target_pairs={{0,1},{1,0},{2,3},{3,2},{4,5},{5,4},{6,7},{7,6},{8,9},{9,8},{10,11... | collective-permute-start | bytes 147464 | tf_op jit(solution)/shard_map/ppermute | solution.py:567
  26.1 0.5 shard_map.140
  26.6 0.4 collective-permute-done.2
  27.0 2.4 %collective-permute-start.3 = (bf16[32,768]{1,0:T(8,128)(2,1)S(1)}, bf16[32,768]{1,0:T(8,128)(2,1)S(1)}, u32[]{:S(2)}, u32[]{:S(2)}) collective-permute-start(bf16[32,768]{1,0:T(8,128)(2,1)S(1)} %add_convert_fusion.4), channel_id=1, source_target_pairs={{0,2},{1,3},{2,0},{3,1},{4,6},{5,7},{6,4},{7,5},{8,10},{9,11},{10,... | collective-permute-start | bytes 147464 | tf_op jit(solution)/shard_map/ppermute | solution.py:567
  29.4 2.0 %collective-permute-start.5 = (bf16[128,1536]{1,0:T(8,128)(2,1)S(1)}, bf16[128,1536]{1,0:T(8,128)(2,1)S(1)}, u32[]{:S(2)}, u32[]{:S(2)}) collective-permute-start(bf16[128,1536]{1,0:T(8,128)(2,1)S(1)} %get-tuple-element.80), channel_id=1, source_target_pairs={{0,1},{1,2},{2,3},{3,4},{4,5},{5,6},{6,7},{7,8},{8,9},{9,10},{10,1... | collective-permute-start | bytes 1179656 | tf_op jit(solution)/shard_map/ppermute | solution.py:642
  31.4 3.5 %shard_map.141 = (bf16[3,128,768]{2,1,0:T(8,128)(2,1)S(1)}, bf16[3,128,768]{2,1,0:T(8,128)(2,1)S(1)}, bf16[128,1536]{1,0:T(8,128)(2,1)S(1)}) custom-call(bf16[3,128,1536]{2,1,0:T(8,128)(2,1)S(1)} %get-tuple-element.73.qkv_ref, bf16[12,128,256]{2,1,0:T(8,128)(2,1)S(1)} %get-tuple-element.74.prob_ref, bf16[128,1536]{1,0:T(8,128)(2,1)S(1)} %get-tuple-element.75.context_ref, ...), custom_call_target="tpu_custom_call" | custom-call | flops 5000000000 | bytes 4923392 | tf_op jit(solution)/shard_map/pallas_call | solution.py:540
  34.9 0.0 collective-permute-done.3
  34.9 0.6 %collective-permute-start.4 = (bf16[32,768]{1,0:T(8,128)(2,1)S(1)}, bf16[32,768]{1,0:T(8,128)(2,1)S(1)}, u32[]{:S(2)}, u32[]{:S(2)}) collective-permute-start(bf16[32,768]{1,0:T(8,128)(2,1)S(1)} %add_convert_fusion.3), channel_id=1, source_target_pairs={{0,8},{1,9},{2,10},{3,11},{4,12},{5,13},{6,14},{7,15},{8,0},{9,1},... | collective-permute-start | bytes 147464 | tf_op jit(solution)/shard_map/ppermute | solution.py:567
  35.5 3.4 %collective-permute-start.7 = (bf16[3,128,768]{2,1,0:T(8,128)(2,1)S(1)}, bf16[3,128,768]{2,1,0:T(8,128)(2,1)S(1)}, u32[]{:S(2)}, u32[]{:S(2)}) collective-permute-start(bf16[3,128,768]{2,1,0:T(8,128)(2,1)S(1)} %get-tuple-element.87), channel_id=1, source_target_pairs={{0,1},{1,2},{2,3},{3,4},{4,5},{5,6},{6,7},{7,8},{8,9},{9,10},{10,1... | collective-permute-start | bytes 1769480 | tf_op jit(solution)/shard_map/ppermute | solution.py:663
  38.9 1.1 %collective-permute-done.4 = bf16[32,768]{1,0:T(8,128)(2,1)S(1)} collective-permute-done((bf16[32,768]{1,0:T(8,128)(2,1)S(1)}, bf16[32,768]{1,0:T(8,128)(2,1)S(1)}, u32[]{:S(2)}, u32[]{:S(2)}) %collective-permute-start.4) | collective-permute-done | bytes 49184 | tf_op jit(solution)/shard_map/ppermute | solution.py:567
  40.0 0.0 collective-permute-done.5.out_came_ref
  40.0 1.6 %collective-permute-start.6 = (bf16[32,768]{1,0:T(8,128)(2,1)S(1)}, bf16[32,768]{1,0:T(8,128)(2,1)S(1)}, u32[]{:S(2)}, u32[]{:S(2)}) collective-permute-start(bf16[32,768]{1,0:T(8,128)(2,1)S(1)} %add_convert_fusion.2), channel_id=1, source_target_pairs={{0,4},{1,5},{2,6},{3,7},{4,0},{5,1},{6,2},{7,3},{8,12},{9,13},{10,... | collective-permute-start | bytes 147464 | tf_op jit(solution)/shard_map/ppermute | solution.py:567
  41.6 1.1 %shard_map.144 = (bf16[3,128,768]{2,1,0:T(8,128)(2,1)S(1)}, bf16[3,128,768]{2,1,0:T(8,128)(2,1)S(1)}) custom-call(bf16[3,128,1536]{2,1,0:T(8,128)(2,1)S(1)} %get-tuple-element.73.qkv_ref, bf16[12,128,256]{2,1,0:T(8,128)(2,1)S(1)} %get-tuple-element.74.prob_ref, bf16[128,1536]{1,0:T(8,128)(2,1)S(1)} %get-tuple-element.75.context_ref, ...), custom_call_target="tpu_custom_call" | custom-call | flops 2000000000 | bytes 3940352 | tf_op jit(solution)/shard_map/pallas_call | solution.py:540
  42.7 1.9 %collective-permute-start.8 = (bf16[3,128,768]{2,1,0:T(8,128)(2,1)S(1)}, bf16[3,128,768]{2,1,0:T(8,128)(2,1)S(1)}, u32[]{:S(2)}, u32[]{:S(2)}) collective-permute-start(bf16[3,128,768]{2,1,0:T(8,128)(2,1)S(1)} %get-tuple-element.92), channel_id=1, source_target_pairs={{0,1},{1,2},{2,3},{3,4},{4,5},{5,6},{6,7},{7,8},{8,9},{9,10},{10,1... | collective-permute-start | bytes 1769480 | tf_op jit(solution)/shard_map/ppermute | solution.py:663
  44.6 2.4 %shard_map.142.grad_ref = bf16[128,1536]{1,0:T(8,128)(2,1)S(1)} custom-call(f32[160,1536]{1,0:T(8,128)S(1)} %get-tuple-element.82.pad_ref, bf16[128,1536]{1,0:T(8,128)(2,1)S(1)} %get-tuple-element.58.context_ref, f32[3968,128]{1,0:T(8,128)S(1)} %get-tuple-element.56.mask_ref, f32[128,128]{1,0:T(8,128)S(1)} %get-tuple-element.55.keep_ref, ...), custom_call_target="tpu_custom_call" | custom-call | flops 3000000000 | bytes 4456448 | tf_op jit(solution)/shard_map/pallas_call | solution.py:540
  47.0 0.0 collective-permute-done.6
  47.1 0.6 %collective-permute-start.9 = (bf16[32,768]{1,0:T(8,128)(2,1)S(1)}, bf16[32,768]{1,0:T(8,128)(2,1)S(1)}, u32[]{:S(2)}, u32[]{:S(2)}) collective-permute-start(bf16[32,768]{1,0:T(8,128)(2,1)S(1)} %add_convert_fusion.1), channel_id=1, source_target_pairs={{0,16},{16,0},{1,17},{17,1},{2,18},{18,2},{3,19},{19,3},{4,20},{20... | collective-permute-start | bytes 147464 | tf_op jit(solution)/shard_map/ppermute | solution.py:567
  47.6 1.3 %shard_map.143.grads_ref = bf16[3,128,1536]{2,1,0:T(8,128)(2,1)S(1)} custom-call(bf16[3,128,1536]{2,1,0:T(8,128)(2,1)S(1)} %bitcast.12, bf16[12,128,256]{2,1,0:T(8,128)(2,1)S(1)} %get-tuple-element.57.prob_ref, bf16[128,1536]{1,0:T(8,128)(2,1)S(1)} %get-tuple-element.58.context_ref, bf16[128,1536]{1,0:T(8,128)(2,1)S(1)} %shard_map.142.grad_ref), custom_call_target="tpu_custom_call" | custom-call | flops 4000000000 | bytes 3932160 | tf_op jit(solution)/shard_map/pallas_call | solution.py:540
  49.0 2.3 %collective-permute-done.9 = bf16[32,768]{1,0:T(8,128)(2,1)S(1)} collective-permute-done((bf16[32,768]{1,0:T(8,128)(2,1)S(1)}, bf16[32,768]{1,0:T(8,128)(2,1)S(1)}, u32[]{:S(2)}, u32[]{:S(2)}) %collective-permute-start.9) | collective-permute-done | bytes 49184 | tf_op jit(solution)/shard_map/ppermute | solution.py:567
  51.2 0.1 collective-permute-start.10
  51.3 1.2 %collective-permute-done.10.came_ref = bf16[32,768]{1,0:T(8,128)(2,1)S(1)} collective-permute-done((bf16[32,768]{1,0:T(8,128)(2,1)S(1)}, bf16[32,768]{1,0:T(8,128)(2,1)S(1)}, u32[]{:S(2)}, u32[]{:S(2)}) %collective-permute-start.10) | collective-permute-done | bytes 49184 | tf_op jit(solution)/shard_map/ppermute | solution.py:567
  52.5 0.7 %shard_map.146 = (f32[1536]{0:T(1024)}, f32[31,1536]{1,0:T(8,128)}, f32[1536]{0:T(1024)}) custom-call(bf16[32,768]{1,0:T(8,128)(2,1)S(1)} %add_convert_fusion.mine_ref, bf16[32,768]{1,0:T(8,128)(2,1)S(1)} %collective-permute-done.10.came_ref, f32[31,1536]{1,0:T(8,128)S(1)} %copy-done, f32[1,1536]{1,0:T(1,128)S(1)} %get-tuple-element.61.gain_ref.refs_0_.norm_ref), custom_call_target="tpu_custom_call" | custom-call | flops 1000000 | bytes 497664 | tf_op jit(solution)/shard_map/pallas_call | solution.py:540
  53.2 0.0 collective-permute-done.7.refs_1_
  53.2 1.7 %collective-permute-done.8.refs_3_ = bf16[3,128,768]{2,1,0:T(8,128)(2,1)S(1)} collective-permute-done((bf16[3,128,768]{2,1,0:T(8,128)(2,1)S(1)}, bf16[3,128,768]{2,1,0:T(8,128)(2,1)S(1)}, u32[]{:S(2)}, u32[]{:S(2)}) %collective-permute-start.8) | collective-permute-done | bytes 589856 | tf_op jit(solution)/shard_map/ppermute | solution.py:663
  55.0 1.4 %shard_map.145 = (bf16[128,1536]{1,0:T(8,128)(2,1)}, bf16[128,1536]{1,0:T(8,128)(2,1)}, bf16[128,1536]{1,0:T(8,128)(2,1)}, bf16[128,1536]{1,0:T(8,128)(2,1)}) custom-call(bf16[3,128,1536]{2,1,0:T(8,128)(2,1)S(1)} %shard_map.143.grads_ref, bf16[128,1536]{1,0:T(8,128)(2,1)S(1)} %get-tuple-element.85.out_both_ref, ...), custom_call_target="tpu_custom_call" | custom-call | flops 1000000000 | bytes 5898240 | tf_op jit(solution)/shard_map/pallas_call | solution.py:540
  (5 shorter events, 0.1 us)
Async XLA Ops:
  0.6 4.1 %copy-start.1 = (bf16[1,128,1536]{2,1,0:T(8,128)(2,1)S(1)}, bf16[1,128,1536]{2,1,0:T(8,128)(2,1)}, u32[]{:S(2)}) copy-start(bf16[1,128,1536]{2,1,0:T(8,128)(2,1)} %param.15) | copy-start | bytes 1179652
  0.6 6.9 %copy-start.4 = (s32[1,2048]{1,0:T(1,128)S(1)}, s32[1,2048]{1,0:T(1,128)}, u32[]{:S(2)}) copy-start(s32[1,2048]{1,0:T(1,128)} %seg_ref.11) | copy-start | bytes 24580
  2.0 16.4 %collective-permute-start.1 = (bf16[384,1536]{1,0:T(8,128)(2,1)S(1)}, bf16[384,1536]{1,0:T(8,128)(2,1)S(1)}, u32[]{:S(2)}, u32[]{:S(2)}) collective-permute-start(bf16[384,1536]{1,0:T(8,128)(2,1)S(1)} %pad_maximum_fusion), channel_id=1, source_target_pairs={{1,0},{2,1},{3,2},{4,3},{5,4},{6,5},{7,6},{8,7},{9,8},{10,9},{11,1... | collective-permute-start | bytes 3538952 | tf_op jit(solution)/shard_map/ppermute | solution.py:583
  4.8 3.1 %copy-start = (f32[31,1536]{1,0:T(8,128)S(1)}, f32[31,1536]{1,0:T(8,128)}, u32[]{:S(2)}) copy-start(f32[31,1536]{1,0:T(8,128)} %weight_ref.1) | copy-start | bytes 571396
  4.8 3.1 %copy-start.2 = (f32[1536]{0:T(1024)S(1)}, f32[1536]{0:T(1024)}, u32[]{:S(2)}) copy-start(f32[1536]{0:T(1024)} %gain_row.1) | copy-start | bytes 18436
  4.8 3.1 %copy-start.3 = (f32[1536]{0:T(1024)S(1)}, f32[1536]{0:T(1024)}, u32[]{:S(2)}) copy-start(f32[1536]{0:T(1024)} %bias_row.1) | copy-start | bytes 18436
  4.8 17.9 %collective-permute-start = (bf16[128,1536]{1,0:T(8,128)(2,1)S(1)}, bf16[128,1536]{1,0:T(8,128)(2,1)S(1)}, u32[]{:S(2)}, u32[]{:S(2)}) collective-permute-start(bf16[128,1536]{1,0:T(8,128)(2,1)S(1)} %bitcast.14), channel_id=1, source_target_pairs={{1,0},{2,1},{3,2},{4,3},{5,4},{6,5},{7,6},{8,7},{9,8},{10,9},{11,1... | collective-permute-start | bytes 1179656 | tf_op jit(solution)/shard_map/ppermute | solution.py:585
  25.1 1.9 %collective-permute-start.2 = (bf16[32,768]{1,0:T(8,128)(2,1)S(1)}, bf16[32,768]{1,0:T(8,128)(2,1)S(1)}, u32[]{:S(2)}, u32[]{:S(2)}) collective-permute-start(bf16[32,768]{1,0:T(8,128)(2,1)S(1)} %get-tuple-element.67), channel_id=1, source_target_pairs={{0,1},{1,0},{2,3},{3,2},{4,5},{5,4},{6,7},{7,6},{8,9},{9,8},{10,11... | collective-permute-start | bytes 147464 | tf_op jit(solution)/shard_map/ppermute | solution.py:567
  27.0 7.9 %collective-permute-start.3 = (bf16[32,768]{1,0:T(8,128)(2,1)S(1)}, bf16[32,768]{1,0:T(8,128)(2,1)S(1)}, u32[]{:S(2)}, u32[]{:S(2)}) collective-permute-start(bf16[32,768]{1,0:T(8,128)(2,1)S(1)} %add_convert_fusion.4), channel_id=1, source_target_pairs={{0,2},{1,3},{2,0},{3,1},{4,6},{5,7},{6,4},{7,5},{8,10},{9,11},{10,... | collective-permute-start | bytes 147464 | tf_op jit(solution)/shard_map/ppermute | solution.py:567
  29.4 10.6 %collective-permute-start.5 = (bf16[128,1536]{1,0:T(8,128)(2,1)S(1)}, bf16[128,1536]{1,0:T(8,128)(2,1)S(1)}, u32[]{:S(2)}, u32[]{:S(2)}) collective-permute-start(bf16[128,1536]{1,0:T(8,128)(2,1)S(1)} %get-tuple-element.80), channel_id=1, source_target_pairs={{0,1},{1,2},{2,3},{3,4},{4,5},{5,6},{6,7},{7,8},{8,9},{9,10},{10,1... | collective-permute-start | bytes 1179656 | tf_op jit(solution)/shard_map/ppermute | solution.py:642
  34.9 5.1 %collective-permute-start.4 = (bf16[32,768]{1,0:T(8,128)(2,1)S(1)}, bf16[32,768]{1,0:T(8,128)(2,1)S(1)}, u32[]{:S(2)}, u32[]{:S(2)}) collective-permute-start(bf16[32,768]{1,0:T(8,128)(2,1)S(1)} %add_convert_fusion.3), channel_id=1, source_target_pairs={{0,8},{1,9},{2,10},{3,11},{4,12},{5,13},{6,14},{7,15},{8,0},{9,1},... | collective-permute-start | bytes 147464 | tf_op jit(solution)/shard_map/ppermute | solution.py:567
  35.5 17.7 %collective-permute-start.7 = (bf16[3,128,768]{2,1,0:T(8,128)(2,1)S(1)}, bf16[3,128,768]{2,1,0:T(8,128)(2,1)S(1)}, u32[]{:S(2)}, u32[]{:S(2)}) collective-permute-start(bf16[3,128,768]{2,1,0:T(8,128)(2,1)S(1)} %get-tuple-element.87), channel_id=1, source_target_pairs={{0,1},{1,2},{2,3},{3,4},{4,5},{5,6},{6,7},{7,8},{8,9},{9,10},{10,1... | collective-permute-start | bytes 1769480 | tf_op jit(solution)/shard_map/ppermute | solution.py:663
  40.0 7.1 %collective-permute-start.6 = (bf16[32,768]{1,0:T(8,128)(2,1)S(1)}, bf16[32,768]{1,0:T(8,128)(2,1)S(1)}, u32[]{:S(2)}, u32[]{:S(2)}) collective-permute-start(bf16[32,768]{1,0:T(8,128)(2,1)S(1)} %add_convert_fusion.2), channel_id=1, source_target_pairs={{0,4},{1,5},{2,6},{3,7},{4,0},{5,1},{6,2},{7,3},{8,12},{9,13},{10,... | collective-permute-start | bytes 147464 | tf_op jit(solution)/shard_map/ppermute | solution.py:567
  42.7 12.3 %collective-permute-start.8 = (bf16[3,128,768]{2,1,0:T(8,128)(2,1)S(1)}, bf16[3,128,768]{2,1,0:T(8,128)(2,1)S(1)}, u32[]{:S(2)}, u32[]{:S(2)}) collective-permute-start(bf16[3,128,768]{2,1,0:T(8,128)(2,1)S(1)} %get-tuple-element.92), channel_id=1, source_target_pairs={{0,1},{1,2},{2,3},{3,4},{4,5},{5,6},{6,7},{7,8},{8,9},{9,10},{10,1... | collective-permute-start | bytes 1769480 | tf_op jit(solution)/shard_map/ppermute | solution.py:663
  47.1 4.2 %collective-permute-start.9 = (bf16[32,768]{1,0:T(8,128)(2,1)S(1)}, bf16[32,768]{1,0:T(8,128)(2,1)S(1)}, u32[]{:S(2)}, u32[]{:S(2)}) collective-permute-start(bf16[32,768]{1,0:T(8,128)(2,1)S(1)} %add_convert_fusion.1), channel_id=1, source_target_pairs={{0,16},{16,0},{1,17},{17,1},{2,18},{18,2},{3,19},{19,3},{4,20},{20... | collective-permute-start | bytes 147464 | tf_op jit(solution)/shard_map/ppermute | solution.py:567
  51.2 1.3 %collective-permute-start.10 = (bf16[32,768]{1,0:T(8,128)(2,1)S(1)}, bf16[32,768]{1,0:T(8,128)(2,1)S(1)}, u32[]{:S(2)}, u32[]{:S(2)}) collective-permute-start(bf16[32,768]{1,0:T(8,128)(2,1)S(1)} %add_convert_fusion.mine_ref), channel_id=1, source_target_pairs={{0,1},{1,0},{2,3},{3,2},{4,5},{5,4},{6,7},{7,6},{8,9},{9,8},{10,11... | collective-permute-start | bytes 147464 | tf_op jit(solution)/shard_map/ppermute | solution.py:567

commit v10 on v9

--- a/solution.py
+++ b/solution.py
@@ -535,6 +535,12 @@
     gain_ref[...] = gain.reshape(width)
 
 
+def last_kernel(scale, *refs):
+    ins, outs = refs[:-7], refs[-7:]
+    finish_kernel(scale, *ins[:4], *outs[:3])
+    merge_kernel(*ins[4:], *outs[3:])
+
+
 def call(kernel, outs, scratch, flops, *args, limit=24):
     size = sum(a.size * a.dtype.itemsize for a in args) + sum(o.size * o.dtype.itemsize for o in outs)
     return pl.pallas_call(
@@ -661,6 +667,9 @@
             sent = added(sent, after(came, own_part))
             came = exchange(sent, *steps[2])
         parts += [own_part, lax.ppermute(after(next_part, sent), "seq", to_right)]
+    for step in steps[GROUPS + 2 :]:
+        sent = added(sent, came)
+        came = exchange(sent, *step)
     (grad_own,) = call(
         own_grad_kernel,
         [rows16],
@@ -668,9 +677,6 @@
         3 * 10**9,
         after(pre_own, sent), context_own, masks, keep, gain, conv_kernel, half_own,
     )
-    for step in steps[GROUPS + 2 :]:
-        sent = added(sent, after(came, grad_own))
-        came = exchange(sent, *step)
     (grads_own,) = call(
         own_back_kernel,
         [three],
@@ -680,16 +686,13 @@
     )
     sent = added(sent, after(came, grads_own))
     came = exchange(sent, *steps[0])
-    query_grad, key_grad, value_grad, conv_out = call(
-        merge_kernel, [rows16] * 4, [], 10**9, grads_own, out_both, out_came, *parts,
-    )
     scale = (lax.axis_size("dp") * count * frames) ** (-0.5)
-    gain_grad, kernel_grad, bias_grad = call(
-        functools.partial(finish_kernel, scale),
-        [sds((width,), F32), sds(conv_kernel.shape, F32), sds((width,), F32)],
+    gain_grad, kernel_grad, bias_grad, query_grad, key_grad, value_grad, conv_out = call(
+        functools.partial(last_kernel, scale),
+        [sds((width,), F32), sds(conv_kernel.shape, F32), sds((width,), F32)] + [rows16] * 4,
         [],
-        10**6,
-        sent, came, conv_kernel, gain,
+        10**9,
+        sent, came, conv_kernel, gain, grads_own, out_both, out_came, *parts,
     )
     return (
         conv_out[None],

time: 56.7 us -> 56.8 us (level)
  waiting for transfers between devices: 7.51 us -> 8.22 us
  Pallas kernels: 27.5 us -> 26.8 us
    ppermute x2, waiting for transfers between devices: 1.72 us -> 4.69 us  [per_device(): parts += [own_part, lax.ppermute(after(next_part, sent), 'seq', to_right)]]
    ppermute x6, waiting for transfers between devices: 4.91 us -> 2.67 us  [exchange(): lax.ppermute(sent, axis, [(i, i ^ step) for i in range(lax.axis_size(axis...]
    pallas_call x12 -> x11, Pallas kernels: 27.5 us -> 26.8 us  [call(): pl.pallas_call(kernel, out_shape=outs, in_specs=[VMEM] * len(args), out_s...]
  transfers between devices with their start and end apart: 11 -> 11, of which waited for: 6 -> 5; matrix products, arithmetic and copies ran while one was open for 0% -> 0% of each run, Pallas kernels for 42% -> 41%
where the time goes in v10:
time: 56.8 us; the launch traced here: 56.4 us
  Pallas kernels  26.8 us (47%)
  starting transfers between devices  19 us (33%)
  waiting for transfers between devices  8.22 us (14%)
  other arithmetic  1.44 us (3%)
  between operations  0.89 us (2%)
    pallas_call x11, Pallas kernels, call(): pl.pallas_call(kernel, out_shape=outs, in_specs=[VMEM] * len(args), out_s...  26.8 us
    ppermute x6, starting transfers between devices, exchange(): lax.ppermute(sent, axis, [(i, i ^ step) for i in range(lax.axis_size(axis...  6.28 us
    ppermute x2, starting transfers between devices, per_device(): parts += [own_part, lax.ppermute(after(next_part, sent), 'seq', to_right)]  5.3 us
    ppermute x2, waiting for transfers between devices, per_device(): parts += [own_part, lax.ppermute(after(next_part, sent), 'seq', to_right)]  4.69 us
    ppermute x1, starting transfers between devices, per_device(): qkv_next = lax.ppermute(qkv, 'seq', to_left).reshape(3, frames, width)  2.72 us
    ppermute x1, starting transfers between devices, per_device(): cot_next = lax.ppermute(cot, 'seq', to_left)  2.72 us
    ppermute x6, waiting for transfers between devices, exchange(): lax.ppermute(sent, axis, [(i, i ^ step) for i in range(lax.axis_size(axis...  2.67 us
    ppermute x1, starting transfers between devices, per_device(): out_came = lax.ppermute(after(out_next, sent), 'seq', to_right)  1.97 us
  transfers between devices with their start and end apart: 11, of which 5 were waited for; matrix products, arithmetic and copies ran while one was open for 0% of the time, Pallas kernels for 41%

profile of v10, /device:TPU:12, one launch (start us, length us, event | category | flops | bytes accessed | tf_op | source)
XLA Modules:
  0.0 56.4 jit_solution(2876505544076943824)
XLA Ops:
  0.6 0.0 copy-start.1
  0.6 0.0 copy-start.4
  0.7 1.4 %pad_maximum_fusion = bf16[384,1536]{1,0:T(8,128)(2,1)S(1)} fusion(bf16[128,1536]{1,0:T(8,128)(2,1)} %bitcast.17, bf16[128,1536]{1,0:T(8,128)(2,1)} %bitcast.18, bf16[128,1536]{1,0:T(8,128)(2,1)} %bitcast.19), kind=kLoop, calls=%fused_computation | loop fusion | flops 3538944 | bytes 2359296 | tf_op jit(solution)/shard_map/concatenate | solution.py:588
  2.0 2.7 %collective-permute-start.1 = (bf16[384,1536]{1,0:T(8,128)(2,1)S(1)}, bf16[384,1536]{1,0:T(8,128)(2,1)S(1)}, u32[]{:S(2)}, u32[]{:S(2)}) collective-permute-start(bf16[384,1536]{1,0:T(8,128)(2,1)S(1)} %pad_maximum_fusion), channel_id=1, source_target_pairs={{1,0},{2,1},{3,2},{4,3},{5,4},{6,5},{7,6},{8,7},{9,8},{10,9},{11,1... | collective-permute-start | bytes 3538952 | tf_op jit(solution)/shard_map/ppermute | solution.py:589
  4.7 0.0 copy-done.1
  4.8 0.0 copy-start
  4.8 0.0 copy-start.2
  4.8 0.0 copy-start.3
  4.8 2.7 %collective-permute-start = (bf16[128,1536]{1,0:T(8,128)(2,1)S(1)}, bf16[128,1536]{1,0:T(8,128)(2,1)S(1)}, u32[]{:S(2)}, u32[]{:S(2)}) collective-permute-start(bf16[128,1536]{1,0:T(8,128)(2,1)S(1)} %bitcast.14), channel_id=1, source_target_pairs={{1,0},{2,1},{3,2},{4,3},{5,4},{6,5},{7,6},{8,7},{9,8},{10,9},{11,1... | collective-permute-start | bytes 1179656 | tf_op jit(solution)/shard_map/ppermute | solution.py:591
  7.5 0.0 copy-done.4
  7.5 0.3 shard_map.135
  7.9 0.0 copy-done
  7.9 0.0 copy-done.2
  7.9 0.0 copy-done.3
  7.9 7.9 %shard_map.136 = (bf16[128,1536]{1,0:T(8,128)(2,1)S(1)}, f32[160,1536]{1,0:T(8,128)S(1)}, bf16[12,128,256]{2,1,0:T(8,128)(2,1)S(1)}, bf16[128,1536]{1,0:T(8,128)...) custom-call(bf16[3,128,1536]{2,1,0:T(8,128)(2,1)S(1)} %bitcast.10, ...), custom_call_target="tpu_custom_call" | custom-call | flops 10000000000 | bytes 6703104 | tf_op jit(solution)/shard_map/pallas_call | solution.py:546
  15.8 1.9 %shard_map.137.half_ref = f32[128,768]{1,0:T(8,128)S(1)} custom-call(f32[160,1536]{1,0:T(8,128)S(1)} %get-tuple-element.81.pad_ref, f32[3968,128]{1,0:T(8,128)S(1)} %get-tuple-element.55.mask_ref, f32[31,1536]{1,0:T(8,128)S(1)} %copy-done), custom_call_target="tpu_custom_call" | custom-call | flops 2000000000 | bytes 3598336 | tf_op jit(solution)/shard_map/pallas_call | solution.py:546
  17.6 0.8 %collective-permute-done.1 = bf16[384,1536]{1,0:T(8,128)(2,1)S(1)} collective-permute-done((bf16[384,1536]{1,0:T(8,128)(2,1)S(1)}, bf16[384,1536]{1,0:T(8,128)(2,1)S(1)}, u32[]{:S(2)}, u32[]{:S(2)}) %collective-permute-start.1) | collective-permute-done | bytes 1179680 | tf_op jit(solution)/shard_map/ppermute | solution.py:589
  18.4 4.2 %shard_map.138 = (bf16[128,1536]{1,0:T(8,128)(2,1)S(1)}, bf16[3,128,1536]{2,1,0:T(8,128)(2,1)S(1)}, bf16[12,128,256]{2,1,0:T(8,128)(2,1)S(1)}, bf16[128,1536]{1,...) custom-call(bf16[3,128,1536]{2,1,0:T(8,128)(2,1)S(1)} %bitcast.11, ...), custom_call_target="tpu_custom_call" | custom-call | flops 4000000000 | bytes 6895616 | tf_op jit(solution)/shard_map/pallas_call | solution.py:546
  22.6 0.0 collective-permute-done.cotn_ref
  22.7 2.4 %shard_map.139 = (f32[128,1536]{1,0:T(8,128)S(1)}, bf16[32,768]{1,0:T(8,128)(2,1)S(1)}, bf16[32,768]{1,0:T(8,128)(2,1)S(1)}) custom-call(bf16[128,1536]{1,0:T(8,128)(2,1)S(1)} %bitcast.16, bf16[128,1536]{1,0:T(8,128)(2,1)S(1)} %collective-permute-done.cotn_ref, s32[1,2048]{1,0:T(1,128)S(1)} %copy-done.4, f32[128,1536]{1,0:T(8,128)S(1)} %get-tuple-element.60.slope_ref, ...), custom_call_target="tpu_custom_call" | custom-call | flops 3000000000 | bytes 3448832 | tf_op jit(solution)/shard_map/pallas_call | solution.py:546
  25.1 1.0 %collective-permute-start.2 = (bf16[32,768]{1,0:T(8,128)(2,1)S(1)}, bf16[32,768]{1,0:T(8,128)(2,1)S(1)}, u32[]{:S(2)}, u32[]{:S(2)}) collective-permute-start(bf16[32,768]{1,0:T(8,128)(2,1)S(1)} %get-tuple-element.64), channel_id=1, source_target_pairs={{0,1},{1,0},{2,3},{3,2},{4,5},{5,4},{6,7},{7,6},{8,9},{9,8},{10,11... | collective-permute-start | bytes 147464 | tf_op jit(solution)/shard_map/ppermute | solution.py:573
  26.1 0.5 shard_map.140
  26.6 0.4 collective-permute-done.2
  27.0 2.4 %collective-permute-start.3 = (bf16[32,768]{1,0:T(8,128)(2,1)S(1)}, bf16[32,768]{1,0:T(8,128)(2,1)S(1)}, u32[]{:S(2)}, u32[]{:S(2)}) collective-permute-start(bf16[32,768]{1,0:T(8,128)(2,1)S(1)} %add_convert_fusion.4), channel_id=1, source_target_pairs={{0,2},{1,3},{2,0},{3,1},{4,6},{5,7},{6,4},{7,5},{8,10},{9,11},{10,... | collective-permute-start | bytes 147464 | tf_op jit(solution)/shard_map/ppermute | solution.py:573
  29.4 2.0 %collective-permute-start.5 = (bf16[128,1536]{1,0:T(8,128)(2,1)S(1)}, bf16[128,1536]{1,0:T(8,128)(2,1)S(1)}, u32[]{:S(2)}, u32[]{:S(2)}) collective-permute-start(bf16[128,1536]{1,0:T(8,128)(2,1)S(1)} %get-tuple-element.77), channel_id=1, source_target_pairs={{0,1},{1,2},{2,3},{3,4},{4,5},{5,6},{6,7},{7,8},{8,9},{9,10},{10,1... | collective-permute-start | bytes 1179656 | tf_op jit(solution)/shard_map/ppermute | solution.py:648
  31.4 3.5 %shard_map.141 = (bf16[3,128,768]{2,1,0:T(8,128)(2,1)S(1)}, bf16[3,128,768]{2,1,0:T(8,128)(2,1)S(1)}, bf16[128,1536]{1,0:T(8,128)(2,1)S(1)}) custom-call(bf16[3,128,1536]{2,1,0:T(8,128)(2,1)S(1)} %get-tuple-element.70.qkv_ref, bf16[12,128,256]{2,1,0:T(8,128)(2,1)S(1)} %get-tuple-element.71.prob_ref, bf16[128,1536]{1,0:T(8,128)(2,1)S(1)} %get-tuple-element.72.context_ref, ...), custom_call_target="tpu_custom_call" | custom-call | flops 5000000000 | bytes 4923392 | tf_op jit(solution)/shard_map/pallas_call | solution.py:546
  34.9 0.0 collective-permute-done.3
  34.9 0.6 %collective-permute-start.4 = (bf16[32,768]{1,0:T(8,128)(2,1)S(1)}, bf16[32,768]{1,0:T(8,128)(2,1)S(1)}, u32[]{:S(2)}, u32[]{:S(2)}) collective-permute-start(bf16[32,768]{1,0:T(8,128)(2,1)S(1)} %add_convert_fusion.3), channel_id=1, source_target_pairs={{0,8},{1,9},{2,10},{3,11},{4,12},{5,13},{6,14},{7,15},{8,0},{9,1},... | collective-permute-start | bytes 147464 | tf_op jit(solution)/shard_map/ppermute | solution.py:573
  35.5 3.4 %collective-permute-start.9 = (bf16[3,128,768]{2,1,0:T(8,128)(2,1)S(1)}, bf16[3,128,768]{2,1,0:T(8,128)(2,1)S(1)}, u32[]{:S(2)}, u32[]{:S(2)}) collective-permute-start(bf16[3,128,768]{2,1,0:T(8,128)(2,1)S(1)} %get-tuple-element.86), channel_id=1, source_target_pairs={{0,1},{1,2},{2,3},{3,4},{4,5},{5,6},{6,7},{7,8},{8,9},{9,10},{10,1... | collective-permute-start | bytes 1769480 | tf_op jit(solution)/shard_map/ppermute | solution.py:669
  38.9 1.1 %collective-permute-done.4 = bf16[32,768]{1,0:T(8,128)(2,1)S(1)} collective-permute-done((bf16[32,768]{1,0:T(8,128)(2,1)S(1)}, bf16[32,768]{1,0:T(8,128)(2,1)S(1)}, u32[]{:S(2)}, u32[]{:S(2)}) %collective-permute-start.4) | collective-permute-done | bytes 49184 | tf_op jit(solution)/shard_map/ppermute | solution.py:573
  40.0 0.0 collective-permute-done.5.refs_6_
  40.0 1.6 %collective-permute-start.6 = (bf16[32,768]{1,0:T(8,128)(2,1)S(1)}, bf16[32,768]{1,0:T(8,128)(2,1)S(1)}, u32[]{:S(2)}, u32[]{:S(2)}) collective-permute-start(bf16[32,768]{1,0:T(8,128)(2,1)S(1)} %add_convert_fusion.2), channel_id=1, source_target_pairs={{0,4},{1,5},{2,6},{3,7},{4,0},{5,1},{6,2},{7,3},{8,12},{9,13},{10,... | collective-permute-start | bytes 147464 | tf_op jit(solution)/shard_map/ppermute | solution.py:573
  41.6 1.1 %shard_map.144 = (bf16[3,128,768]{2,1,0:T(8,128)(2,1)S(1)}, bf16[3,128,768]{2,1,0:T(8,128)(2,1)S(1)}) custom-call(bf16[3,128,1536]{2,1,0:T(8,128)(2,1)S(1)} %get-tuple-element.70.qkv_ref, bf16[12,128,256]{2,1,0:T(8,128)(2,1)S(1)} %get-tuple-element.71.prob_ref, bf16[128,1536]{1,0:T(8,128)(2,1)S(1)} %get-tuple-element.72.context_ref, ...), custom_call_target="tpu_custom_call" | custom-call | flops 2000000000 | bytes 3940352 | tf_op jit(solution)/shard_map/pallas_call | solution.py:546
  42.7 1.9 %collective-permute-start.10 = (bf16[3,128,768]{2,1,0:T(8,128)(2,1)S(1)}, bf16[3,128,768]{2,1,0:T(8,128)(2,1)S(1)}, u32[]{:S(2)}, u32[]{:S(2)}) collective-permute-start(bf16[3,128,768]{2,1,0:T(8,128)(2,1)S(1)} %get-tuple-element.91), channel_id=1, source_target_pairs={{0,1},{1,2},{2,3},{3,4},{4,5},{5,6},{6,7},{7,8},{8,9},{9,10},{10,1... | collective-permute-start | bytes 1769480 | tf_op jit(solution)/shard_map/ppermute | solution.py:669
  44.6 0.0 collective-permute-done.6
  44.7 0.6 %collective-permute-start.7 = (bf16[32,768]{1,0:T(8,128)(2,1)S(1)}, bf16[32,768]{1,0:T(8,128)(2,1)S(1)}, u32[]{:S(2)}, u32[]{:S(2)}) collective-permute-start(bf16[32,768]{1,0:T(8,128)(2,1)S(1)} %add_convert_fusion.1), channel_id=1, source_target_pairs={{0,16},{16,0},{1,17},{17,1},{2,18},{18,2},{3,19},{19,3},{4,20},{20... | collective-permute-start | bytes 147464 | tf_op jit(solution)/shard_map/ppermute | solution.py:573
  45.2 2.4 %shard_map.142.grad_ref = bf16[128,1536]{1,0:T(8,128)(2,1)S(1)} custom-call(f32[160,1536]{1,0:T(8,128)S(1)} %get-tuple-element.81.pad_ref, bf16[128,1536]{1,0:T(8,128)(2,1)S(1)} %get-tuple-element.80.context_ref, f32[3968,128]{1,0:T(8,128)S(1)} %get-tuple-element.55.mask_ref, f32[128,128]{1,0:T(8,128)S(1)} %get-tuple-element.54.keep_ref, ...), custom_call_target="tpu_custom_call" | custom-call | flops 3000000000 | bytes 4456448 | tf_op jit(solution)/shard_map/pallas_call | solution.py:546
  47.6 1.3 %shard_map.143.refs_4_ = bf16[3,128,1536]{2,1,0:T(8,128)(2,1)S(1)} custom-call(bf16[3,128,1536]{2,1,0:T(8,128)(2,1)S(1)} %bitcast.12, bf16[12,128,256]{2,1,0:T(8,128)(2,1)S(1)} %get-tuple-element.79.prob_ref, bf16[128,1536]{1,0:T(8,128)(2,1)S(1)} %get-tuple-element.80.context_ref, bf16[128,1536]{1,0:T(8,128)(2,1)S(1)} %shard_map.142.grad_ref), custom_call_target="tpu_custom_call" | custom-call | flops 4000000000 | bytes 3932160 | tf_op jit(solution)/shard_map/pallas_call | solution.py:546
  48.9 0.0 collective-permute-done.7
  49.0 0.1 collective-permute-start.8
  49.1 1.2 %collective-permute-done.8.refs_1_ = bf16[32,768]{1,0:T(8,128)(2,1)S(1)} collective-permute-done((bf16[32,768]{1,0:T(8,128)(2,1)S(1)}, bf16[32,768]{1,0:T(8,128)(2,1)S(1)}, u32[]{:S(2)}, u32[]{:S(2)}) %collective-permute-start.8) | collective-permute-done | bytes 49184 | tf_op jit(solution)/shard_map/ppermute | solution.py:573
  50.3 0.0 collective-permute-done.9.refs_8_
  50.3 4.7 %collective-permute-done.10.refs_10_ = bf16[3,128,768]{2,1,0:T(8,128)(2,1)S(1)} collective-permute-done((bf16[3,128,768]{2,1,0:T(8,128)(2,1)S(1)}, bf16[3,128,768]{2,1,0:T(8,128)(2,1)S(1)}, u32[]{:S(2)}, u32[]{:S(2)}) %collective-permute-start.10) | collective-permute-done | bytes 589856 | tf_op jit(solution)/shard_map/ppermute | solution.py:669
  55.0 1.4 %shard_map.145 = (f32[1536]{0:T(1024)}, f32[31,1536]{1,0:T(8,128)}, f32[1536]{0:T(1024)}, bf16[128,1536]{1,0:T(8,128)(2,1)}, bf16[128,1536]{1,0:T(8,128)(2,1)}, ...) custom-call(bf16[32,768]{1,0:T(8,128)(2,1)S(1)} %add_convert_fusion.refs_0_, ...), custom_call_target="tpu_custom_call" | custom-call | flops 1000000000 | bytes 6395904 | tf_op jit(solution)/shard_map/pallas_call | solution.py:546
  (5 shorter events, 0.1 us)
Async XLA Ops:
  0.6 4.1 %copy-start.1 = (bf16[1,128,1536]{2,1,0:T(8,128)(2,1)S(1)}, bf16[1,128,1536]{2,1,0:T(8,128)(2,1)}, u32[]{:S(2)}) copy-start(bf16[1,128,1536]{2,1,0:T(8,128)(2,1)} %param.15) | copy-start | bytes 1179652
  0.6 6.9 %copy-start.4 = (s32[1,2048]{1,0:T(1,128)S(1)}, s32[1,2048]{1,0:T(1,128)}, u32[]{:S(2)}) copy-start(s32[1,2048]{1,0:T(1,128)} %seg_ref.11) | copy-start | bytes 24580
  2.0 16.4 %collective-permute-start.1 = (bf16[384,1536]{1,0:T(8,128)(2,1)S(1)}, bf16[384,1536]{1,0:T(8,128)(2,1)S(1)}, u32[]{:S(2)}, u32[]{:S(2)}) collective-permute-start(bf16[384,1536]{1,0:T(8,128)(2,1)S(1)} %pad_maximum_fusion), channel_id=1, source_target_pairs={{1,0},{2,1},{3,2},{4,3},{5,4},{6,5},{7,6},{8,7},{9,8},{10,9},{11,1... | collective-permute-start | bytes 3538952 | tf_op jit(solution)/shard_map/ppermute | solution.py:589
  4.8 3.1 %copy-start = (f32[31,1536]{1,0:T(8,128)S(1)}, f32[31,1536]{1,0:T(8,128)}, u32[]{:S(2)}) copy-start(f32[31,1536]{1,0:T(8,128)} %refs_2_.1) | copy-start | bytes 571396
  4.8 3.1 %copy-start.2 = (f32[1536]{0:T(1024)S(1)}, f32[1536]{0:T(1024)}, u32[]{:S(2)}) copy-start(f32[1536]{0:T(1024)} %gain_row.1) | copy-start | bytes 18436
  4.8 3.1 %copy-start.3 = (f32[1536]{0:T(1024)S(1)}, f32[1536]{0:T(1024)}, u32[]{:S(2)}) copy-start(f32[1536]{0:T(1024)} %bias_row.1) | copy-start | bytes 18436
  4.8 17.9 %collective-permute-start = (bf16[128,1536]{1,0:T(8,128)(2,1)S(1)}, bf16[128,1536]{1,0:T(8,128)(2,1)S(1)}, u32[]{:S(2)}, u32[]{:S(2)}) collective-permute-start(bf16[128,1536]{1,0:T(8,128)(2,1)S(1)} %bitcast.14), channel_id=1, source_target_pairs={{1,0},{2,1},{3,2},{4,3},{5,4},{6,5},{7,6},{8,7},{9,8},{10,9},{11,1... | collective-permute-start | bytes 1179656 | tf_op jit(solution)/shard_map/ppermute | solution.py:591
  25.1 1.9 %collective-permute-start.2 = (bf16[32,768]{1,0:T(8,128)(2,1)S(1)}, bf16[32,768]{1,0:T(8,128)(2,1)S(1)}, u32[]{:S(2)}, u32[]{:S(2)}) collective-permute-start(bf16[32,768]{1,0:T(8,128)(2,1)S(1)} %get-tuple-element.64), channel_id=1, source_target_pairs={{0,1},{1,0},{2,3},{3,2},{4,5},{5,4},{6,7},{7,6},{8,9},{9,8},{10,11... | collective-permute-start | bytes 147464 | tf_op jit(solution)/shard_map/ppermute | solution.py:573
  27.0 7.9 %collective-permute-start.3 = (bf16[32,768]{1,0:T(8,128)(2,1)S(1)}, bf16[32,768]{1,0:T(8,128)(2,1)S(1)}, u32[]{:S(2)}, u32[]{:S(2)}) collective-permute-start(bf16[32,768]{1,0:T(8,128)(2,1)S(1)} %add_convert_fusion.4), channel_id=1, source_target_pairs={{0,2},{1,3},{2,0},{3,1},{4,6},{5,7},{6,4},{7,5},{8,10},{9,11},{10,... | collective-permute-start | bytes 147464 | tf_op jit(solution)/shard_map/ppermute | solution.py:573
  29.4 10.6 %collective-permute-start.5 = (bf16[128,1536]{1,0:T(8,128)(2,1)S(1)}, bf16[128,1536]{1,0:T(8,128)(2,1)S(1)}, u32[]{:S(2)}, u32[]{:S(2)}) collective-permute-start(bf16[128,1536]{1,0:T(8,128)(2,1)S(1)} %get-tuple-element.77), channel_id=1, source_target_pairs={{0,1},{1,2},{2,3},{3,4},{4,5},{5,6},{6,7},{7,8},{8,9},{9,10},{10,1... | collective-permute-start | bytes 1179656 | tf_op jit(solution)/shard_map/ppermute | solution.py:648
  34.9 5.1 %collective-permute-start.4 = (bf16[32,768]{1,0:T(8,128)(2,1)S(1)}, bf16[32,768]{1,0:T(8,128)(2,1)S(1)}, u32[]{:S(2)}, u32[]{:S(2)}) collective-permute-start(bf16[32,768]{1,0:T(8,128)(2,1)S(1)} %add_convert_fusion.3), channel_id=1, source_target_pairs={{0,8},{1,9},{2,10},{3,11},{4,12},{5,13},{6,14},{7,15},{8,0},{9,1},... | collective-permute-start | bytes 147464 | tf_op jit(solution)/shard_map/ppermute | solution.py:573
  35.5 14.8 %collective-permute-start.9 = (bf16[3,128,768]{2,1,0:T(8,128)(2,1)S(1)}, bf16[3,128,768]{2,1,0:T(8,128)(2,1)S(1)}, u32[]{:S(2)}, u32[]{:S(2)}) collective-permute-start(bf16[3,128,768]{2,1,0:T(8,128)(2,1)S(1)} %get-tuple-element.86), channel_id=1, source_target_pairs={{0,1},{1,2},{2,3},{3,4},{4,5},{5,6},{6,7},{7,8},{8,9},{9,10},{10,1... | collective-permute-start | bytes 1769480 | tf_op jit(solution)/shard_map/ppermute | solution.py:669
  40.0 4.7 %collective-permute-start.6 = (bf16[32,768]{1,0:T(8,128)(2,1)S(1)}, bf16[32,768]{1,0:T(8,128)(2,1)S(1)}, u32[]{:S(2)}, u32[]{:S(2)}) collective-permute-start(bf16[32,768]{1,0:T(8,128)(2,1)S(1)} %add_convert_fusion.2), channel_id=1, source_target_pairs={{0,4},{1,5},{2,6},{3,7},{4,0},{5,1},{6,2},{7,3},{8,12},{9,13},{10,... | collective-permute-start | bytes 147464 | tf_op jit(solution)/shard_map/ppermute | solution.py:573
  42.7 12.3 %collective-permute-start.10 = (bf16[3,128,768]{2,1,0:T(8,128)(2,1)S(1)}, bf16[3,128,768]{2,1,0:T(8,128)(2,1)S(1)}, u32[]{:S(2)}, u32[]{:S(2)}) collective-permute-start(bf16[3,128,768]{2,1,0:T(8,128)(2,1)S(1)} %get-tuple-element.91), channel_id=1, source_target_pairs={{0,1},{1,2},{2,3},{3,4},{4,5},{5,6},{6,7},{7,8},{8,9},{9,10},{10,1... | collective-permute-start | bytes 1769480 | tf_op jit(solution)/shard_map/ppermute | solution.py:669
  44.7 4.3 %collective-permute-start.7 = (bf16[32,768]{1,0:T(8,128)(2,1)S(1)}, bf16[32,768]{1,0:T(8,128)(2,1)S(1)}, u32[]{:S(2)}, u32[]{:S(2)}) collective-permute-start(bf16[32,768]{1,0:T(8,128)(2,1)S(1)} %add_convert_fusion.1), channel_id=1, source_target_pairs={{0,16},{16,0},{1,17},{17,1},{2,18},{18,2},{3,19},{19,3},{4,20},{20... | collective-permute-start | bytes 147464 | tf_op jit(solution)/shard_map/ppermute | solution.py:573
  49.0 1.3 %collective-permute-start.8 = (bf16[32,768]{1,0:T(8,128)(2,1)S(1)}, bf16[32,768]{1,0:T(8,128)(2,1)S(1)}, u32[]{:S(2)}, u32[]{:S(2)}) collective-permute-start(bf16[32,768]{1,0:T(8,128)(2,1)S(1)} %add_convert_fusion.refs_0_), channel_id=1, source_target_pairs={{0,1},{1,0},{2,3},{3,2},{4,5},{5,4},{6,7},{7,6},{8,9},{9,8},{10,11... | collective-permute-start | bytes 147464 | tf_op jit(solution)/shard_map/ppermute | solution.py:573
